TPU v7x, 32 devices: a whole 2x2x4 slice. The times are simulated.
32 devices in a mesh: rep: 8 (over z, x), tp: 4 (over y, core).
Axes of the slice: x: 2, y: 2, z: 4, core: 2. Of those that a mesh axis runs over, the one named last changes fastest.
Arguments:
- tokens: bfloat16 [1024, 1024], P('rep', 'tp'), may hold values from -6 to 6
- attn_gain: float32 [1024], replicated, may hold values from 0.1 to 1.9
- ffn_gain: float32 [1024], replicated, may hold values from 0.1 to 1.9
- w_query: bfloat16 [1024, 1024], P(None, 'tp'), may hold values from -0.0625 to 0.0625
- w_key: bfloat16 [1024, 1024], P(None, 'tp'), may hold values from -0.1875 to 0.1875
- w_value: bfloat16 [1024, 1024], P(None, 'tp'), may hold values from -0.1875 to 0.1875
- w_out: bfloat16 [1024, 1024], P('tp'), may hold values from -0.1875 to 0.1875
- w_inner: bfloat16 [1024, 2048], P(None, 'tp'), may hold values from -0.1875 to 0.1875
- w_outer: bfloat16 [2048, 1024], P('tp'), may hold values from -0.125 to 0.125
- bias_table: float32 [32, 16], P(None, 'tp'), may hold values from -3 to 3
- cache_keys: bfloat16 [16, 64, 1024], P('rep', None, 'tp'), may hold values from -68 to 68
- cache_values: bfloat16 [16, 64, 1024], P('rep', None, 'tp'), may hold values from -6 to 6
- new_counts: int32 [2, 8], P(None, 'rep'), may hold values from 1 to 64, 256 in all within a row
- cached_lengths: int32 [2, 8], P(None, 'rep'), may hold values from 1 to 64, 256 in all within a row
- deal: int32 [8, 128], P('rep'), may hold values from 0 to 127, each once within a row
Outputs:
- dealt: bfloat16 [1024, 1024], P('rep', 'tp')
Inputs may be any that keep to these rules, and one draw needn't show every extreme that they name: `new_counts`: for each j the counts over the replicas sum to 256. `cached_lengths`: for each j the lengths over the replicas sum to 256. `deal`: each row holds every number of 0 to 127 once.
All inputs are finite; a program needn't handle non-finite values. No bound on the sum of `new_counts` or of `cached_lengths` on one device may be relied on, other than what follows from the above.
Results may differ from a plain program's by a relative error of at most 0.013.
The roundings to bfloat16 on the way count: a program that leaves them out, or rounds other values in their place, can miss the bound.
Values may be sent and summed in bfloat16 or wider, within the bound.
No kernel may reach another device: no remote copies, remote signals or barrier semaphores. Data moves between devices by JAX's collectives and lax.ppermute only.
A program may use at most 64 MiB of HBM per device.

v0:
```python
import jax
import jax.numpy as jnp
from jax import lax
from jax.sharding import PartitionSpec as P

EPSILON = 1e-06
THRESHOLDS = (12, 16, 23, 32, 46, 64, 91)


def bucket_of(relative):
    distance = jnp.abs(relative)
    larger = 8 + sum(((distance >= threshold).astype(jnp.int32) for threshold in THRESHOLDS))
    near = jnp.where(distance < 8, distance, larger)
    return near + 16 * (relative > 0).astype(jnp.int32)


def arrange(values, order, replicas):
    placed = jnp.zeros_like(values).at[order].set(values)
    return placed.reshape(values.shape[0] // replicas, replicas, values.shape[1])


def on_device(
    tokens,
    attn_gain,
    ffn_gain,
    w_query,
    w_key,
    w_value,
    w_out,
    w_inner,
    w_outer,
    bias_table,
    cache_keys,
    cache_values,
    new_counts,
    cached_lengths,
    deal,
):
    requests, cached, local_width = cache_keys.shape
    token_rows = tokens.shape[0]
    new_slots = token_rows // requests
    head_count = bias_table.shape[1]
    head_size = local_width // head_count
    replicas = lax.axis_size("rep")
    share_width = tokens.shape[1]
    first_col = lax.axis_index("tp") * share_width
    gathered = lax.all_gather(tokens, "tp", axis=1, tiled=True)
    model_width = gathered.shape[1]
    stream = gathered.astype(jnp.float32)
    inverse = lax.rsqrt(jnp.mean(stream * stream, axis=1, keepdims=True) + EPSILON)
    normed = (stream * inverse * attn_gain).astype(jnp.bfloat16)
    queries = jnp.dot(normed, w_query, preferred_element_type=jnp.float32).astype(jnp.bfloat16)
    new_keys = jnp.dot(normed, w_key, preferred_element_type=jnp.float32).astype(jnp.bfloat16)
    new_values = jnp.dot(normed, w_value, preferred_element_type=jnp.float32).astype(jnp.bfloat16)
    key_slots = cached + new_slots
    queries = queries.reshape(requests, new_slots, head_count, head_size)
    all_keys = jnp.concatenate(
        [cache_keys, new_keys.reshape(requests, new_slots, local_width)], axis=1
    ).reshape(requests, key_slots, head_count, head_size)
    all_values = jnp.concatenate(
        [cache_values, new_values.reshape(requests, new_slots, local_width)], axis=1
    ).reshape(requests, key_slots, head_count, head_size)
    counts = new_counts[:, 0]
    lengths = cached_lengths[:, 0]
    key_index = jnp.arange(key_slots, dtype=jnp.int32)
    offsets = jnp.arange(new_slots, dtype=jnp.int32)
    is_cache = key_index[None, :] < cached
    key_position = jnp.where(
        is_cache, key_index[None, :], lengths[:, None] + key_index[None, :] - cached
    )
    live_key = jnp.where(
        is_cache,
        key_index[None, :] < lengths[:, None],
        key_index[None, :] - cached < counts[:, None],
    )
    relative = key_position[:, None, :] - (lengths[:, None] + offsets[None, :])[:, :, None]
    rel_bias = jnp.take(bias_table.T, bucket_of(relative), axis=1)
    scores = jnp.einsum("gqhd,gkhd->ghqk", queries, all_keys, preferred_element_type=jnp.float32)
    scores = scores + jnp.moveaxis(rel_bias, 0, 1)
    scores = jnp.where(live_key[:, None, None, :], scores, -1e30)
    row_max = jnp.max(scores, axis=3, keepdims=True)
    weights = jnp.exp(scores - row_max)
    attn_probs = (weights / jnp.sum(weights, axis=3, keepdims=True)).astype(jnp.bfloat16)
    context = jnp.einsum(
        "ghqk,gkhd->gqhd", attn_probs, all_values, preferred_element_type=jnp.float32
    )
    context = context.astype(jnp.bfloat16).reshape(token_rows, local_width)
    partial_value = jnp.dot(context, w_out, preferred_element_type=jnp.float32)
    live_rows = (offsets[None, :] < counts[:, None]).reshape(token_rows, 1)
    order = deal[0]
    summed = lax.psum(partial_value, "tp")
    mixed = jnp.where(live_rows, stream + summed, 0.0)
    dealt_rows = lax.all_to_all(
        arrange(mixed, order, replicas), "rep", split_axis=1, concat_axis=0, tiled=True
    ).reshape(token_rows, model_width)
    inverse_ffn = lax.rsqrt(jnp.mean(dealt_rows * dealt_rows, axis=1, keepdims=True) + EPSILON)
    ffn_input = (dealt_rows * inverse_ffn * ffn_gain).astype(jnp.bfloat16)
    own_cols = lax.dynamic_slice_in_dim(dealt_rows, first_col, share_width, 1)
    hidden = jnp.maximum(
        jnp.dot(ffn_input, w_inner, preferred_element_type=jnp.float32), 0.0
    ).astype(jnp.bfloat16)
    projected = jnp.dot(hidden, w_outer, preferred_element_type=jnp.float32)
    ffn_share = lax.psum_scatter(
        projected.astype(jnp.bfloat16), "tp", scatter_dimension=1, tiled=True
    ).astype(jnp.float32)
    return (own_cols + ffn_share).astype(jnp.bfloat16)


def solution(mesh):
    in_specs = (
        P("rep", "tp"),
        P(),
        P(),
        P(None, "tp"),
        P(None, "tp"),
        P(None, "tp"),
        P("tp", None),
        P(None, "tp"),
        P("tp", None),
        P(None, "tp"),
        P("rep", None, "tp"),
        P("rep", None, "tp"),
        P(None, "rep"),
        P(None, "rep"),
        P("rep", None),
    )
    out_specs = P("rep", "tp")
    return jax.shard_map(
        on_device, mesh=mesh, in_specs=in_specs, out_specs=out_specs, check_vma=False
    )
```

profile of v0, /device:TPU:0, one launch (start us, length us, event | category | flops | bytes accessed | tf_op | source)
XLA Modules:
  0.0 169.3 jit_solution(4046229286145538980)
XLA Ops:
  6.5 0.0 copy-start
  6.5 0.0 all-reduce.2.cloned.1.call-start
  6.6 0.8 iota_add_fusion
  7.4 0.7 add_select_fusion
  8.1 0.1 compare_select_fusion
  8.3 0.2 compare_and_fusion
  8.5 7.4 %all_gather.3 = bf16[128,1024]{1,0:T(8,128)(2,1)S(1)} all-gather(bf16[128,256]{1,0:T(8,128)(2,1)} %param.15), channel_id=1, replica_groups=mesh['rep'=8,'tp'=4] {'tp'}, dimensions={1}, use_global_device_ids=true | all-gather | bytes 327680 | tf_op jit(solution)/shard_map/all_gather | solution.py:47
  15.9 0.1 fusion.6
  16.0 1.3 convolution_convert_fusion.2
  17.4 0.1 concatenate.20
  17.5 0.1 copy.48
  17.6 1.3 convolution_convert_fusion.3
  19.0 0.1 reshape.314
  19.1 0.8 copy.50
  19.9 54.4 %gather_fusion = f32[16384,4]{1,0:T(8,128)} fusion(f32[4,32]{0,1:T(8,128)S(1)} %bitcast.33, s32[16384]{0:T(1024)S(1)} %broadcast_clamp_fusion), kind=kCustom, calls=%fused_computation | custom fusion | bytes 589824 | tf_op jit(solution)/shard_map/jit(_take)/gather | solution.py:77
  74.3 5.3 %copy.52 = f32[2,64,128,4]{2,1,3,0:T(8,128)S(1)} copy(f32[2,64,128,4]{3,2,1,0:T(8,128)} %bitcast.34) | data formatting | bytes 524288 | tf_op jit(solution)/shard_map/jit(_take)/gather | solution.py:77
  79.6 0.0 copy-done.2
  79.7 0.1 copy.47
  79.8 0.0 copy-done.5
  79.8 0.0 copy-done.6
  79.8 0.1 compare_select_fusion.5
  79.9 0.2 fusion.2
  80.1 0.2 fusion.52
  80.4 0.0 copy-done.7
  80.4 1.3 convolution_convert_fusion.4
  81.7 0.1 concatenate.17
  81.8 0.1 copy.46
  82.0 0.0 copy-done.3
  82.0 0.1 copy.45
  82.1 1.0 fusion.5
  83.2 0.1 copy.53
  83.3 0.1 reshape.315
  83.5 2.1 %fusion.53 = f32[128,1024]{1,0:T(8,128)} fusion(bf16[128,256]{1,0:T(8,128)(2,1)S(1)} %reshape.315, bf16[256,1024]{1,0:T(8,128)(2,1)} %param.21), kind=kOutput, calls=%fused_computation.82 | convolution fusion | flops 67108864 | bytes 1114112 | tf_op jit(solution)/shard_map/dot_general | solution.py:88
  85.5 0.0 all-reduce.2.cloned.1.call-update
  85.6 0.0 reduce-scatter.2.cloned.1.call-start
  85.6 0.1 iota_compare_fusion
  85.7 0.1 lt.127
  85.8 0.0 copy-done.8
  85.8 34.4 %all-reduce.2.cloned.1.call-done = f32[128,1024]{1,0:T(8,128)} async-done(((f32[128,1024]{1,0:T(8,128)}), f32[128,1024]{1,0:T(8,128)}) %all-reduce.2.cloned.1.call-update) | async-done | bytes 524304 | tf_op jit(solution)/shard_map/psum | solution.py:91
  120.2 1.7 %scatter_custom_fusion = f32[128,1024]{1,0:T(8,128)S(1)} fusion(s32[128]{0:T(128)S(1)} %fusion.44, f32[]{:T(128)} %constant.21.clone.1, f32[128,1024]{1,0:T(8,128)} %all-reduce.2.cloned.1.call-done, bf16[128,1024]{1,0:T(8,128)(2,1)S(1)} %all_gather.3, pred[128]{0:T(512)(128)(4,1)S(1)} %lt.127), kind=kCustom, calls=%fused_computation.28 | custom fusion | flops 393216 | bytes 1312256 | tf_op jit(solution)/shard_map/scatter | solution.py:18
  121.9 0.3 copy.54
  122.3 18.9 %all_to_all.15 = f32[16,8,1024]{2,0,1:T(8,128)S(1)} all-to-all(f32[16,8,1024]{2,0,1:T(8,128)S(1)} %copy.54), channel_id=1, replica_groups=mesh['rep'=8,'tp'=4] {'rep'}, dimensions={1} | all-to-all | bytes 1048576 | tf_op jit(solution)/shard_map/all_to_all | solution.py:93
  141.1 0.1 fusion.10
  141.2 0.1 rsqrt.21
  141.3 1.3 convolution_convert_fusion
  142.6 0.0 reduce-scatter.2.cloned.1.call-update
  142.7 18.3 %reduce-scatter.2.cloned.1.call-done = bf16[128,256]{1,0:T(8,128)(2,1)} async-done(((bf16[128,1024]{1,0:T(8,128)(2,1)}), bf16[128,256]{1,0:T(8,128)(2,1)}) %reduce-scatter.2.cloned.1.call-update) | async-done | bytes 65552 | tf_op jit(solution)/shard_map/reduce_scatter | solution.py:103
  161.0 1.5 add_convert_fusion
  (17 shorter events, 0.1 us)
Async XLA Ops:
  6.5 134.8 %copy-start = (bf16[512,1024]{1,0:T(8,128)(2,1)S(1)}, bf16[512,1024]{1,0:T(8,128)(2,1)}, u32[]{:S(2)}) copy-start(bf16[512,1024]{1,0:T(8,128)(2,1)} %param.23) | copy-start | bytes 3145732
  6.5 73.2 %copy-start.5 = (s32[2,1]{0,1:T(1,128)S(1)}, s32[2,1]{0,1:T(1,128)}, u32[]{:S(2)}) copy-start(s32[2,1]{0,1:T(1,128)} %param.28) | copy-start | bytes 28
  6.5 73.8 %copy-start.7 = (f32[1024]{0:T(1024)S(1)}, f32[1024]{0:T(1024)}, u32[]{:S(2)}) copy-start(f32[1024]{0:T(1024)} %param.16) | copy-start | bytes 12292
  6.5 73.1 %copy-start.2 = (bf16[2,64,256]{2,1,0:T(8,128)(2,1)S(1)}, bf16[2,64,256]{2,1,0:T(8,128)(2,1)}, u32[]{:S(2)}) copy-start(bf16[2,64,256]{2,1,0:T(8,128)(2,1)} %param.25) | copy-start | bytes 196612
  6.5 73.2 %copy-start.6 = (s32[2,1]{0,1:T(1,128)S(1)}, s32[2,1]{0,1:T(1,128)}, u32[]{:S(2)}) copy-start(s32[2,1]{0,1:T(1,128)} %param.27) | copy-start | bytes 28
  6.5 113.6 %all-reduce.2.cloned.1.call-start = ((), (), s32[]{:S(2)}) async-start(), calls=%async_computation.2 | async-start | bytes 1048576 | tf_op jit(solution)/shard_map/psum | solution.py:91
  15.9 66.1 %copy-start.3 = (bf16[2,64,256]{2,1,0:T(8,128)(2,1)S(1)}, bf16[2,64,256]{2,1,0:T(8,128)(2,1)}, u32[]{:S(2)}) copy-start(bf16[2,64,256]{2,1,0:T(8,128)(2,1)} %param.26) | copy-start | bytes 196612
  19.9 65.9 %copy-start.8 = (s32[1,128]{1,0:T(1,128)S(1)}, s32[1,128]{1,0:T(1,128)}, u32[]{:S(2)}) copy-start(s32[1,128]{1,0:T(1,128)} %param.29) | copy-start | bytes 1540
  74.3 67.0 %copy-start.1 = (bf16[1024,512]{1,0:T(8,128)(2,1)S(1)}, bf16[1024,512]{1,0:T(8,128)(2,1)}, u32[]{:S(2)}) copy-start(bf16[1024,512]{1,0:T(8,128)(2,1)} %param.22) | copy-start | bytes 3145732
  74.3 67.0 %copy-start.4 = (f32[1024]{0:T(1024)S(1)}, f32[1024]{0:T(1024)}, u32[]{:S(2)}) copy-start(f32[1024]{0:T(1024)} %param.17) | copy-start | bytes 12292
  85.6 75.4 %reduce-scatter.2.cloned.1.call-start = ((), (), s32[]{:S(2)}) async-start(), calls=%async_computation.3 | async-start | bytes 327680 | tf_op jit(solution)/shard_map/reduce_scatter | solution.py:103
Sparse Core Ops, SparseCore 0:
  85.7 34.4 all-reduce.1
  142.8 18.1 reduce-scatter.1
where the time goes:
time: 170 us; the launch traced here: 169 us
  local copies, waits for them, and re-layouts  62.2 us (37%)
  waiting for transfers between devices  52.8 us (31%)
  blocking collectives  26.3 us (15%)
  between operations  13.6 us (8%)
  matrix products  8.65 us (5%)
  other arithmetic  5.74 us (3%)
    gather x2, local copies, waits for them, and re-layouts, on_device(): rel_bias = jnp.take(bias_table.T, bucket_of(relative), axis=1)  59.7 us
    psum x1, waiting for transfers between devices, on_device(): summed = lax.psum(partial_value, 'tp')  34.4 us
    all_to_all x1, blocking collectives, on_device(): lax.all_to_all(arrange(mixed, order, replicas), 'rep', split_axis=1, conc...  18.9 us
    reduce_scatter x1, waiting for transfers between devices, on_device(): lax.psum_scatter(projected.astype(jnp.bfloat16), 'tp', scatter_dimension=...  18.3 us
    all_gather x1, blocking collectives, on_device(): gathered = lax.all_gather(tokens, 'tp', axis=1, tiled=True)  7.43 us
  transfers between devices with their start and end apart: 2, of which 2 were waited for; matrix products, arithmetic and copies ran while one was open for 0% of the time, Pallas kernels for 0%

commit v1 on v0

v1 whole, which is shorter than its diff:
```python
import functools

import jax
import jax.numpy as jnp
from jax import lax
from jax.experimental import pallas as pl
from jax.experimental.pallas import tpu as pltpu
from jax.sharding import Mesh, PartitionSpec as P

EPSILON = 1e-06
THRESHOLDS = (1, 2, 3, 4, 5, 6, 7, 8, 12, 16, 23, 32, 46, 64, 91)
BF16 = jnp.bfloat16
F32 = jnp.float32
VMEM = pl.BlockSpec(memory_space=pltpu.VMEM)
SMEM = pl.BlockSpec(memory_space=pltpu.SMEM)
VMEM_LIMIT = 24 * 1024 * 1024


def dot(a, b):
    return jnp.dot(a, b, preferred_element_type=F32)


def deal_matrix(deal, counts_ref, replicas, new_slots, half, core):
    rows = deal.shape[1]
    share = rows // replicas
    lane = lax.broadcasted_iota(jnp.int32, (1, rows), 1)
    live = jnp.zeros((1, rows), jnp.bool_)
    for j in range(rows // new_slots):
        offset = lane - j * new_slots
        live = live | ((offset >= 0) & (offset < jnp.minimum(counts_ref[j, 0], new_slots)))
    slot = lax.rem(deal, replicas) * share + lax.div(deal, replicas)
    slot = jnp.where(live, slot, -1)
    row = lax.broadcasted_iota(jnp.int32, (rows, rows), 0)
    row = jnp.where(core == 0, row, jnp.where(row < half, row + half, row - half))
    return jnp.where(row == slot, 1.0, 0.0).astype(BF16)


def bias_of(table_ref, relative, head):
    distance = jnp.abs(relative)
    before = jnp.full(relative.shape, table_ref[0, head], F32)
    after = jnp.full(relative.shape, table_ref[17, head], F32)
    for step, threshold in enumerate(THRESHOLDS):
        far = distance >= threshold
        before = jnp.where(far, table_ref[step + 1, head], before)
        after = jnp.where(far, table_ref[step + 17, head], after)
    return jnp.where(relative > 0, after, before)


def attend_kernel(
    replicas,
    x_ref,
    gain_ref,
    w_query_ref,
    w_key_ref,
    w_value_ref,
    w_out_ref,
    table_ref,
    cache_keys_ref,
    cache_values_ref,
    counts_ref,
    lengths_ref,
    deal_ref,
    keep_ref,
    send_ref,
):
    core = lax.axis_index("lo")
    blocks, rows, width = x_ref.shape
    model_width = blocks * width
    requests, cached, local_width = cache_keys_ref.shape
    new_slots = rows // requests
    head_count = table_ref.shape[1]
    head_size = local_width // head_count
    half = rows // 2

    squares = 0.0
    for b in range(blocks):
        block = x_ref[b].astype(F32)
        squares = squares + jnp.sum(block * block, axis=1, keepdims=True)
    inverse = lax.rsqrt(squares / model_width + EPSILON)
    normed = jnp.concatenate(
        [
            (x_ref[b].astype(F32) * inverse * gain_ref[:, b * width : (b + 1) * width]).astype(BF16)
            for b in range(blocks)
        ],
        axis=1,
    )
    queries = dot(normed, w_query_ref[...]).astype(BF16)
    new_keys = dot(normed, w_key_ref[...]).astype(BF16)
    new_values = dot(normed, w_value_ref[...]).astype(BF16)

    key_slots = cached + new_slots
    lane_head = lax.broadcasted_iota(jnp.int32, (new_slots, local_width), 1) // head_size
    key_index = lax.broadcasted_iota(jnp.int32, (new_slots, key_slots), 1)
    query_index = lax.broadcasted_iota(jnp.int32, (new_slots, key_slots), 0)
    is_cache = key_index < cached
    contexts = []
    for j in range(requests):
        own = slice(j * new_slots, (j + 1) * new_slots)
        length = lengths_ref[j, 0]
        count = counts_ref[j, 0]
        position = jnp.where(is_cache, key_index, length + key_index - cached)
        relative = position - (length + query_index)
        live = jnp.where(is_cache, key_index - length, key_index - cached - count) < 0
        query = queries[own]
        stacked = jnp.concatenate(
            [jnp.where(lane_head == h, query, jnp.zeros_like(query)) for h in range(head_count)],
            axis=0,
        )
        keys = jnp.concatenate([cache_keys_ref[j], new_keys[own]], axis=0)
        values = jnp.concatenate([cache_values_ref[j], new_values[own]], axis=0)
        scores = lax.dot_general(
            stacked, keys, (((1,), (1,)), ((), ())), preferred_element_type=F32
        )
        probs = []
        for h in range(head_count):
            score = scores[h * new_slots : (h + 1) * new_slots]
            score = jnp.where(live, score + bias_of(table_ref, relative, h), -1e30)
            weight = jnp.exp(score - jnp.max(score, axis=1, keepdims=True))
            probs.append((weight / jnp.sum(weight, axis=1, keepdims=True)).astype(BF16))
        mixed = dot(jnp.concatenate(probs, axis=0), values)
        context = jnp.zeros((new_slots, local_width), F32)
        for h in range(head_count):
            context = jnp.where(lane_head == h, mixed[h * new_slots : (h + 1) * new_slots], context)
        contexts.append(context.astype(BF16))
    picked = deal_matrix(deal_ref[...], counts_ref, replicas, new_slots, half, core)
    context = dot(picked, jnp.concatenate(contexts, axis=0)).astype(BF16)
    send_ref[...] = dot(context[half:], w_out_ref[...]).astype(BF16)
    keep_ref[...] = dot(context[:half], w_out_ref[...])


def stream_kernel(replicas, new_slots, x_ref, counts_ref, deal_ref, stream_ref):
    core = lax.axis_index("lo")
    blocks, rows, width = x_ref.shape
    picked = deal_matrix(deal_ref[...], counts_ref, replicas, new_slots, rows // 2, core)
    for b in range(blocks):
        stream_ref[:, b * width : (b + 1) * width] = dot(picked, x_ref[b]).astype(BF16)


def ffn_kernel(own_ref, other_ref, stream_ref, gain_ref, w_inner_ref, w_outer_ref, keep_ref, send_ref):
    core = lax.axis_index("lo")
    upper = lax.axis_index("hi")
    half, model_width = own_ref.shape
    groups, _, width = keep_ref.shape
    for part, ref in enumerate((own_ref, other_ref)):
        start = pl.multiple_of(lax.rem(core + part, 2) * half, half)
        mixed = ref[...].astype(F32) + stream_ref[part * half : (part + 1) * half].astype(F32)
        square = jnp.sum(mixed * mixed, axis=1, keepdims=True)
        inverse = lax.rsqrt(square / model_width + EPSILON)
        ffn_input = (mixed * inverse * gain_ref[...]).astype(BF16)
        hidden = jnp.maximum(dot(ffn_input, w_inner_ref[...]), 0.0).astype(BF16)
        projected = dot(hidden, w_outer_ref[...])
        for g in range(groups):
            for c in range(2):
                columns = slice((g * 2 + c) * width, (g * 2 + c + 1) * width)
                mine = (upper == g) & (core == c)
                value = projected[:, columns] + jnp.where(mine, mixed[:, columns], 0.0)

                @pl.when(core == c)
                def _():
                    keep_ref[g, pl.ds(start, half), :] = value

                @pl.when(core != c)
                def _():
                    send_ref[g, pl.ds(start, half), :] = value.astype(BF16)


def swap(value, axis):
    return lax.ppermute(value, axis, [(0, 1), (1, 0)])


def on_device(
    replicas,
    tokens,
    attn_gain,
    ffn_gain,
    w_query,
    w_key,
    w_value,
    w_out,
    w_inner,
    w_outer,
    bias_table,
    cache_keys,
    cache_values,
    new_counts,
    cached_lengths,
    deal,
):
    rows, width = tokens.shape
    requests = cache_keys.shape[0]
    new_slots = rows // requests
    model_width = attn_gain.shape[0]
    half = rows // 2
    params = pltpu.CompilerParams(vmem_limit_bytes=VMEM_LIMIT)
    x = lax.all_gather(tokens, ("hi", "lo"), axis=0, tiled=False)
    keep, send = pl.pallas_call(
        functools.partial(attend_kernel, replicas),
        out_shape=(
            jax.ShapeDtypeStruct((half, model_width), F32),
            jax.ShapeDtypeStruct((half, model_width), BF16),
        ),
        in_specs=[VMEM] * 6 + [SMEM] + [VMEM] * 2 + [SMEM] * 2 + [VMEM],
        out_specs=(VMEM, VMEM),
        compiler_params=params,
        name="attend",
    )(
        x,
        attn_gain.reshape(1, model_width),
        w_query,
        w_key,
        w_value,
        w_out,
        bias_table,
        cache_keys,
        cache_values,
        new_counts,
        cached_lengths,
        deal,
    )
    stream = pl.pallas_call(
        functools.partial(stream_kernel, replicas, new_slots),
        out_shape=jax.ShapeDtypeStruct((rows, model_width), BF16),
        in_specs=[VMEM, SMEM, VMEM],
        out_specs=VMEM,
        compiler_params=params,
        name="stream",
    )(x, new_counts, deal)
    pair = (keep + swap(send, "lo").astype(F32)).astype(BF16)
    total = (pair.astype(F32) + swap(pair, "hi").astype(F32)).astype(BF16)
    other = swap(total, "lo")
    groups = lax.axis_size("hi")
    keep, send = pl.pallas_call(
        ffn_kernel,
        out_shape=(
            jax.ShapeDtypeStruct((groups, rows, width), F32),
            jax.ShapeDtypeStruct((groups, rows, width), BF16),
        ),
        in_specs=[VMEM] * 6,
        out_specs=(VMEM, VMEM),
        compiler_params=params,
        name="ffn",
    )(total, other, stream, ffn_gain.reshape(1, model_width), w_inner, w_outer)
    pair = (keep + swap(send, "lo").astype(F32)).astype(BF16)
    parts = lax.all_to_all(
        pair.reshape(groups * replicas, rows // replicas, width), ("hi", "rep"), 0, 0, tiled=True
    )
    return jnp.sum(parts.reshape(groups, rows, width).astype(F32), axis=0).astype(BF16)


def solution(mesh):
    replicas, tp = mesh.shape["rep"], mesh.shape["tp"]
    split = Mesh(mesh.devices.reshape(replicas, tp // 2, 2), ("rep", "hi", "lo"))
    cols = ("hi", "lo")
    in_specs = (
        P("rep", cols),
        P(),
        P(),
        P(None, cols),
        P(None, cols),
        P(None, cols),
        P(cols, None),
        P(None, cols),
        P(cols, None),
        P(None, cols),
        P("rep", None, cols),
        P("rep", None, cols),
        P(None, "rep"),
        P(None, "rep"),
        P("rep", None),
    )
    return jax.shard_map(
        functools.partial(on_device, replicas),
        mesh=split,
        in_specs=in_specs,
        out_specs=P("rep", cols),
        check_vma=False,
    )
```

time: 170 us -> 42.9 us (0.25)
  local copies, waits for them, and re-layouts: 62.2 us -> 5.69 us
  waiting for transfers between devices: 52.8 us -> 6.97 us
  between operations: 13.6 us -> 0.08 us
  matrix products: 8.65 us -> 0 us
  other arithmetic: 5.74 us -> 0.74 us
  Pallas kernels: 0 us -> 4.66 us
  blocking collectives: 26.3 us -> 22 us
  starting transfers between devices: 0.08 us -> 2.3 us
    gather x2 -> x0, local copies, waits for them, and re-layouts: 59.7 us -> none  [on_device(): rel_bias = jnp.take(bias_table.T, bucket_of(relative), axis=1)]
    psum x1 -> x0, waiting for transfers between devices: 34.4 us -> none  [on_device(): summed = lax.psum(partial_value, 'tp')]
    reduce_scatter x1 -> x0, waiting for transfers between devices: 18.3 us -> none  [on_device(): lax.psum_scatter(projected.astype(jnp.bfloat16), 'tp', scatter_dimension=...]
    dot_general x7 -> x0, matrix products: 8.65 us -> none  [the longest x1 2.09 us: on_device(): partial_value = jnp.dot(context, w_out, preferred_element_type=jnp.float32)]
    ppermute x0 -> x4, waiting for transfers between devices: none -> 6.97 us  [swap(): return lax.ppermute(value, axis, [(0, 1), (1, 0)])]
    pallas_call x0 -> x3, Pallas kernels: none -> 4.66 us  [the longest x1 2.57 us: on_device(): pl.pallas_call(functools.partial(attend_kernel, replicas), out_shape=(jax...]
    unnamed x21 -> x31, local copies, waits for them, and re-layouts: 1.04 us -> 5.69 us
    all_to_all x1, blocking collectives: 18.9 us -> 14.5 us  [on_device(): lax.all_to_all(pair.reshape(groups * replicas, rows // replicas, width),...]
  transfers between devices with their start and end apart: 2 -> 4, of which waited for: 2 -> 4; matrix products, arithmetic and copies ran while one was open for 0% -> 0% of each run, Pallas kernels for 0% -> 2%
where the time goes in v1:
time: 42.9 us; the launch traced here: 42.5 us
  blocking collectives  22 us (51%)
  waiting for transfers between devices  6.97 us (16%)
  local copies, waits for them, and re-layouts  5.69 us (13%)
  Pallas kernels  4.66 us (11%)
  starting transfers between devices  2.3 us (5%)
  other arithmetic  0.74 us (2%)
    all_to_all x1, blocking collectives, on_device(): lax.all_to_all(pair.reshape(groups * replicas, rows // replicas, width),...  14.5 us
    all_gather x1, blocking collectives, on_device(): x = lax.all_gather(tokens, ('hi', 'lo'), axis=0, tiled=False)  7.58 us
    ppermute x4, waiting for transfers between devices, swap(): return lax.ppermute(value, axis, [(0, 1), (1, 0)])  6.97 us
    unnamed x31, local copies, waits for them, and re-layouts  5.69 us
    pallas_call x1, Pallas kernels, on_device(): pl.pallas_call(functools.partial(attend_kernel, replicas), out_shape=(jax...  2.57 us
    ppermute x4, starting transfers between devices, swap(): return lax.ppermute(value, axis, [(0, 1), (1, 0)])  2.3 us
    pallas_call x1, Pallas kernels, on_device(): pl.pallas_call(ffn_kernel, out_shape=(jax.ShapeDtypeStruct((groups, rows,...  1.32 us
  transfers between devices with their start and end apart: 4, of which 4 were waited for; matrix products, arithmetic and copies ran while one was open for 0% of the time, Pallas kernels for 2%

profile of v1, /device:TPU:0, one launch (start us, length us, event | category | flops | bytes accessed | tf_op | source)
XLA Modules:
  0.0 42.5 jit_solution(17666746903868324090)
XLA Ops:
  0.0 0.0 copy-start.12
  0.0 0.0 copy-start.11
  0.0 0.0 copy-start.6
  0.0 0.0 copy-start.7
  0.0 7.6 %all-gather = bf16[512,256]{1,0:T(8,128)(2,1)S(1)} all-gather(bf16[128,256]{1,0:T(8,128)(2,1)} %param.15), channel_id=2, replica_groups=mesh['rep'=8,'hi'=2,'lo'=2] {'hi','lo'}, dimensions={0}, use_global_device_ids=true | all-gather | bytes 327680 | tf_op jit(solution)/shard_map/all_gather | solution.py:195
  7.6 0.0 copy-done.12
  7.6 0.1 copy.17.counts_ref
  7.7 0.0 copy-done.11
  7.7 0.0 copy-start.13
  7.7 0.1 copy.16.table_ref
  7.8 0.6 %copy-done.13 = s32[2,1]{0,1:T(1,128)S(1)} copy-done((s32[2,1]{0,1:T(1,128)S(1)}, s32[2,1]{0,1:T(1,128)}, u32[]{:S(2)}) %copy-start.13) | copy-done | bytes 32
  8.3 0.0 copy-start.8
  8.3 0.1 copy.18.lengths_ref
  8.4 0.0 copy-start.10
  8.4 0.0 copy-done.6
  8.4 0.0 copy-done.7
  8.4 0.6 %copy-done.8 = f32[1024]{0:T(1024)S(1)} copy-done((f32[1024]{0:T(1024)S(1)}, f32[1024]{0:T(1024)}, u32[]{:S(2)}) %copy-start.8) | copy-done | bytes 4120
  9.0 0.1 copy-done.10
  9.1 0.0 copy-start.2
  9.1 1.0 %copy-done.2 = bf16[1024,256]{1,0:T(8,128)(2,1)S(1)} copy-done((bf16[1024,256]{1,0:T(8,128)(2,1)S(1)}, bf16[1024,256]{1,0:T(8,128)(2,1)}, u32[]{:S(2)}) %copy-start.2) | copy-done | bytes 524312
  10.1 0.0 copy-start.3
  10.1 1.0 %copy-done.3 = bf16[1024,256]{1,0:T(8,128)(2,1)S(1)} copy-done((bf16[1024,256]{1,0:T(8,128)(2,1)S(1)}, bf16[1024,256]{1,0:T(8,128)(2,1)}, u32[]{:S(2)}) %copy-start.3) | copy-done | bytes 524312
  11.2 0.0 copy-start.4
  11.2 1.0 %copy-done.4 = bf16[1024,256]{1,0:T(8,128)(2,1)S(1)} copy-done((bf16[1024,256]{1,0:T(8,128)(2,1)S(1)}, bf16[1024,256]{1,0:T(8,128)(2,1)}, u32[]{:S(2)}) %copy-start.4) | copy-done | bytes 524312
  12.2 0.0 copy-start.5
  12.2 1.0 %copy-done.5 = bf16[256,1024]{1,0:T(8,128)(2,1)S(1)} copy-done((bf16[256,1024]{1,0:T(8,128)(2,1)S(1)}, bf16[256,1024]{1,0:T(8,128)(2,1)}, u32[]{:S(2)}) %copy-start.5) | copy-done | bytes 524312
  13.3 0.0 copy-start.1
  13.3 2.6 %attend.1 = (f32[64,1024]{1,0:T(8,128)S(1)}, bf16[64,1024]{1,0:T(8,128)(2,1)S(1)}) custom-call(bf16[4,128,256]{2,1,0:T(8,128)(2,1)S(1)} %bitcast.7, f32[1,1024]{1,0:T(1,128)S(1)} %bitcast.9, bf16[1024,256]{1,0:T(8,128)(2,1)S(1)} %copy-done.2, bf16[1024,256]{1,0:T(8,128)(2,1)S(1)} %copy-done.3, bf16[1024,256]{1,0:T(8,128)(2,1)S(1)} %copy-done.4, ...), custom_call_target="tpu_custom_call" | custom-call | tf_op jit(solution)/shard_map/attend/pallas_call | solution.py:196
  15.8 0.0 copy-start
  15.9 0.4 collective-permute-start
  16.3 1.0 %collective-permute-done = bf16[64,1024]{1,0:T(8,128)(2,1)S(1)} collective-permute-done((bf16[64,1024]{1,0:T(8,128)(2,1)S(1)}, bf16[64,1024]{1,0:T(8,128)(2,1)S(1)}, u32[]{:S(2)}, u32[]{:S(2)}) %collective-permute-start) | collective-permute-done | bytes 131104 | tf_op jit(solution)/shard_map/ppermute | solution.py:168
  17.3 1.6 %collective-permute-start.1 = (bf16[64,1024]{1,0:T(8,128)(2,1)S(1)}, bf16[64,1024]{1,0:T(8,128)(2,1)S(1)}, u32[]{:S(2)}, u32[]{:S(2)}) collective-permute-start(bf16[64,1024]{1,0:T(8,128)(2,1)S(1)} %add_convert_fusion.2), channel_id=1, source_target_pairs={{0,2},{2,0},{1,3},{3,1},{4,6},{6,4},{5,7},{7,5},{8,10},{10,8},{9,1... | collective-permute-start | bytes 393224 | tf_op jit(solution)/shard_map/ppermute | solution.py:168
  18.9 4.2 %collective-permute-done.1 = bf16[64,1024]{1,0:T(8,128)(2,1)S(1)} collective-permute-done((bf16[64,1024]{1,0:T(8,128)(2,1)S(1)}, bf16[64,1024]{1,0:T(8,128)(2,1)S(1)}, u32[]{:S(2)}, u32[]{:S(2)}) %collective-permute-start.1) | collective-permute-done | bytes 131104 | tf_op jit(solution)/shard_map/ppermute | solution.py:168
  23.2 0.1 collective-permute-start.2
  23.2 0.0 copy-start.9
  23.2 0.8 %stream.1.stream_ref = bf16[128,1024]{1,0:T(8,128)(2,1)S(1)} custom-call(bf16[4,128,256]{2,1,0:T(8,128)(2,1)S(1)} %bitcast.8, s32[2,1]{1,0:T(2,128)S(1)} %copy.17.counts_ref, s32[1,128]{1,0:T(1,128)S(1)} %copy-done.10), custom_call_target="tpu_custom_call" | custom-call | tf_op jit(solution)/shard_map/stream/pallas_call | solution.py:220
  24.0 0.6 %collective-permute-done.2.other_ref = bf16[64,1024]{1,0:T(8,128)(2,1)S(1)} collective-permute-done((bf16[64,1024]{1,0:T(8,128)(2,1)S(1)}, bf16[64,1024]{1,0:T(8,128)(2,1)S(1)}, u32[]{:S(2)}, u32[]{:S(2)}) %collective-permute-start.2) | collective-permute-done | bytes 131104 | tf_op jit(solution)/shard_map/ppermute | solution.py:168
  24.6 0.0 copy-done.1
  24.6 0.0 copy-done
  24.6 0.0 copy-done.9
  24.6 1.3 %ffn.1 = (f32[2,128,256]{2,1,0:T(8,128)S(1)}, bf16[2,128,256]{2,1,0:T(8,128)(2,1)S(1)}) custom-call(bf16[64,1024]{1,0:T(8,128)(2,1)S(1)} %add_convert_fusion.1.own_ref, bf16[64,1024]{1,0:T(8,128)(2,1)S(1)} %collective-permute-done.2.other_ref, bf16[128,1024]{1,0:T(8,128)(2,1)S(1)} %stream.1.stream_ref, f32[1,1024]{1,0:T(1,128)S(1)} %bitcast.10, ...), custom_call_target="tpu_custom_call" | custom-call | tf_op jit(solution)/shard_map/ffn/pallas_call | solution.py:232
  25.9 0.2 collective-permute-start.3
  26.1 1.2 %collective-permute-done.3 = bf16[2,128,256]{2,1,0:T(8,128)(2,1)S(1)} collective-permute-done((bf16[2,128,256]{2,1,0:T(8,128)(2,1)S(1)}, bf16[2,128,256]{2,1,0:T(8,128)(2,1)S(1)}, u32[]{:S(2)}, u32[]{:S(2)}) %collective-permute-start.3) | collective-permute-done | bytes 131104 | tf_op jit(solution)/shard_map/ppermute | solution.py:168
  27.4 14.5 %all_to_all.5 = bf16[16,16,256]{2,1,0:T(8,128)(2,1)S(1)} all-to-all(bf16[16,16,256]{2,1,0:T(8,128)(2,1)S(1)} %bitcast.12), channel_id=1, replica_groups=mesh['rep'=8,'hi'=2,'lo'=2] {'hi','rep'}, dimensions={0} | all-to-all | bytes 262144 | tf_op jit(solution)/shard_map/all_to_all | solution.py:244
  41.8 0.6 %bitcast_reduce_fusion = bf16[128,256]{1,0:T(8,128)(2,1)} fusion(bf16[2,128,256]{2,1,0:T(8,128)(2,1)S(1)} %bitcast.11), kind=kLoop, calls=%fused_computation.3 | loop fusion | flops 32768 | bytes 196608 | tf_op jit(solution)/shard_map/reduce_sum | solution.py:247
  (3 shorter events, 0.1 us)
Async XLA Ops:
  0.0 7.6 %copy-start.12 = (s32[2,1]{0,1:T(1,128)S(1)}, s32[2,1]{0,1:T(1,128)}, u32[]{:S(2)}) copy-start(s32[2,1]{0,1:T(1,128)} %param.27) | copy-start | bytes 28
  0.0 7.7 %copy-start.11 = (f32[32,4]{0,1:T(4,128)S(1)}, f32[32,4]{0,1:T(4,128)}, u32[]{:S(2)}) copy-start(f32[32,4]{0,1:T(4,128)} %param.24) | copy-start | bytes 1540
  0.0 8.4 %copy-start.6 = (bf16[2,64,256]{2,1,0:T(8,128)(2,1)S(1)}, bf16[2,64,256]{2,1,0:T(8,128)(2,1)}, u32[]{:S(2)}) copy-start(bf16[2,64,256]{2,1,0:T(8,128)(2,1)} %cache_keys_ref.1) | copy-start | bytes 196612
  0.0 8.4 %copy-start.7 = (bf16[2,64,256]{2,1,0:T(8,128)(2,1)S(1)}, bf16[2,64,256]{2,1,0:T(8,128)(2,1)}, u32[]{:S(2)}) copy-start(bf16[2,64,256]{2,1,0:T(8,128)(2,1)} %cache_values_ref.1) | copy-start | bytes 196612
  7.7 0.7 %copy-start.13 = (s32[2,1]{0,1:T(1,128)S(1)}, s32[2,1]{0,1:T(1,128)}, u32[]{:S(2)}) copy-start(s32[2,1]{0,1:T(1,128)} %param.28) | copy-start | bytes 28
  8.3 0.7 %copy-start.8 = (f32[1024]{0:T(1024)S(1)}, f32[1024]{0:T(1024)}, u32[]{:S(2)}) copy-start(f32[1024]{0:T(1024)} %param.16) | copy-start | bytes 12292
  8.4 0.7 %copy-start.10 = (s32[1,128]{1,0:T(1,128)S(1)}, s32[1,128]{1,0:T(1,128)}, u32[]{:S(2)}) copy-start(s32[1,128]{1,0:T(1,128)} %deal_ref.3) | copy-start | bytes 1540
  9.1 1.0 %copy-start.2 = (bf16[1024,256]{1,0:T(8,128)(2,1)S(1)}, bf16[1024,256]{1,0:T(8,128)(2,1)}, u32[]{:S(2)}) copy-start(bf16[1024,256]{1,0:T(8,128)(2,1)} %w_query_ref.1) | copy-start | bytes 1572868
  10.1 1.0 %copy-start.3 = (bf16[1024,256]{1,0:T(8,128)(2,1)S(1)}, bf16[1024,256]{1,0:T(8,128)(2,1)}, u32[]{:S(2)}) copy-start(bf16[1024,256]{1,0:T(8,128)(2,1)} %w_key_ref.1) | copy-start | bytes 1572868
  11.2 1.0 %copy-start.4 = (bf16[1024,256]{1,0:T(8,128)(2,1)S(1)}, bf16[1024,256]{1,0:T(8,128)(2,1)}, u32[]{:S(2)}) copy-start(bf16[1024,256]{1,0:T(8,128)(2,1)} %w_value_ref.1) | copy-start | bytes 1572868
  12.2 1.0 %copy-start.5 = (bf16[256,1024]{1,0:T(8,128)(2,1)S(1)}, bf16[256,1024]{1,0:T(8,128)(2,1)}, u32[]{:S(2)}) copy-start(bf16[256,1024]{1,0:T(8,128)(2,1)} %w_out_ref.1) | copy-start | bytes 1572868
  13.3 11.3 %copy-start.1 = (bf16[512,1024]{1,0:T(8,128)(2,1)S(1)}, bf16[512,1024]{1,0:T(8,128)(2,1)}, u32[]{:S(2)}) copy-start(bf16[512,1024]{1,0:T(8,128)(2,1)} %w_outer_ref.1) | copy-start | bytes 3145732
  15.8 8.7 %copy-start = (bf16[1024,512]{1,0:T(8,128)(2,1)S(1)}, bf16[1024,512]{1,0:T(8,128)(2,1)}, u32[]{:S(2)}) copy-start(bf16[1024,512]{1,0:T(8,128)(2,1)} %w_inner_ref.1) | copy-start | bytes 3145732
  15.9 1.4 %collective-permute-start = (bf16[64,1024]{1,0:T(8,128)(2,1)S(1)}, bf16[64,1024]{1,0:T(8,128)(2,1)S(1)}, u32[]{:S(2)}, u32[]{:S(2)}) collective-permute-start(bf16[64,1024]{1,0:T(8,128)(2,1)S(1)} %get-tuple-element.10), channel_id=1, source_target_pairs={{0,1},{1,0},{2,3},{3,2},{4,5},{5,4},{6,7},{7,6},{8,9},{9,8},{10,11... | collective-permute-start | bytes 393224 | tf_op jit(solution)/shard_map/ppermute | solution.py:168
  17.3 5.8 %collective-permute-start.1 = (bf16[64,1024]{1,0:T(8,128)(2,1)S(1)}, bf16[64,1024]{1,0:T(8,128)(2,1)S(1)}, u32[]{:S(2)}, u32[]{:S(2)}) collective-permute-start(bf16[64,1024]{1,0:T(8,128)(2,1)S(1)} %add_convert_fusion.2), channel_id=1, source_target_pairs={{0,2},{2,0},{1,3},{3,1},{4,6},{6,4},{5,7},{7,5},{8,10},{10,8},{9,1... | collective-permute-start | bytes 393224 | tf_op jit(solution)/shard_map/ppermute | solution.py:168
  23.2 1.4 %collective-permute-start.2 = (bf16[64,1024]{1,0:T(8,128)(2,1)S(1)}, bf16[64,1024]{1,0:T(8,128)(2,1)S(1)}, u32[]{:S(2)}, u32[]{:S(2)}) collective-permute-start(bf16[64,1024]{1,0:T(8,128)(2,1)S(1)} %add_convert_fusion.1.own_ref), channel_id=1, source_target_pairs={{0,1},{1,0},{2,3},{3,2},{4,5},{5,4},{6,7},{7,6},{8,9},{9,8},{10,11... | collective-permute-start | bytes 393224 | tf_op jit(solution)/shard_map/ppermute | solution.py:168
  23.2 1.3 %copy-start.9 = (f32[1024]{0:T(1024)S(1)}, f32[1024]{0:T(1024)}, u32[]{:S(2)}) copy-start(f32[1024]{0:T(1024)} %param.17) | copy-start | bytes 12292
  25.9 1.4 %collective-permute-start.3 = (bf16[2,128,256]{2,1,0:T(8,128)(2,1)S(1)}, bf16[2,128,256]{2,1,0:T(8,128)(2,1)S(1)}, u32[]{:S(2)}, u32[]{:S(2)}) collective-permute-start(bf16[2,128,256]{2,1,0:T(8,128)(2,1)S(1)} %get-tuple-element.12), channel_id=1, source_target_pairs={{0,1},{1,0},{2,3},{3,2},{4,5},{5,4},{6,7},{7,6},{8,9},{9,8},{10,11... | collective-permute-start | bytes 393224 | tf_op jit(solution)/shard_map/ppermute | solution.py:168

commit v2 on v1

v2 whole, which is shorter than its diff:
```python
import functools

import jax
import jax.numpy as jnp
from jax import lax
from jax.experimental import pallas as pl
from jax.experimental.pallas import tpu as pltpu
from jax.sharding import Mesh, PartitionSpec as P

EPSILON = 1e-06
THRESHOLDS = (1, 2, 3, 4, 5, 6, 7, 8, 12, 16, 23, 32, 46, 64, 91)
BF16 = jnp.bfloat16
F32 = jnp.float32
VMEM = pl.BlockSpec(memory_space=pltpu.VMEM)
SMEM = pl.BlockSpec(memory_space=pltpu.SMEM)
PREPARE_FLOPS = 7 * 10**9
VMEM_LIMIT = 24 * 1024 * 1024


def dot(a, b):
    return jnp.dot(a, b, preferred_element_type=F32)


def place():
    upper, lower = lax.axis_index("hi"), lax.axis_index("lo")
    return upper * 2 + lower, upper ^ lower


def deal_matrix(deal, counts_ref, replicas, new_slots, half, side):
    rows = deal.shape[1]
    share = rows // replicas
    lane = lax.broadcasted_iota(jnp.int32, (1, rows), 1)
    live = jnp.zeros((1, rows), jnp.bool_)
    for j in range(rows // new_slots):
        offset = lane - j * new_slots
        live = live | ((offset >= 0) & (offset < jnp.minimum(counts_ref[0, j], new_slots)))
    slot = lax.rem(deal, replicas) * share + lax.div(deal, replicas)
    slot = jnp.where(live, slot, -1)
    row = lax.broadcasted_iota(jnp.int32, (rows, rows), 0)
    row = jnp.where(side == 0, row, jnp.where(row < half, row + half, row - half))
    return jnp.where(row == slot, 1.0, 0.0).astype(BF16)


def bias_of(table_ref, relative, head):
    distance = jnp.abs(relative)
    before = jnp.full(relative.shape, table_ref[head, 0], F32)
    after = jnp.full(relative.shape, table_ref[head, 17], F32)
    for step, threshold in enumerate(THRESHOLDS):
        far = distance >= threshold
        before = jnp.where(far, table_ref[head, step + 1], before)
        after = jnp.where(far, table_ref[head, step + 17], after)
    return jnp.where(relative > 0, after, before)


def columns_of(index, xor, width):
    return pl.ds(pl.multiple_of((index ^ xor) * width, width), width)


def prepare_kernel(
    replicas,
    cached,
    new_slots,
    table_ref,
    counts_ref,
    lengths_ref,
    deal_ref,
    bias_ref,
    picked_ref,
):
    _, side = place()
    picked_ref[...] = deal_matrix(
        deal_ref[...], counts_ref, replicas, new_slots, picked_ref.shape[0] // 2, side
    )
    requests, _, key_slots = bias_ref.shape
    key_index = lax.broadcasted_iota(jnp.int32, (new_slots, key_slots), 1)
    query_index = lax.broadcasted_iota(jnp.int32, (new_slots, key_slots), 0)
    is_cache = key_index < cached
    for j in range(requests):
        length = lengths_ref[0, j]
        count = counts_ref[0, j]
        position = jnp.where(is_cache, key_index, length + key_index - cached)
        relative = position - (length + query_index)
        live = jnp.where(is_cache, key_index - length, key_index - cached - count) < 0
        for h in range(table_ref.shape[0]):
            bias = bias_of(table_ref, relative, h)
            bias_ref[j, h * new_slots : (h + 1) * new_slots] = jnp.where(live, bias, -1e30)


def attend_kernel(
    own_ref,
    far_ref,
    near_ref,
    near_far_ref,
    gain_ref,
    w_query_ref,
    w_key_ref,
    w_value_ref,
    w_out_ref,
    bias_ref,
    picked_ref,
    cache_keys_ref,
    cache_values_ref,
    keep_ref,
    send_ref,
):
    index, _ = place()
    rows, width = own_ref.shape
    model_width = gain_ref.shape[1]
    requests, cached, local_width = cache_keys_ref.shape
    new_slots = rows // requests
    head_count = bias_ref.shape[1] // new_slots
    head_size = local_width // head_count
    half = rows // 2

    blocks = [(own_ref[...], 0), (far_ref[...], 3), (near_ref[...], 1), (near_far_ref[...], 2)]
    squares = 0.0
    for block, _ in blocks:
        block = block.astype(F32)
        squares = squares + jnp.sum(block * block, axis=1, keepdims=True)
    inverse = lax.rsqrt(squares / model_width + EPSILON)
    queries = new_keys = new_values = 0.0
    for block, xor in blocks:
        columns = columns_of(index, xor, width)
        normed = (block.astype(F32) * inverse * gain_ref[:, columns]).astype(BF16)
        queries = queries + dot(normed, w_query_ref[columns, :])
        new_keys = new_keys + dot(normed, w_key_ref[columns, :])
        new_values = new_values + dot(normed, w_value_ref[columns, :])
    queries, new_keys, new_values = (v.astype(BF16) for v in (queries, new_keys, new_values))

    lane_head = lax.broadcasted_iota(jnp.int32, (new_slots, local_width), 1) // head_size
    contexts = []
    for j in range(requests):
        own = slice(j * new_slots, (j + 1) * new_slots)
        query = queries[own]
        stacked = jnp.concatenate(
            [jnp.where(lane_head == h, query, jnp.zeros_like(query)) for h in range(head_count)],
            axis=0,
        )
        keys = jnp.concatenate([cache_keys_ref[j], new_keys[own]], axis=0)
        values = jnp.concatenate([cache_values_ref[j], new_values[own]], axis=0)
        scores = lax.dot_general(
            stacked, keys, (((1,), (1,)), ((), ())), preferred_element_type=F32
        )
        scores = scores + bias_ref[j]
        weights = jnp.exp(scores - jnp.max(scores, axis=1, keepdims=True))
        probs = (weights / jnp.sum(weights, axis=1, keepdims=True)).astype(BF16)
        mixed = dot(probs, values)
        context = jnp.zeros((new_slots, local_width), F32)
        for h in range(head_count):
            context = jnp.where(lane_head == h, mixed[h * new_slots : (h + 1) * new_slots], context)
        contexts.append(context.astype(BF16))
    context = dot(picked_ref[...], jnp.concatenate(contexts, axis=0)).astype(BF16)
    send_ref[...] = dot(context[half:], w_out_ref[...]).astype(BF16)
    keep_ref[...] = dot(context[:half], w_out_ref[...])


def stream_kernel(own_ref, far_ref, near_ref, near_far_ref, picked_ref, stream_ref):
    index, _ = place()
    width = own_ref.shape[1]
    for ref, xor in ((own_ref, 0), (far_ref, 3), (near_ref, 1), (near_far_ref, 2)):
        stream_ref[:, columns_of(index, xor, width)] = dot(picked_ref[...], ref[...]).astype(BF16)


def ffn_kernel(own_ref, other_ref, stream_ref, gain_ref, w_inner_ref, w_outer_ref, keep_ref, send_ref):
    _, side = place()
    core = lax.axis_index("lo")
    upper = lax.axis_index("hi")
    half, model_width = own_ref.shape
    groups, _, width = keep_ref.shape
    for part, ref in enumerate((own_ref, other_ref)):
        start = pl.multiple_of((side ^ part) * half, half)
        mixed = ref[...].astype(F32) + stream_ref[part * half : (part + 1) * half].astype(F32)
        square = jnp.sum(mixed * mixed, axis=1, keepdims=True)
        inverse = lax.rsqrt(square / model_width + EPSILON)
        ffn_input = (mixed * inverse * gain_ref[...]).astype(BF16)
        hidden = jnp.maximum(dot(ffn_input, w_inner_ref[...]), 0.0).astype(BF16)
        projected = dot(hidden, w_outer_ref[...])
        for g in range(groups):
            for c in range(2):
                columns = slice((g * 2 + c) * width, (g * 2 + c + 1) * width)
                mine = (upper == g) & (core == c)
                value = projected[:, columns] + jnp.where(mine, mixed[:, columns], 0.0)

                @pl.when(core == c)
                def _():
                    keep_ref[g, pl.ds(start, half), :] = value

                @pl.when(core != c)
                def _():
                    send_ref[g, pl.ds(start, half), :] = value.astype(BF16)


def swap(value, xor):
    return lax.ppermute(value, ("hi", "lo"), [(i, i ^ xor) for i in range(4)])


def on_device(
    replicas,
    tokens,
    attn_gain,
    ffn_gain,
    w_query,
    w_key,
    w_value,
    w_out,
    w_inner,
    w_outer,
    bias_table,
    cache_keys,
    cache_values,
    new_counts,
    cached_lengths,
    deal,
):
    rows, width = tokens.shape
    requests = cache_keys.shape[0]
    new_slots = rows // requests
    model_width = attn_gain.shape[0]
    half = rows // 2
    params = pltpu.CompilerParams(vmem_limit_bytes=VMEM_LIMIT)
    far = swap(tokens, 3)
    near = swap(tokens, 1)
    cached, head_count = cache_keys.shape[1], bias_table.shape[1]
    shape = jax.ShapeDtypeStruct
    bias, picked = pl.pallas_call(
        functools.partial(prepare_kernel, replicas, cached, new_slots),
        out_shape=(
            shape((requests, head_count * new_slots, cached + new_slots), F32),
            shape((rows, rows), BF16),
        ),
        in_specs=[SMEM] * 3 + [VMEM],
        out_specs=(VMEM,) * 2,
        compiler_params=params,
        cost_estimate=pl.CostEstimate(flops=PREPARE_FLOPS, bytes_accessed=0, transcendentals=0),
        name="prepare",
    )(bias_table.T, new_counts.T, cached_lengths.T, deal)
    blocks = (tokens, far, near, swap(far, 1))
    keep, send = pl.pallas_call(
        attend_kernel,
        out_shape=(shape((half, model_width), F32), shape((half, model_width), BF16)),
        in_specs=[VMEM] * 13,
        out_specs=(VMEM, VMEM),
        compiler_params=params,
        name="attend",
    )(
        *blocks,
        attn_gain.reshape(1, model_width),
        w_query,
        w_key,
        w_value,
        w_out,
        bias,
        picked,
        cache_keys,
        cache_values,
    )
    stream = pl.pallas_call(
        stream_kernel,
        out_shape=shape((rows, model_width), BF16),
        in_specs=[VMEM] * 5,
        out_specs=VMEM,
        compiler_params=params,
        name="stream",
    )(*blocks, picked)
    pair = (keep + swap(send, 1).astype(F32)).astype(BF16)
    total = (pair.astype(F32) + swap(pair, 3).astype(F32)).astype(BF16)
    other = swap(total, 1)
    groups = lax.axis_size("hi")
    keep, send = pl.pallas_call(
        ffn_kernel,
        out_shape=(
            jax.ShapeDtypeStruct((groups, rows, width), F32),
            jax.ShapeDtypeStruct((groups, rows, width), BF16),
        ),
        in_specs=[VMEM] * 6,
        out_specs=(VMEM, VMEM),
        compiler_params=params,
        name="ffn",
    )(total, other, stream, ffn_gain.reshape(1, model_width), w_inner, w_outer)
    pair = (keep + swap(send, 1).astype(F32)).astype(BF16)
    parts = lax.all_to_all(
        pair.reshape(groups * replicas, rows // replicas, width), ("hi", "rep"), 0, 0, tiled=True
    )
    return jnp.sum(parts.reshape(groups, rows, width).astype(F32), axis=0).astype(BF16)


def solution(mesh):
    replicas, tp = mesh.shape["rep"], mesh.shape["tp"]
    split = Mesh(mesh.devices.reshape(replicas, tp // 2, 2), ("rep", "hi", "lo"))
    cols = ("hi", "lo")
    in_specs = (
        P("rep", cols),
        P(),
        P(),
        P(None, cols),
        P(None, cols),
        P(None, cols),
        P(cols, None),
        P(None, cols),
        P(cols, None),
        P(None, cols),
        P("rep", None, cols),
        P("rep", None, cols),
        P(None, "rep"),
        P(None, "rep"),
        P("rep", None),
    )
    return jax.shard_map(
        functools.partial(on_device, replicas),
        mesh=split,
        in_specs=in_specs,
        out_specs=P("rep", cols),
        check_vma=False,
    )
```

time: 42.9 us -> 37.1 us (0.86)
  blocking collectives: 22 us -> 14.7 us
  local copies, waits for them, and re-layouts: 5.69 us -> 1.48 us
  starting transfers between devices: 2.3 us -> 6.49 us
  waiting for transfers between devices: 6.97 us -> 8.99 us
    all_gather x1 -> x0, blocking collectives: 7.58 us -> none  [on_device(): x = lax.all_gather(tokens, ('hi', 'lo'), axis=0, tiled=False)]
    unnamed x31 -> x30, local copies, waits for them, and re-layouts: 5.69 us -> 1.48 us
    ppermute x4 -> x7, starting transfers between devices: 2.3 us -> 6.49 us  [swap(): return lax.ppermute(value, ('hi', 'lo'), [(i, i ^ xor) for i in range(4)])]
    ppermute x4 -> x7, waiting for transfers between devices: 6.97 us -> 8.99 us  [swap(): return lax.ppermute(value, ('hi', 'lo'), [(i, i ^ xor) for i in range(4)])]
    pallas_call x2 -> x3, Pallas kernels: 3.33 us -> 2.97 us  [the longest x1 1.68 us: on_device(): pl.pallas_call(attend_kernel, out_shape=(shape((half, model_width), F32),...]
  transfers between devices with their start and end apart: 4 -> 7, of which waited for: 4 -> 5; matrix products, arithmetic and copies ran while one was open for 0% -> 0% of each run, Pallas kernels for 2% -> 3%
where the time goes in v2:
time: 37.1 us; the launch traced here: 36.8 us
  blocking collectives  14.7 us (40%)
  waiting for transfers between devices  8.99 us (24%)
  starting transfers between devices  6.49 us (17%)
  Pallas kernels  4.29 us (12%)
  local copies, waits for them, and re-layouts  1.48 us (4%)
  other arithmetic  0.75 us (2%)
    all_to_all x1, blocking collectives, on_device(): lax.all_to_all(pair.reshape(groups * replicas, rows // replicas, width),...  14.7 us
    ppermute x7, waiting for transfers between devices, swap(): return lax.ppermute(value, ('hi', 'lo'), [(i, i ^ xor) for i in range(4)])  8.99 us
    ppermute x7, starting transfers between devices, swap(): return lax.ppermute(value, ('hi', 'lo'), [(i, i ^ xor) for i in range(4)])  6.49 us
    pallas_call x1, Pallas kernels, on_device(): pl.pallas_call(attend_kernel, out_shape=(shape((half, model_width), F32),...  1.68 us
    unnamed x30, local copies, waits for them, and re-layouts  1.48 us
    pallas_call x1, Pallas kernels, on_device(): pl.pallas_call(ffn_kernel, out_shape=(jax.ShapeDtypeStruct((groups, rows,...  1.32 us
    pallas_call x1, Pallas kernels, on_device(): pl.pallas_call(functools.partial(prepare_kernel, replicas, cached, new_sl...  1.07 us
  transfers between devices with their start and end apart: 7, of which 5 were waited for; matrix products, arithmetic and copies ran while one was open for 0% of the time, Pallas kernels for 3%

profile of v2, /device:TPU:0, one launch (start us, length us, event | category | flops | bytes accessed | tf_op | source)
XLA Modules:
  0.0 36.8 jit_solution(13690287759440133922)
XLA Ops:
  0.0 2.4 %collective-permute-start = (bf16[128,256]{1,0:T(8,128)(2,1)}, bf16[128,256]{1,0:T(8,128)(2,1)S(1)}, u32[]{:S(2)}, u32[]{:S(2)}) collective-permute-start(bf16[128,256]{1,0:T(8,128)(2,1)} %own_ref.3), channel_id=1, source_target_pairs={{0,3},{1,2},{2,1},{3,0},{4,7},{5,6},{6,5},{7,4},{8,11},{9,10},{10,... | collective-permute-start | bytes 196616 | tf_op jit(solution)/shard_map/ppermute | solution.py:194
  2.4 0.7 %collective-permute-start.1 = (bf16[128,256]{1,0:T(8,128)(2,1)}, bf16[128,256]{1,0:T(8,128)(2,1)S(1)}, u32[]{:S(2)}, u32[]{:S(2)}) collective-permute-start(bf16[128,256]{1,0:T(8,128)(2,1)} %own_ref.3), channel_id=1, source_target_pairs={{0,1},{1,0},{2,3},{3,2},{4,5},{5,4},{6,7},{7,6},{8,9},{9,8},{10,11... | collective-permute-start | bytes 196616 | tf_op jit(solution)/shard_map/ppermute | solution.py:194
  3.1 2.1 %collective-permute-done.far_ref = bf16[128,256]{1,0:T(8,128)(2,1)S(1)} collective-permute-done((bf16[128,256]{1,0:T(8,128)(2,1)}, bf16[128,256]{1,0:T(8,128)(2,1)S(1)}, u32[]{:S(2)}, u32[]{:S(2)}) %collective-permute-start) | collective-permute-done | bytes 65568 | tf_op jit(solution)/shard_map/ppermute | solution.py:194
  5.2 0.1 collective-permute-start.2
  5.3 0.0 copy-start.11
  5.3 0.0 copy-start.12
  5.3 0.0 copy-start.13
  5.3 0.0 copy-start.14
  5.3 0.7 %copy-done.11 = f32[32,4]{0,1:T(4,128)S(1)} copy-done((f32[32,4]{0,1:T(4,128)S(1)}, f32[32,4]{0,1:T(4,128)}, u32[]{:S(2)}) %copy-start.11) | copy-done | bytes 536
  6.0 0.0 copy-done.12
  6.0 0.0 copy-done.13
  6.0 0.0 copy-done.14
  6.0 0.0 copy-start.2
  6.0 0.0 copy-start.3
  6.0 0.0 copy-start.4
  6.0 0.0 copy-start.5
  6.0 0.0 copy-start.6
  6.0 0.0 copy-start.7
  6.0 0.0 copy-start.8
  6.1 1.1 %prepare.1 = (f32[2,256,128]{2,1,0:T(8,128)S(1)}, bf16[128,128]{1,0:T(8,128)(2,1)S(1)}) custom-call(f32[4,32]{1,0:T(4,128)S(1)} %bitcast.11, s32[1,2]{1,0:T(1,128)S(1)} %bitcast.12, s32[1,2]{1,0:T(1,128)S(1)} %bitcast.13, s32[1,128]{1,0:T(1,128)S(1)} %copy-done.14), custom_call_target="tpu_custom_call" | custom-call | flops 7000000000 | tf_op jit(solution)/shard_map/prepare/pallas_call | solution.py:225
  7.1 0.0 copy-start.9
  7.1 0.0 collective-permute-done.1.near_ref
  7.2 0.0 collective-permute-done.2.near_far_ref
  7.2 0.0 copy-done.2
  7.2 0.0 copy-done.3
  7.2 0.2 copy-done.4
  7.4 0.2 copy-done.5
  7.5 0.0 copy-done.6
  7.5 0.0 copy-done.7
  7.5 0.0 copy-done.8
  7.5 0.4 %copy-done.9 = f32[1024]{0:T(1024)S(1)} copy-done((f32[1024]{0:T(1024)S(1)}, f32[1024]{0:T(1024)}, u32[]{:S(2)}) %copy-start.9) | copy-done | bytes 4120
  7.9 1.7 %attend.1 = (f32[64,1024]{1,0:T(8,128)S(1)}, bf16[64,1024]{1,0:T(8,128)(2,1)S(1)}) custom-call(bf16[128,256]{1,0:T(8,128)(2,1)S(1)} %copy-done.6, bf16[128,256]{1,0:T(8,128)(2,1)S(1)} %collective-permute-done.far_ref, bf16[128,256]{1,0:T(8,128)(2,1)S(1)} %collective-permute-done.1.near_ref, bf16[128,256]{1,0:T(8,128)(2,1)S(1)} %collective-permute-done.2.near_far_ref, ...), custom_call_target="tpu_custom_call" | custom-call | tf_op jit(solution)/shard_map/attend/pallas_call | solution.py:238
  9.6 0.0 copy-start
  9.6 0.5 %collective-permute-start.3 = (bf16[64,1024]{1,0:T(8,128)(2,1)S(1)}, bf16[64,1024]{1,0:T(8,128)(2,1)S(1)}, u32[]{:S(2)}, u32[]{:S(2)}) collective-permute-start(bf16[64,1024]{1,0:T(8,128)(2,1)S(1)} %get-tuple-element.14), channel_id=1, source_target_pairs={{0,1},{1,0},{2,3},{3,2},{4,5},{5,4},{6,7},{7,6},{8,9},{9,8},{10,11... | collective-permute-start | bytes 393224 | tf_op jit(solution)/shard_map/ppermute | solution.py:194
  10.1 1.0 %collective-permute-done.3 = bf16[64,1024]{1,0:T(8,128)(2,1)S(1)} collective-permute-done((bf16[64,1024]{1,0:T(8,128)(2,1)S(1)}, bf16[64,1024]{1,0:T(8,128)(2,1)S(1)}, u32[]{:S(2)}, u32[]{:S(2)}) %collective-permute-start.3) | collective-permute-done | bytes 131104 | tf_op jit(solution)/shard_map/ppermute | solution.py:194
  11.1 2.4 %collective-permute-start.4 = (bf16[64,1024]{1,0:T(8,128)(2,1)S(1)}, bf16[64,1024]{1,0:T(8,128)(2,1)S(1)}, u32[]{:S(2)}, u32[]{:S(2)}) collective-permute-start(bf16[64,1024]{1,0:T(8,128)(2,1)S(1)} %add_convert_fusion.2), channel_id=1, source_target_pairs={{0,3},{1,2},{2,1},{3,0},{4,7},{5,6},{6,5},{7,4},{8,11},{9,10},{10,... | collective-permute-start | bytes 393224 | tf_op jit(solution)/shard_map/ppermute | solution.py:194
  13.5 3.7 %collective-permute-done.4 = bf16[64,1024]{1,0:T(8,128)(2,1)S(1)} collective-permute-done((bf16[64,1024]{1,0:T(8,128)(2,1)S(1)}, bf16[64,1024]{1,0:T(8,128)(2,1)S(1)}, u32[]{:S(2)}, u32[]{:S(2)}) %collective-permute-start.4) | collective-permute-done | bytes 131104 | tf_op jit(solution)/shard_map/ppermute | solution.py:194
  17.3 0.2 collective-permute-start.5
  17.5 0.2 stream.1.stream_ref
  17.7 1.0 %collective-permute-done.5.other_ref = bf16[64,1024]{1,0:T(8,128)(2,1)S(1)} collective-permute-done((bf16[64,1024]{1,0:T(8,128)(2,1)S(1)}, bf16[64,1024]{1,0:T(8,128)(2,1)S(1)}, u32[]{:S(2)}, u32[]{:S(2)}) %collective-permute-start.5) | collective-permute-done | bytes 131104 | tf_op jit(solution)/shard_map/ppermute | solution.py:194
  18.7 0.0 copy-done.1
  18.7 0.0 copy-done
  18.7 0.0 copy-done.10
  18.7 1.3 %ffn.1 = (f32[2,128,256]{2,1,0:T(8,128)S(1)}, bf16[2,128,256]{2,1,0:T(8,128)(2,1)S(1)}) custom-call(bf16[64,1024]{1,0:T(8,128)(2,1)S(1)} %add_convert_fusion.1.own_ref, bf16[64,1024]{1,0:T(8,128)(2,1)S(1)} %collective-permute-done.5.other_ref, bf16[128,1024]{1,0:T(8,128)(2,1)S(1)} %stream.1.stream_ref, f32[1,1024]{1,0:T(1,128)S(1)} %bitcast.10, ...), custom_call_target="tpu_custom_call" | custom-call | tf_op jit(solution)/shard_map/ffn/pallas_call | solution.py:269
  20.0 0.2 collective-permute-start.6
  20.3 1.2 %collective-permute-done.6 = bf16[2,128,256]{2,1,0:T(8,128)(2,1)S(1)} collective-permute-done((bf16[2,128,256]{2,1,0:T(8,128)(2,1)S(1)}, bf16[2,128,256]{2,1,0:T(8,128)(2,1)S(1)}, u32[]{:S(2)}, u32[]{:S(2)}) %collective-permute-start.6) | collective-permute-done | bytes 131104 | tf_op jit(solution)/shard_map/ppermute | solution.py:194
  21.5 14.7 %all_to_all.5 = bf16[16,16,256]{2,1,0:T(8,128)(2,1)S(1)} all-to-all(bf16[16,16,256]{2,1,0:T(8,128)(2,1)S(1)} %bitcast.15), channel_id=1, replica_groups=mesh['rep'=8,'hi'=2,'lo'=2] {'hi','rep'}, dimensions={0} | all-to-all | bytes 262144 | tf_op jit(solution)/shard_map/all_to_all | solution.py:281
  36.2 0.6 %bitcast_reduce_fusion = bf16[128,256]{1,0:T(8,128)(2,1)} fusion(bf16[2,128,256]{2,1,0:T(8,128)(2,1)S(1)} %bitcast.14), kind=kLoop, calls=%fused_computation.3 | loop fusion | flops 32768 | bytes 196608 | tf_op jit(solution)/shard_map/reduce_sum | solution.py:284
  (5 shorter events, 0.1 us)
Async XLA Ops:
  0.0 5.2 %collective-permute-start = (bf16[128,256]{1,0:T(8,128)(2,1)}, bf16[128,256]{1,0:T(8,128)(2,1)S(1)}, u32[]{:S(2)}, u32[]{:S(2)}) collective-permute-start(bf16[128,256]{1,0:T(8,128)(2,1)} %own_ref.3), channel_id=1, source_target_pairs={{0,3},{1,2},{2,1},{3,0},{4,7},{5,6},{6,5},{7,4},{8,11},{9,10},{10,... | collective-permute-start | bytes 196616 | tf_op jit(solution)/shard_map/ppermute | solution.py:194
  2.4 4.7 %collective-permute-start.1 = (bf16[128,256]{1,0:T(8,128)(2,1)}, bf16[128,256]{1,0:T(8,128)(2,1)S(1)}, u32[]{:S(2)}, u32[]{:S(2)}) collective-permute-start(bf16[128,256]{1,0:T(8,128)(2,1)} %own_ref.3), channel_id=1, source_target_pairs={{0,1},{1,0},{2,3},{3,2},{4,5},{5,4},{6,7},{7,6},{8,9},{9,8},{10,11... | collective-permute-start | bytes 196616 | tf_op jit(solution)/shard_map/ppermute | solution.py:194
  5.2 2.0 %collective-permute-start.2 = (bf16[128,256]{1,0:T(8,128)(2,1)S(1)}, bf16[128,256]{1,0:T(8,128)(2,1)S(1)}, u32[]{:S(2)}, u32[]{:S(2)}) collective-permute-start(bf16[128,256]{1,0:T(8,128)(2,1)S(1)} %collective-permute-done.far_ref), channel_id=1, source_target_pairs={{0,1},{1,0},{2,3},{3,2},{4,5},{5,4},{6,7},{7,6},{8,9},{9,8},{10,11... | collective-permute-start | bytes 196616 | tf_op jit(solution)/shard_map/ppermute | solution.py:194
  5.3 0.7 %copy-start.11 = (f32[32,4]{0,1:T(4,128)S(1)}, f32[32,4]{0,1:T(4,128)}, u32[]{:S(2)}) copy-start(f32[32,4]{0,1:T(4,128)} %param.24) | copy-start | bytes 1540
  5.3 0.7 %copy-start.12 = (s32[2,1]{0,1:T(1,128)S(1)}, s32[2,1]{0,1:T(1,128)}, u32[]{:S(2)}) copy-start(s32[2,1]{0,1:T(1,128)} %param.27) | copy-start | bytes 28
  5.3 0.7 %copy-start.13 = (s32[2,1]{0,1:T(1,128)S(1)}, s32[2,1]{0,1:T(1,128)}, u32[]{:S(2)}) copy-start(s32[2,1]{0,1:T(1,128)} %param.28) | copy-start | bytes 28
  5.3 0.7 %copy-start.14 = (s32[1,128]{1,0:T(1,128)S(1)}, s32[1,128]{1,0:T(1,128)}, u32[]{:S(2)}) copy-start(s32[1,128]{1,0:T(1,128)} %deal_ref.1) | copy-start | bytes 1540
  6.0 1.2 %copy-start.2 = (bf16[1024,256]{1,0:T(8,128)(2,1)S(1)}, bf16[1024,256]{1,0:T(8,128)(2,1)}, u32[]{:S(2)}) copy-start(bf16[1024,256]{1,0:T(8,128)(2,1)} %w_query_ref.1) | copy-start | bytes 1572868
  6.0 1.2 %copy-start.3 = (bf16[1024,256]{1,0:T(8,128)(2,1)S(1)}, bf16[1024,256]{1,0:T(8,128)(2,1)}, u32[]{:S(2)}) copy-start(bf16[1024,256]{1,0:T(8,128)(2,1)} %w_key_ref.1) | copy-start | bytes 1572868
  6.0 1.4 %copy-start.4 = (bf16[1024,256]{1,0:T(8,128)(2,1)S(1)}, bf16[1024,256]{1,0:T(8,128)(2,1)}, u32[]{:S(2)}) copy-start(bf16[1024,256]{1,0:T(8,128)(2,1)} %w_value_ref.1) | copy-start | bytes 1572868
  6.0 1.5 %copy-start.5 = (bf16[256,1024]{1,0:T(8,128)(2,1)S(1)}, bf16[256,1024]{1,0:T(8,128)(2,1)}, u32[]{:S(2)}) copy-start(bf16[256,1024]{1,0:T(8,128)(2,1)} %w_out_ref.1) | copy-start | bytes 1572868
  6.0 1.5 %copy-start.6 = (bf16[128,256]{1,0:T(8,128)(2,1)S(1)}, bf16[128,256]{1,0:T(8,128)(2,1)}, u32[]{:S(2)}) copy-start(bf16[128,256]{1,0:T(8,128)(2,1)} %own_ref.3) | copy-start | bytes 196612
  6.0 1.5 %copy-start.7 = (bf16[2,64,256]{2,1,0:T(8,128)(2,1)S(1)}, bf16[2,64,256]{2,1,0:T(8,128)(2,1)}, u32[]{:S(2)}) copy-start(bf16[2,64,256]{2,1,0:T(8,128)(2,1)} %cache_keys_ref.1) | copy-start | bytes 196612
  6.0 1.5 %copy-start.8 = (bf16[2,64,256]{2,1,0:T(8,128)(2,1)S(1)}, bf16[2,64,256]{2,1,0:T(8,128)(2,1)}, u32[]{:S(2)}) copy-start(bf16[2,64,256]{2,1,0:T(8,128)(2,1)} %cache_values_ref.1) | copy-start | bytes 196612
  7.1 0.8 %copy-start.9 = (f32[1024]{0:T(1024)S(1)}, f32[1024]{0:T(1024)}, u32[]{:S(2)}) copy-start(f32[1024]{0:T(1024)} %param.16) | copy-start | bytes 12292
  7.9 10.8 %copy-start.1 = (bf16[512,1024]{1,0:T(8,128)(2,1)S(1)}, bf16[512,1024]{1,0:T(8,128)(2,1)}, u32[]{:S(2)}) copy-start(bf16[512,1024]{1,0:T(8,128)(2,1)} %w_outer_ref.1) | copy-start | bytes 3145732
  9.6 9.1 %copy-start = (bf16[1024,512]{1,0:T(8,128)(2,1)S(1)}, bf16[1024,512]{1,0:T(8,128)(2,1)}, u32[]{:S(2)}) copy-start(bf16[1024,512]{1,0:T(8,128)(2,1)} %w_inner_ref.1) | copy-start | bytes 3145732
  9.6 1.5 %collective-permute-start.3 = (bf16[64,1024]{1,0:T(8,128)(2,1)S(1)}, bf16[64,1024]{1,0:T(8,128)(2,1)S(1)}, u32[]{:S(2)}, u32[]{:S(2)}) collective-permute-start(bf16[64,1024]{1,0:T(8,128)(2,1)S(1)} %get-tuple-element.14), channel_id=1, source_target_pairs={{0,1},{1,0},{2,3},{3,2},{4,5},{5,4},{6,7},{7,6},{8,9},{9,8},{10,11... | collective-permute-start | bytes 393224 | tf_op jit(solution)/shard_map/ppermute | solution.py:194
  11.1 6.1 %collective-permute-start.4 = (bf16[64,1024]{1,0:T(8,128)(2,1)S(1)}, bf16[64,1024]{1,0:T(8,128)(2,1)S(1)}, u32[]{:S(2)}, u32[]{:S(2)}) collective-permute-start(bf16[64,1024]{1,0:T(8,128)(2,1)S(1)} %add_convert_fusion.2), channel_id=1, source_target_pairs={{0,3},{1,2},{2,1},{3,0},{4,7},{5,6},{6,5},{7,4},{8,11},{9,10},{10,... | collective-permute-start | bytes 393224 | tf_op jit(solution)/shard_map/ppermute | solution.py:194
  17.3 1.4 %collective-permute-start.5 = (bf16[64,1024]{1,0:T(8,128)(2,1)S(1)}, bf16[64,1024]{1,0:T(8,128)(2,1)S(1)}, u32[]{:S(2)}, u32[]{:S(2)}) collective-permute-start(bf16[64,1024]{1,0:T(8,128)(2,1)S(1)} %add_convert_fusion.1.own_ref), channel_id=1, source_target_pairs={{0,1},{1,0},{2,3},{3,2},{4,5},{5,4},{6,7},{7,6},{8,9},{9,8},{10,11... | collective-permute-start | bytes 393224 | tf_op jit(solution)/shard_map/ppermute | solution.py:194
  17.5 1.2 %copy-start.10 = (f32[1024]{0:T(1024)S(1)}, f32[1024]{0:T(1024)}, u32[]{:S(2)}) copy-start(f32[1024]{0:T(1024)} %param.17) | copy-start | bytes 12292
  20.0 1.4 %collective-permute-start.6 = (bf16[2,128,256]{2,1,0:T(8,128)(2,1)S(1)}, bf16[2,128,256]{2,1,0:T(8,128)(2,1)S(1)}, u32[]{:S(2)}, u32[]{:S(2)}) collective-permute-start(bf16[2,128,256]{2,1,0:T(8,128)(2,1)S(1)} %get-tuple-element.16), channel_id=1, source_target_pairs={{0,1},{1,0},{2,3},{3,2},{4,5},{5,4},{6,7},{7,6},{8,9},{9,8},{10,11... | collective-permute-start | bytes 393224 | tf_op jit(solution)/shard_map/ppermute | solution.py:194

commit v3 on v2

--- a/solution.py
+++ b/solution.py
@@ -100,8 +100,8 @@
     picked_ref,
     cache_keys_ref,
     cache_values_ref,
-    keep_ref,
     send_ref,
+    context_ref,
 ):
     index, _ = place()
     rows, width = own_ref.shape
@@ -151,7 +151,11 @@
         contexts.append(context.astype(BF16))
     context = dot(picked_ref[...], jnp.concatenate(contexts, axis=0)).astype(BF16)
     send_ref[...] = dot(context[half:], w_out_ref[...]).astype(BF16)
-    keep_ref[...] = dot(context[:half], w_out_ref[...])
+    context_ref[...] = context[:half]
+
+
+def project_kernel(context_ref, w_out_ref, keep_ref):
+    keep_ref[...] = dot(context_ref[...], w_out_ref[...])
 
 
 def stream_kernel(own_ref, far_ref, near_ref, near_far_ref, picked_ref, stream_ref):
@@ -161,33 +165,48 @@
         stream_ref[:, columns_of(index, xor, width)] = dot(picked_ref[...], ref[...]).astype(BF16)
 
 
-def ffn_kernel(own_ref, other_ref, stream_ref, gain_ref, w_inner_ref, w_outer_ref, keep_ref, send_ref):
+def hidden_of(total_ref, stream_ref, gain_ref, w_inner_ref):
+    mixed = total_ref[...].astype(F32) + stream_ref[...].astype(F32)
+    square = jnp.sum(mixed * mixed, axis=1, keepdims=True)
+    inverse = lax.rsqrt(square / mixed.shape[1] + EPSILON)
+    ffn_input = (mixed * inverse * gain_ref[...]).astype(BF16)
+    return jnp.maximum(dot(ffn_input, w_inner_ref[...]), 0.0).astype(BF16)
+
+
+def inner_kernel(total_ref, stream_ref, gain_ref, w_inner_ref, hidden_ref):
+    hidden_ref[...] = hidden_of(total_ref, stream_ref.at[: total_ref.shape[0]], gain_ref, w_inner_ref)
+
+
+def send_kernel(
+    total_ref, stream_ref, gain_ref, w_inner_ref, w_outer_ref, first_ref, second_ref, send_ref
+):
+    core = lax.axis_index("lo")
     _, side = place()
-    core = lax.axis_index("lo")
-    upper = lax.axis_index("hi")
-    half, model_width = own_ref.shape
+    half = total_ref.shape[0]
+    groups, _, width = send_ref.shape
+    second = hidden_of(total_ref, stream_ref.at[half:], gain_ref, w_inner_ref)
+    second_ref[...] = second
+    for g in range(groups):
+        weight = w_outer_ref[:, columns_of(g * 2 + 1 - core, 0, width)]
+        for part, hidden in enumerate((first_ref[...], second)):
+            start = pl.multiple_of((side ^ part) * half, half)
+            send_ref[g, pl.ds(start, half), :] = dot(hidden, weight).astype(BF16)
+
+
+def keep_kernel(own_ref, other_ref, stream_ref, first_ref, second_ref, w_outer_ref, keep_ref):
+    core, upper = lax.axis_index("lo"), lax.axis_index("hi")
+    index, side = place()
+    half = own_ref.shape[0]
     groups, _, width = keep_ref.shape
-    for part, ref in enumerate((own_ref, other_ref)):
+    columns = columns_of(index, 0, width)
+    for part, total_ref, hidden_ref in ((0, own_ref, first_ref), (1, other_ref, second_ref)):
         start = pl.multiple_of((side ^ part) * half, half)
-        mixed = ref[...].astype(F32) + stream_ref[part * half : (part + 1) * half].astype(F32)
-        square = jnp.sum(mixed * mixed, axis=1, keepdims=True)
-        inverse = lax.rsqrt(square / model_width + EPSILON)
-        ffn_input = (mixed * inverse * gain_ref[...]).astype(BF16)
-        hidden = jnp.maximum(dot(ffn_input, w_inner_ref[...]), 0.0).astype(BF16)
-        projected = dot(hidden, w_outer_ref[...])
+        rows = slice(part * half, (part + 1) * half)
+        mixed = total_ref[:, columns].astype(F32) + stream_ref[rows, columns].astype(F32)
         for g in range(groups):
-            for c in range(2):
-                columns = slice((g * 2 + c) * width, (g * 2 + c + 1) * width)
-                mine = (upper == g) & (core == c)
-                value = projected[:, columns] + jnp.where(mine, mixed[:, columns], 0.0)
-
-                @pl.when(core == c)
-                def _():
-                    keep_ref[g, pl.ds(start, half), :] = value
-
-                @pl.when(core != c)
-                def _():
-                    send_ref[g, pl.ds(start, half), :] = value.astype(BF16)
+            weight = w_outer_ref[:, columns_of(g * 2 + core, 0, width)]
+            value = dot(hidden_ref[...], weight) + jnp.where(upper == g, mixed, 0.0)
+            keep_ref[g, pl.ds(start, half), :] = value
 
 
 def swap(value, xor):
@@ -219,7 +238,6 @@
     half = rows // 2
     params = pltpu.CompilerParams(vmem_limit_bytes=VMEM_LIMIT)
     far = swap(tokens, 3)
-    near = swap(tokens, 1)
     cached, head_count = cache_keys.shape[1], bias_table.shape[1]
     shape = jax.ShapeDtypeStruct
     bias, picked = pl.pallas_call(
@@ -234,10 +252,11 @@
         cost_estimate=pl.CostEstimate(flops=PREPARE_FLOPS, bytes_accessed=0, transcendentals=0),
         name="prepare",
     )(bias_table.T, new_counts.T, cached_lengths.T, deal)
-    blocks = (tokens, far, near, swap(far, 1))
-    keep, send = pl.pallas_call(
+    far, own, bias, picked = lax.optimization_barrier((far, tokens, bias, picked))
+    blocks = (tokens, far, swap(own, 1), swap(far, 1))
+    send, context = pl.pallas_call(
         attend_kernel,
-        out_shape=(shape((half, model_width), F32), shape((half, model_width), BF16)),
+        out_shape=(shape((half, model_width), BF16), shape((half, w_out.shape[0]), BF16)),
         in_specs=[VMEM] * 13,
         out_specs=(VMEM, VMEM),
         compiler_params=params,
@@ -254,29 +273,48 @@
         cache_keys,
         cache_values,
     )
-    stream = pl.pallas_call(
+    local = functools.partial(pl.pallas_call, compiler_params=params)
+    keep = local(
+        project_kernel,
+        out_shape=shape((half, model_width), F32),
+        in_specs=[VMEM] * 2,
+        out_specs=VMEM,
+        name="project",
+    )(context, w_out)
+    stream = local(
         stream_kernel,
         out_shape=shape((rows, model_width), BF16),
         in_specs=[VMEM] * 5,
         out_specs=VMEM,
-        compiler_params=params,
         name="stream",
     )(*blocks, picked)
     pair = (keep + swap(send, 1).astype(F32)).astype(BF16)
     total = (pair.astype(F32) + swap(pair, 3).astype(F32)).astype(BF16)
     other = swap(total, 1)
+    gain = ffn_gain.reshape(1, model_width)
+    hidden_shape = shape((half, w_inner.shape[1]), BF16)
+    first = local(
+        inner_kernel,
+        out_shape=hidden_shape,
+        in_specs=[VMEM] * 4,
+        out_specs=VMEM,
+        name="inner",
+    )(total, stream, gain, w_inner)
     groups = lax.axis_size("hi")
-    keep, send = pl.pallas_call(
-        ffn_kernel,
-        out_shape=(
-            jax.ShapeDtypeStruct((groups, rows, width), F32),
-            jax.ShapeDtypeStruct((groups, rows, width), BF16),
-        ),
+    second, send = local(
+        send_kernel,
+        out_shape=(hidden_shape, shape((groups, rows, width), BF16)),
         in_specs=[VMEM] * 6,
         out_specs=(VMEM, VMEM),
-        compiler_params=params,
-        name="ffn",
-    )(total, other, stream, ffn_gain.reshape(1, model_width), w_inner, w_outer)
+        name="send",
+    )(other, stream, gain, w_inner, w_outer, first)
+    keep = local(
+        keep_kernel,
+        out_shape=shape((groups, rows, width), F32),
+        in_specs=[VMEM] * 6,
+        out_specs=VMEM,
+        name="keep",
+    )(total, other, stream, first, second, w_outer)
     pair = (keep + swap(send, 1).astype(F32)).astype(BF16)
     parts = lax.all_to_all(
         pair.reshape(groups * replicas, rows // replicas, width), ("hi", "rep"), 0, 0, tiled=True

time: 37.1 us -> 34.9 us (0.941)
  waiting for transfers between devices: 8.99 us -> 7.63 us
  local copies, waits for them, and re-layouts: 1.48 us -> 0.92 us
    ppermute x7, waiting for transfers between devices: 8.99 us -> 7.63 us  [swap(): return lax.ppermute(value, ('hi', 'lo'), [(i, i ^ xor) for i in range(4)])]
    unnamed x30, local copies, waits for them, and re-layouts: 1.48 us -> 0.92 us
    pallas_call x3 -> x6, Pallas kernels: 3.22 us -> 3.31 us  [the longest x1 1.6 us: on_device(): pl.pallas_call(attend_kernel, out_shape=(shape((half, model_width), BF16)...]
  transfers between devices with their start and end apart: 7 -> 7, of which waited for: 5 -> 7; matrix products, arithmetic and copies ran while one was open for 0% -> 0% of each run, Pallas kernels for 3% -> 6%
where the time goes in v3:
time: 34.9 us; the launch traced here: 34.7 us
  blocking collectives  14.7 us (42%)
  waiting for transfers between devices  7.63 us (22%)
  starting transfers between devices  6.17 us (18%)
  Pallas kernels  4.38 us (13%)
  local copies, waits for them, and re-layouts  0.92 us (3%)
  other arithmetic  0.74 us (2%)
    all_to_all x1, blocking collectives, on_device(): lax.all_to_all(pair.reshape(groups * replicas, rows // replicas, width),...  14.7 us
    ppermute x7, waiting for transfers between devices, swap(): return lax.ppermute(value, ('hi', 'lo'), [(i, i ^ xor) for i in range(4)])  7.63 us
    ppermute x7, starting transfers between devices, swap(): return lax.ppermute(value, ('hi', 'lo'), [(i, i ^ xor) for i in range(4)])  6.17 us
    pallas_call x1, Pallas kernels, on_device(): pl.pallas_call(attend_kernel, out_shape=(shape((half, model_width), BF16)...  1.6 us
    pallas_call x1, Pallas kernels, on_device(): pl.pallas_call(functools.partial(prepare_kernel, replicas, cached, new_sl...  1.07 us
    unnamed x30, local copies, waits for them, and re-layouts  0.92 us
  transfers between devices with their start and end apart: 7, of which 7 were waited for; matrix products, arithmetic and copies ran while one was open for 0% of the time, Pallas kernels for 6%

profile of v3, /device:TPU:0, one launch (start us, length us, event | category | flops | bytes accessed | tf_op | source)
XLA Modules:
  0.0 34.7 jit_solution(13939045589626451014)
XLA Ops:
  0.0 2.4 %collective-permute-start = (bf16[128,256]{1,0:T(8,128)(2,1)}, bf16[128,256]{1,0:T(8,128)(2,1)S(1)}, u32[]{:S(2)}, u32[]{:S(2)}) collective-permute-start(bf16[128,256]{1,0:T(8,128)(2,1)} %own_ref.3), channel_id=1, source_target_pairs={{0,3},{1,2},{2,1},{3,0},{4,7},{5,6},{6,5},{7,4},{8,11},{9,10},{10,... | collective-permute-start | bytes 196616 | tf_op jit(solution)/shard_map/ppermute | solution.py:213
  2.4 0.0 copy-start.11
  2.4 0.0 copy-start.12
  2.4 0.0 copy-start.13
  2.4 0.0 copy-start.14
  2.4 0.7 %copy-done.11 = f32[32,4]{0,1:T(4,128)S(1)} copy-done((f32[32,4]{0,1:T(4,128)S(1)}, f32[32,4]{0,1:T(4,128)}, u32[]{:S(2)}) %copy-start.11) | copy-done | bytes 536
  3.1 0.0 copy-done.12
  3.1 0.0 copy-done.13
  3.1 0.0 copy-done.14
  3.1 0.0 copy-start.4
  3.1 0.0 copy-start.5
  3.1 0.0 copy-start.7
  3.2 0.0 copy-start.8
  3.2 1.1 %prepare.1 = (f32[2,256,128]{2,1,0:T(8,128)S(1)}, bf16[128,128]{1,0:T(8,128)(2,1)S(1)}) custom-call(f32[4,32]{1,0:T(4,128)S(1)} %bitcast.12, s32[1,2]{1,0:T(1,128)S(1)} %bitcast.13, s32[1,2]{1,0:T(1,128)S(1)} %bitcast.14, s32[1,128]{1,0:T(1,128)S(1)} %copy-done.14), custom_call_target="tpu_custom_call" | custom-call | flops 7000000000 | tf_op jit(solution)/shard_map/prepare/pallas_call | solution.py:243
  4.2 0.0 copy-start.10
  4.3 0.9 %collective-permute-done.far_ref = bf16[128,256]{1,0:T(8,128)(2,1)S(1)} collective-permute-done((bf16[128,256]{1,0:T(8,128)(2,1)}, bf16[128,256]{1,0:T(8,128)(2,1)S(1)}, u32[]{:S(2)}, u32[]{:S(2)}) %collective-permute-start) | collective-permute-done | bytes 65568 | tf_op jit(solution)/shard_map/ppermute | solution.py:213
  5.2 0.0 copy-done.6
  5.2 0.1 collective-permute-start.1
  5.3 0.4 %collective-permute-start.2 = (bf16[128,256]{1,0:T(8,128)(2,1)S(1)}, bf16[128,256]{1,0:T(8,128)(2,1)S(1)}, u32[]{:S(2)}, u32[]{:S(2)}) collective-permute-start(bf16[128,256]{1,0:T(8,128)(2,1)S(1)} %collective-permute-done.far_ref), channel_id=1, source_target_pairs={{0,1},{1,0},{2,3},{3,2},{4,5},{5,4},{6,7},{7,6},{8,9},{9,8},{10,11... | collective-permute-start | bytes 196616 | tf_op jit(solution)/shard_map/ppermute | solution.py:213
  5.7 0.7 %collective-permute-done.1.near_ref = bf16[128,256]{1,0:T(8,128)(2,1)S(1)} collective-permute-done((bf16[128,256]{1,0:T(8,128)(2,1)S(1)}, bf16[128,256]{1,0:T(8,128)(2,1)S(1)}, u32[]{:S(2)}, u32[]{:S(2)}) %collective-permute-start.1) | collective-permute-done | bytes 65568 | tf_op jit(solution)/shard_map/ppermute | solution.py:213
  6.5 0.2 collective-permute-done.2.near_far_ref
  6.6 0.0 copy-done.2
  6.6 0.0 copy-done.3
  6.6 0.0 copy-done.4
  6.6 0.0 copy-done.5
  6.6 0.0 copy-done.7
  6.6 0.0 copy-done.8
  6.6 0.0 copy-done.10
  6.7 1.6 %attend.1 = (bf16[64,1024]{1,0:T(8,128)(2,1)S(1)}, bf16[64,256]{1,0:T(8,128)(2,1)S(1)}) custom-call(bf16[128,256]{1,0:T(8,128)(2,1)S(1)} %copy-done.6, bf16[128,256]{1,0:T(8,128)(2,1)S(1)} %collective-permute-done.far_ref, bf16[128,256]{1,0:T(8,128)(2,1)S(1)} %collective-permute-done.1.near_ref, bf16[128,256]{1,0:T(8,128)(2,1)S(1)} %collective-permute-done.2.near_far_ref, ...), custom_call_target="tpu_custom_call" | custom-call | tf_op jit(solution)/shard_map/attend/pallas_call | solution.py:257
  8.3 0.4 %collective-permute-start.3 = (bf16[64,1024]{1,0:T(8,128)(2,1)S(1)}, bf16[64,1024]{1,0:T(8,128)(2,1)S(1)}, u32[]{:S(2)}, u32[]{:S(2)}) collective-permute-start(bf16[64,1024]{1,0:T(8,128)(2,1)S(1)} %get-tuple-element.22), channel_id=1, source_target_pairs={{0,1},{1,0},{2,3},{3,2},{4,5},{5,4},{6,7},{7,6},{8,9},{9,8},{10,11... | collective-permute-start | bytes 393224 | tf_op jit(solution)/shard_map/ppermute | solution.py:213
  8.7 0.2 project.1
  8.9 0.8 %collective-permute-done.3 = bf16[64,1024]{1,0:T(8,128)(2,1)S(1)} collective-permute-done((bf16[64,1024]{1,0:T(8,128)(2,1)S(1)}, bf16[64,1024]{1,0:T(8,128)(2,1)S(1)}, u32[]{:S(2)}, u32[]{:S(2)}) %collective-permute-start.3) | collective-permute-done | bytes 131104 | tf_op jit(solution)/shard_map/ppermute | solution.py:213
  9.7 2.4 %collective-permute-start.4 = (bf16[64,1024]{1,0:T(8,128)(2,1)S(1)}, bf16[64,1024]{1,0:T(8,128)(2,1)S(1)}, u32[]{:S(2)}, u32[]{:S(2)}) collective-permute-start(bf16[64,1024]{1,0:T(8,128)(2,1)S(1)} %add_convert_fusion.2), channel_id=1, source_target_pairs={{0,3},{1,2},{2,1},{3,0},{4,7},{5,6},{6,5},{7,4},{8,11},{9,10},{10,... | collective-permute-start | bytes 393224 | tf_op jit(solution)/shard_map/ppermute | solution.py:213
  12.1 3.7 %collective-permute-done.4 = bf16[64,1024]{1,0:T(8,128)(2,1)S(1)} collective-permute-done((bf16[64,1024]{1,0:T(8,128)(2,1)S(1)}, bf16[64,1024]{1,0:T(8,128)(2,1)S(1)}, u32[]{:S(2)}, u32[]{:S(2)}) %collective-permute-start.4) | collective-permute-done | bytes 131104 | tf_op jit(solution)/shard_map/ppermute | solution.py:213
  15.9 0.0 copy-start.1
  15.9 0.2 collective-permute-start.5
  16.1 0.2 stream.1.stream_ref
  16.3 0.0 copy-done
  16.3 0.2 copy-done.9
  16.5 0.4 %inner.1.first_ref = bf16[64,512]{1,0:T(8,128)(2,1)S(1)} custom-call(bf16[64,1024]{1,0:T(8,128)(2,1)S(1)} %add_convert_fusion.1.total_ref.own_ref, bf16[128,1024]{1,0:T(8,128)(2,1)S(1)} %stream.1.stream_ref, f32[1,1024]{1,0:T(1,128)S(1)} %bitcast.9, bf16[1024,512]{1,0:T(8,128)(2,1)S(1)} %copy-done), custom_call_target="tpu_custom_call" | custom-call | tf_op jit(solution)/shard_map/inner/pallas_call | solution.py:296
  16.9 0.4 %collective-permute-done.5.total_ref.other_ref = bf16[64,1024]{1,0:T(8,128)(2,1)S(1)} collective-permute-done((bf16[64,1024]{1,0:T(8,128)(2,1)S(1)}, bf16[64,1024]{1,0:T(8,128)(2,1)S(1)}, u32[]{:S(2)}, u32[]{:S(2)}) %collective-permute-start.5) | collective-permute-done | bytes 131104 | tf_op jit(solution)/shard_map/ppermute | solution.py:213
  17.3 0.0 copy-done.1
  17.3 0.6 %send.1 = (bf16[64,512]{1,0:T(8,128)(2,1)S(1)}, bf16[2,128,256]{2,1,0:T(8,128)(2,1)S(1)}) custom-call(bf16[64,1024]{1,0:T(8,128)(2,1)S(1)} %collective-permute-done.5.total_ref.other_ref, bf16[128,1024]{1,0:T(8,128)(2,1)S(1)} %stream.1.stream_ref, f32[1,1024]{1,0:T(1,128)S(1)} %bitcast.10, bf16[1024,512]{1,0:T(8,128)(2,1)S(1)} %copy-done, ...), custom_call_target="tpu_custom_call" | custom-call | tf_op jit(solution)/shard_map/send/pallas_call | solution.py:304
  17.9 0.2 collective-permute-start.6
  18.1 0.3 keep.1
  18.4 0.9 %collective-permute-done.6 = bf16[2,128,256]{2,1,0:T(8,128)(2,1)S(1)} collective-permute-done((bf16[2,128,256]{2,1,0:T(8,128)(2,1)S(1)}, bf16[2,128,256]{2,1,0:T(8,128)(2,1)S(1)}, u32[]{:S(2)}, u32[]{:S(2)}) %collective-permute-start.6) | collective-permute-done | bytes 131104 | tf_op jit(solution)/shard_map/ppermute | solution.py:213
  19.4 14.7 %all_to_all.5 = bf16[16,16,256]{2,1,0:T(8,128)(2,1)S(1)} all-to-all(bf16[16,16,256]{2,1,0:T(8,128)(2,1)S(1)} %bitcast.16), channel_id=1, replica_groups=mesh['rep'=8,'hi'=2,'lo'=2] {'hi','rep'}, dimensions={0} | all-to-all | bytes 262144 | tf_op jit(solution)/shard_map/all_to_all | solution.py:319
  34.1 0.6 %bitcast_reduce_fusion = bf16[128,256]{1,0:T(8,128)(2,1)} fusion(bf16[2,128,256]{2,1,0:T(8,128)(2,1)S(1)} %bitcast.15), kind=kLoop, calls=%fused_computation.3 | loop fusion | flops 32768 | bytes 196608 | tf_op jit(solution)/shard_map/reduce_sum | solution.py:322
  (8 shorter events, 0.1 us)
Async XLA Ops:
  0.0 5.2 %collective-permute-start = (bf16[128,256]{1,0:T(8,128)(2,1)}, bf16[128,256]{1,0:T(8,128)(2,1)S(1)}, u32[]{:S(2)}, u32[]{:S(2)}) collective-permute-start(bf16[128,256]{1,0:T(8,128)(2,1)} %own_ref.3), channel_id=1, source_target_pairs={{0,3},{1,2},{2,1},{3,0},{4,7},{5,6},{6,5},{7,4},{8,11},{9,10},{10,... | collective-permute-start | bytes 196616 | tf_op jit(solution)/shard_map/ppermute | solution.py:213
  2.4 0.7 %copy-start.11 = (f32[32,4]{0,1:T(4,128)S(1)}, f32[32,4]{0,1:T(4,128)}, u32[]{:S(2)}) copy-start(f32[32,4]{0,1:T(4,128)} %param.24) | copy-start | bytes 1540
  2.4 0.7 %copy-start.12 = (s32[2,1]{0,1:T(1,128)S(1)}, s32[2,1]{0,1:T(1,128)}, u32[]{:S(2)}) copy-start(s32[2,1]{0,1:T(1,128)} %param.27) | copy-start | bytes 28
  2.4 0.7 %copy-start.13 = (s32[2,1]{0,1:T(1,128)S(1)}, s32[2,1]{0,1:T(1,128)}, u32[]{:S(2)}) copy-start(s32[2,1]{0,1:T(1,128)} %param.28) | copy-start | bytes 28
  2.4 0.7 %copy-start.14 = (s32[1,128]{1,0:T(1,128)S(1)}, s32[1,128]{1,0:T(1,128)}, u32[]{:S(2)}) copy-start(s32[1,128]{1,0:T(1,128)} %deal_ref.1) | copy-start | bytes 1540
  3.1 2.1 %copy-start.6 = (bf16[128,256]{1,0:T(8,128)(2,1)S(1)}, bf16[128,256]{1,0:T(8,128)(2,1)}, u32[]{:S(2)}) copy-start(bf16[128,256]{1,0:T(8,128)(2,1)} %own_ref.3) | copy-start | bytes 196612
  3.1 3.5 %copy-start.2 = (bf16[256,1024]{1,0:T(8,128)(2,1)S(1)}, bf16[256,1024]{1,0:T(8,128)(2,1)}, u32[]{:S(2)}) copy-start(bf16[256,1024]{1,0:T(8,128)(2,1)} %w_out_ref.3) | copy-start | bytes 1572868
  3.1 3.5 %copy-start.3 = (bf16[1024,256]{1,0:T(8,128)(2,1)S(1)}, bf16[1024,256]{1,0:T(8,128)(2,1)}, u32[]{:S(2)}) copy-start(bf16[1024,256]{1,0:T(8,128)(2,1)} %w_query_ref.1) | copy-start | bytes 1572868
  3.1 3.5 %copy-start.4 = (bf16[1024,256]{1,0:T(8,128)(2,1)S(1)}, bf16[1024,256]{1,0:T(8,128)(2,1)}, u32[]{:S(2)}) copy-start(bf16[1024,256]{1,0:T(8,128)(2,1)} %w_key_ref.1) | copy-start | bytes 1572868
  3.1 3.5 %copy-start.5 = (bf16[1024,256]{1,0:T(8,128)(2,1)S(1)}, bf16[1024,256]{1,0:T(8,128)(2,1)}, u32[]{:S(2)}) copy-start(bf16[1024,256]{1,0:T(8,128)(2,1)} %w_value_ref.1) | copy-start | bytes 1572868
  3.1 3.5 %copy-start.7 = (bf16[2,64,256]{2,1,0:T(8,128)(2,1)S(1)}, bf16[2,64,256]{2,1,0:T(8,128)(2,1)}, u32[]{:S(2)}) copy-start(bf16[2,64,256]{2,1,0:T(8,128)(2,1)} %cache_keys_ref.1) | copy-start | bytes 196612
  3.2 3.5 %copy-start.8 = (bf16[2,64,256]{2,1,0:T(8,128)(2,1)S(1)}, bf16[2,64,256]{2,1,0:T(8,128)(2,1)}, u32[]{:S(2)}) copy-start(bf16[2,64,256]{2,1,0:T(8,128)(2,1)} %cache_values_ref.1) | copy-start | bytes 196612
  4.2 2.4 %copy-start.10 = (f32[1024]{0:T(1024)S(1)}, f32[1024]{0:T(1024)}, u32[]{:S(2)}) copy-start(f32[1024]{0:T(1024)} %param.16) | copy-start | bytes 12292
  5.2 1.3 %collective-permute-start.1 = (bf16[128,256]{1,0:T(8,128)(2,1)S(1)}, bf16[128,256]{1,0:T(8,128)(2,1)S(1)}, u32[]{:S(2)}, u32[]{:S(2)}) collective-permute-start(bf16[128,256]{1,0:T(8,128)(2,1)S(1)} %copy-done.6), channel_id=1, source_target_pairs={{0,1},{1,0},{2,3},{3,2},{4,5},{5,4},{6,7},{7,6},{8,9},{9,8},{10,11... | collective-permute-start | bytes 196616 | tf_op jit(solution)/shard_map/ppermute | solution.py:213
  5.3 1.3 %collective-permute-start.2 = (bf16[128,256]{1,0:T(8,128)(2,1)S(1)}, bf16[128,256]{1,0:T(8,128)(2,1)S(1)}, u32[]{:S(2)}, u32[]{:S(2)}) collective-permute-start(bf16[128,256]{1,0:T(8,128)(2,1)S(1)} %collective-permute-done.far_ref), channel_id=1, source_target_pairs={{0,1},{1,0},{2,3},{3,2},{4,5},{5,4},{6,7},{7,6},{8,9},{9,8},{10,11... | collective-permute-start | bytes 196616 | tf_op jit(solution)/shard_map/ppermute | solution.py:213
  8.3 1.4 %collective-permute-start.3 = (bf16[64,1024]{1,0:T(8,128)(2,1)S(1)}, bf16[64,1024]{1,0:T(8,128)(2,1)S(1)}, u32[]{:S(2)}, u32[]{:S(2)}) collective-permute-start(bf16[64,1024]{1,0:T(8,128)(2,1)S(1)} %get-tuple-element.22), channel_id=1, source_target_pairs={{0,1},{1,0},{2,3},{3,2},{4,5},{5,4},{6,7},{7,6},{8,9},{9,8},{10,11... | collective-permute-start | bytes 393224 | tf_op jit(solution)/shard_map/ppermute | solution.py:213
  8.7 7.6 %copy-start = (bf16[1024,512]{1,0:T(8,128)(2,1)S(1)}, bf16[1024,512]{1,0:T(8,128)(2,1)}, u32[]{:S(2)}) copy-start(bf16[1024,512]{1,0:T(8,128)(2,1)} %w_inner_ref.3) | copy-start | bytes 3145732
  9.7 6.1 %collective-permute-start.4 = (bf16[64,1024]{1,0:T(8,128)(2,1)S(1)}, bf16[64,1024]{1,0:T(8,128)(2,1)S(1)}, u32[]{:S(2)}, u32[]{:S(2)}) collective-permute-start(bf16[64,1024]{1,0:T(8,128)(2,1)S(1)} %add_convert_fusion.2), channel_id=1, source_target_pairs={{0,3},{1,2},{2,1},{3,0},{4,7},{5,6},{6,5},{7,4},{8,11},{9,10},{10,... | collective-permute-start | bytes 393224 | tf_op jit(solution)/shard_map/ppermute | solution.py:213
  15.8 0.7 %copy-start.9 = (f32[1024]{0:T(1024)S(1)}, f32[1024]{0:T(1024)}, u32[]{:S(2)}) copy-start(f32[1024]{0:T(1024)} %param.17) | copy-start | bytes 12292
  15.9 1.4 %copy-start.1 = (bf16[512,1024]{1,0:T(8,128)(2,1)S(1)}, bf16[512,1024]{1,0:T(8,128)(2,1)}, u32[]{:S(2)}) copy-start(bf16[512,1024]{1,0:T(8,128)(2,1)} %w_outer_ref.3) | copy-start | bytes 3145732
  15.9 1.4 %collective-permute-start.5 = (bf16[64,1024]{1,0:T(8,128)(2,1)S(1)}, bf16[64,1024]{1,0:T(8,128)(2,1)S(1)}, u32[]{:S(2)}, u32[]{:S(2)}) collective-permute-start(bf16[64,1024]{1,0:T(8,128)(2,1)S(1)} %add_convert_fusion.1.total_ref.own_ref), channel_id=1, source_target_pairs={{0,1},{1,0},{2,3},{3,2},{4,5},{5,4},{6,7},{7,6},{8,9},{9,8},{10,11... | collective-permute-start | bytes 393224 | tf_op jit(solution)/shard_map/ppermute | solution.py:213
  17.9 1.4 %collective-permute-start.6 = (bf16[2,128,256]{2,1,0:T(8,128)(2,1)S(1)}, bf16[2,128,256]{2,1,0:T(8,128)(2,1)S(1)}, u32[]{:S(2)}, u32[]{:S(2)}) collective-permute-start(bf16[2,128,256]{2,1,0:T(8,128)(2,1)S(1)} %get-tuple-element.24), channel_id=1, source_target_pairs={{0,1},{1,0},{2,3},{3,2},{4,5},{5,4},{6,7},{7,6},{8,9},{9,8},{10,11... | collective-permute-start | bytes 393224 | tf_op jit(solution)/shard_map/ppermute | solution.py:213

commit v4 on v3

v4 whole, which is shorter than its diff:
```python
import functools

import jax
import jax.numpy as jnp
from jax import lax
from jax.experimental import pallas as pl
from jax.experimental.pallas import tpu as pltpu
from jax.sharding import Mesh, PartitionSpec as P

EPSILON = 1e-06
THRESHOLDS = (1, 2, 3, 4, 5, 6, 7, 8, 12, 16, 23, 32, 46, 64, 91)
BF16 = jnp.bfloat16
F32 = jnp.float32
VMEM = pl.BlockSpec(memory_space=pltpu.VMEM)
SMEM = pl.BlockSpec(memory_space=pltpu.SMEM)
PREPARE_FLOPS = 7 * 10**9
INNER_FLOPS = 40 * 10**9
VMEM_LIMIT = 24 * 1024 * 1024


def dot(a, b):
    return jnp.dot(a, b, preferred_element_type=F32)


def place():
    upper, lower = lax.axis_index("hi"), lax.axis_index("lo")
    return upper * 2 + lower, upper ^ lower


def columns_of(index, width):
    return pl.ds(pl.multiple_of(index * width, width), width)


def bias_of(table_ref, relative, head):
    distance = jnp.abs(relative)
    before = jnp.full(relative.shape, table_ref[head, 0], F32)
    after = jnp.full(relative.shape, table_ref[head, 17], F32)
    for step, threshold in enumerate(THRESHOLDS):
        far = distance >= threshold
        before = jnp.where(far, table_ref[head, step + 1], before)
        after = jnp.where(far, table_ref[head, step + 17], after)
    return jnp.where(relative > 0, after, before)


def prepare_kernel(
    replicas, cached, table_ref, counts_ref, lengths_ref, deal_ref, bias_ref, picked_ref
):
    _, side = place()
    rows = deal_ref.shape[1]
    new_slots = rows // 2
    deal = deal_ref[...]
    slot = lax.rem(deal, replicas) * (rows // replicas) + lax.div(deal, replicas)
    lane = lax.broadcasted_iota(jnp.int32, (1, rows), 1)
    live = lane < jnp.where(
        lane < new_slots, counts_ref[0, 0], jnp.minimum(counts_ref[0, 1], new_slots) + new_slots
    )
    slot = jnp.where(live, slot, -1)
    turned = jnp.concatenate([slot[:, new_slots:], slot[:, :new_slots]], axis=1)
    slot = jnp.where(side == 0, slot, turned)[:, :new_slots]
    row = lax.broadcasted_iota(jnp.int32, (rows, new_slots), 0)
    picked_ref[...] = jnp.where(row == slot, 1.0, 0.0).astype(BF16)

    requests, _, key_slots = bias_ref.shape
    key_index = lax.broadcasted_iota(jnp.int32, (new_slots, key_slots), 1)
    query_index = lax.broadcasted_iota(jnp.int32, (new_slots, key_slots), 0)
    is_cache = key_index < cached
    for j in range(requests):
        length, count = lengths_ref[0, j], counts_ref[0, j]
        position = jnp.where(is_cache, key_index, length + key_index - cached)
        relative = position - (length + query_index)
        live = jnp.where(is_cache, key_index - length, key_index - cached - count) < 0
        for h in range(table_ref.shape[0]):
            bias = jnp.where(live, bias_of(table_ref, relative, h), -1e30)
            bias_ref[j, h * new_slots : (h + 1) * new_slots] = bias


def attend(query, new_keys, new_values, old_keys, old_values, bias):
    new_slots, local_width = query.shape
    head_count = bias.shape[0] // new_slots
    lane = lax.broadcasted_iota(jnp.int32, (new_slots, local_width), 1)
    lane_head = lane // (local_width // head_count)
    stacked = jnp.concatenate(
        [jnp.where(lane_head == h, query, jnp.zeros_like(query)) for h in range(head_count)],
        axis=0,
    )
    keys = jnp.concatenate([old_keys, new_keys], axis=0)
    values = jnp.concatenate([old_values, new_values], axis=0)
    scores = lax.dot_general(stacked, keys, (((1,), (1,)), ((), ())), preferred_element_type=F32)
    scores = scores + bias
    weights = jnp.exp(scores - jnp.max(scores, axis=1, keepdims=True))
    probs = (weights / jnp.sum(weights, axis=1, keepdims=True)).astype(BF16)
    mixed = dot(probs, values)
    context = jnp.zeros((new_slots, local_width), F32)
    for h in range(head_count):
        context = jnp.where(lane_head == h, mixed[h * new_slots : (h + 1) * new_slots], context)
    return context.astype(BF16)


def first_kernel(
    own_ref,
    near_ref,
    far_ref,
    across_ref,
    gain_ref,
    w_query_ref,
    w_key_ref,
    w_value_ref,
    w_out_ref,
    cache_keys_ref,
    cache_values_ref,
    bias_ref,
    send_ref,
    query_ref,
    key_ref,
    value_ref,
):
    index, side = place()
    rows, width = own_ref.shape
    model_width = gain_ref.shape[1]
    new_slots = rows // 2
    blocks = [(own_ref, 0), (near_ref, 1), (far_ref, 3), (across_ref, 2)]
    squares = 0.0
    for ref, _ in blocks:
        block = ref[...].astype(F32)
        squares = squares + jnp.sum(block * block, axis=1, keepdims=True)
    inverse = lax.rsqrt(squares / model_width + EPSILON)
    queries = new_keys = new_values = 0.0
    for ref, xor in blocks:
        columns = columns_of(index ^ xor, width)
        normed = (ref[...].astype(F32) * inverse * gain_ref[:, columns]).astype(BF16)
        queries = queries + dot(normed, w_query_ref[columns, :])
        new_keys = new_keys + dot(normed, w_key_ref[columns, :])
        new_values = new_values + dot(normed, w_value_ref[columns, :])
    query_ref[...] = queries.astype(BF16)
    key_ref[...] = new_keys.astype(BF16)
    value_ref[...] = new_values.astype(BF16)
    other = 1 - side
    own = columns_of(other, new_slots)
    context = attend(
        query_ref[own, :],
        key_ref[own, :],
        value_ref[own, :],
        cache_keys_ref[other],
        cache_values_ref[other],
        bias_ref[other],
    )
    send_ref[...] = dot(context, w_out_ref[...]).astype(BF16)


def second_kernel(
    query_ref, key_ref, value_ref, w_out_ref, cache_keys_ref, cache_values_ref, bias_ref, keep_ref
):
    _, side = place()
    own = columns_of(side, keep_ref.shape[0])
    context = attend(
        query_ref[own, :],
        key_ref[own, :],
        value_ref[own, :],
        cache_keys_ref[side],
        cache_values_ref[side],
        bias_ref[side],
    )
    keep_ref[...] = dot(context, w_out_ref[...])


def stream_kernel(own_ref, near_ref, far_ref, across_ref, stream_ref):
    index, side = place()
    width = own_ref.shape[1]
    rows = columns_of(side, stream_ref.shape[0])
    for ref, xor in ((own_ref, 0), (near_ref, 1), (far_ref, 3), (across_ref, 2)):
        stream_ref[:, columns_of(index ^ xor, width)] = ref[rows, :]


def project(hidden_refs, w_outer_refs, mixed_ref, picked_ref, group, core):
    upper = lax.axis_index("hi")
    width = mixed_ref.shape[1] // 4
    columns = columns_of(group * 2 + core, width)
    value = jnp.where(upper == group, mixed_ref[:, columns], 0.0)
    for hidden_ref, w_outer_ref in zip(hidden_refs, w_outer_refs):
        value = value + dot(hidden_ref[...], w_outer_ref[:, columns])
    return dot(picked_ref[...], value.astype(BF16)).astype(BF16)


def inner_kernel(
    pair_ref, other_ref, stream_ref, gain_ref, w_inner_ref, mixed_ref, input_ref, hidden_ref
):
    mixed = pair_ref[...].astype(F32) + other_ref[...].astype(F32) + stream_ref[...].astype(F32)
    mixed_ref[...] = mixed
    square = jnp.sum(mixed * mixed, axis=1, keepdims=True)
    inverse = lax.rsqrt(square / mixed.shape[1] + EPSILON)
    ffn_input = (mixed * inverse * gain_ref[...]).astype(BF16)
    input_ref[...] = ffn_input
    hidden_ref[...] = jnp.maximum(dot(ffn_input, w_inner_ref[...]), 0.0).astype(BF16)


def send_kernel(
    mixed_ref,
    input_ref,
    own_hidden_ref,
    near_inner_ref,
    own_outer_ref,
    near_outer_ref,
    picked_ref,
    near_hidden_ref,
    send_ref,
):
    hidden = jnp.maximum(dot(input_ref[...], near_inner_ref[...]), 0.0)
    near_hidden_ref[...] = hidden.astype(BF16)
    hidden_refs, outer_refs = (own_hidden_ref, near_hidden_ref), (own_outer_ref, near_outer_ref)
    core = 1 - lax.axis_index("lo")
    for g in range(send_ref.shape[0]):
        send_ref[g] = project(hidden_refs, outer_refs, mixed_ref, picked_ref, g, core)


def keep_kernel(
    mixed_ref,
    own_hidden_ref,
    near_hidden_ref,
    own_outer_ref,
    near_outer_ref,
    picked_ref,
    keep_ref,
):
    hidden_refs, outer_refs = (own_hidden_ref, near_hidden_ref), (own_outer_ref, near_outer_ref)
    core = lax.axis_index("lo")
    for g in range(keep_ref.shape[0]):
        keep_ref[g] = project(hidden_refs, outer_refs, mixed_ref, picked_ref, g, core)


def swap(value, xor):
    return lax.ppermute(value, ("hi", "lo"), [(i, i ^ xor) for i in range(4)])


def on_device(
    replicas,
    tokens,
    attn_gain,
    ffn_gain,
    w_query,
    w_key,
    w_value,
    w_out,
    w_inner,
    w_outer,
    bias_table,
    cache_keys,
    cache_values,
    new_counts,
    cached_lengths,
    deal,
):
    rows, width = tokens.shape
    requests, cached, local_width = cache_keys.shape
    new_slots = rows // requests
    model_width = attn_gain.shape[0]
    head_count = bias_table.shape[1]
    groups = lax.axis_size("hi")
    shape = jax.ShapeDtypeStruct
    local = functools.partial(
        pl.pallas_call, compiler_params=pltpu.CompilerParams(vmem_limit_bytes=VMEM_LIMIT)
    )
    across, far = swap(tokens, 2), swap(tokens, 3)
    bias, picked = local(
        functools.partial(prepare_kernel, replicas, cached),
        out_shape=(
            shape((requests, head_count * new_slots, cached + new_slots), F32),
            shape((rows, new_slots), BF16),
        ),
        in_specs=[SMEM] * 3 + [VMEM],
        out_specs=(VMEM,) * 2,
        cost_estimate=pl.CostEstimate(flops=PREPARE_FLOPS, bytes_accessed=0, transcendentals=0),
        name="prepare",
    )(bias_table.T, new_counts.T, cached_lengths.T, deal)
    late, bias, picked = lax.optimization_barrier((tokens, bias, picked))
    blocks = (tokens, swap(late, 1), far, across)
    projected = shape((rows, local_width), BF16)
    send, *projections = local(
        first_kernel,
        out_shape=(shape((new_slots, model_width), BF16),) + (projected,) * 3,
        in_specs=[VMEM] * 12,
        out_specs=(VMEM,) * 4,
        name="first",
    )(
        *blocks,
        attn_gain.reshape(1, model_width),
        w_query,
        w_key,
        w_value,
        w_out,
        cache_keys,
        cache_values,
        bias,
    )
    keep = local(
        second_kernel,
        out_shape=shape((new_slots, model_width), F32),
        in_specs=[VMEM] * 7,
        out_specs=VMEM,
        name="second",
    )(*projections, w_out, cache_keys, cache_values, bias)
    stream = local(
        stream_kernel,
        out_shape=shape((new_slots, model_width), BF16),
        in_specs=[VMEM] * 4,
        out_specs=VMEM,
        name="stream",
    )(*blocks)
    pair = (keep + swap(send, 1).astype(F32)).astype(BF16)
    late_inner, late_outer, pair = lax.optimization_barrier((w_inner, w_outer, pair))
    ff_width = w_inner.shape[1]
    hidden = shape((new_slots, ff_width), BF16)
    dealt = shape((groups, rows, width), BF16)
    mixed, ffn_input, first = local(
        inner_kernel,
        out_shape=(
            shape((new_slots, model_width), F32),
            shape((new_slots, model_width), BF16),
            hidden,
        ),
        in_specs=[VMEM] * 5,
        out_specs=(VMEM,) * 3,
        cost_estimate=pl.CostEstimate(flops=INNER_FLOPS, bytes_accessed=0, transcendentals=0),
        name="inner",
    )(pair, swap(pair, 3), stream, ffn_gain.reshape(1, model_width), w_inner)
    outer = (w_outer, swap(late_outer, 1))
    second, send = local(
        send_kernel,
        out_shape=(hidden, dealt),
        in_specs=[VMEM] * 7,
        out_specs=(VMEM,) * 2,
        name="send",
    )(mixed, ffn_input, first, swap(late_inner, 1), *outer, picked)
    keep = local(
        keep_kernel,
        out_shape=dealt,
        in_specs=[VMEM] * 6,
        out_specs=VMEM,
        name="keep",
    )(mixed, first, second, *outer, picked)
    pair = keep + swap(send, 1)
    parts = lax.all_to_all(
        pair.reshape(groups * replicas, rows // replicas, width), ("hi", "rep"), 0, 0, tiled=True
    )
    return jnp.sum(parts.reshape(groups, rows, width).astype(F32), axis=0).astype(BF16)


def solution(mesh):
    replicas, tp = mesh.shape["rep"], mesh.shape["tp"]
    split = Mesh(mesh.devices.reshape(replicas, tp // 2, 2), ("rep", "hi", "lo"))
    cols = ("hi", "lo")
    in_specs = (
        P("rep", cols),
        P(),
        P(),
        P(None, cols),
        P(None, cols),
        P(None, cols),
        P(cols, None),
        P(None, cols),
        P(cols, None),
        P(None, cols),
        P("rep", None, cols),
        P("rep", None, cols),
        P(None, "rep"),
        P(None, "rep"),
        P("rep", None),
    )
    return jax.shard_map(
        functools.partial(on_device, replicas),
        mesh=split,
        in_specs=in_specs,
        out_specs=P("rep", cols),
        check_vma=False,
    )
```

time: 34.9 us -> 33 us (0.946)
  starting transfers between devices: 6.17 us -> 4.72 us
  blocking collectives: 14.7 us -> 13.8 us
  Pallas kernels: 4.38 us -> 4.95 us
    ppermute x7 -> x8, starting transfers between devices: 6.17 us -> 4.72 us  [swap(): return lax.ppermute(value, ('hi', 'lo'), [(i, i ^ xor) for i in range(4)])]
    all_to_all x1, blocking collectives: 14.7 us -> 13.8 us  [on_device(): lax.all_to_all(pair.reshape(groups * replicas, rows // replicas, width),...]
    pallas_call x7, Pallas kernels: 4.38 us -> 4.95 us  [the longest x1 1.18 us: on_device(): local(first_kernel, out_shape=(shape((new_slots, model_width), BF16),) +...]
    ppermute x7 -> x8, waiting for transfers between devices: 7.63 us -> 7.6 us  [swap(): return lax.ppermute(value, ('hi', 'lo'), [(i, i ^ xor) for i in range(4)])]
  transfers between devices with their start and end apart: 7 -> 8, of which waited for: 7 -> 5; matrix products, arithmetic and copies ran while one was open for 0% -> 0% of each run, Pallas kernels for 6% -> 9%
where the time goes in v4:
time: 33 us; the launch traced here: 32.8 us
  blocking collectives  13.8 us (42%)
  waiting for transfers between devices  7.6 us (23%)
  Pallas kernels  4.95 us (15%)
  starting transfers between devices  4.72 us (14%)
  local copies, waits for them, and re-layouts  0.74 us (2%)
  other arithmetic  0.71 us (2%)
    all_to_all x1, blocking collectives, on_device(): lax.all_to_all(pair.reshape(groups * replicas, rows // replicas, width),...  13.8 us
    ppermute x8, waiting for transfers between devices, swap(): return lax.ppermute(value, ('hi', 'lo'), [(i, i ^ xor) for i in range(4)])  7.6 us
    ppermute x8, starting transfers between devices, swap(): return lax.ppermute(value, ('hi', 'lo'), [(i, i ^ xor) for i in range(4)])  4.72 us
    pallas_call x1, Pallas kernels, on_device(): local(first_kernel, out_shape=(shape((new_slots, model_width), BF16),) +...  1.18 us
    pallas_call x1, Pallas kernels, on_device(): local(functools.partial(prepare_kernel, replicas, cached), out_shape=(sha...  1.1 us
    pallas_call x1, Pallas kernels, on_device(): local(send_kernel, out_shape=(hidden, dealt), in_specs=[VMEM] * 7, out_sp...  0.87 us
    unnamed x30, local copies, waits for them, and re-layouts  0.74 us
    pallas_call x1, Pallas kernels, on_device(): local(second_kernel, out_shape=shape((new_slots, model_width), F32), in_s...  0.7 us
  transfers between devices with their start and end apart: 8, of which 5 were waited for; matrix products, arithmetic and copies ran while one was open for 0% of the time, Pallas kernels for 9%

profile of v4, /device:TPU:0, one launch (start us, length us, event | category | flops | bytes accessed | tf_op | source)
XLA Modules:
  0.0 32.8 jit_solution(1376698339951156528)
XLA Ops:
  0.0 3.0 %collective-permute-start.2 = (bf16[128,256]{1,0:T(8,128)(2,1)}, bf16[128,256]{1,0:T(8,128)(2,1)S(1)}, u32[]{:S(2)}, u32[]{:S(2)}) collective-permute-start(bf16[128,256]{1,0:T(8,128)(2,1)} %own_ref.3), channel_id=1, source_target_pairs={{0,2},{1,3},{2,0},{3,1},{4,6},{5,7},{6,4},{7,5},{8,10},{9,11},{10,... | collective-permute-start | bytes 196616 | tf_op jit(solution)/shard_map/ppermute | solution.py:231
  3.0 0.0 collective-permute-start.1
  3.0 0.0 copy-start.14
  3.0 0.7 %copy-done.11 = f32[32,4]{0,1:T(4,128)S(1)} copy-done((f32[32,4]{0,1:T(4,128)S(1)}, f32[32,4]{0,1:T(4,128)}, u32[]{:S(2)}) %copy-start.11) | copy-done | bytes 536
  3.7 0.0 copy-done.12
  3.7 0.0 copy-done.13
  3.7 0.0 copy-done.14
  3.7 0.0 copy-start.3
  3.7 0.0 copy-start.4
  3.7 0.0 copy-start.6
  3.7 0.0 copy-start.7
  3.7 1.1 %prepare.1 = (f32[2,256,128]{2,1,0:T(8,128)S(1)}, bf16[128,64]{1,0:T(8,128)(2,1)S(1)}) custom-call(f32[4,32]{1,0:T(4,128)S(1)} %bitcast.11, s32[1,2]{1,0:T(1,128)S(1)} %bitcast.12, s32[1,2]{1,0:T(1,128)S(1)} %bitcast.13, s32[1,128]{1,0:T(1,128)S(1)} %copy-done.14), custom_call_target="tpu_custom_call" | custom-call | flops 7000000000 | tf_op jit(solution)/shard_map/prepare/pallas_call | solution.py:263
  4.8 0.0 copy-start.8
  4.9 0.0 copy-done.5
  4.9 0.2 collective-permute-start
  5.1 0.3 %collective-permute-done.2.across_ref = bf16[128,256]{1,0:T(8,128)(2,1)S(1)} collective-permute-done((bf16[128,256]{1,0:T(8,128)(2,1)}, bf16[128,256]{1,0:T(8,128)(2,1)S(1)}, u32[]{:S(2)}, u32[]{:S(2)}) %collective-permute-start.2) | collective-permute-done | bytes 65568 | tf_op jit(solution)/shard_map/ppermute | solution.py:231
  5.4 1.9 %collective-permute-done.1.far_ref = bf16[128,256]{1,0:T(8,128)(2,1)S(1)} collective-permute-done((bf16[128,256]{1,0:T(8,128)(2,1)}, bf16[128,256]{1,0:T(8,128)(2,1)S(1)}, u32[]{:S(2)}, u32[]{:S(2)}) %collective-permute-start.1) | collective-permute-done | bytes 65568 | tf_op jit(solution)/shard_map/ppermute | solution.py:231
  7.3 0.0 collective-permute-done.near_ref
  7.3 0.0 copy-done.1
  7.3 0.0 copy-done.2
  7.3 0.0 copy-done.3
  7.3 0.0 copy-done.4
  7.3 0.0 copy-done.6
  7.3 0.0 copy-done.7
  7.4 0.0 copy-done.8
  7.4 1.2 %first.1 = (bf16[64,1024]{1,0:T(8,128)(2,1)S(1)}, bf16[128,256]{1,0:T(8,128)(2,1)S(1)}, bf16[128,256]{1,0:T(8,128)(2,1)S(1)}, bf16[128,256]{1,0:T(8,128)(2,1)S(1)}) custom-call(bf16[128,256]{1,0:T(8,128)(2,1)S(1)} %copy-done.5, bf16[128,256]{1,0:T(8,128)(2,1)S(1)} %collective-permute-done.near_ref, bf16[128,256]{1,0:T(8,128)(2,1)S(1)} %collective-permute-done.1.far_ref, ...), custom_call_target="tpu_custom_call" | custom-call | tf_op jit(solution)/shard_map/first/pallas_call | solution.py:277
  8.6 0.1 collective-permute-start.3
  8.6 0.0 copy-start.9
  8.6 0.0 copy-start
  8.7 0.7 %second.1 = f32[64,1024]{1,0:T(8,128)S(1)} custom-call(bf16[128,256]{1,0:T(8,128)(2,1)S(1)} %get-tuple-element.26.query_ref, bf16[128,256]{1,0:T(8,128)(2,1)S(1)} %get-tuple-element.27.key_ref, bf16[128,256]{1,0:T(8,128)(2,1)S(1)} %get-tuple-element.28.value_ref, bf16[256,1024]{1,0:T(8,128)(2,1)S(1)} %copy-done.1, bf16[2,64,256]{2,1,0:T(8,128)(2,1)S(1)} %copy-done.6, ...), custom_call_target="tpu_custom_call" | custom-call | tf_op jit(solution)/shard_map/second/pallas_call | solution.py:294
  9.4 0.6 %collective-permute-done.3 = bf16[64,1024]{1,0:T(8,128)(2,1)S(1)} collective-permute-done((bf16[64,1024]{1,0:T(8,128)(2,1)S(1)}, bf16[64,1024]{1,0:T(8,128)(2,1)S(1)}, u32[]{:S(2)}, u32[]{:S(2)}) %collective-permute-start.3) | collective-permute-done | bytes 131104 | tf_op jit(solution)/shard_map/ppermute | solution.py:231
  10.0 0.0 copy-start.10
  10.0 0.7 %collective-permute-start.4 = (bf16[64,1024]{1,0:T(8,128)(2,1)S(1)}, bf16[64,1024]{1,0:T(8,128)(2,1)S(1)}, u32[]{:S(2)}, u32[]{:S(2)}) collective-permute-start(bf16[64,1024]{1,0:T(8,128)(2,1)S(1)} %add_convert_fusion.pair_ref), channel_id=1, source_target_pairs={{0,3},{1,2},{2,1},{3,0},{4,7},{5,6},{6,5},{7,4},{8,11},{9,10},{10,... | collective-permute-start | bytes 393224 | tf_op jit(solution)/shard_map/ppermute | solution.py:231
  10.7 0.0 copy-done.9
  10.7 0.2 collective-permute-start.5
  10.9 0.0 copy-done
  10.9 0.3 %collective-permute-start.6 = (bf16[512,1024]{1,0:T(8,128)(2,1)S(1)}, bf16[512,1024]{1,0:T(8,128)(2,1)S(1)}, u32[]{:S(2)}, u32[]{:S(2)}) collective-permute-start(bf16[512,1024]{1,0:T(8,128)(2,1)S(1)} %copy-done), channel_id=1, source_target_pairs={{0,1},{1,0},{2,3},{3,2},{4,5},{5,4},{6,7},{7,6},{8,9},{9,8},{10,11... | collective-permute-start | bytes 3145736 | tf_op jit(solution)/shard_map/ppermute | solution.py:231
  11.3 4.3 %collective-permute-done.4.other_ref = bf16[64,1024]{1,0:T(8,128)(2,1)S(1)} collective-permute-done((bf16[64,1024]{1,0:T(8,128)(2,1)S(1)}, bf16[64,1024]{1,0:T(8,128)(2,1)S(1)}, u32[]{:S(2)}, u32[]{:S(2)}) %collective-permute-start.4) | collective-permute-done | bytes 131104 | tf_op jit(solution)/shard_map/ppermute | solution.py:231
  15.5 0.0 copy-done.10
  15.5 0.4 %inner.1 = (f32[64,1024]{1,0:T(8,128)S(1)}, bf16[64,1024]{1,0:T(8,128)(2,1)S(1)}, bf16[64,512]{1,0:T(8,128)(2,1)S(1)}) custom-call(bf16[64,1024]{1,0:T(8,128)(2,1)S(1)} %add_convert_fusion.pair_ref, bf16[64,1024]{1,0:T(8,128)(2,1)S(1)} %collective-permute-done.4.other_ref, bf16[64,1024]{1,0:T(8,128)(2,1)S(1)} %stream.1.stream_ref, f32[1,1024]{1,0:T(1,128)S(1)} %bitcast.10, ...), custom_call_target="tpu_custom_call" | custom-call | flops 40000000000 | tf_op jit(solution)/shard_map/inner/pallas_call | solution.py:313
  15.9 0.0 collective-permute-done.5.near_inner_ref
  16.0 0.0 collective-permute-done.6.near_outer_ref
  16.0 0.9 %send.1 = (bf16[64,512]{1,0:T(8,128)(2,1)S(1)}, bf16[2,128,256]{2,1,0:T(8,128)(2,1)S(1)}) custom-call(f32[64,1024]{1,0:T(8,128)S(1)} %get-tuple-element.31.mixed_ref, bf16[64,1024]{1,0:T(8,128)(2,1)S(1)} %get-tuple-element.33.input_ref, bf16[64,512]{1,0:T(8,128)(2,1)S(1)} %get-tuple-element.32.own_hidden_ref, ...), custom_call_target="tpu_custom_call" | custom-call | tf_op jit(solution)/shard_map/send/pallas_call | solution.py:326
  16.8 0.2 collective-permute-start.7
  17.1 0.7 %keep.1 = bf16[2,128,256]{2,1,0:T(8,128)(2,1)S(1)} custom-call(f32[64,1024]{1,0:T(8,128)S(1)} %get-tuple-element.31.mixed_ref, bf16[64,512]{1,0:T(8,128)(2,1)S(1)} %get-tuple-element.32.own_hidden_ref, bf16[64,512]{1,0:T(8,128)(2,1)S(1)} %get-tuple-element.37.near_hidden_ref, bf16[512,1024]{1,0:T(8,128)(2,1)S(1)} %copy-done, ...), custom_call_target="tpu_custom_call" | custom-call | tf_op jit(solution)/shard_map/keep/pallas_call | solution.py:333
  17.8 0.5 %collective-permute-done.7 = bf16[2,128,256]{2,1,0:T(8,128)(2,1)S(1)} collective-permute-done((bf16[2,128,256]{2,1,0:T(8,128)(2,1)S(1)}, bf16[2,128,256]{2,1,0:T(8,128)(2,1)S(1)}, u32[]{:S(2)}, u32[]{:S(2)}) %collective-permute-start.7) | collective-permute-done | bytes 131104 | tf_op jit(solution)/shard_map/ppermute | solution.py:231
  18.3 13.8 %all_to_all.5 = bf16[16,16,256]{2,1,0:T(8,128)(2,1)S(1)} all-to-all(bf16[16,16,256]{2,1,0:T(8,128)(2,1)S(1)} %bitcast.14), channel_id=1, replica_groups=mesh['rep'=8,'hi'=2,'lo'=2] {'hi','rep'}, dimensions={0} | all-to-all | bytes 262144 | tf_op jit(solution)/shard_map/all_to_all | solution.py:341
  32.1 0.6 %bitcast_reduce_fusion = bf16[128,256]{1,0:T(8,128)(2,1)} fusion(bf16[2,128,256]{2,1,0:T(8,128)(2,1)S(1)} %bitcast.15), kind=kLoop, calls=%fused_computation.1 | loop fusion | flops 32768 | bytes 196608 | tf_op jit(solution)/shard_map/reduce_sum | solution.py:344
  (9 shorter events, 0.1 us)
Async XLA Ops:
  0.0 5.4 %collective-permute-start.2 = (bf16[128,256]{1,0:T(8,128)(2,1)}, bf16[128,256]{1,0:T(8,128)(2,1)S(1)}, u32[]{:S(2)}, u32[]{:S(2)}) collective-permute-start(bf16[128,256]{1,0:T(8,128)(2,1)} %own_ref.3), channel_id=1, source_target_pairs={{0,2},{1,3},{2,0},{3,1},{4,6},{5,7},{6,4},{7,5},{8,10},{9,11},{10,... | collective-permute-start | bytes 196616 | tf_op jit(solution)/shard_map/ppermute | solution.py:231
  3.0 4.3 %collective-permute-start.1 = (bf16[128,256]{1,0:T(8,128)(2,1)}, bf16[128,256]{1,0:T(8,128)(2,1)S(1)}, u32[]{:S(2)}, u32[]{:S(2)}) collective-permute-start(bf16[128,256]{1,0:T(8,128)(2,1)} %own_ref.3), channel_id=1, source_target_pairs={{0,3},{1,2},{2,1},{3,0},{4,7},{5,6},{6,5},{7,4},{8,11},{9,10},{10,... | collective-permute-start | bytes 196616 | tf_op jit(solution)/shard_map/ppermute | solution.py:231
  3.0 0.7 %copy-start.11 = (f32[32,4]{0,1:T(4,128)S(1)}, f32[32,4]{0,1:T(4,128)}, u32[]{:S(2)}) copy-start(f32[32,4]{0,1:T(4,128)} %param.24) | copy-start | bytes 1540
  3.0 0.7 %copy-start.12 = (s32[2,1]{0,1:T(1,128)S(1)}, s32[2,1]{0,1:T(1,128)}, u32[]{:S(2)}) copy-start(s32[2,1]{0,1:T(1,128)} %param.27) | copy-start | bytes 28
  3.0 0.7 %copy-start.13 = (s32[2,1]{0,1:T(1,128)S(1)}, s32[2,1]{0,1:T(1,128)}, u32[]{:S(2)}) copy-start(s32[2,1]{0,1:T(1,128)} %param.28) | copy-start | bytes 28
  3.0 0.7 %copy-start.14 = (s32[1,128]{1,0:T(1,128)S(1)}, s32[1,128]{1,0:T(1,128)}, u32[]{:S(2)}) copy-start(s32[1,128]{1,0:T(1,128)} %deal_ref.1) | copy-start | bytes 1540
  3.7 1.2 %copy-start.5 = (bf16[128,256]{1,0:T(8,128)(2,1)S(1)}, bf16[128,256]{1,0:T(8,128)(2,1)}, u32[]{:S(2)}) copy-start(bf16[128,256]{1,0:T(8,128)(2,1)} %own_ref.3) | copy-start | bytes 196612
  3.7 3.6 %copy-start.1 = (bf16[256,1024]{1,0:T(8,128)(2,1)S(1)}, bf16[256,1024]{1,0:T(8,128)(2,1)}, u32[]{:S(2)}) copy-start(bf16[256,1024]{1,0:T(8,128)(2,1)} %w_out_ref.3) | copy-start | bytes 1572868
  3.7 3.6 %copy-start.2 = (bf16[1024,256]{1,0:T(8,128)(2,1)S(1)}, bf16[1024,256]{1,0:T(8,128)(2,1)}, u32[]{:S(2)}) copy-start(bf16[1024,256]{1,0:T(8,128)(2,1)} %w_query_ref.1) | copy-start | bytes 1572868
  3.7 3.6 %copy-start.3 = (bf16[1024,256]{1,0:T(8,128)(2,1)S(1)}, bf16[1024,256]{1,0:T(8,128)(2,1)}, u32[]{:S(2)}) copy-start(bf16[1024,256]{1,0:T(8,128)(2,1)} %w_key_ref.1) | copy-start | bytes 1572868
  3.7 3.6 %copy-start.4 = (bf16[1024,256]{1,0:T(8,128)(2,1)S(1)}, bf16[1024,256]{1,0:T(8,128)(2,1)}, u32[]{:S(2)}) copy-start(bf16[1024,256]{1,0:T(8,128)(2,1)} %w_value_ref.1) | copy-start | bytes 1572868
  3.7 3.6 %copy-start.6 = (bf16[2,64,256]{2,1,0:T(8,128)(2,1)S(1)}, bf16[2,64,256]{2,1,0:T(8,128)(2,1)}, u32[]{:S(2)}) copy-start(bf16[2,64,256]{2,1,0:T(8,128)(2,1)} %cache_keys_ref.3) | copy-start | bytes 196612
  3.7 3.6 %copy-start.7 = (bf16[2,64,256]{2,1,0:T(8,128)(2,1)S(1)}, bf16[2,64,256]{2,1,0:T(8,128)(2,1)}, u32[]{:S(2)}) copy-start(bf16[2,64,256]{2,1,0:T(8,128)(2,1)} %cache_values_ref.3) | copy-start | bytes 196612
  4.8 2.5 %copy-start.8 = (f32[1024]{0:T(1024)S(1)}, f32[1024]{0:T(1024)}, u32[]{:S(2)}) copy-start(f32[1024]{0:T(1024)} %param.16) | copy-start | bytes 12292
  4.9 2.4 %collective-permute-start = (bf16[128,256]{1,0:T(8,128)(2,1)S(1)}, bf16[128,256]{1,0:T(8,128)(2,1)S(1)}, u32[]{:S(2)}, u32[]{:S(2)}) collective-permute-start(bf16[128,256]{1,0:T(8,128)(2,1)S(1)} %copy-done.5), channel_id=1, source_target_pairs={{0,1},{1,0},{2,3},{3,2},{4,5},{5,4},{6,7},{7,6},{8,9},{9,8},{10,11... | collective-permute-start | bytes 196616 | tf_op jit(solution)/shard_map/ppermute | solution.py:231
  8.6 1.4 %collective-permute-start.3 = (bf16[64,1024]{1,0:T(8,128)(2,1)S(1)}, bf16[64,1024]{1,0:T(8,128)(2,1)S(1)}, u32[]{:S(2)}, u32[]{:S(2)}) collective-permute-start(bf16[64,1024]{1,0:T(8,128)(2,1)S(1)} %get-tuple-element.29), channel_id=1, source_target_pairs={{0,1},{1,0},{2,3},{3,2},{4,5},{5,4},{6,7},{7,6},{8,9},{9,8},{10,11... | collective-permute-start | bytes 393224 | tf_op jit(solution)/shard_map/ppermute | solution.py:231
  8.6 2.1 %copy-start.9 = (bf16[1024,512]{1,0:T(8,128)(2,1)S(1)}, bf16[1024,512]{1,0:T(8,128)(2,1)}, u32[]{:S(2)}) copy-start(bf16[1024,512]{1,0:T(8,128)(2,1)} %w_inner_ref.1) | copy-start | bytes 3145732
  8.6 2.3 %copy-start = (bf16[512,1024]{1,0:T(8,128)(2,1)S(1)}, bf16[512,1024]{1,0:T(8,128)(2,1)}, u32[]{:S(2)}) copy-start(bf16[512,1024]{1,0:T(8,128)(2,1)} %own_outer_ref.3) | copy-start | bytes 3145732
  10.0 5.5 %copy-start.10 = (f32[1024]{0:T(1024)S(1)}, f32[1024]{0:T(1024)}, u32[]{:S(2)}) copy-start(f32[1024]{0:T(1024)} %param.17) | copy-start | bytes 12292
  10.0 5.5 %collective-permute-start.4 = (bf16[64,1024]{1,0:T(8,128)(2,1)S(1)}, bf16[64,1024]{1,0:T(8,128)(2,1)S(1)}, u32[]{:S(2)}, u32[]{:S(2)}) collective-permute-start(bf16[64,1024]{1,0:T(8,128)(2,1)S(1)} %add_convert_fusion.pair_ref), channel_id=1, source_target_pairs={{0,3},{1,2},{2,1},{3,0},{4,7},{5,6},{6,5},{7,4},{8,11},{9,10},{10,... | collective-permute-start | bytes 393224 | tf_op jit(solution)/shard_map/ppermute | solution.py:231
  10.7 5.2 %collective-permute-start.5 = (bf16[1024,512]{1,0:T(8,128)(2,1)S(1)}, bf16[1024,512]{1,0:T(8,128)(2,1)S(1)}, u32[]{:S(2)}, u32[]{:S(2)}) collective-permute-start(bf16[1024,512]{1,0:T(8,128)(2,1)S(1)} %copy-done.9), channel_id=1, source_target_pairs={{0,1},{1,0},{2,3},{3,2},{4,5},{5,4},{6,7},{7,6},{8,9},{9,8},{10,11... | collective-permute-start | bytes 3145736 | tf_op jit(solution)/shard_map/ppermute | solution.py:231
  10.9 5.0 %collective-permute-start.6 = (bf16[512,1024]{1,0:T(8,128)(2,1)S(1)}, bf16[512,1024]{1,0:T(8,128)(2,1)S(1)}, u32[]{:S(2)}, u32[]{:S(2)}) collective-permute-start(bf16[512,1024]{1,0:T(8,128)(2,1)S(1)} %copy-done), channel_id=1, source_target_pairs={{0,1},{1,0},{2,3},{3,2},{4,5},{5,4},{6,7},{7,6},{8,9},{9,8},{10,11... | collective-permute-start | bytes 3145736 | tf_op jit(solution)/shard_map/ppermute | solution.py:231
  16.8 1.4 %collective-permute-start.7 = (bf16[2,128,256]{2,1,0:T(8,128)(2,1)S(1)}, bf16[2,128,256]{2,1,0:T(8,128)(2,1)S(1)}, u32[]{:S(2)}, u32[]{:S(2)}) collective-permute-start(bf16[2,128,256]{2,1,0:T(8,128)(2,1)S(1)} %get-tuple-element.38), channel_id=1, source_target_pairs={{0,1},{1,0},{2,3},{3,2},{4,5},{5,4},{6,7},{7,6},{8,9},{9,8},{10,11... | collective-permute-start | bytes 393224 | tf_op jit(solution)/shard_map/ppermute | solution.py:231

commit v5 on v4

--- a/solution.py
+++ b/solution.py
@@ -24,7 +24,11 @@
 
 def place():
     upper, lower = lax.axis_index("hi"), lax.axis_index("lo")
-    return upper * 2 + lower, upper ^ lower
+    return upper * 2 + lower, lower
+
+
+def halved(share):
+    return share % 2 == 0
 
 
 def columns_of(index, width):
@@ -48,16 +52,21 @@
     _, side = place()
     rows = deal_ref.shape[1]
     new_slots = rows // 2
+    half, share = rows // 2, rows // replicas
     deal = deal_ref[...]
-    slot = lax.rem(deal, replicas) * (rows // replicas) + lax.div(deal, replicas)
+    slot = lax.rem(deal, replicas) * share + lax.div(deal, replicas)
     lane = lax.broadcasted_iota(jnp.int32, (1, rows), 1)
     live = lane < jnp.where(
         lane < new_slots, counts_ref[0, 0], jnp.minimum(counts_ref[0, 1], new_slots) + new_slots
     )
     slot = jnp.where(live, slot, -1)
-    turned = jnp.concatenate([slot[:, new_slots:], slot[:, :new_slots]], axis=1)
-    slot = jnp.where(side == 0, slot, turned)[:, :new_slots]
-    row = lax.broadcasted_iota(jnp.int32, (rows, new_slots), 0)
+    row = lax.broadcasted_iota(jnp.int32, (rows, rows), 0)
+    part = jnp.where(row < half, side, 1 - side)
+    row = jnp.where(row < half, row, row - half)
+    if halved(share):
+        row = lax.div(row, share // 2) * share + part * (share // 2) + lax.rem(row, share // 2)
+    else:
+        row = part * half + row
     picked_ref[...] = jnp.where(row == slot, 1.0, 0.0).astype(BF16)
 
     requests, _, key_slots = bias_ref.shape
@@ -96,7 +105,7 @@
     return context.astype(BF16)
 
 
-def first_kernel(
+def attend_kernel(
     own_ref,
     near_ref,
     far_ref,
@@ -109,15 +118,15 @@
     cache_keys_ref,
     cache_values_ref,
     bias_ref,
+    picked_ref,
     send_ref,
-    query_ref,
-    key_ref,
-    value_ref,
-):
-    index, side = place()
+    context_ref,
+):
+    index, _ = place()
     rows, width = own_ref.shape
     model_width = gain_ref.shape[1]
-    new_slots = rows // 2
+    requests = bias_ref.shape[0]
+    new_slots, half = rows // requests, rows // 2
     blocks = [(own_ref, 0), (near_ref, 1), (far_ref, 3), (across_ref, 2)]
     squares = 0.0
     for ref, _ in blocks:
@@ -131,54 +140,35 @@
         queries = queries + dot(normed, w_query_ref[columns, :])
         new_keys = new_keys + dot(normed, w_key_ref[columns, :])
         new_values = new_values + dot(normed, w_value_ref[columns, :])
-    query_ref[...] = queries.astype(BF16)
-    key_ref[...] = new_keys.astype(BF16)
-    value_ref[...] = new_values.astype(BF16)
-    other = 1 - side
-    own = columns_of(other, new_slots)
-    context = attend(
-        query_ref[own, :],
-        key_ref[own, :],
-        value_ref[own, :],
-        cache_keys_ref[other],
-        cache_values_ref[other],
-        bias_ref[other],
-    )
-    send_ref[...] = dot(context, w_out_ref[...]).astype(BF16)
-
-
-def second_kernel(
-    query_ref, key_ref, value_ref, w_out_ref, cache_keys_ref, cache_values_ref, bias_ref, keep_ref
-):
-    _, side = place()
-    own = columns_of(side, keep_ref.shape[0])
-    context = attend(
-        query_ref[own, :],
-        key_ref[own, :],
-        value_ref[own, :],
-        cache_keys_ref[side],
-        cache_values_ref[side],
-        bias_ref[side],
-    )
-    keep_ref[...] = dot(context, w_out_ref[...])
-
-
-def stream_kernel(own_ref, near_ref, far_ref, across_ref, stream_ref):
-    index, side = place()
+    queries, new_keys, new_values = (v.astype(BF16) for v in (queries, new_keys, new_values))
+    contexts = []
+    for j in range(requests):
+        own = slice(j * new_slots, (j + 1) * new_slots)
+        contexts.append(
+            attend(
+                queries[own],
+                new_keys[own],
+                new_values[own],
+                cache_keys_ref[j],
+                cache_values_ref[j],
+                bias_ref[j],
+            )
+        )
+    context = dot(picked_ref[...], jnp.concatenate(contexts, axis=0)).astype(BF16)
+    send_ref[...] = dot(context[half:], w_out_ref[...]).astype(BF16)
+    context_ref[...] = context[:half]
+
+
+def project_kernel(context_ref, w_out_ref, keep_ref):
+    keep_ref[...] = dot(context_ref[...], w_out_ref[...])
+
+
+def stream_kernel(own_ref, near_ref, far_ref, across_ref, picked_ref, stream_ref):
+    index, _ = place()
     width = own_ref.shape[1]
-    rows = columns_of(side, stream_ref.shape[0])
+    picked = picked_ref[: stream_ref.shape[0]]
     for ref, xor in ((own_ref, 0), (near_ref, 1), (far_ref, 3), (across_ref, 2)):
-        stream_ref[:, columns_of(index ^ xor, width)] = ref[rows, :]
-
-
-def project(hidden_refs, w_outer_refs, mixed_ref, picked_ref, group, core):
-    upper = lax.axis_index("hi")
-    width = mixed_ref.shape[1] // 4
-    columns = columns_of(group * 2 + core, width)
-    value = jnp.where(upper == group, mixed_ref[:, columns], 0.0)
-    for hidden_ref, w_outer_ref in zip(hidden_refs, w_outer_refs):
-        value = value + dot(hidden_ref[...], w_outer_ref[:, columns])
-    return dot(picked_ref[...], value.astype(BF16)).astype(BF16)
+        stream_ref[:, columns_of(index ^ xor, width)] = dot(picked, ref[...]).astype(BF16)
 
 
 def inner_kernel(
@@ -193,38 +183,24 @@
     hidden_ref[...] = jnp.maximum(dot(ffn_input, w_inner_ref[...]), 0.0).astype(BF16)
 
 
-def send_kernel(
+def outer_kernel(
     mixed_ref,
     input_ref,
     own_hidden_ref,
     near_inner_ref,
     own_outer_ref,
     near_outer_ref,
-    picked_ref,
-    near_hidden_ref,
-    send_ref,
-):
-    hidden = jnp.maximum(dot(input_ref[...], near_inner_ref[...]), 0.0)
-    near_hidden_ref[...] = hidden.astype(BF16)
-    hidden_refs, outer_refs = (own_hidden_ref, near_hidden_ref), (own_outer_ref, near_outer_ref)
-    core = 1 - lax.axis_index("lo")
-    for g in range(send_ref.shape[0]):
-        send_ref[g] = project(hidden_refs, outer_refs, mixed_ref, picked_ref, g, core)
-
-
-def keep_kernel(
-    mixed_ref,
-    own_hidden_ref,
-    near_hidden_ref,
-    own_outer_ref,
-    near_outer_ref,
-    picked_ref,
-    keep_ref,
-):
-    hidden_refs, outer_refs = (own_hidden_ref, near_hidden_ref), (own_outer_ref, near_outer_ref)
-    core = lax.axis_index("lo")
-    for g in range(keep_ref.shape[0]):
-        keep_ref[g] = project(hidden_refs, outer_refs, mixed_ref, picked_ref, g, core)
+    out_ref,
+):
+    upper = lax.axis_index("hi")
+    width = out_ref.shape[2]
+    hidden = jnp.maximum(dot(input_ref[...], near_inner_ref[...]), 0.0).astype(BF16)
+    for t in range(out_ref.shape[0]):
+        columns = slice(t * width, (t + 1) * width)
+        value = dot(own_hidden_ref[...], own_outer_ref[:, columns])
+        value = value + dot(hidden, near_outer_ref[:, columns])
+        value = value + jnp.where(upper == t // 2, mixed_ref[:, columns], 0.0)
+        out_ref[t] = value.astype(BF16)
 
 
 def swap(value, xor):
@@ -255,6 +231,7 @@
     model_width = attn_gain.shape[0]
     head_count = bias_table.shape[1]
     groups = lax.axis_size("hi")
+    _, side = place()
     shape = jax.ShapeDtypeStruct
     local = functools.partial(
         pl.pallas_call, compiler_params=pltpu.CompilerParams(vmem_limit_bytes=VMEM_LIMIT)
@@ -264,7 +241,7 @@
         functools.partial(prepare_kernel, replicas, cached),
         out_shape=(
             shape((requests, head_count * new_slots, cached + new_slots), F32),
-            shape((rows, new_slots), BF16),
+            shape((rows, rows), BF16),
         ),
         in_specs=[SMEM] * 3 + [VMEM],
         out_specs=(VMEM,) * 2,
@@ -273,13 +250,13 @@
     )(bias_table.T, new_counts.T, cached_lengths.T, deal)
     late, bias, picked = lax.optimization_barrier((tokens, bias, picked))
     blocks = (tokens, swap(late, 1), far, across)
-    projected = shape((rows, local_width), BF16)
-    send, *projections = local(
-        first_kernel,
-        out_shape=(shape((new_slots, model_width), BF16),) + (projected,) * 3,
-        in_specs=[VMEM] * 12,
-        out_specs=(VMEM,) * 4,
-        name="first",
+    half = rows // 2
+    send, context = local(
+        attend_kernel,
+        out_shape=(shape((half, model_width), BF16), shape((half, local_width), BF16)),
+        in_specs=[VMEM] * 13,
+        out_specs=(VMEM,) * 2,
+        name="attend",
     )(
         *blocks,
         attn_gain.reshape(1, model_width),
@@ -290,58 +267,55 @@
         cache_keys,
         cache_values,
         bias,
+        picked,
     )
     keep = local(
-        second_kernel,
-        out_shape=shape((new_slots, model_width), F32),
-        in_specs=[VMEM] * 7,
+        project_kernel,
+        out_shape=shape((half, model_width), F32),
+        in_specs=[VMEM] * 2,
         out_specs=VMEM,
-        name="second",
-    )(*projections, w_out, cache_keys, cache_values, bias)
+        name="project",
+    )(context, w_out)
     stream = local(
         stream_kernel,
-        out_shape=shape((new_slots, model_width), BF16),
-        in_specs=[VMEM] * 4,
+        out_shape=shape((half, model_width), BF16),
+        in_specs=[VMEM] * 5,
         out_specs=VMEM,
         name="stream",
-    )(*blocks)
+    )(*blocks, picked)
     pair = (keep + swap(send, 1).astype(F32)).astype(BF16)
     late_inner, late_outer, pair = lax.optimization_barrier((w_inner, w_outer, pair))
     ff_width = w_inner.shape[1]
-    hidden = shape((new_slots, ff_width), BF16)
-    dealt = shape((groups, rows, width), BF16)
-    mixed, ffn_input, first = local(
+    mixed, ffn_input, hidden = local(
         inner_kernel,
         out_shape=(
-            shape((new_slots, model_width), F32),
-            shape((new_slots, model_width), BF16),
-            hidden,
+            shape((half, model_width), F32),
+            shape((half, model_width), BF16),
+            shape((half, ff_width), BF16),
         ),
         in_specs=[VMEM] * 5,
         out_specs=(VMEM,) * 3,
         cost_estimate=pl.CostEstimate(flops=INNER_FLOPS, bytes_accessed=0, transcendentals=0),
         name="inner",
-    )(pair, swap(pair, 3), stream, ffn_gain.reshape(1, model_width), w_inner)
-    outer = (w_outer, swap(late_outer, 1))
-    second, send = local(
-        send_kernel,
-        out_shape=(hidden, dealt),
-        in_specs=[VMEM] * 7,
-        out_specs=(VMEM,) * 2,
-        name="send",
-    )(mixed, ffn_input, first, swap(late_inner, 1), *outer, picked)
-    keep = local(
-        keep_kernel,
-        out_shape=dealt,
+    )(pair, swap(pair, 2), stream, ffn_gain.reshape(1, model_width), w_inner)
+    out = local(
+        outer_kernel,
+        out_shape=shape((groups * 2, half, width), BF16),
         in_specs=[VMEM] * 6,
         out_specs=VMEM,
-        name="keep",
-    )(mixed, first, second, *outer, picked)
-    pair = keep + swap(send, 1)
+        name="outer",
+    )(mixed, ffn_input, hidden, swap(late_inner, 1), w_outer, swap(late_outer, 1))
+    share = rows // replicas
+    if not halved(share):
+        padded = jnp.zeros((groups * 2, rows, width), BF16)
+        out = lax.dynamic_update_slice_in_dim(padded, out, side * half, 1)
     parts = lax.all_to_all(
-        pair.reshape(groups * replicas, rows // replicas, width), ("hi", "rep"), 0, 0, tiled=True
-    )
-    return jnp.sum(parts.reshape(groups, rows, width).astype(F32), axis=0).astype(BF16)
+        out.reshape(groups * 2 * replicas, -1, width), ("hi", "lo", "rep"), 0, 0, tiled=True
+    )
+    parts = parts.reshape(groups, 2, replicas, -1, width).astype(F32)
+    if halved(share):
+        return jnp.sum(parts, axis=0).swapaxes(0, 1).reshape(rows, width).astype(BF16)
+    return jnp.sum(parts, axis=(0, 1)).reshape(rows, width).astype(BF16)
 
 
 def solution(mesh):

time: 33 us -> 31.1 us (0.942)
  blocking collectives: 13.8 us -> 13 us
  Pallas kernels: 4.95 us -> 4.19 us
  other arithmetic: 0.71 us -> 0.05 us
  local copies, waits for them, and re-layouts: 0.74 us -> 1.38 us
    all_to_all x1, blocking collectives: 13.8 us -> 13 us  [on_device(): lax.all_to_all(out.reshape(groups * 2 * replicas, -1, width), ('hi', 'lo'...]
    pallas_call x6 -> x5, Pallas kernels: 3.85 us -> 3.11 us  [the longest x1 1.6 us: on_device(): local(attend_kernel, out_shape=(shape((half, model_width), BF16), shape((...]
    convert_element_type x0 -> x1, local copies, waits for them, and re-layouts: none -> 0.63 us  [on_device(): jnp.sum(parts, axis=0).swapaxes(0, 1).reshape(rows, width).astype(BF16)]
    reduce_sum x1, other arithmetic: 0.65 us -> 0.02 us  [on_device(): jnp.sum(parts, axis=0).swapaxes(0, 1).reshape(rows, width).astype(BF16)]
    ppermute x8 -> x7, starting transfers between devices: 4.72 us -> 4.52 us  [swap(): return lax.ppermute(value, ('hi', 'lo'), [(i, i ^ xor) for i in range(4)])]
    ppermute x8 -> x7, waiting for transfers between devices: 7.6 us -> 7.54 us  [swap(): return lax.ppermute(value, ('hi', 'lo'), [(i, i ^ xor) for i in range(4)])]
  transfers between devices with their start and end apart: 8 -> 7, of which waited for: 5 -> 4; matrix products, arithmetic and copies ran while one was open for 0% -> 0% of each run, Pallas kernels for 9% -> 6%
where the time goes in v5:
time: 31.1 us; the launch traced here: 30.9 us
  blocking collectives  13 us (42%)
  waiting for transfers between devices  7.54 us (24%)
  starting transfers between devices  4.52 us (15%)
  Pallas kernels  4.19 us (13%)
  local copies, waits for them, and re-layouts  1.38 us (4%)
    all_to_all x1, blocking collectives, on_device(): lax.all_to_all(out.reshape(groups * 2 * replicas, -1, width), ('hi', 'lo'...  13 us
    ppermute x7, waiting for transfers between devices, swap(): return lax.ppermute(value, ('hi', 'lo'), [(i, i ^ xor) for i in range(4)])  7.54 us
    ppermute x7, starting transfers between devices, swap(): return lax.ppermute(value, ('hi', 'lo'), [(i, i ^ xor) for i in range(4)])  4.52 us
    pallas_call x1, Pallas kernels, on_device(): local(attend_kernel, out_shape=(shape((half, model_width), BF16), shape((...  1.6 us
    pallas_call x1, Pallas kernels, on_device(): local(functools.partial(prepare_kernel, replicas, cached), out_shape=(sha...  1.08 us
    unnamed x30, local copies, waits for them, and re-layouts  0.74 us
    pallas_call x1, Pallas kernels, on_device(): local(outer_kernel, out_shape=shape((groups * 2, half, width), BF16), in_...  0.74 us
    convert_element_type x1, local copies, waits for them, and re-layouts, on_device(): jnp.sum(parts, axis=0).swapaxes(0, 1).reshape(rows, width).astype(BF16)  0.63 us
  transfers between devices with their start and end apart: 7, of which 4 were waited for; matrix products, arithmetic and copies ran while one was open for 0% of the time, Pallas kernels for 6%

profile of v5, /device:TPU:0, one launch (start us, length us, event | category | flops | bytes accessed | tf_op | source)
XLA Modules:
  0.0 30.9 jit_solution(77548978408977381)
XLA Ops:
  0.0 3.0 %collective-permute-start.2 = (bf16[128,256]{1,0:T(8,128)(2,1)}, bf16[128,256]{1,0:T(8,128)(2,1)S(1)}, u32[]{:S(2)}, u32[]{:S(2)}) collective-permute-start(bf16[128,256]{1,0:T(8,128)(2,1)} %own_ref.3), channel_id=1, source_target_pairs={{0,2},{1,3},{2,0},{3,1},{4,6},{5,7},{6,4},{7,5},{8,10},{9,11},{10,... | collective-permute-start | bytes 196616 | tf_op jit(solution)/shard_map/ppermute | solution.py:207
  3.0 0.0 collective-permute-start.1
  3.0 0.0 copy-start.11
  3.0 0.0 copy-start.12
  3.0 0.0 copy-start.14
  3.0 0.7 %copy-done.11 = f32[32,4]{0,1:T(4,128)S(1)} copy-done((f32[32,4]{0,1:T(4,128)S(1)}, f32[32,4]{0,1:T(4,128)}, u32[]{:S(2)}) %copy-start.11) | copy-done | bytes 536
  3.7 0.0 copy-done.12
  3.7 0.0 copy-done.13
  3.7 0.0 copy-done.14
  3.7 0.0 copy-start.3
  3.7 0.0 copy-start.4
  3.7 0.0 copy-start.6
  3.7 0.0 copy-start.7
  3.7 1.1 %prepare.1 = (f32[2,256,128]{2,1,0:T(8,128)S(1)}, bf16[128,128]{1,0:T(8,128)(2,1)S(1)}) custom-call(f32[4,32]{1,0:T(4,128)S(1)} %bitcast.12, s32[1,2]{1,0:T(1,128)S(1)} %bitcast.13, s32[1,2]{1,0:T(1,128)S(1)} %bitcast.14, s32[1,128]{1,0:T(1,128)S(1)} %copy-done.14), custom_call_target="tpu_custom_call" | custom-call | flops 7000000000 | tf_op jit(solution)/shard_map/prepare/pallas_call | solution.py:240
  4.8 0.0 copy-start.8
  4.8 0.0 copy-done.5
  4.8 0.2 collective-permute-start
  5.0 0.4 %collective-permute-done.2.across_ref = bf16[128,256]{1,0:T(8,128)(2,1)S(1)} collective-permute-done((bf16[128,256]{1,0:T(8,128)(2,1)}, bf16[128,256]{1,0:T(8,128)(2,1)S(1)}, u32[]{:S(2)}, u32[]{:S(2)}) %collective-permute-start.2) | collective-permute-done | bytes 65568 | tf_op jit(solution)/shard_map/ppermute | solution.py:207
  5.4 1.9 %collective-permute-done.1.far_ref = bf16[128,256]{1,0:T(8,128)(2,1)S(1)} collective-permute-done((bf16[128,256]{1,0:T(8,128)(2,1)}, bf16[128,256]{1,0:T(8,128)(2,1)S(1)}, u32[]{:S(2)}, u32[]{:S(2)}) %collective-permute-start.1) | collective-permute-done | bytes 65568 | tf_op jit(solution)/shard_map/ppermute | solution.py:207
  7.3 0.0 collective-permute-done.near_ref
  7.3 0.0 copy-done
  7.3 0.0 copy-done.2
  7.3 0.0 copy-done.3
  7.3 0.0 copy-done.4
  7.3 0.0 copy-done.6
  7.3 0.0 copy-done.7
  7.4 0.0 copy-done.8
  7.4 0.0 copy-start.9
  7.4 1.6 %attend.1 = (bf16[64,1024]{1,0:T(8,128)(2,1)S(1)}, bf16[64,256]{1,0:T(8,128)(2,1)S(1)}) custom-call(bf16[128,256]{1,0:T(8,128)(2,1)S(1)} %copy-done.5, bf16[128,256]{1,0:T(8,128)(2,1)S(1)} %collective-permute-done.near_ref, bf16[128,256]{1,0:T(8,128)(2,1)S(1)} %collective-permute-done.1.far_ref, bf16[128,256]{1,0:T(8,128)(2,1)S(1)} %collective-permute-done.2.across_ref, ...), custom_call_target="tpu_custom_call" | custom-call | tf_op jit(solution)/shard_map/attend/pallas_call | solution.py:254
  9.0 0.0 copy-start.1
  9.0 0.1 collective-permute-start.3
  9.1 0.2 project.1
  9.3 1.1 %collective-permute-done.3 = bf16[64,1024]{1,0:T(8,128)(2,1)S(1)} collective-permute-done((bf16[64,1024]{1,0:T(8,128)(2,1)S(1)}, bf16[64,1024]{1,0:T(8,128)(2,1)S(1)}, u32[]{:S(2)}, u32[]{:S(2)}) %collective-permute-start.3) | collective-permute-done | bytes 131104 | tf_op jit(solution)/shard_map/ppermute | solution.py:207
  10.4 0.0 copy-start.10
  10.5 0.7 %collective-permute-start.4 = (bf16[64,1024]{1,0:T(8,128)(2,1)S(1)}, bf16[64,1024]{1,0:T(8,128)(2,1)S(1)}, u32[]{:S(2)}, u32[]{:S(2)}) collective-permute-start(bf16[64,1024]{1,0:T(8,128)(2,1)S(1)} %add_convert_fusion.pair_ref), channel_id=1, source_target_pairs={{0,2},{1,3},{2,0},{3,1},{4,6},{5,7},{6,4},{7,5},{8,10},{9,11},{10,... | collective-permute-start | bytes 393224 | tf_op jit(solution)/shard_map/ppermute | solution.py:207
  11.1 0.2 stream.1.stream_ref
  11.3 0.0 copy-done.9
  11.3 0.1 collective-permute-start.5
  11.5 0.0 copy-done.1
  11.5 0.4 %collective-permute-start.6 = (bf16[512,1024]{1,0:T(8,128)(2,1)S(1)}, bf16[512,1024]{1,0:T(8,128)(2,1)S(1)}, u32[]{:S(2)}, u32[]{:S(2)}) collective-permute-start(bf16[512,1024]{1,0:T(8,128)(2,1)S(1)} %copy-done.1), channel_id=1, source_target_pairs={{0,1},{1,0},{2,3},{3,2},{4,5},{5,4},{6,7},{7,6},{8,9},{9,8},{10,11... | collective-permute-start | bytes 3145736 | tf_op jit(solution)/shard_map/ppermute | solution.py:207
  11.9 4.1 %collective-permute-done.4.other_ref = bf16[64,1024]{1,0:T(8,128)(2,1)S(1)} collective-permute-done((bf16[64,1024]{1,0:T(8,128)(2,1)S(1)}, bf16[64,1024]{1,0:T(8,128)(2,1)S(1)}, u32[]{:S(2)}, u32[]{:S(2)}) %collective-permute-start.4) | collective-permute-done | bytes 131104 | tf_op jit(solution)/shard_map/ppermute | solution.py:207
  16.1 0.0 copy-done.10
  16.1 0.4 %inner.1 = (f32[64,1024]{1,0:T(8,128)S(1)}, bf16[64,1024]{1,0:T(8,128)(2,1)S(1)}, bf16[64,512]{1,0:T(8,128)(2,1)S(1)}) custom-call(bf16[64,1024]{1,0:T(8,128)(2,1)S(1)} %add_convert_fusion.pair_ref, bf16[64,1024]{1,0:T(8,128)(2,1)S(1)} %collective-permute-done.4.other_ref, bf16[64,1024]{1,0:T(8,128)(2,1)S(1)} %stream.1.stream_ref, f32[1,1024]{1,0:T(1,128)S(1)} %bitcast.11, ...), custom_call_target="tpu_custom_call" | custom-call | flops 40000000000 | tf_op jit(solution)/shard_map/inner/pallas_call | solution.py:289
  16.5 0.0 collective-permute-done.5.near_inner_ref
  16.5 0.0 collective-permute-done.6.near_outer_ref
  16.5 0.7 %outer.1 = bf16[4,64,256]{2,1,0:T(8,128)(2,1)S(1)} custom-call(f32[64,1024]{1,0:T(8,128)S(1)} %get-tuple-element.26.mixed_ref, bf16[64,1024]{1,0:T(8,128)(2,1)S(1)} %get-tuple-element.27.input_ref, bf16[64,512]{1,0:T(8,128)(2,1)S(1)} %get-tuple-element.28.own_hidden_ref, bf16[1024,512]{1,0:T(8,128)(2,1)S(1)} %collective-permute-done.5.near_inner_ref, ...), custom_call_target="tpu_custom_call" | custom-call | tf_op jit(solution)/shard_map/outer/pallas_call | solution.py:301
  17.2 13.0 %all_to_all.5 = bf16[32,8,256]{2,1,0:T(8,128)(2,1)S(1)} all-to-all(bf16[32,8,256]{2,1,0:T(8,128)(2,1)S(1)} %bitcast.9), channel_id=1, replica_groups=mesh['rep'=8,'hi'=2,'lo'=2] {'hi','lo','rep'}, dimensions={0} | all-to-all | bytes 262144 | tf_op jit(solution)/shard_map/all_to_all | solution.py:312
  30.3 0.6 %copy.16 = bf16[8,2,8,256]{3,2,1,0:T(8,128)(2,1)} copy(bf16[8,2,8,256]{3,2,0,1:T(8,128)(2,1)S(1)} %bitcast.16) | data formatting | bytes 131072 | tf_op jit(solution)/shard_map/convert_element_type | solution.py:317
  (6 shorter events, 0.1 us)
Async XLA Ops:
  0.0 5.4 %collective-permute-start.2 = (bf16[128,256]{1,0:T(8,128)(2,1)}, bf16[128,256]{1,0:T(8,128)(2,1)S(1)}, u32[]{:S(2)}, u32[]{:S(2)}) collective-permute-start(bf16[128,256]{1,0:T(8,128)(2,1)} %own_ref.3), channel_id=1, source_target_pairs={{0,2},{1,3},{2,0},{3,1},{4,6},{5,7},{6,4},{7,5},{8,10},{9,11},{10,... | collective-permute-start | bytes 196616 | tf_op jit(solution)/shard_map/ppermute | solution.py:207
  3.0 4.3 %collective-permute-start.1 = (bf16[128,256]{1,0:T(8,128)(2,1)}, bf16[128,256]{1,0:T(8,128)(2,1)S(1)}, u32[]{:S(2)}, u32[]{:S(2)}) collective-permute-start(bf16[128,256]{1,0:T(8,128)(2,1)} %own_ref.3), channel_id=1, source_target_pairs={{0,3},{1,2},{2,1},{3,0},{4,7},{5,6},{6,5},{7,4},{8,11},{9,10},{10,... | collective-permute-start | bytes 196616 | tf_op jit(solution)/shard_map/ppermute | solution.py:207
  3.0 0.7 %copy-start.11 = (f32[32,4]{0,1:T(4,128)S(1)}, f32[32,4]{0,1:T(4,128)}, u32[]{:S(2)}) copy-start(f32[32,4]{0,1:T(4,128)} %param.24) | copy-start | bytes 1540
  3.0 0.7 %copy-start.12 = (s32[2,1]{0,1:T(1,128)S(1)}, s32[2,1]{0,1:T(1,128)}, u32[]{:S(2)}) copy-start(s32[2,1]{0,1:T(1,128)} %param.27) | copy-start | bytes 28
  3.0 0.7 %copy-start.13 = (s32[2,1]{0,1:T(1,128)S(1)}, s32[2,1]{0,1:T(1,128)}, u32[]{:S(2)}) copy-start(s32[2,1]{0,1:T(1,128)} %param.28) | copy-start | bytes 28
  3.0 0.7 %copy-start.14 = (s32[1,128]{1,0:T(1,128)S(1)}, s32[1,128]{1,0:T(1,128)}, u32[]{:S(2)}) copy-start(s32[1,128]{1,0:T(1,128)} %deal_ref.1) | copy-start | bytes 1540
  3.7 1.2 %copy-start.5 = (bf16[128,256]{1,0:T(8,128)(2,1)S(1)}, bf16[128,256]{1,0:T(8,128)(2,1)}, u32[]{:S(2)}) copy-start(bf16[128,256]{1,0:T(8,128)(2,1)} %own_ref.3) | copy-start | bytes 196612
  3.7 3.6 %copy-start = (bf16[256,1024]{1,0:T(8,128)(2,1)S(1)}, bf16[256,1024]{1,0:T(8,128)(2,1)}, u32[]{:S(2)}) copy-start(bf16[256,1024]{1,0:T(8,128)(2,1)} %w_out_ref.3) | copy-start | bytes 1572868
  3.7 3.6 %copy-start.2 = (bf16[1024,256]{1,0:T(8,128)(2,1)S(1)}, bf16[1024,256]{1,0:T(8,128)(2,1)}, u32[]{:S(2)}) copy-start(bf16[1024,256]{1,0:T(8,128)(2,1)} %w_query_ref.1) | copy-start | bytes 1572868
  3.7 3.6 %copy-start.3 = (bf16[1024,256]{1,0:T(8,128)(2,1)S(1)}, bf16[1024,256]{1,0:T(8,128)(2,1)}, u32[]{:S(2)}) copy-start(bf16[1024,256]{1,0:T(8,128)(2,1)} %w_key_ref.1) | copy-start | bytes 1572868
  3.7 3.6 %copy-start.4 = (bf16[1024,256]{1,0:T(8,128)(2,1)S(1)}, bf16[1024,256]{1,0:T(8,128)(2,1)}, u32[]{:S(2)}) copy-start(bf16[1024,256]{1,0:T(8,128)(2,1)} %w_value_ref.1) | copy-start | bytes 1572868
  3.7 3.6 %copy-start.6 = (bf16[2,64,256]{2,1,0:T(8,128)(2,1)S(1)}, bf16[2,64,256]{2,1,0:T(8,128)(2,1)}, u32[]{:S(2)}) copy-start(bf16[2,64,256]{2,1,0:T(8,128)(2,1)} %cache_keys_ref.1) | copy-start | bytes 196612
  3.7 3.6 %copy-start.7 = (bf16[2,64,256]{2,1,0:T(8,128)(2,1)S(1)}, bf16[2,64,256]{2,1,0:T(8,128)(2,1)}, u32[]{:S(2)}) copy-start(bf16[2,64,256]{2,1,0:T(8,128)(2,1)} %cache_values_ref.1) | copy-start | bytes 196612
  4.8 2.5 %copy-start.8 = (f32[1024]{0:T(1024)S(1)}, f32[1024]{0:T(1024)}, u32[]{:S(2)}) copy-start(f32[1024]{0:T(1024)} %param.16) | copy-start | bytes 12292
  4.8 2.5 %collective-permute-start = (bf16[128,256]{1,0:T(8,128)(2,1)S(1)}, bf16[128,256]{1,0:T(8,128)(2,1)S(1)}, u32[]{:S(2)}, u32[]{:S(2)}) collective-permute-start(bf16[128,256]{1,0:T(8,128)(2,1)S(1)} %copy-done.5), channel_id=1, source_target_pairs={{0,1},{1,0},{2,3},{3,2},{4,5},{5,4},{6,7},{7,6},{8,9},{9,8},{10,11... | collective-permute-start | bytes 196616 | tf_op jit(solution)/shard_map/ppermute | solution.py:207
  7.4 4.0 %copy-start.9 = (bf16[1024,512]{1,0:T(8,128)(2,1)S(1)}, bf16[1024,512]{1,0:T(8,128)(2,1)}, u32[]{:S(2)}) copy-start(bf16[1024,512]{1,0:T(8,128)(2,1)} %w_inner_ref.1) | copy-start | bytes 3145732
  9.0 2.5 %copy-start.1 = (bf16[512,1024]{1,0:T(8,128)(2,1)S(1)}, bf16[512,1024]{1,0:T(8,128)(2,1)}, u32[]{:S(2)}) copy-start(bf16[512,1024]{1,0:T(8,128)(2,1)} %own_outer_ref.1) | copy-start | bytes 3145732
  9.0 1.4 %collective-permute-start.3 = (bf16[64,1024]{1,0:T(8,128)(2,1)S(1)}, bf16[64,1024]{1,0:T(8,128)(2,1)S(1)}, u32[]{:S(2)}, u32[]{:S(2)}) collective-permute-start(bf16[64,1024]{1,0:T(8,128)(2,1)S(1)} %get-tuple-element.24), channel_id=1, source_target_pairs={{0,1},{1,0},{2,3},{3,2},{4,5},{5,4},{6,7},{7,6},{8,9},{9,8},{10,11... | collective-permute-start | bytes 393224 | tf_op jit(solution)/shard_map/ppermute | solution.py:207
  10.4 5.6 %copy-start.10 = (f32[1024]{0:T(1024)S(1)}, f32[1024]{0:T(1024)}, u32[]{:S(2)}) copy-start(f32[1024]{0:T(1024)} %param.17) | copy-start | bytes 12292
  10.5 5.6 %collective-permute-start.4 = (bf16[64,1024]{1,0:T(8,128)(2,1)S(1)}, bf16[64,1024]{1,0:T(8,128)(2,1)S(1)}, u32[]{:S(2)}, u32[]{:S(2)}) collective-permute-start(bf16[64,1024]{1,0:T(8,128)(2,1)S(1)} %add_convert_fusion.pair_ref), channel_id=1, source_target_pairs={{0,2},{1,3},{2,0},{3,1},{4,6},{5,7},{6,4},{7,5},{8,10},{9,11},{10,... | collective-permute-start | bytes 393224 | tf_op jit(solution)/shard_map/ppermute | solution.py:207
  11.3 5.1 %collective-permute-start.5 = (bf16[1024,512]{1,0:T(8,128)(2,1)S(1)}, bf16[1024,512]{1,0:T(8,128)(2,1)S(1)}, u32[]{:S(2)}, u32[]{:S(2)}) collective-permute-start(bf16[1024,512]{1,0:T(8,128)(2,1)S(1)} %copy-done.9), channel_id=1, source_target_pairs={{0,1},{1,0},{2,3},{3,2},{4,5},{5,4},{6,7},{7,6},{8,9},{9,8},{10,11... | collective-permute-start | bytes 3145736 | tf_op jit(solution)/shard_map/ppermute | solution.py:207
  11.5 5.0 %collective-permute-start.6 = (bf16[512,1024]{1,0:T(8,128)(2,1)S(1)}, bf16[512,1024]{1,0:T(8,128)(2,1)S(1)}, u32[]{:S(2)}, u32[]{:S(2)}) collective-permute-start(bf16[512,1024]{1,0:T(8,128)(2,1)S(1)} %copy-done.1), channel_id=1, source_target_pairs={{0,1},{1,0},{2,3},{3,2},{4,5},{5,4},{6,7},{7,6},{8,9},{9,8},{10,11... | collective-permute-start | bytes 3145736 | tf_op jit(solution)/shard_map/ppermute | solution.py:207

commit v6 on v5

--- a/solution.py
+++ b/solution.py
@@ -15,6 +15,7 @@
 SMEM = pl.BlockSpec(memory_space=pltpu.SMEM)
 PREPARE_FLOPS = 7 * 10**9
 INNER_FLOPS = 40 * 10**9
+LANES = 128
 VMEM_LIMIT = 24 * 1024 * 1024
 
 
@@ -105,11 +106,49 @@
     return context.astype(BF16)
 
 
-def attend_kernel(
+def products(ref, columns, gain_ref, weight_refs):
+    block = ref[...].astype(F32)
+    scaled = (block * gain_ref[:, columns]).astype(BF16)
+    return jnp.sum(block * block, axis=1, keepdims=True), [
+        dot(scaled, weight_ref[columns, :]) for weight_ref in weight_refs
+    ]
+
+
+def early_kernel(
     own_ref,
     near_ref,
+    across_ref,
+    gain_ref,
+    w_query_ref,
+    w_key_ref,
+    w_value_ref,
+    w_out_ref,
+    cache_keys_ref,
+    cache_values_ref,
+    squares_ref,
+    query_ref,
+    key_ref,
+    value_ref,
+):
+    del w_out_ref, cache_keys_ref, cache_values_ref
+    index, _ = place()
+    width = own_ref.shape[1]
+    squares, sums = 0.0, (0.0, 0.0, 0.0)
+    for ref, xor in ((own_ref, 0), (near_ref, 1), (across_ref, 2)):
+        square, more = products(
+            ref, columns_of(index ^ xor, width), gain_ref, (w_query_ref, w_key_ref, w_value_ref)
+        )
+        squares, sums = squares + square, [a + b for a, b in zip(sums, more)]
+    squares_ref[...] = jnp.broadcast_to(squares, squares_ref.shape)
+    query_ref[...], key_ref[...], value_ref[...] = sums
+
+
+def attend_kernel(
     far_ref,
-    across_ref,
+    squares_ref,
+    query_ref,
+    key_ref,
+    value_ref,
     gain_ref,
     w_query_ref,
     w_key_ref,
@@ -123,24 +162,18 @@
     context_ref,
 ):
     index, _ = place()
-    rows, width = own_ref.shape
-    model_width = gain_ref.shape[1]
+    rows, width = far_ref.shape
     requests = bias_ref.shape[0]
     new_slots, half = rows // requests, rows // 2
-    blocks = [(own_ref, 0), (near_ref, 1), (far_ref, 3), (across_ref, 2)]
-    squares = 0.0
-    for ref, _ in blocks:
-        block = ref[...].astype(F32)
-        squares = squares + jnp.sum(block * block, axis=1, keepdims=True)
-    inverse = lax.rsqrt(squares / model_width + EPSILON)
-    queries = new_keys = new_values = 0.0
-    for ref, xor in blocks:
-        columns = columns_of(index ^ xor, width)
-        normed = (ref[...].astype(F32) * inverse * gain_ref[:, columns]).astype(BF16)
-        queries = queries + dot(normed, w_query_ref[columns, :])
-        new_keys = new_keys + dot(normed, w_key_ref[columns, :])
-        new_values = new_values + dot(normed, w_value_ref[columns, :])
-    queries, new_keys, new_values = (v.astype(BF16) for v in (queries, new_keys, new_values))
+    squares, sums = products(
+        far_ref, columns_of(index ^ 3, width), gain_ref, (w_query_ref, w_key_ref, w_value_ref)
+    )
+    squares = squares_ref[:, :1] + squares
+    inverse = lax.rsqrt(squares / gain_ref.shape[1] + EPSILON)
+    queries, new_keys, new_values = (
+        ((ref[...] + more) * inverse).astype(BF16)
+        for ref, more in zip((query_ref, key_ref, value_ref), sums)
+    )
     contexts = []
     for j in range(requests):
         own = slice(j * new_slots, (j + 1) * new_slots)
@@ -172,20 +205,30 @@
 
 
 def inner_kernel(
-    pair_ref, other_ref, stream_ref, gain_ref, w_inner_ref, mixed_ref, input_ref, hidden_ref
+    pair_ref,
+    other_ref,
+    stream_ref,
+    gain_ref,
+    w_inner_ref,
+    mixed_ref,
+    input_ref,
+    inverse_ref,
+    hidden_ref,
 ):
     mixed = pair_ref[...].astype(F32) + other_ref[...].astype(F32) + stream_ref[...].astype(F32)
     mixed_ref[...] = mixed
     square = jnp.sum(mixed * mixed, axis=1, keepdims=True)
     inverse = lax.rsqrt(square / mixed.shape[1] + EPSILON)
-    ffn_input = (mixed * inverse * gain_ref[...]).astype(BF16)
-    input_ref[...] = ffn_input
-    hidden_ref[...] = jnp.maximum(dot(ffn_input, w_inner_ref[...]), 0.0).astype(BF16)
+    inverse_ref[...] = jnp.broadcast_to(inverse, inverse_ref.shape)
+    scaled = (mixed * gain_ref[...]).astype(BF16)
+    input_ref[...] = scaled
+    hidden_ref[...] = jnp.maximum(dot(scaled, w_inner_ref[...]) * inverse, 0.0).astype(BF16)
 
 
 def outer_kernel(
     mixed_ref,
     input_ref,
+    inverse_ref,
     own_hidden_ref,
     near_inner_ref,
     own_outer_ref,
@@ -194,7 +237,8 @@
 ):
     upper = lax.axis_index("hi")
     width = out_ref.shape[2]
-    hidden = jnp.maximum(dot(input_ref[...], near_inner_ref[...]), 0.0).astype(BF16)
+    hidden = dot(input_ref[...], near_inner_ref[...]) * inverse_ref[:, :1]
+    hidden = jnp.maximum(hidden, 0.0).astype(BF16)
     for t in range(out_ref.shape[0]):
         columns = slice(t * width, (t + 1) * width)
         value = dot(own_hidden_ref[...], own_outer_ref[:, columns])
@@ -248,21 +292,28 @@
         cost_estimate=pl.CostEstimate(flops=PREPARE_FLOPS, bytes_accessed=0, transcendentals=0),
         name="prepare",
     )(bias_table.T, new_counts.T, cached_lengths.T, deal)
-    late, bias, picked = lax.optimization_barrier((tokens, bias, picked))
-    blocks = (tokens, swap(late, 1), far, across)
+    near = swap(tokens, 1)
     half = rows // 2
+    gain = attn_gain.reshape(1, model_width)
+    projections = (w_query, w_key, w_value)
+    sums = local(
+        early_kernel,
+        out_shape=(shape((rows, LANES), F32),) + (shape((rows, local_width), F32),) * 3,
+        in_specs=[VMEM] * 10,
+        out_specs=(VMEM,) * 4,
+        name="early",
+    )(tokens, near, across, gain, *projections, w_out, cache_keys, cache_values)
     send, context = local(
         attend_kernel,
         out_shape=(shape((half, model_width), BF16), shape((half, local_width), BF16)),
-        in_specs=[VMEM] * 13,
+        in_specs=[VMEM] * 14,
         out_specs=(VMEM,) * 2,
         name="attend",
     )(
-        *blocks,
-        attn_gain.reshape(1, model_width),
-        w_query,
-        w_key,
-        w_value,
+        far,
+        *sums,
+        gain,
+        *projections,
         w_out,
         cache_keys,
         cache_values,
@@ -282,29 +333,30 @@
         in_specs=[VMEM] * 5,
         out_specs=VMEM,
         name="stream",
-    )(*blocks, picked)
+    )(tokens, near, far, across, picked)
     pair = (keep + swap(send, 1).astype(F32)).astype(BF16)
     late_inner, late_outer, pair = lax.optimization_barrier((w_inner, w_outer, pair))
     ff_width = w_inner.shape[1]
-    mixed, ffn_input, hidden = local(
+    mixed, ffn_input, inverse, hidden = local(
         inner_kernel,
         out_shape=(
             shape((half, model_width), F32),
             shape((half, model_width), BF16),
+            shape((half, LANES), F32),
             shape((half, ff_width), BF16),
         ),
         in_specs=[VMEM] * 5,
-        out_specs=(VMEM,) * 3,
+        out_specs=(VMEM,) * 4,
         cost_estimate=pl.CostEstimate(flops=INNER_FLOPS, bytes_accessed=0, transcendentals=0),
         name="inner",
     )(pair, swap(pair, 2), stream, ffn_gain.reshape(1, model_width), w_inner)
     out = local(
         outer_kernel,
         out_shape=shape((groups * 2, half, width), BF16),
-        in_specs=[VMEM] * 6,
+        in_specs=[VMEM] * 7,
         out_specs=VMEM,
         name="outer",
-    )(mixed, ffn_input, hidden, swap(late_inner, 1), w_outer, swap(late_outer, 1))
+    )(mixed, ffn_input, inverse, hidden, swap(late_inner, 1), w_outer, swap(late_outer, 1))
     share = rows // replicas
     if not halved(share):
         padded = jnp.zeros((groups * 2, rows, width), BF16)

time: 31.1 us -> 30.6 us (0.984)
  waiting for transfers between devices: 7.54 us -> 5.97 us
  starting transfers between devices: 4.52 us -> 5.62 us
    ppermute x7, waiting for transfers between devices: 7.54 us -> 5.97 us  [swap(): return lax.ppermute(value, ('hi', 'lo'), [(i, i ^ xor) for i in range(4)])]
    ppermute x7, starting transfers between devices: 4.52 us -> 5.62 us  [swap(): return lax.ppermute(value, ('hi', 'lo'), [(i, i ^ xor) for i in range(4)])]
    pallas_call x1, Pallas kernels: 1.6 us -> 1.16 us  [on_device(): local(attend_kernel, out_shape=(shape((half, model_width), BF16), shape((...]
    pallas_call x0 -> x1, Pallas kernels: none -> 0.34 us  [on_device(): local(early_kernel, out_shape=(shape((rows, LANES), F32),) + (shape((rows...]
  transfers between devices with their start and end apart: 7 -> 7, of which waited for: 4 -> 4; matrix products, arithmetic and copies ran while one was open for 0% -> 0% of each run, Pallas kernels for 6% -> 7%
where the time goes in v6:
time: 30.6 us; the launch traced here: 30.4 us
  blocking collectives  13.2 us (43%)
  waiting for transfers between devices  5.97 us (20%)
  starting transfers between devices  5.62 us (18%)
  Pallas kernels  4.01 us (13%)
  local copies, waits for them, and re-layouts  1.38 us (5%)
    all_to_all x1, blocking collectives, on_device(): lax.all_to_all(out.reshape(groups * 2 * replicas, -1, width), ('hi', 'lo'...  13.2 us
    ppermute x7, waiting for transfers between devices, swap(): return lax.ppermute(value, ('hi', 'lo'), [(i, i ^ xor) for i in range(4)])  5.97 us
    ppermute x7, starting transfers between devices, swap(): return lax.ppermute(value, ('hi', 'lo'), [(i, i ^ xor) for i in range(4)])  5.62 us
    pallas_call x1, Pallas kernels, on_device(): local(attend_kernel, out_shape=(shape((half, model_width), BF16), shape((...  1.16 us
    pallas_call x1, Pallas kernels, on_device(): local(functools.partial(prepare_kernel, replicas, cached), out_shape=(sha...  1.08 us
    unnamed x30, local copies, waits for them, and re-layouts  0.75 us
    pallas_call x1, Pallas kernels, on_device(): local(outer_kernel, out_shape=shape((groups * 2, half, width), BF16), in_...  0.74 us
    convert_element_type x1, local copies, waits for them, and re-layouts, on_device(): jnp.sum(parts, axis=0).swapaxes(0, 1).reshape(rows, width).astype(BF16)  0.63 us
  transfers between devices with their start and end apart: 7, of which 4 were waited for; matrix products, arithmetic and copies ran while one was open for 0% of the time, Pallas kernels for 7%

profile of v6, /device:TPU:0, one launch (start us, length us, event | category | flops | bytes accessed | tf_op | source)
XLA Modules:
  0.0 30.4 jit_solution(17755849557198052157)
XLA Ops:
  0.0 3.0 %collective-permute-start.2 = (bf16[128,256]{1,0:T(8,128)(2,1)}, bf16[128,256]{1,0:T(8,128)(2,1)S(1)}, u32[]{:S(2)}, u32[]{:S(2)}) collective-permute-start(bf16[128,256]{1,0:T(8,128)(2,1)} %own_ref.3), channel_id=1, source_target_pairs={{0,2},{1,3},{2,0},{3,1},{4,6},{5,7},{6,4},{7,5},{8,10},{9,11},{10,... | collective-permute-start | bytes 196616 | tf_op jit(solution)/shard_map/ppermute | solution.py:251
  3.0 0.0 collective-permute-start.1
  3.0 0.1 collective-permute-start
  3.1 0.0 copy-start.11
  3.1 0.0 copy-start.12
  3.1 0.0 copy-start.13
  3.1 0.7 %copy-done.11 = f32[32,4]{0,1:T(4,128)S(1)} copy-done((f32[32,4]{0,1:T(4,128)S(1)}, f32[32,4]{0,1:T(4,128)}, u32[]{:S(2)}) %copy-start.11) | copy-done | bytes 536
  3.8 0.0 copy-done.12
  3.8 0.0 copy-done.13
  3.8 0.0 copy-done.14
  3.8 0.0 copy-start.3
  3.8 0.0 copy-start.5
  3.8 0.0 copy-start.6
  3.8 0.0 copy-start.7
  3.8 0.0 copy-start.8
  3.9 1.1 %prepare.1 = (f32[2,256,128]{2,1,0:T(8,128)S(1)}, bf16[128,128]{1,0:T(8,128)(2,1)S(1)}) custom-call(f32[4,32]{1,0:T(4,128)S(1)} %bitcast.13, s32[1,2]{1,0:T(1,128)S(1)} %bitcast.14, s32[1,2]{1,0:T(1,128)S(1)} %bitcast.15, s32[1,128]{1,0:T(1,128)S(1)} %copy-done.14), custom_call_target="tpu_custom_call" | custom-call | flops 7000000000 | tf_op jit(solution)/shard_map/prepare/pallas_call | solution.py:284
  4.9 0.7 %collective-permute-done.2.across_ref = bf16[128,256]{1,0:T(8,128)(2,1)S(1)} collective-permute-done((bf16[128,256]{1,0:T(8,128)(2,1)}, bf16[128,256]{1,0:T(8,128)(2,1)S(1)}, u32[]{:S(2)}, u32[]{:S(2)}) %collective-permute-start.2) | collective-permute-done | bytes 65568 | tf_op jit(solution)/shard_map/ppermute | solution.py:251
  5.6 0.0 collective-permute-done.1.near_ref
  5.6 0.0 copy-done
  5.6 0.0 copy-done.1
  5.6 0.0 copy-done.2
  5.6 0.0 copy-done.3
  5.6 0.0 copy-done.5
  5.6 0.0 copy-done.6
  5.6 0.0 copy-done.7
  5.6 0.0 copy-done.8
  5.7 0.3 %early.1 = (f32[128,128]{1,0:T(8,128)S(1)}, f32[128,256]{1,0:T(8,128)S(1)}, f32[128,256]{1,0:T(8,128)S(1)}, f32[128,256]{1,0:T(8,128)S(1)}) custom-call(bf16[128,256]{1,0:T(8,128)(2,1)S(1)} %copy-done.7, bf16[128,256]{1,0:T(8,128)(2,1)S(1)} %collective-permute-done.1.near_ref, bf16[128,256]{1,0:T(8,128)(2,1)S(1)} %collective-permute-done.2.across_ref, ...), custom_call_target="tpu_custom_call" | custom-call | tf_op jit(solution)/shard_map/early/pallas_call | solution.py:299
  6.0 0.9 %collective-permute-done.far_ref = bf16[128,256]{1,0:T(8,128)(2,1)S(1)} collective-permute-done((bf16[128,256]{1,0:T(8,128)(2,1)}, bf16[128,256]{1,0:T(8,128)(2,1)S(1)}, u32[]{:S(2)}, u32[]{:S(2)}) %collective-permute-start) | collective-permute-done | bytes 65568 | tf_op jit(solution)/shard_map/ppermute | solution.py:251
  6.9 1.2 %attend.1 = (bf16[64,1024]{1,0:T(8,128)(2,1)S(1)}, bf16[64,256]{1,0:T(8,128)(2,1)S(1)}) custom-call(bf16[128,256]{1,0:T(8,128)(2,1)S(1)} %collective-permute-done.far_ref, f32[128,128]{1,0:T(8,128)S(1)} %get-tuple-element.20.squares_ref, f32[128,256]{1,0:T(8,128)S(1)} %get-tuple-element.21.query_ref, f32[128,256]{1,0:T(8,128)S(1)} %get-tuple-element.22.key_ref, ...), custom_call_target="tpu_custom_call" | custom-call | tf_op jit(solution)/shard_map/attend/pallas_call | solution.py:306
  8.1 0.0 copy-start.4
  8.1 0.5 %collective-permute-start.3 = (bf16[64,1024]{1,0:T(8,128)(2,1)S(1)}, bf16[64,1024]{1,0:T(8,128)(2,1)S(1)}, u32[]{:S(2)}, u32[]{:S(2)}) collective-permute-start(bf16[64,1024]{1,0:T(8,128)(2,1)S(1)} %get-tuple-element.27), channel_id=1, source_target_pairs={{0,1},{1,0},{2,3},{3,2},{4,5},{5,4},{6,7},{7,6},{8,9},{9,8},{10,11... | collective-permute-start | bytes 393224 | tf_op jit(solution)/shard_map/ppermute | solution.py:251
  8.6 0.2 project.1
  8.8 0.8 %collective-permute-done.3 = bf16[64,1024]{1,0:T(8,128)(2,1)S(1)} collective-permute-done((bf16[64,1024]{1,0:T(8,128)(2,1)S(1)}, bf16[64,1024]{1,0:T(8,128)(2,1)S(1)}, u32[]{:S(2)}, u32[]{:S(2)}) %collective-permute-start.3) | collective-permute-done | bytes 131104 | tf_op jit(solution)/shard_map/ppermute | solution.py:251
  9.7 0.0 copy-start.10
  9.7 1.4 %collective-permute-start.4 = (bf16[64,1024]{1,0:T(8,128)(2,1)S(1)}, bf16[64,1024]{1,0:T(8,128)(2,1)S(1)}, u32[]{:S(2)}, u32[]{:S(2)}) collective-permute-start(bf16[64,1024]{1,0:T(8,128)(2,1)S(1)} %add_convert_fusion.pair_ref), channel_id=1, source_target_pairs={{0,2},{1,3},{2,0},{3,1},{4,6},{5,7},{6,4},{7,5},{8,10},{9,11},{10,... | collective-permute-start | bytes 393224 | tf_op jit(solution)/shard_map/ppermute | solution.py:251
  11.1 0.2 stream.1.stream_ref
  11.3 0.0 copy-done.9
  11.3 0.1 collective-permute-start.5
  11.4 0.0 copy-done.4
  11.4 0.5 %collective-permute-start.6 = (bf16[512,1024]{1,0:T(8,128)(2,1)S(1)}, bf16[512,1024]{1,0:T(8,128)(2,1)S(1)}, u32[]{:S(2)}, u32[]{:S(2)}) collective-permute-start(bf16[512,1024]{1,0:T(8,128)(2,1)S(1)} %copy-done.4), channel_id=1, source_target_pairs={{0,1},{1,0},{2,3},{3,2},{4,5},{5,4},{6,7},{7,6},{8,9},{9,8},{10,11... | collective-permute-start | bytes 3145736 | tf_op jit(solution)/shard_map/ppermute | solution.py:251
  11.9 3.6 %collective-permute-done.4.other_ref = bf16[64,1024]{1,0:T(8,128)(2,1)S(1)} collective-permute-done((bf16[64,1024]{1,0:T(8,128)(2,1)S(1)}, bf16[64,1024]{1,0:T(8,128)(2,1)S(1)}, u32[]{:S(2)}, u32[]{:S(2)}) %collective-permute-start.4) | collective-permute-done | bytes 131104 | tf_op jit(solution)/shard_map/ppermute | solution.py:251
  15.5 0.0 copy-done.10
  15.5 0.3 %inner.1 = (f32[64,1024]{1,0:T(8,128)S(1)}, bf16[64,1024]{1,0:T(8,128)(2,1)S(1)}, f32[64,128]{1,0:T(8,128)S(1)}, bf16[64,512]{1,0:T(8,128)(2,1)S(1)}) custom-call(bf16[64,1024]{1,0:T(8,128)(2,1)S(1)} %add_convert_fusion.pair_ref, bf16[64,1024]{1,0:T(8,128)(2,1)S(1)} %collective-permute-done.4.other_ref, bf16[64,1024]{1,0:T(8,128)(2,1)S(1)} %stream.1.stream_ref, ...), custom_call_target="tpu_custom_call" | custom-call | flops 40000000000 | tf_op jit(solution)/shard_map/inner/pallas_call | solution.py:340
  15.8 0.0 collective-permute-done.5.near_inner_ref
  15.8 0.0 collective-permute-done.6.near_outer_ref
  15.8 0.7 %outer.1 = bf16[4,64,256]{2,1,0:T(8,128)(2,1)S(1)} custom-call(f32[64,1024]{1,0:T(8,128)S(1)} %get-tuple-element.29.mixed_ref, bf16[64,1024]{1,0:T(8,128)(2,1)S(1)} %get-tuple-element.30.input_ref, f32[64,128]{1,0:T(8,128)S(1)} %get-tuple-element.31.inverse_ref, bf16[64,512]{1,0:T(8,128)(2,1)S(1)} %get-tuple-element.32.own_hidden_ref, ...), custom_call_target="tpu_custom_call" | custom-call | tf_op jit(solution)/shard_map/outer/pallas_call | solution.py:353
  16.6 13.2 %all_to_all.5 = bf16[32,8,256]{2,1,0:T(8,128)(2,1)S(1)} all-to-all(bf16[32,8,256]{2,1,0:T(8,128)(2,1)S(1)} %bitcast.9), channel_id=1, replica_groups=mesh['rep'=8,'hi'=2,'lo'=2] {'hi','lo','rep'}, dimensions={0} | all-to-all | bytes 262144 | tf_op jit(solution)/shard_map/all_to_all | solution.py:364
  29.8 0.6 %copy.16 = bf16[8,2,8,256]{3,2,1,0:T(8,128)(2,1)} copy(bf16[8,2,8,256]{3,2,0,1:T(8,128)(2,1)S(1)} %bitcast.17) | data formatting | bytes 131072 | tf_op jit(solution)/shard_map/convert_element_type | solution.py:369
  (7 shorter events, 0.1 us)
Async XLA Ops:
  0.0 5.6 %collective-permute-start.2 = (bf16[128,256]{1,0:T(8,128)(2,1)}, bf16[128,256]{1,0:T(8,128)(2,1)S(1)}, u32[]{:S(2)}, u32[]{:S(2)}) collective-permute-start(bf16[128,256]{1,0:T(8,128)(2,1)} %own_ref.3), channel_id=1, source_target_pairs={{0,2},{1,3},{2,0},{3,1},{4,6},{5,7},{6,4},{7,5},{8,10},{9,11},{10,... | collective-permute-start | bytes 196616 | tf_op jit(solution)/shard_map/ppermute | solution.py:251
  3.0 2.6 %collective-permute-start.1 = (bf16[128,256]{1,0:T(8,128)(2,1)}, bf16[128,256]{1,0:T(8,128)(2,1)S(1)}, u32[]{:S(2)}, u32[]{:S(2)}) collective-permute-start(bf16[128,256]{1,0:T(8,128)(2,1)} %own_ref.3), channel_id=1, source_target_pairs={{0,1},{1,0},{2,3},{3,2},{4,5},{5,4},{6,7},{7,6},{8,9},{9,8},{10,11... | collective-permute-start | bytes 196616 | tf_op jit(solution)/shard_map/ppermute | solution.py:251
  3.0 4.0 %collective-permute-start = (bf16[128,256]{1,0:T(8,128)(2,1)}, bf16[128,256]{1,0:T(8,128)(2,1)S(1)}, u32[]{:S(2)}, u32[]{:S(2)}) collective-permute-start(bf16[128,256]{1,0:T(8,128)(2,1)} %own_ref.3), channel_id=1, source_target_pairs={{0,3},{1,2},{2,1},{3,0},{4,7},{5,6},{6,5},{7,4},{8,11},{9,10},{10,... | collective-permute-start | bytes 196616 | tf_op jit(solution)/shard_map/ppermute | solution.py:251
  3.1 0.7 %copy-start.11 = (f32[32,4]{0,1:T(4,128)S(1)}, f32[32,4]{0,1:T(4,128)}, u32[]{:S(2)}) copy-start(f32[32,4]{0,1:T(4,128)} %param.24) | copy-start | bytes 1540
  3.1 0.7 %copy-start.12 = (s32[2,1]{0,1:T(1,128)S(1)}, s32[2,1]{0,1:T(1,128)}, u32[]{:S(2)}) copy-start(s32[2,1]{0,1:T(1,128)} %param.27) | copy-start | bytes 28
  3.1 0.7 %copy-start.13 = (s32[2,1]{0,1:T(1,128)S(1)}, s32[2,1]{0,1:T(1,128)}, u32[]{:S(2)}) copy-start(s32[2,1]{0,1:T(1,128)} %param.28) | copy-start | bytes 28
  3.1 0.7 %copy-start.14 = (s32[1,128]{1,0:T(1,128)S(1)}, s32[1,128]{1,0:T(1,128)}, u32[]{:S(2)}) copy-start(s32[1,128]{1,0:T(1,128)} %deal_ref.1) | copy-start | bytes 1540
  3.8 1.8 %copy-start = (bf16[256,1024]{1,0:T(8,128)(2,1)S(1)}, bf16[256,1024]{1,0:T(8,128)(2,1)}, u32[]{:S(2)}) copy-start(bf16[256,1024]{1,0:T(8,128)(2,1)} %w_out_ref.5) | copy-start | bytes 1572868
  3.8 1.8 %copy-start.1 = (bf16[1024,256]{1,0:T(8,128)(2,1)S(1)}, bf16[1024,256]{1,0:T(8,128)(2,1)}, u32[]{:S(2)}) copy-start(bf16[1024,256]{1,0:T(8,128)(2,1)} %w_query_ref.3) | copy-start | bytes 1572868
  3.8 1.8 %copy-start.2 = (bf16[1024,256]{1,0:T(8,128)(2,1)S(1)}, bf16[1024,256]{1,0:T(8,128)(2,1)}, u32[]{:S(2)}) copy-start(bf16[1024,256]{1,0:T(8,128)(2,1)} %w_key_ref.3) | copy-start | bytes 1572868
  3.8 1.8 %copy-start.3 = (bf16[1024,256]{1,0:T(8,128)(2,1)S(1)}, bf16[1024,256]{1,0:T(8,128)(2,1)}, u32[]{:S(2)}) copy-start(bf16[1024,256]{1,0:T(8,128)(2,1)} %w_value_ref.3) | copy-start | bytes 1572868
  3.8 1.8 %copy-start.5 = (bf16[2,64,256]{2,1,0:T(8,128)(2,1)S(1)}, bf16[2,64,256]{2,1,0:T(8,128)(2,1)}, u32[]{:S(2)}) copy-start(bf16[2,64,256]{2,1,0:T(8,128)(2,1)} %cache_keys_ref.3) | copy-start | bytes 196612
  3.8 1.8 %copy-start.6 = (bf16[2,64,256]{2,1,0:T(8,128)(2,1)S(1)}, bf16[2,64,256]{2,1,0:T(8,128)(2,1)}, u32[]{:S(2)}) copy-start(bf16[2,64,256]{2,1,0:T(8,128)(2,1)} %cache_values_ref.3) | copy-start | bytes 196612
  3.8 1.8 %copy-start.7 = (bf16[128,256]{1,0:T(8,128)(2,1)S(1)}, bf16[128,256]{1,0:T(8,128)(2,1)}, u32[]{:S(2)}) copy-start(bf16[128,256]{1,0:T(8,128)(2,1)} %own_ref.3) | copy-start | bytes 196612
  3.8 1.8 %copy-start.8 = (f32[1024]{0:T(1024)S(1)}, f32[1024]{0:T(1024)}, u32[]{:S(2)}) copy-start(f32[1024]{0:T(1024)} %param.16) | copy-start | bytes 12292
  6.9 4.4 %copy-start.9 = (bf16[1024,512]{1,0:T(8,128)(2,1)S(1)}, bf16[1024,512]{1,0:T(8,128)(2,1)}, u32[]{:S(2)}) copy-start(bf16[1024,512]{1,0:T(8,128)(2,1)} %w_inner_ref.1) | copy-start | bytes 3145732
  8.1 3.3 %copy-start.4 = (bf16[512,1024]{1,0:T(8,128)(2,1)S(1)}, bf16[512,1024]{1,0:T(8,128)(2,1)}, u32[]{:S(2)}) copy-start(bf16[512,1024]{1,0:T(8,128)(2,1)} %own_outer_ref.1) | copy-start | bytes 3145732
  8.1 1.5 %collective-permute-start.3 = (bf16[64,1024]{1,0:T(8,128)(2,1)S(1)}, bf16[64,1024]{1,0:T(8,128)(2,1)S(1)}, u32[]{:S(2)}, u32[]{:S(2)}) collective-permute-start(bf16[64,1024]{1,0:T(8,128)(2,1)S(1)} %get-tuple-element.27), channel_id=1, source_target_pairs={{0,1},{1,0},{2,3},{3,2},{4,5},{5,4},{6,7},{7,6},{8,9},{9,8},{10,11... | collective-permute-start | bytes 393224 | tf_op jit(solution)/shard_map/ppermute | solution.py:251
  9.7 5.8 %copy-start.10 = (f32[1024]{0:T(1024)S(1)}, f32[1024]{0:T(1024)}, u32[]{:S(2)}) copy-start(f32[1024]{0:T(1024)} %param.17) | copy-start | bytes 12292
  9.7 5.8 %collective-permute-start.4 = (bf16[64,1024]{1,0:T(8,128)(2,1)S(1)}, bf16[64,1024]{1,0:T(8,128)(2,1)S(1)}, u32[]{:S(2)}, u32[]{:S(2)}) collective-permute-start(bf16[64,1024]{1,0:T(8,128)(2,1)S(1)} %add_convert_fusion.pair_ref), channel_id=1, source_target_pairs={{0,2},{1,3},{2,0},{3,1},{4,6},{5,7},{6,4},{7,5},{8,10},{9,11},{10,... | collective-permute-start | bytes 393224 | tf_op jit(solution)/shard_map/ppermute | solution.py:251
  11.3 4.5 %collective-permute-start.5 = (bf16[1024,512]{1,0:T(8,128)(2,1)S(1)}, bf16[1024,512]{1,0:T(8,128)(2,1)S(1)}, u32[]{:S(2)}, u32[]{:S(2)}) collective-permute-start(bf16[1024,512]{1,0:T(8,128)(2,1)S(1)} %copy-done.9), channel_id=1, source_target_pairs={{0,1},{1,0},{2,3},{3,2},{4,5},{5,4},{6,7},{7,6},{8,9},{9,8},{10,11... | collective-permute-start | bytes 3145736 | tf_op jit(solution)/shard_map/ppermute | solution.py:251
  11.4 4.4 %collective-permute-start.6 = (bf16[512,1024]{1,0:T(8,128)(2,1)S(1)}, bf16[512,1024]{1,0:T(8,128)(2,1)S(1)}, u32[]{:S(2)}, u32[]{:S(2)}) collective-permute-start(bf16[512,1024]{1,0:T(8,128)(2,1)S(1)} %copy-done.4), channel_id=1, source_target_pairs={{0,1},{1,0},{2,3},{3,2},{4,5},{5,4},{6,7},{7,6},{8,9},{9,8},{10,11... | collective-permute-start | bytes 3145736 | tf_op jit(solution)/shard_map/ppermute | solution.py:251

commit v7 on v5

--- a/solution.py
+++ b/solution.py
@@ -15,6 +15,7 @@
 SMEM = pl.BlockSpec(memory_space=pltpu.SMEM)
 PREPARE_FLOPS = 7 * 10**9
 INNER_FLOPS = 40 * 10**9
+LANES = 128
 VMEM_LIMIT = 24 * 1024 * 1024
 
 
@@ -83,24 +84,28 @@
             bias_ref[j, h * new_slots : (h + 1) * new_slots] = bias
 
 
-def attend(query, new_keys, new_values, old_keys, old_values, bias):
-    new_slots, local_width = query.shape
-    head_count = bias.shape[0] // new_slots
-    lane = lax.broadcasted_iota(jnp.int32, (new_slots, local_width), 1)
-    lane_head = lane // (local_width // head_count)
+def heads_of(shape, heads):
+    return lax.broadcasted_iota(jnp.int32, shape, 1) // (shape[1] // heads)
+
+
+def scores_of(query, keys, bias):
+    heads = bias.shape[0] // query.shape[0]
+    lane_head = heads_of(query.shape, heads)
     stacked = jnp.concatenate(
-        [jnp.where(lane_head == h, query, jnp.zeros_like(query)) for h in range(head_count)],
-        axis=0,
-    )
-    keys = jnp.concatenate([old_keys, new_keys], axis=0)
-    values = jnp.concatenate([old_values, new_values], axis=0)
+        [jnp.where(lane_head == h, query, jnp.zeros_like(query)) for h in range(heads)], axis=0
+    )
     scores = lax.dot_general(stacked, keys, (((1,), (1,)), ((), ())), preferred_element_type=F32)
-    scores = scores + bias
+    return scores + bias
+
+
+def context_of(scores, values, new_slots):
     weights = jnp.exp(scores - jnp.max(scores, axis=1, keepdims=True))
     probs = (weights / jnp.sum(weights, axis=1, keepdims=True)).astype(BF16)
     mixed = dot(probs, values)
-    context = jnp.zeros((new_slots, local_width), F32)
-    for h in range(head_count):
+    heads = scores.shape[0] // new_slots
+    context = mixed[:new_slots]
+    lane_head = heads_of(context.shape, heads)
+    for h in range(1, heads):
         context = jnp.where(lane_head == h, mixed[h * new_slots : (h + 1) * new_slots], context)
     return context.astype(BF16)
 
@@ -121,6 +126,7 @@
     picked_ref,
     send_ref,
     context_ref,
+    normed_ref,
 ):
     index, _ = place()
     rows, width = own_ref.shape
@@ -133,34 +139,32 @@
         block = ref[...].astype(F32)
         squares = squares + jnp.sum(block * block, axis=1, keepdims=True)
     inverse = lax.rsqrt(squares / model_width + EPSILON)
-    queries = new_keys = new_values = 0.0
     for ref, xor in blocks:
         columns = columns_of(index ^ xor, width)
-        normed = (ref[...].astype(F32) * inverse * gain_ref[:, columns]).astype(BF16)
-        queries = queries + dot(normed, w_query_ref[columns, :])
-        new_keys = new_keys + dot(normed, w_key_ref[columns, :])
-        new_values = new_values + dot(normed, w_value_ref[columns, :])
-    queries, new_keys, new_values = (v.astype(BF16) for v in (queries, new_keys, new_values))
+        normed = ref[...].astype(F32) * inverse * gain_ref[:, columns]
+        normed_ref[:, columns] = normed.astype(BF16)
+    queries = dot(normed_ref[...], w_query_ref[...]).astype(BF16)
+    new_keys = dot(normed_ref[...], w_key_ref[...]).astype(BF16)
+    scores = []
+    for j in range(requests):
+        own = slice(j * new_slots, (j + 1) * new_slots)
+        keys = jnp.concatenate([cache_keys_ref[j], new_keys[own]], axis=0)
+        scores.append(scores_of(queries[own], keys, bias_ref[j]))
+    new_values = dot(normed_ref[...], w_value_ref[...]).astype(BF16)
     contexts = []
     for j in range(requests):
         own = slice(j * new_slots, (j + 1) * new_slots)
-        contexts.append(
-            attend(
-                queries[own],
-                new_keys[own],
-                new_values[own],
-                cache_keys_ref[j],
-                cache_values_ref[j],
-                bias_ref[j],
-            )
-        )
-    context = dot(picked_ref[...], jnp.concatenate(contexts, axis=0)).astype(BF16)
-    send_ref[...] = dot(context[half:], w_out_ref[...]).astype(BF16)
-    context_ref[...] = context[:half]
-
-
-def project_kernel(context_ref, w_out_ref, keep_ref):
-    keep_ref[...] = dot(context_ref[...], w_out_ref[...])
+        values = jnp.concatenate([cache_values_ref[j], new_values[own]], axis=0)
+        contexts.append(context_of(scores[j], values, new_slots))
+    context = jnp.concatenate(contexts, axis=0)
+    context_ref[...] = context
+    dealt = dot(picked_ref[half:], context).astype(BF16)
+    send_ref[...] = dot(dealt, w_out_ref[...]).astype(BF16)
+
+
+def project_kernel(context_ref, picked_ref, w_out_ref, keep_ref):
+    dealt = dot(picked_ref[: keep_ref.shape[0]], context_ref[...]).astype(BF16)
+    keep_ref[...] = dot(dealt, w_out_ref[...])
 
 
 def stream_kernel(own_ref, near_ref, far_ref, across_ref, picked_ref, stream_ref):
@@ -172,20 +176,30 @@
 
 
 def inner_kernel(
-    pair_ref, other_ref, stream_ref, gain_ref, w_inner_ref, mixed_ref, input_ref, hidden_ref
+    pair_ref,
+    other_ref,
+    stream_ref,
+    gain_ref,
+    w_inner_ref,
+    mixed_ref,
+    input_ref,
+    inverse_ref,
+    hidden_ref,
 ):
     mixed = pair_ref[...].astype(F32) + other_ref[...].astype(F32) + stream_ref[...].astype(F32)
     mixed_ref[...] = mixed
     square = jnp.sum(mixed * mixed, axis=1, keepdims=True)
     inverse = lax.rsqrt(square / mixed.shape[1] + EPSILON)
-    ffn_input = (mixed * inverse * gain_ref[...]).astype(BF16)
-    input_ref[...] = ffn_input
-    hidden_ref[...] = jnp.maximum(dot(ffn_input, w_inner_ref[...]), 0.0).astype(BF16)
+    inverse_ref[...] = jnp.broadcast_to(inverse, inverse_ref.shape)
+    scaled = (mixed * gain_ref[...]).astype(BF16)
+    input_ref[...] = scaled
+    hidden_ref[...] = jnp.maximum(dot(scaled, w_inner_ref[...]) * inverse, 0.0).astype(BF16)
 
 
 def outer_kernel(
     mixed_ref,
     input_ref,
+    inverse_ref,
     own_hidden_ref,
     near_inner_ref,
     own_outer_ref,
@@ -194,7 +208,8 @@
 ):
     upper = lax.axis_index("hi")
     width = out_ref.shape[2]
-    hidden = jnp.maximum(dot(input_ref[...], near_inner_ref[...]), 0.0).astype(BF16)
+    hidden = dot(input_ref[...], near_inner_ref[...]) * inverse_ref[:, :1]
+    hidden = jnp.maximum(hidden, 0.0).astype(BF16)
     for t in range(out_ref.shape[0]):
         columns = slice(t * width, (t + 1) * width)
         value = dot(own_hidden_ref[...], own_outer_ref[:, columns])
@@ -253,9 +268,10 @@
     half = rows // 2
     send, context = local(
         attend_kernel,
-        out_shape=(shape((half, model_width), BF16), shape((half, local_width), BF16)),
+        out_shape=(shape((half, model_width), BF16), shape((rows, local_width), BF16)),
         in_specs=[VMEM] * 13,
         out_specs=(VMEM,) * 2,
+        scratch_shapes=[pltpu.VMEM((rows, model_width), BF16)],
         name="attend",
     )(
         *blocks,
@@ -272,10 +288,10 @@
     keep = local(
         project_kernel,
         out_shape=shape((half, model_width), F32),
-        in_specs=[VMEM] * 2,
+        in_specs=[VMEM] * 3,
         out_specs=VMEM,
         name="project",
-    )(context, w_out)
+    )(context, picked, w_out)
     stream = local(
         stream_kernel,
         out_shape=shape((half, model_width), BF16),
@@ -286,25 +302,26 @@
     pair = (keep + swap(send, 1).astype(F32)).astype(BF16)
     late_inner, late_outer, pair = lax.optimization_barrier((w_inner, w_outer, pair))
     ff_width = w_inner.shape[1]
-    mixed, ffn_input, hidden = local(
+    mixed, ffn_input, inverse, hidden = local(
         inner_kernel,
         out_shape=(
             shape((half, model_width), F32),
             shape((half, model_width), BF16),
+            shape((half, LANES), F32),
             shape((half, ff_width), BF16),
         ),
         in_specs=[VMEM] * 5,
-        out_specs=(VMEM,) * 3,
+        out_specs=(VMEM,) * 4,
         cost_estimate=pl.CostEstimate(flops=INNER_FLOPS, bytes_accessed=0, transcendentals=0),
         name="inner",
     )(pair, swap(pair, 2), stream, ffn_gain.reshape(1, model_width), w_inner)
     out = local(
         outer_kernel,
         out_shape=shape((groups * 2, half, width), BF16),
-        in_specs=[VMEM] * 6,
+        in_specs=[VMEM] * 7,
         out_specs=VMEM,
         name="outer",
-    )(mixed, ffn_input, hidden, swap(late_inner, 1), w_outer, swap(late_outer, 1))
+    )(mixed, ffn_input, inverse, hidden, swap(late_inner, 1), w_outer, swap(late_outer, 1))
     share = rows // replicas
     if not halved(share):
         padded = jnp.zeros((groups * 2, rows, width), BF16)

time: 31.1 us -> 30.8 us (level)
  no operation moved by 1% of the time
where the time goes in v7:
time: 30.8 us; the launch traced here: 30.6 us
  blocking collectives  13 us (42%)
  waiting for transfers between devices  7.44 us (24%)
  starting transfers between devices  4.52 us (15%)
  Pallas kernels  3.99 us (13%)
  local copies, waits for them, and re-layouts  1.38 us (4%)
    all_to_all x1, blocking collectives, on_device(): lax.all_to_all(out.reshape(groups * 2 * replicas, -1, width), ('hi', 'lo'...  13 us
    ppermute x7, waiting for transfers between devices, swap(): return lax.ppermute(value, ('hi', 'lo'), [(i, i ^ xor) for i in range(4)])  7.44 us
    ppermute x7, starting transfers between devices, swap(): return lax.ppermute(value, ('hi', 'lo'), [(i, i ^ xor) for i in range(4)])  4.52 us
    pallas_call x1, Pallas kernels, on_device(): local(attend_kernel, out_shape=(shape((half, model_width), BF16), shape((...  1.38 us
    pallas_call x1, Pallas kernels, on_device(): local(functools.partial(prepare_kernel, replicas, cached), out_shape=(sha...  1.08 us
    unnamed x30, local copies, waits for them, and re-layouts  0.74 us
    pallas_call x1, Pallas kernels, on_device(): local(outer_kernel, out_shape=shape((groups * 2, half, width), BF16), in_...  0.74 us
    convert_element_type x1, local copies, waits for them, and re-layouts, on_device(): jnp.sum(parts, axis=0).swapaxes(0, 1).reshape(rows, width).astype(BF16)  0.63 us
  transfers between devices with their start and end apart: 7, of which 4 were waited for; matrix products, arithmetic and copies ran while one was open for 0% of the time, Pallas kernels for 6%

profile of v7, /device:TPU:0, one launch (start us, length us, event | category | flops | bytes accessed | tf_op | source)
XLA Modules:
  0.0 30.6 jit_solution(16518127234983034807)
XLA Ops:
  0.0 3.0 %collective-permute-start.2 = (bf16[128,256]{1,0:T(8,128)(2,1)}, bf16[128,256]{1,0:T(8,128)(2,1)S(1)}, u32[]{:S(2)}, u32[]{:S(2)}) collective-permute-start(bf16[128,256]{1,0:T(8,128)(2,1)} %own_ref.3), channel_id=1, source_target_pairs={{0,2},{1,3},{2,0},{3,1},{4,6},{5,7},{6,4},{7,5},{8,10},{9,11},{10,... | collective-permute-start | bytes 196616 | tf_op jit(solution)/shard_map/ppermute | solution.py:222
  3.0 0.0 collective-permute-start.1
  3.0 0.0 copy-start.11
  3.0 0.0 copy-start.12
  3.0 0.0 copy-start.14
  3.0 0.7 %copy-done.11 = f32[32,4]{0,1:T(4,128)S(1)} copy-done((f32[32,4]{0,1:T(4,128)S(1)}, f32[32,4]{0,1:T(4,128)}, u32[]{:S(2)}) %copy-start.11) | copy-done | bytes 536
  3.7 0.0 copy-done.12
  3.7 0.0 copy-done.13
  3.7 0.0 copy-done.14
  3.7 0.0 copy-start.3
  3.7 0.0 copy-start.4
  3.7 0.0 copy-start.6
  3.7 0.0 copy-start.7
  3.7 1.1 %prepare.1 = (f32[2,256,128]{2,1,0:T(8,128)S(1)}, bf16[128,128]{1,0:T(8,128)(2,1)S(1)}) custom-call(f32[4,32]{1,0:T(4,128)S(1)} %bitcast.12, s32[1,2]{1,0:T(1,128)S(1)} %bitcast.13, s32[1,2]{1,0:T(1,128)S(1)} %bitcast.14, s32[1,128]{1,0:T(1,128)S(1)} %copy-done.14), custom_call_target="tpu_custom_call" | custom-call | flops 7000000000 | tf_op jit(solution)/shard_map/prepare/pallas_call | solution.py:255
  4.8 0.0 copy-start.8
  4.8 0.0 copy-done.5
  4.8 0.2 collective-permute-start
  5.0 0.4 %collective-permute-done.2.across_ref = bf16[128,256]{1,0:T(8,128)(2,1)S(1)} collective-permute-done((bf16[128,256]{1,0:T(8,128)(2,1)}, bf16[128,256]{1,0:T(8,128)(2,1)S(1)}, u32[]{:S(2)}, u32[]{:S(2)}) %collective-permute-start.2) | collective-permute-done | bytes 65568 | tf_op jit(solution)/shard_map/ppermute | solution.py:222
  5.4 1.9 %collective-permute-done.1.far_ref = bf16[128,256]{1,0:T(8,128)(2,1)S(1)} collective-permute-done((bf16[128,256]{1,0:T(8,128)(2,1)}, bf16[128,256]{1,0:T(8,128)(2,1)S(1)}, u32[]{:S(2)}, u32[]{:S(2)}) %collective-permute-start.1) | collective-permute-done | bytes 65568 | tf_op jit(solution)/shard_map/ppermute | solution.py:222
  7.3 0.0 collective-permute-done.near_ref
  7.3 0.0 copy-done
  7.3 0.0 copy-done.2
  7.3 0.0 copy-done.3
  7.3 0.0 copy-done.4
  7.3 0.0 copy-done.6
  7.3 0.0 copy-done.7
  7.4 0.0 copy-done.8
  7.4 0.0 copy-start.9
  7.4 1.4 %attend.1 = (bf16[64,1024]{1,0:T(8,128)(2,1)S(1)}, bf16[128,256]{1,0:T(8,128)(2,1)S(1)}) custom-call(bf16[128,256]{1,0:T(8,128)(2,1)S(1)} %copy-done.5, bf16[128,256]{1,0:T(8,128)(2,1)S(1)} %collective-permute-done.near_ref, bf16[128,256]{1,0:T(8,128)(2,1)S(1)} %collective-permute-done.1.far_ref, bf16[128,256]{1,0:T(8,128)(2,1)S(1)} %collective-permute-done.2.across_ref, ...), custom_call_target="tpu_custom_call" | custom-call | tf_op jit(solution)/shard_map/attend/pallas_call | solution.py:269
  8.8 0.0 copy-start.1
  8.8 0.1 collective-permute-start.3
  8.9 0.3 project.1
  9.2 1.0 %collective-permute-done.3 = bf16[64,1024]{1,0:T(8,128)(2,1)S(1)} collective-permute-done((bf16[64,1024]{1,0:T(8,128)(2,1)S(1)}, bf16[64,1024]{1,0:T(8,128)(2,1)S(1)}, u32[]{:S(2)}, u32[]{:S(2)}) %collective-permute-start.3) | collective-permute-done | bytes 131104 | tf_op jit(solution)/shard_map/ppermute | solution.py:222
  10.2 0.0 copy-start.10
  10.2 0.7 %collective-permute-start.4 = (bf16[64,1024]{1,0:T(8,128)(2,1)S(1)}, bf16[64,1024]{1,0:T(8,128)(2,1)S(1)}, u32[]{:S(2)}, u32[]{:S(2)}) collective-permute-start(bf16[64,1024]{1,0:T(8,128)(2,1)S(1)} %add_convert_fusion.pair_ref), channel_id=1, source_target_pairs={{0,2},{1,3},{2,0},{3,1},{4,6},{5,7},{6,4},{7,5},{8,10},{9,11},{10,... | collective-permute-start | bytes 393224 | tf_op jit(solution)/shard_map/ppermute | solution.py:222
  10.9 0.2 stream.1.stream_ref
  11.1 0.0 copy-done.9
  11.1 0.1 collective-permute-start.5
  11.3 0.0 copy-done.1
  11.3 0.4 %collective-permute-start.6 = (bf16[512,1024]{1,0:T(8,128)(2,1)S(1)}, bf16[512,1024]{1,0:T(8,128)(2,1)S(1)}, u32[]{:S(2)}, u32[]{:S(2)}) collective-permute-start(bf16[512,1024]{1,0:T(8,128)(2,1)S(1)} %copy-done.1), channel_id=1, source_target_pairs={{0,1},{1,0},{2,3},{3,2},{4,5},{5,4},{6,7},{7,6},{8,9},{9,8},{10,11... | collective-permute-start | bytes 3145736 | tf_op jit(solution)/shard_map/ppermute | solution.py:222
  11.7 4.1 %collective-permute-done.4.other_ref = bf16[64,1024]{1,0:T(8,128)(2,1)S(1)} collective-permute-done((bf16[64,1024]{1,0:T(8,128)(2,1)S(1)}, bf16[64,1024]{1,0:T(8,128)(2,1)S(1)}, u32[]{:S(2)}, u32[]{:S(2)}) %collective-permute-start.4) | collective-permute-done | bytes 131104 | tf_op jit(solution)/shard_map/ppermute | solution.py:222
  15.9 0.0 copy-done.10
  15.9 0.3 %inner.1 = (f32[64,1024]{1,0:T(8,128)S(1)}, bf16[64,1024]{1,0:T(8,128)(2,1)S(1)}, f32[64,128]{1,0:T(8,128)S(1)}, bf16[64,512]{1,0:T(8,128)(2,1)S(1)}) custom-call(bf16[64,1024]{1,0:T(8,128)(2,1)S(1)} %add_convert_fusion.pair_ref, bf16[64,1024]{1,0:T(8,128)(2,1)S(1)} %collective-permute-done.4.other_ref, bf16[64,1024]{1,0:T(8,128)(2,1)S(1)} %stream.1.stream_ref, ...), custom_call_target="tpu_custom_call" | custom-call | flops 40000000000 | tf_op jit(solution)/shard_map/inner/pallas_call | solution.py:305
  16.2 0.0 collective-permute-done.5.near_inner_ref
  16.2 0.0 collective-permute-done.6.near_outer_ref
  16.2 0.7 %outer.1 = bf16[4,64,256]{2,1,0:T(8,128)(2,1)S(1)} custom-call(f32[64,1024]{1,0:T(8,128)S(1)} %get-tuple-element.27.mixed_ref, bf16[64,1024]{1,0:T(8,128)(2,1)S(1)} %get-tuple-element.28.input_ref, f32[64,128]{1,0:T(8,128)S(1)} %get-tuple-element.29.inverse_ref, bf16[64,512]{1,0:T(8,128)(2,1)S(1)} %get-tuple-element.30.own_hidden_ref, ...), custom_call_target="tpu_custom_call" | custom-call | tf_op jit(solution)/shard_map/outer/pallas_call | solution.py:318
  16.9 13.0 %all_to_all.5 = bf16[32,8,256]{2,1,0:T(8,128)(2,1)S(1)} all-to-all(bf16[32,8,256]{2,1,0:T(8,128)(2,1)S(1)} %bitcast.9), channel_id=1, replica_groups=mesh['rep'=8,'hi'=2,'lo'=2] {'hi','lo','rep'}, dimensions={0} | all-to-all | bytes 262144 | tf_op jit(solution)/shard_map/all_to_all | solution.py:329
  30.0 0.6 %copy.16 = bf16[8,2,8,256]{3,2,1,0:T(8,128)(2,1)} copy(bf16[8,2,8,256]{3,2,0,1:T(8,128)(2,1)S(1)} %bitcast.16) | data formatting | bytes 131072 | tf_op jit(solution)/shard_map/convert_element_type | solution.py:334
  (6 shorter events, 0.1 us)
Async XLA Ops:
  0.0 5.4 %collective-permute-start.2 = (bf16[128,256]{1,0:T(8,128)(2,1)}, bf16[128,256]{1,0:T(8,128)(2,1)S(1)}, u32[]{:S(2)}, u32[]{:S(2)}) collective-permute-start(bf16[128,256]{1,0:T(8,128)(2,1)} %own_ref.3), channel_id=1, source_target_pairs={{0,2},{1,3},{2,0},{3,1},{4,6},{5,7},{6,4},{7,5},{8,10},{9,11},{10,... | collective-permute-start | bytes 196616 | tf_op jit(solution)/shard_map/ppermute | solution.py:222
  3.0 4.3 %collective-permute-start.1 = (bf16[128,256]{1,0:T(8,128)(2,1)}, bf16[128,256]{1,0:T(8,128)(2,1)S(1)}, u32[]{:S(2)}, u32[]{:S(2)}) collective-permute-start(bf16[128,256]{1,0:T(8,128)(2,1)} %own_ref.3), channel_id=1, source_target_pairs={{0,3},{1,2},{2,1},{3,0},{4,7},{5,6},{6,5},{7,4},{8,11},{9,10},{10,... | collective-permute-start | bytes 196616 | tf_op jit(solution)/shard_map/ppermute | solution.py:222
  3.0 0.7 %copy-start.11 = (f32[32,4]{0,1:T(4,128)S(1)}, f32[32,4]{0,1:T(4,128)}, u32[]{:S(2)}) copy-start(f32[32,4]{0,1:T(4,128)} %param.24) | copy-start | bytes 1540
  3.0 0.7 %copy-start.12 = (s32[2,1]{0,1:T(1,128)S(1)}, s32[2,1]{0,1:T(1,128)}, u32[]{:S(2)}) copy-start(s32[2,1]{0,1:T(1,128)} %param.27) | copy-start | bytes 28
  3.0 0.7 %copy-start.13 = (s32[2,1]{0,1:T(1,128)S(1)}, s32[2,1]{0,1:T(1,128)}, u32[]{:S(2)}) copy-start(s32[2,1]{0,1:T(1,128)} %param.28) | copy-start | bytes 28
  3.0 0.7 %copy-start.14 = (s32[1,128]{1,0:T(1,128)S(1)}, s32[1,128]{1,0:T(1,128)}, u32[]{:S(2)}) copy-start(s32[1,128]{1,0:T(1,128)} %deal_ref.1) | copy-start | bytes 1540
  3.7 1.2 %copy-start.5 = (bf16[128,256]{1,0:T(8,128)(2,1)S(1)}, bf16[128,256]{1,0:T(8,128)(2,1)}, u32[]{:S(2)}) copy-start(bf16[128,256]{1,0:T(8,128)(2,1)} %own_ref.3) | copy-start | bytes 196612
  3.7 3.6 %copy-start = (bf16[256,1024]{1,0:T(8,128)(2,1)S(1)}, bf16[256,1024]{1,0:T(8,128)(2,1)}, u32[]{:S(2)}) copy-start(bf16[256,1024]{1,0:T(8,128)(2,1)} %w_out_ref.3) | copy-start | bytes 1572868
  3.7 3.6 %copy-start.2 = (bf16[1024,256]{1,0:T(8,128)(2,1)S(1)}, bf16[1024,256]{1,0:T(8,128)(2,1)}, u32[]{:S(2)}) copy-start(bf16[1024,256]{1,0:T(8,128)(2,1)} %w_query_ref.1) | copy-start | bytes 1572868
  3.7 3.6 %copy-start.3 = (bf16[1024,256]{1,0:T(8,128)(2,1)S(1)}, bf16[1024,256]{1,0:T(8,128)(2,1)}, u32[]{:S(2)}) copy-start(bf16[1024,256]{1,0:T(8,128)(2,1)} %w_key_ref.1) | copy-start | bytes 1572868
  3.7 3.6 %copy-start.4 = (bf16[1024,256]{1,0:T(8,128)(2,1)S(1)}, bf16[1024,256]{1,0:T(8,128)(2,1)}, u32[]{:S(2)}) copy-start(bf16[1024,256]{1,0:T(8,128)(2,1)} %w_value_ref.1) | copy-start | bytes 1572868
  3.7 3.6 %copy-start.6 = (bf16[2,64,256]{2,1,0:T(8,128)(2,1)S(1)}, bf16[2,64,256]{2,1,0:T(8,128)(2,1)}, u32[]{:S(2)}) copy-start(bf16[2,64,256]{2,1,0:T(8,128)(2,1)} %cache_keys_ref.1) | copy-start | bytes 196612
  3.7 3.6 %copy-start.7 = (bf16[2,64,256]{2,1,0:T(8,128)(2,1)S(1)}, bf16[2,64,256]{2,1,0:T(8,128)(2,1)}, u32[]{:S(2)}) copy-start(bf16[2,64,256]{2,1,0:T(8,128)(2,1)} %cache_values_ref.1) | copy-start | bytes 196612
  4.8 2.5 %copy-start.8 = (f32[1024]{0:T(1024)S(1)}, f32[1024]{0:T(1024)}, u32[]{:S(2)}) copy-start(f32[1024]{0:T(1024)} %param.16) | copy-start | bytes 12292
  4.8 2.5 %collective-permute-start = (bf16[128,256]{1,0:T(8,128)(2,1)S(1)}, bf16[128,256]{1,0:T(8,128)(2,1)S(1)}, u32[]{:S(2)}, u32[]{:S(2)}) collective-permute-start(bf16[128,256]{1,0:T(8,128)(2,1)S(1)} %copy-done.5), channel_id=1, source_target_pairs={{0,1},{1,0},{2,3},{3,2},{4,5},{5,4},{6,7},{7,6},{8,9},{9,8},{10,11... | collective-permute-start | bytes 196616 | tf_op jit(solution)/shard_map/ppermute | solution.py:222
  7.4 3.8 %copy-start.9 = (bf16[1024,512]{1,0:T(8,128)(2,1)S(1)}, bf16[1024,512]{1,0:T(8,128)(2,1)}, u32[]{:S(2)}) copy-start(bf16[1024,512]{1,0:T(8,128)(2,1)} %w_inner_ref.1) | copy-start | bytes 3145732
  8.8 2.5 %copy-start.1 = (bf16[512,1024]{1,0:T(8,128)(2,1)S(1)}, bf16[512,1024]{1,0:T(8,128)(2,1)}, u32[]{:S(2)}) copy-start(bf16[512,1024]{1,0:T(8,128)(2,1)} %own_outer_ref.1) | copy-start | bytes 3145732
  8.8 1.4 %collective-permute-start.3 = (bf16[64,1024]{1,0:T(8,128)(2,1)S(1)}, bf16[64,1024]{1,0:T(8,128)(2,1)S(1)}, u32[]{:S(2)}, u32[]{:S(2)}) collective-permute-start(bf16[64,1024]{1,0:T(8,128)(2,1)S(1)} %get-tuple-element.25), channel_id=1, source_target_pairs={{0,1},{1,0},{2,3},{3,2},{4,5},{5,4},{6,7},{7,6},{8,9},{9,8},{10,11... | collective-permute-start | bytes 393224 | tf_op jit(solution)/shard_map/ppermute | solution.py:222
  10.2 5.6 %copy-start.10 = (f32[1024]{0:T(1024)S(1)}, f32[1024]{0:T(1024)}, u32[]{:S(2)}) copy-start(f32[1024]{0:T(1024)} %param.17) | copy-start | bytes 12292
  10.2 5.6 %collective-permute-start.4 = (bf16[64,1024]{1,0:T(8,128)(2,1)S(1)}, bf16[64,1024]{1,0:T(8,128)(2,1)S(1)}, u32[]{:S(2)}, u32[]{:S(2)}) collective-permute-start(bf16[64,1024]{1,0:T(8,128)(2,1)S(1)} %add_convert_fusion.pair_ref), channel_id=1, source_target_pairs={{0,2},{1,3},{2,0},{3,1},{4,6},{5,7},{6,4},{7,5},{8,10},{9,11},{10,... | collective-permute-start | bytes 393224 | tf_op jit(solution)/shard_map/ppermute | solution.py:222
  11.1 5.0 %collective-permute-start.5 = (bf16[1024,512]{1,0:T(8,128)(2,1)S(1)}, bf16[1024,512]{1,0:T(8,128)(2,1)S(1)}, u32[]{:S(2)}, u32[]{:S(2)}) collective-permute-start(bf16[1024,512]{1,0:T(8,128)(2,1)S(1)} %copy-done.9), channel_id=1, source_target_pairs={{0,1},{1,0},{2,3},{3,2},{4,5},{5,4},{6,7},{7,6},{8,9},{9,8},{10,11... | collective-permute-start | bytes 3145736 | tf_op jit(solution)/shard_map/ppermute | solution.py:222
  11.3 4.9 %collective-permute-start.6 = (bf16[512,1024]{1,0:T(8,128)(2,1)S(1)}, bf16[512,1024]{1,0:T(8,128)(2,1)S(1)}, u32[]{:S(2)}, u32[]{:S(2)}) collective-permute-start(bf16[512,1024]{1,0:T(8,128)(2,1)S(1)} %copy-done.1), channel_id=1, source_target_pairs={{0,1},{1,0},{2,3},{3,2},{4,5},{5,4},{6,7},{7,6},{8,9},{9,8},{10,11... | collective-permute-start | bytes 3145736 | tf_op jit(solution)/shard_map/ppermute | solution.py:222

commit v8 on v7

--- a/solution.py
+++ b/solution.py
@@ -100,8 +100,7 @@
 
 def context_of(scores, values, new_slots):
     weights = jnp.exp(scores - jnp.max(scores, axis=1, keepdims=True))
-    probs = (weights / jnp.sum(weights, axis=1, keepdims=True)).astype(BF16)
-    mixed = dot(probs, values)
+    mixed = dot(weights.astype(BF16), values) / jnp.sum(weights, axis=1, keepdims=True)
     heads = scores.shape[0] // new_slots
     context = mixed[:new_slots]
     lane_head = heads_of(context.shape, heads)
@@ -119,7 +118,6 @@
     w_query_ref,
     w_key_ref,
     w_value_ref,
-    w_out_ref,
     cache_keys_ref,
     cache_values_ref,
     bias_ref,
@@ -158,13 +156,16 @@
         contexts.append(context_of(scores[j], values, new_slots))
     context = jnp.concatenate(contexts, axis=0)
     context_ref[...] = context
-    dealt = dot(picked_ref[half:], context).astype(BF16)
-    send_ref[...] = dot(dealt, w_out_ref[...]).astype(BF16)
+    send_ref[...] = dot(picked_ref[half:], context).astype(BF16)
 
 
 def project_kernel(context_ref, picked_ref, w_out_ref, keep_ref):
     dealt = dot(picked_ref[: keep_ref.shape[0]], context_ref[...]).astype(BF16)
     keep_ref[...] = dot(dealt, w_out_ref[...])
+
+
+def pair_kernel(keep_ref, near_ref, near_out_ref, pair_ref):
+    pair_ref[...] = (keep_ref[...] + dot(near_ref[...], near_out_ref[...])).astype(BF16)
 
 
 def stream_kernel(own_ref, near_ref, far_ref, across_ref, picked_ref, stream_ref):
@@ -268,10 +269,11 @@
     half = rows // 2
     send, context = local(
         attend_kernel,
-        out_shape=(shape((half, model_width), BF16), shape((rows, local_width), BF16)),
-        in_specs=[VMEM] * 13,
+        out_shape=(shape((half, local_width), BF16), shape((rows, local_width), BF16)),
+        in_specs=[VMEM] * 12,
         out_specs=(VMEM,) * 2,
         scratch_shapes=[pltpu.VMEM((rows, model_width), BF16)],
+        cost_estimate=pl.CostEstimate(flops=INNER_FLOPS, bytes_accessed=0, transcendentals=0),
         name="attend",
     )(
         *blocks,
@@ -279,7 +281,6 @@
         w_query,
         w_key,
         w_value,
-        w_out,
         cache_keys,
         cache_values,
         bias,
@@ -299,7 +300,13 @@
         out_specs=VMEM,
         name="stream",
     )(*blocks, picked)
-    pair = (keep + swap(send, 1).astype(F32)).astype(BF16)
+    pair = local(
+        pair_kernel,
+        out_shape=shape((half, model_width), BF16),
+        in_specs=[VMEM] * 3,
+        out_specs=VMEM,
+        name="pair",
+    )(keep, swap(send, 1), swap(w_out, 1))
     late_inner, late_outer, pair = lax.optimization_barrier((w_inner, w_outer, pair))
     ff_width = w_inner.shape[1]
     mixed, ffn_input, inverse, hidden = local(

time: 30.8 us -> 30.6 us (level)
  waiting for transfers between devices: 7.44 us -> 6.95 us
    ppermute x7 -> x8, waiting for transfers between devices: 7.44 us -> 6.95 us  [swap(): return lax.ppermute(value, ('hi', 'lo'), [(i, i ^ xor) for i in range(4)])]
    ppermute x7 -> x8, starting transfers between devices: 4.52 us -> 4.82 us  [swap(): return lax.ppermute(value, ('hi', 'lo'), [(i, i ^ xor) for i in range(4)])]
    pallas_call x1 -> x2, Pallas kernels: 1.38 us -> 1.34 us  [the longest x1 1.14 us: on_device(): local(attend_kernel, out_shape=(shape((half, local_width), BF16), shape((...]
  transfers between devices with their start and end apart: 7 -> 8, of which waited for: 4 -> 3; matrix products, arithmetic and copies ran while one was open for 0% -> 0% of each run, Pallas kernels for 6% -> 10%
where the time goes in v8:
time: 30.6 us; the launch traced here: 30.3 us
  blocking collectives  13 us (42%)
  waiting for transfers between devices  6.95 us (23%)
  starting transfers between devices  4.82 us (16%)
  Pallas kernels  3.95 us (13%)
  local copies, waits for them, and re-layouts  1.38 us (5%)
    all_to_all x1, blocking collectives, on_device(): lax.all_to_all(out.reshape(groups * 2 * replicas, -1, width), ('hi', 'lo'...  13 us
    ppermute x8, waiting for transfers between devices, swap(): return lax.ppermute(value, ('hi', 'lo'), [(i, i ^ xor) for i in range(4)])  6.95 us
    ppermute x8, starting transfers between devices, swap(): return lax.ppermute(value, ('hi', 'lo'), [(i, i ^ xor) for i in range(4)])  4.82 us
    pallas_call x1, Pallas kernels, on_device(): local(attend_kernel, out_shape=(shape((half, local_width), BF16), shape((...  1.14 us
    pallas_call x1, Pallas kernels, on_device(): local(functools.partial(prepare_kernel, replicas, cached), out_shape=(sha...  1.08 us
    unnamed x30, local copies, waits for them, and re-layouts  0.74 us
    pallas_call x1, Pallas kernels, on_device(): local(outer_kernel, out_shape=shape((groups * 2, half, width), BF16), in_...  0.74 us
    convert_element_type x1, local copies, waits for them, and re-layouts, on_device(): jnp.sum(parts, axis=0).swapaxes(0, 1).reshape(rows, width).astype(BF16)  0.63 us
  transfers between devices with their start and end apart: 8, of which 3 were waited for; matrix products, arithmetic and copies ran while one was open for 0% of the time, Pallas kernels for 10%

profile of v8, /device:TPU:0, one launch (start us, length us, event | category | flops | bytes accessed | tf_op | source)
XLA Modules:
  0.0 30.3 jit_solution(4725365904963308094)
XLA Ops:
  0.0 3.0 %collective-permute-start.2 = (bf16[128,256]{1,0:T(8,128)(2,1)}, bf16[128,256]{1,0:T(8,128)(2,1)S(1)}, u32[]{:S(2)}, u32[]{:S(2)}) collective-permute-start(bf16[128,256]{1,0:T(8,128)(2,1)} %own_ref.3), channel_id=1, source_target_pairs={{0,2},{1,3},{2,0},{3,1},{4,6},{5,7},{6,4},{7,5},{8,10},{9,11},{10,... | collective-permute-start | bytes 196616 | tf_op jit(solution)/shard_map/ppermute | solution.py:223
  3.0 0.0 collective-permute-start.1
  3.0 0.0 copy-start.14
  3.0 0.7 %copy-done.11 = f32[32,4]{0,1:T(4,128)S(1)} copy-done((f32[32,4]{0,1:T(4,128)S(1)}, f32[32,4]{0,1:T(4,128)}, u32[]{:S(2)}) %copy-start.11) | copy-done | bytes 536
  3.7 0.0 copy-done.12
  3.7 0.0 copy-done.13
  3.7 0.0 copy-done.14
  3.7 0.0 copy-start.5
  3.7 0.0 copy-start.6
  3.7 0.0 copy-start.7
  3.7 0.0 copy-start.8
  3.7 1.1 %prepare.1 = (f32[2,256,128]{2,1,0:T(8,128)S(1)}, bf16[128,128]{1,0:T(8,128)(2,1)S(1)}) custom-call(f32[4,32]{1,0:T(4,128)S(1)} %bitcast.12, s32[1,2]{1,0:T(1,128)S(1)} %bitcast.13, s32[1,2]{1,0:T(1,128)S(1)} %bitcast.14, s32[1,128]{1,0:T(1,128)S(1)} %copy-done.14), custom_call_target="tpu_custom_call" | custom-call | flops 7000000000 | tf_op jit(solution)/shard_map/prepare/pallas_call | solution.py:256
  4.8 0.0 copy-start.9
  4.8 0.0 copy-done.2
  4.8 0.2 collective-permute-start
  5.0 0.0 copy-done.1
  5.0 0.4 %collective-permute-start.4 = (bf16[256,1024]{1,0:T(8,128)(2,1)S(1)}, bf16[256,1024]{1,0:T(8,128)(2,1)S(1)}, u32[]{:S(2)}, u32[]{:S(2)}) collective-permute-start(bf16[256,1024]{1,0:T(8,128)(2,1)S(1)} %copy-done.1), channel_id=1, source_target_pairs={{0,1},{1,0},{2,3},{3,2},{4,5},{5,4},{6,7},{7,6},{8,9},{9,8},{10,11... | collective-permute-start | bytes 1572872 | tf_op jit(solution)/shard_map/ppermute | solution.py:223
  5.4 0.0 collective-permute-done.2.across_ref
  5.4 1.9 %collective-permute-done.1.far_ref = bf16[128,256]{1,0:T(8,128)(2,1)S(1)} collective-permute-done((bf16[128,256]{1,0:T(8,128)(2,1)}, bf16[128,256]{1,0:T(8,128)(2,1)S(1)}, u32[]{:S(2)}, u32[]{:S(2)}) %collective-permute-start.1) | collective-permute-done | bytes 65568 | tf_op jit(solution)/shard_map/ppermute | solution.py:223
  7.3 0.0 collective-permute-done.near_ref
  7.3 0.0 copy-done.4
  7.3 0.0 copy-done.5
  7.3 0.0 copy-done.6
  7.3 0.0 copy-done.7
  7.3 0.0 copy-done.8
  7.3 0.0 copy-done.9
  7.4 1.1 %attend.1 = (bf16[64,256]{1,0:T(8,128)(2,1)S(1)}, bf16[128,256]{1,0:T(8,128)(2,1)S(1)}) custom-call(bf16[128,256]{1,0:T(8,128)(2,1)S(1)} %copy-done.2, bf16[128,256]{1,0:T(8,128)(2,1)S(1)} %collective-permute-done.near_ref, bf16[128,256]{1,0:T(8,128)(2,1)S(1)} %collective-permute-done.1.far_ref, bf16[128,256]{1,0:T(8,128)(2,1)S(1)} %collective-permute-done.2.across_ref, ...), custom_call_target="tpu_custom_call" | custom-call | flops 40000000000 | tf_op jit(solution)/shard_map/attend/pallas_call | solution.py:270
  8.5 0.0 collective-permute-start.3
  8.5 0.0 copy-start.3
  8.5 0.0 copy-start
  8.5 0.3 project.1.keep_ref
  8.8 0.9 %collective-permute-done.3.near_ref = bf16[64,256]{1,0:T(8,128)(2,1)S(1)} collective-permute-done((bf16[64,256]{1,0:T(8,128)(2,1)S(1)}, bf16[64,256]{1,0:T(8,128)(2,1)S(1)}, u32[]{:S(2)}, u32[]{:S(2)}) %collective-permute-start.3) | collective-permute-done | bytes 32800 | tf_op jit(solution)/shard_map/ppermute | solution.py:223
  9.7 0.0 collective-permute-done.4.near_out_ref
  9.7 0.2 pair.1.pair_ref
  9.9 0.0 copy-start.10
  9.9 0.7 %collective-permute-start.5 = (bf16[64,1024]{1,0:T(8,128)(2,1)S(1)}, bf16[64,1024]{1,0:T(8,128)(2,1)S(1)}, u32[]{:S(2)}, u32[]{:S(2)}) collective-permute-start(bf16[64,1024]{1,0:T(8,128)(2,1)S(1)} %pair.1.pair_ref), channel_id=1, source_target_pairs={{0,2},{1,3},{2,0},{3,1},{4,6},{5,7},{6,4},{7,5},{8,10},{9,11},{10,... | collective-permute-start | bytes 393224 | tf_op jit(solution)/shard_map/ppermute | solution.py:223
  10.6 0.2 stream.1.stream_ref
  10.8 0.0 copy-done.3
  10.8 0.1 collective-permute-start.6
  11.0 0.4 %collective-permute-start.7 = (bf16[512,1024]{1,0:T(8,128)(2,1)S(1)}, bf16[512,1024]{1,0:T(8,128)(2,1)S(1)}, u32[]{:S(2)}, u32[]{:S(2)}) collective-permute-start(bf16[512,1024]{1,0:T(8,128)(2,1)S(1)} %copy-done), channel_id=1, source_target_pairs={{0,1},{1,0},{2,3},{3,2},{4,5},{5,4},{6,7},{7,6},{8,9},{9,8},{10,11... | collective-permute-start | bytes 3145736 | tf_op jit(solution)/shard_map/ppermute | solution.py:223
  11.4 4.2 %collective-permute-done.5.other_ref = bf16[64,1024]{1,0:T(8,128)(2,1)S(1)} collective-permute-done((bf16[64,1024]{1,0:T(8,128)(2,1)S(1)}, bf16[64,1024]{1,0:T(8,128)(2,1)S(1)}, u32[]{:S(2)}, u32[]{:S(2)}) %collective-permute-start.5) | collective-permute-done | bytes 131104 | tf_op jit(solution)/shard_map/ppermute | solution.py:223
  15.6 0.0 copy-done.10
  15.6 0.3 %inner.1 = (f32[64,1024]{1,0:T(8,128)S(1)}, bf16[64,1024]{1,0:T(8,128)(2,1)S(1)}, f32[64,128]{1,0:T(8,128)S(1)}, bf16[64,512]{1,0:T(8,128)(2,1)S(1)}) custom-call(bf16[64,1024]{1,0:T(8,128)(2,1)S(1)} %pair.1.pair_ref, bf16[64,1024]{1,0:T(8,128)(2,1)S(1)} %collective-permute-done.5.other_ref, bf16[64,1024]{1,0:T(8,128)(2,1)S(1)} %stream.1.stream_ref, ...), custom_call_target="tpu_custom_call" | custom-call | flops 40000000000 | tf_op jit(solution)/shard_map/inner/pallas_call | solution.py:312
  15.9 0.0 collective-permute-done.6.near_inner_ref
  15.9 0.0 collective-permute-done.7.near_outer_ref
  15.9 0.7 %outer.1 = bf16[4,64,256]{2,1,0:T(8,128)(2,1)S(1)} custom-call(f32[64,1024]{1,0:T(8,128)S(1)} %get-tuple-element.27.mixed_ref, bf16[64,1024]{1,0:T(8,128)(2,1)S(1)} %get-tuple-element.28.input_ref, f32[64,128]{1,0:T(8,128)S(1)} %get-tuple-element.29.inverse_ref, bf16[64,512]{1,0:T(8,128)(2,1)S(1)} %get-tuple-element.30.own_hidden_ref, ...), custom_call_target="tpu_custom_call" | custom-call | tf_op jit(solution)/shard_map/outer/pallas_call | solution.py:325
  16.7 13.0 %all_to_all.5 = bf16[32,8,256]{2,1,0:T(8,128)(2,1)S(1)} all-to-all(bf16[32,8,256]{2,1,0:T(8,128)(2,1)S(1)} %bitcast.9), channel_id=1, replica_groups=mesh['rep'=8,'hi'=2,'lo'=2] {'hi','lo','rep'}, dimensions={0} | all-to-all | bytes 262144 | tf_op jit(solution)/shard_map/all_to_all | solution.py:336
  29.7 0.6 %copy.16 = bf16[8,2,8,256]{3,2,1,0:T(8,128)(2,1)} copy(bf16[8,2,8,256]{3,2,0,1:T(8,128)(2,1)S(1)} %bitcast.16) | data formatting | bytes 131072 | tf_op jit(solution)/shard_map/convert_element_type | solution.py:341
  (8 shorter events, 0.0 us)
Async XLA Ops:
  0.0 5.4 %collective-permute-start.2 = (bf16[128,256]{1,0:T(8,128)(2,1)}, bf16[128,256]{1,0:T(8,128)(2,1)S(1)}, u32[]{:S(2)}, u32[]{:S(2)}) collective-permute-start(bf16[128,256]{1,0:T(8,128)(2,1)} %own_ref.3), channel_id=1, source_target_pairs={{0,2},{1,3},{2,0},{3,1},{4,6},{5,7},{6,4},{7,5},{8,10},{9,11},{10,... | collective-permute-start | bytes 196616 | tf_op jit(solution)/shard_map/ppermute | solution.py:223
  3.0 4.3 %collective-permute-start.1 = (bf16[128,256]{1,0:T(8,128)(2,1)}, bf16[128,256]{1,0:T(8,128)(2,1)S(1)}, u32[]{:S(2)}, u32[]{:S(2)}) collective-permute-start(bf16[128,256]{1,0:T(8,128)(2,1)} %own_ref.3), channel_id=1, source_target_pairs={{0,3},{1,2},{2,1},{3,0},{4,7},{5,6},{6,5},{7,4},{8,11},{9,10},{10,... | collective-permute-start | bytes 196616 | tf_op jit(solution)/shard_map/ppermute | solution.py:223
  3.0 0.7 %copy-start.11 = (f32[32,4]{0,1:T(4,128)S(1)}, f32[32,4]{0,1:T(4,128)}, u32[]{:S(2)}) copy-start(f32[32,4]{0,1:T(4,128)} %param.24) | copy-start | bytes 1540
  3.0 0.7 %copy-start.12 = (s32[2,1]{0,1:T(1,128)S(1)}, s32[2,1]{0,1:T(1,128)}, u32[]{:S(2)}) copy-start(s32[2,1]{0,1:T(1,128)} %param.27) | copy-start | bytes 28
  3.0 0.7 %copy-start.13 = (s32[2,1]{0,1:T(1,128)S(1)}, s32[2,1]{0,1:T(1,128)}, u32[]{:S(2)}) copy-start(s32[2,1]{0,1:T(1,128)} %param.28) | copy-start | bytes 28
  3.0 0.7 %copy-start.14 = (s32[1,128]{1,0:T(1,128)S(1)}, s32[1,128]{1,0:T(1,128)}, u32[]{:S(2)}) copy-start(s32[1,128]{1,0:T(1,128)} %deal_ref.1) | copy-start | bytes 1540
  3.7 1.2 %copy-start.2 = (bf16[128,256]{1,0:T(8,128)(2,1)S(1)}, bf16[128,256]{1,0:T(8,128)(2,1)}, u32[]{:S(2)}) copy-start(bf16[128,256]{1,0:T(8,128)(2,1)} %own_ref.3) | copy-start | bytes 196612
  3.7 1.4 %copy-start.1 = (bf16[256,1024]{1,0:T(8,128)(2,1)S(1)}, bf16[256,1024]{1,0:T(8,128)(2,1)}, u32[]{:S(2)}) copy-start(bf16[256,1024]{1,0:T(8,128)(2,1)} %w_out_ref.1) | copy-start | bytes 1572868
  3.7 3.6 %copy-start.4 = (bf16[1024,256]{1,0:T(8,128)(2,1)S(1)}, bf16[1024,256]{1,0:T(8,128)(2,1)}, u32[]{:S(2)}) copy-start(bf16[1024,256]{1,0:T(8,128)(2,1)} %w_query_ref.1) | copy-start | bytes 1572868
  3.7 3.6 %copy-start.5 = (bf16[1024,256]{1,0:T(8,128)(2,1)S(1)}, bf16[1024,256]{1,0:T(8,128)(2,1)}, u32[]{:S(2)}) copy-start(bf16[1024,256]{1,0:T(8,128)(2,1)} %w_key_ref.1) | copy-start | bytes 1572868
  3.7 3.6 %copy-start.6 = (bf16[1024,256]{1,0:T(8,128)(2,1)S(1)}, bf16[1024,256]{1,0:T(8,128)(2,1)}, u32[]{:S(2)}) copy-start(bf16[1024,256]{1,0:T(8,128)(2,1)} %w_value_ref.1) | copy-start | bytes 1572868
  3.7 3.6 %copy-start.7 = (bf16[2,64,256]{2,1,0:T(8,128)(2,1)S(1)}, bf16[2,64,256]{2,1,0:T(8,128)(2,1)}, u32[]{:S(2)}) copy-start(bf16[2,64,256]{2,1,0:T(8,128)(2,1)} %cache_keys_ref.1) | copy-start | bytes 196612
  3.7 3.6 %copy-start.8 = (bf16[2,64,256]{2,1,0:T(8,128)(2,1)S(1)}, bf16[2,64,256]{2,1,0:T(8,128)(2,1)}, u32[]{:S(2)}) copy-start(bf16[2,64,256]{2,1,0:T(8,128)(2,1)} %cache_values_ref.1) | copy-start | bytes 196612
  4.8 2.5 %copy-start.9 = (f32[1024]{0:T(1024)S(1)}, f32[1024]{0:T(1024)}, u32[]{:S(2)}) copy-start(f32[1024]{0:T(1024)} %param.16) | copy-start | bytes 12292
  4.8 2.5 %collective-permute-start = (bf16[128,256]{1,0:T(8,128)(2,1)S(1)}, bf16[128,256]{1,0:T(8,128)(2,1)S(1)}, u32[]{:S(2)}, u32[]{:S(2)}) collective-permute-start(bf16[128,256]{1,0:T(8,128)(2,1)S(1)} %copy-done.2), channel_id=1, source_target_pairs={{0,1},{1,0},{2,3},{3,2},{4,5},{5,4},{6,7},{7,6},{8,9},{9,8},{10,11... | collective-permute-start | bytes 196616 | tf_op jit(solution)/shard_map/ppermute | solution.py:223
  5.0 4.7 %collective-permute-start.4 = (bf16[256,1024]{1,0:T(8,128)(2,1)S(1)}, bf16[256,1024]{1,0:T(8,128)(2,1)S(1)}, u32[]{:S(2)}, u32[]{:S(2)}) collective-permute-start(bf16[256,1024]{1,0:T(8,128)(2,1)S(1)} %copy-done.1), channel_id=1, source_target_pairs={{0,1},{1,0},{2,3},{3,2},{4,5},{5,4},{6,7},{7,6},{8,9},{9,8},{10,11... | collective-permute-start | bytes 1572872 | tf_op jit(solution)/shard_map/ppermute | solution.py:223
  8.5 1.2 %collective-permute-start.3 = (bf16[64,256]{1,0:T(8,128)(2,1)S(1)}, bf16[64,256]{1,0:T(8,128)(2,1)S(1)}, u32[]{:S(2)}, u32[]{:S(2)}) collective-permute-start(bf16[64,256]{1,0:T(8,128)(2,1)S(1)} %get-tuple-element.25), channel_id=1, source_target_pairs={{0,1},{1,0},{2,3},{3,2},{4,5},{5,4},{6,7},{7,6},{8,9},{9,8},{10,11... | collective-permute-start | bytes 98312 | tf_op jit(solution)/shard_map/ppermute | solution.py:223
  8.5 2.3 %copy-start.3 = (bf16[1024,512]{1,0:T(8,128)(2,1)S(1)}, bf16[1024,512]{1,0:T(8,128)(2,1)}, u32[]{:S(2)}) copy-start(bf16[1024,512]{1,0:T(8,128)(2,1)} %w_inner_ref.1) | copy-start | bytes 3145732
  8.5 2.5 %copy-start = (bf16[512,1024]{1,0:T(8,128)(2,1)S(1)}, bf16[512,1024]{1,0:T(8,128)(2,1)}, u32[]{:S(2)}) copy-start(bf16[512,1024]{1,0:T(8,128)(2,1)} %own_outer_ref.1) | copy-start | bytes 3145732
  9.9 5.6 %copy-start.10 = (f32[1024]{0:T(1024)S(1)}, f32[1024]{0:T(1024)}, u32[]{:S(2)}) copy-start(f32[1024]{0:T(1024)} %param.17) | copy-start | bytes 12292
  9.9 5.6 %collective-permute-start.5 = (bf16[64,1024]{1,0:T(8,128)(2,1)S(1)}, bf16[64,1024]{1,0:T(8,128)(2,1)S(1)}, u32[]{:S(2)}, u32[]{:S(2)}) collective-permute-start(bf16[64,1024]{1,0:T(8,128)(2,1)S(1)} %pair.1.pair_ref), channel_id=1, source_target_pairs={{0,2},{1,3},{2,0},{3,1},{4,6},{5,7},{6,4},{7,5},{8,10},{9,11},{10,... | collective-permute-start | bytes 393224 | tf_op jit(solution)/shard_map/ppermute | solution.py:223
  10.8 5.1 %collective-permute-start.6 = (bf16[1024,512]{1,0:T(8,128)(2,1)S(1)}, bf16[1024,512]{1,0:T(8,128)(2,1)S(1)}, u32[]{:S(2)}, u32[]{:S(2)}) collective-permute-start(bf16[1024,512]{1,0:T(8,128)(2,1)S(1)} %copy-done.3), channel_id=1, source_target_pairs={{0,1},{1,0},{2,3},{3,2},{4,5},{5,4},{6,7},{7,6},{8,9},{9,8},{10,11... | collective-permute-start | bytes 3145736 | tf_op jit(solution)/shard_map/ppermute | solution.py:223
  11.0 4.9 %collective-permute-start.7 = (bf16[512,1024]{1,0:T(8,128)(2,1)S(1)}, bf16[512,1024]{1,0:T(8,128)(2,1)S(1)}, u32[]{:S(2)}, u32[]{:S(2)}) collective-permute-start(bf16[512,1024]{1,0:T(8,128)(2,1)S(1)} %copy-done), channel_id=1, source_target_pairs={{0,1},{1,0},{2,3},{3,2},{4,5},{5,4},{6,7},{7,6},{8,9},{9,8},{10,11... | collective-permute-start | bytes 3145736 | tf_op jit(solution)/shard_map/ppermute | solution.py:223

commit v9 on v8

--- a/solution.py
+++ b/solution.py
@@ -111,8 +111,8 @@
 
 def attend_kernel(
     own_ref,
+    far_ref,
     near_ref,
-    far_ref,
     across_ref,
     gain_ref,
     w_query_ref,
@@ -164,11 +164,12 @@
     keep_ref[...] = dot(dealt, w_out_ref[...])
 
 
-def pair_kernel(keep_ref, near_ref, near_out_ref, pair_ref):
+def pair_kernel(keep_ref, near_ref, near_out_ref, near_inner_ref, pair_ref):
+    del near_inner_ref
     pair_ref[...] = (keep_ref[...] + dot(near_ref[...], near_out_ref[...])).astype(BF16)
 
 
-def stream_kernel(own_ref, near_ref, far_ref, across_ref, picked_ref, stream_ref):
+def stream_kernel(own_ref, far_ref, near_ref, across_ref, picked_ref, stream_ref):
     index, _ = place()
     width = own_ref.shape[1]
     picked = picked_ref[: stream_ref.shape[0]]
@@ -264,8 +265,7 @@
         cost_estimate=pl.CostEstimate(flops=PREPARE_FLOPS, bytes_accessed=0, transcendentals=0),
         name="prepare",
     )(bias_table.T, new_counts.T, cached_lengths.T, deal)
-    late, bias, picked = lax.optimization_barrier((tokens, bias, picked))
-    blocks = (tokens, swap(late, 1), far, across)
+    blocks = (tokens, far, swap(tokens, 1), across)
     half = rows // 2
     send, context = local(
         attend_kernel,
@@ -300,14 +300,15 @@
         out_specs=VMEM,
         name="stream",
     )(*blocks, picked)
+    near_inner = swap(w_inner, 1)
     pair = local(
         pair_kernel,
         out_shape=shape((half, model_width), BF16),
-        in_specs=[VMEM] * 3,
+        in_specs=[VMEM] * 4,
         out_specs=VMEM,
         name="pair",
-    )(keep, swap(send, 1), swap(w_out, 1))
-    late_inner, late_outer, pair = lax.optimization_barrier((w_inner, w_outer, pair))
+    )(keep, swap(send, 1), swap(w_out, 1), near_inner)
+    late_outer, pair = lax.optimization_barrier((w_outer, pair))
     ff_width = w_inner.shape[1]
     mixed, ffn_input, inverse, hidden = local(
         inner_kernel,
@@ -328,7 +329,7 @@
         in_specs=[VMEM] * 7,
         out_specs=VMEM,
         name="outer",
-    )(mixed, ffn_input, inverse, hidden, swap(late_inner, 1), w_outer, swap(late_outer, 1))
+    )(mixed, ffn_input, inverse, hidden, near_inner, w_outer, swap(late_outer, 1))
     share = rows // replicas
     if not halved(share):
         padded = jnp.zeros((groups * 2, rows, width), BF16)

time: 30.6 us -> 30.5 us (level)
  waiting for transfers between devices: 6.95 us -> 6.34 us
  starting transfers between devices: 4.82 us -> 5.37 us
    ppermute x8, waiting for transfers between devices: 6.95 us -> 6.34 us  [swap(): return lax.ppermute(value, ('hi', 'lo'), [(i, i ^ xor) for i in range(4)])]
    ppermute x8, starting transfers between devices: 4.82 us -> 5.37 us  [swap(): return lax.ppermute(value, ('hi', 'lo'), [(i, i ^ xor) for i in range(4)])]
  transfers between devices with their start and end apart: 8 -> 8, of which waited for: 3 -> 4; matrix products, arithmetic and copies ran while one was open for 0% -> 0% of each run, Pallas kernels for 10% -> 10%
where the time goes in v9:
time: 30.5 us; the launch traced here: 30.3 us
  blocking collectives  13.1 us (43%)
  waiting for transfers between devices  6.34 us (21%)
  starting transfers between devices  5.37 us (18%)
  Pallas kernels  3.95 us (13%)
  local copies, waits for them, and re-layouts  1.39 us (5%)
    all_to_all x1, blocking collectives, on_device(): lax.all_to_all(out.reshape(groups * 2 * replicas, -1, width), ('hi', 'lo'...  13.1 us
    ppermute x8, waiting for transfers between devices, swap(): return lax.ppermute(value, ('hi', 'lo'), [(i, i ^ xor) for i in range(4)])  6.34 us
    ppermute x8, starting transfers between devices, swap(): return lax.ppermute(value, ('hi', 'lo'), [(i, i ^ xor) for i in range(4)])  5.37 us
    pallas_call x1, Pallas kernels, on_device(): local(attend_kernel, out_shape=(shape((half, local_width), BF16), shape((...  1.14 us
    pallas_call x1, Pallas kernels, on_device(): local(functools.partial(prepare_kernel, replicas, cached), out_shape=(sha...  1.08 us
    unnamed x30, local copies, waits for them, and re-layouts  0.75 us
    pallas_call x1, Pallas kernels, on_device(): local(outer_kernel, out_shape=shape((groups * 2, half, width), BF16), in_...  0.74 us
    convert_element_type x1, local copies, waits for them, and re-layouts, on_device(): jnp.sum(parts, axis=0).swapaxes(0, 1).reshape(rows, width).astype(BF16)  0.63 us
  transfers between devices with their start and end apart: 8, of which 4 were waited for; matrix products, arithmetic and copies ran while one was open for 0% of the time, Pallas kernels for 10%

profile of v9, /device:TPU:0, one launch (start us, length us, event | category | flops | bytes accessed | tf_op | source)
XLA Modules:
  0.0 30.3 jit_solution(14392913559066519201)
XLA Ops:
  0.0 3.0 %collective-permute-start.2 = (bf16[128,256]{1,0:T(8,128)(2,1)}, bf16[128,256]{1,0:T(8,128)(2,1)S(1)}, u32[]{:S(2)}, u32[]{:S(2)}) collective-permute-start(bf16[128,256]{1,0:T(8,128)(2,1)} %own_ref.3), channel_id=1, source_target_pairs={{0,2},{1,3},{2,0},{3,1},{4,6},{5,7},{6,4},{7,5},{8,10},{9,11},{10,... | collective-permute-start | bytes 196616 | tf_op jit(solution)/shard_map/ppermute | solution.py:224
  3.0 0.0 collective-permute-start.1
  3.0 0.1 collective-permute-start
  3.1 0.4 %collective-permute-start.4 = (bf16[256,1024]{1,0:T(8,128)(2,1)}, bf16[256,1024]{1,0:T(8,128)(2,1)S(1)}, u32[]{:S(2)}, u32[]{:S(2)}) collective-permute-start(bf16[256,1024]{1,0:T(8,128)(2,1)} %w_out_ref.1), channel_id=1, source_target_pairs={{0,1},{1,0},{2,3},{3,2},{4,5},{5,4},{6,7},{7,6},{8,9},{9,8},{10,11... | collective-permute-start | bytes 1572872 | tf_op jit(solution)/shard_map/ppermute | solution.py:224
  3.5 0.1 collective-permute-start.5
  3.6 0.7 %copy-done.11 = f32[32,4]{0,1:T(4,128)S(1)} copy-done((f32[32,4]{0,1:T(4,128)S(1)}, f32[32,4]{0,1:T(4,128)}, u32[]{:S(2)}) %copy-start.11) | copy-done | bytes 536
  4.3 0.0 copy-done.12
  4.3 0.0 copy-done.13
  4.3 0.0 copy-done.14
  4.3 0.0 copy-start.6
  4.3 0.0 copy-start.7
  4.3 0.0 copy-start.8
  4.3 1.1 %prepare.1 = (f32[2,256,128]{2,1,0:T(8,128)S(1)}, bf16[128,128]{1,0:T(8,128)(2,1)S(1)}) custom-call(f32[4,32]{1,0:T(4,128)S(1)} %bitcast.12, s32[1,2]{1,0:T(1,128)S(1)} %bitcast.13, s32[1,2]{1,0:T(1,128)S(1)} %bitcast.14, s32[1,128]{1,0:T(1,128)S(1)} %copy-done.14), custom_call_target="tpu_custom_call" | custom-call | flops 7000000000 | tf_op jit(solution)/shard_map/prepare/pallas_call | solution.py:257
  5.4 0.0 copy-start.9
  5.4 0.2 collective-permute-done.2.across_ref
  5.6 0.0 collective-permute-done.1.near_ref
  5.6 1.3 %collective-permute-done.far_ref = bf16[128,256]{1,0:T(8,128)(2,1)S(1)} collective-permute-done((bf16[128,256]{1,0:T(8,128)(2,1)}, bf16[128,256]{1,0:T(8,128)(2,1)S(1)}, u32[]{:S(2)}, u32[]{:S(2)}) %collective-permute-start) | collective-permute-done | bytes 65568 | tf_op jit(solution)/shard_map/ppermute | solution.py:224
  6.9 0.0 copy-done.2
  6.9 0.0 copy-done.4
  6.9 0.0 copy-done.5
  6.9 0.0 copy-done.6
  6.9 0.0 copy-done.7
  7.0 0.0 copy-done.8
  7.0 0.0 copy-done.9
  7.0 0.0 copy-start.1
  7.0 1.1 %attend.1 = (bf16[64,256]{1,0:T(8,128)(2,1)S(1)}, bf16[128,256]{1,0:T(8,128)(2,1)S(1)}) custom-call(bf16[128,256]{1,0:T(8,128)(2,1)S(1)} %copy-done.2, bf16[128,256]{1,0:T(8,128)(2,1)S(1)} %collective-permute-done.far_ref, bf16[128,256]{1,0:T(8,128)(2,1)S(1)} %collective-permute-done.1.near_ref, bf16[128,256]{1,0:T(8,128)(2,1)S(1)} %collective-permute-done.2.across_ref, ...), custom_call_target="tpu_custom_call" | custom-call | flops 40000000000 | tf_op jit(solution)/shard_map/attend/pallas_call | solution.py:270
  8.1 0.5 %collective-permute-start.3 = (bf16[64,256]{1,0:T(8,128)(2,1)S(1)}, bf16[64,256]{1,0:T(8,128)(2,1)S(1)}, u32[]{:S(2)}, u32[]{:S(2)}) collective-permute-start(bf16[64,256]{1,0:T(8,128)(2,1)S(1)} %get-tuple-element.18), channel_id=1, source_target_pairs={{0,1},{1,0},{2,3},{3,2},{4,5},{5,4},{6,7},{7,6},{8,9},{9,8},{10,11... | collective-permute-start | bytes 98312 | tf_op jit(solution)/shard_map/ppermute | solution.py:224
  8.6 0.0 copy-done.1
  8.6 0.3 project.1.keep_ref
  8.9 0.0 copy-start
  8.9 0.0 copy-start.3
  8.9 0.5 %collective-permute-done.3.near_ref = bf16[64,256]{1,0:T(8,128)(2,1)S(1)} collective-permute-done((bf16[64,256]{1,0:T(8,128)(2,1)S(1)}, bf16[64,256]{1,0:T(8,128)(2,1)S(1)}, u32[]{:S(2)}, u32[]{:S(2)}) %collective-permute-start.3) | collective-permute-done | bytes 32800 | tf_op jit(solution)/shard_map/ppermute | solution.py:224
  9.5 0.0 collective-permute-done.4.near_out_ref
  9.5 0.0 collective-permute-done.5.near_inner_ref
  9.5 0.2 pair.1.pair_ref
  9.7 0.0 copy-start.10
  9.7 1.2 %collective-permute-start.6 = (bf16[64,1024]{1,0:T(8,128)(2,1)S(1)}, bf16[64,1024]{1,0:T(8,128)(2,1)S(1)}, u32[]{:S(2)}, u32[]{:S(2)}) collective-permute-start(bf16[64,1024]{1,0:T(8,128)(2,1)S(1)} %pair.1.pair_ref), channel_id=1, source_target_pairs={{0,2},{1,3},{2,0},{3,1},{4,6},{5,7},{6,4},{7,5},{8,10},{9,11},{10,... | collective-permute-start | bytes 393224 | tf_op jit(solution)/shard_map/ppermute | solution.py:224
  10.9 0.2 stream.1.stream_ref
  11.1 0.0 copy-done
  11.1 0.1 collective-permute-start.7
  11.2 4.3 %collective-permute-done.6.other_ref = bf16[64,1024]{1,0:T(8,128)(2,1)S(1)} collective-permute-done((bf16[64,1024]{1,0:T(8,128)(2,1)S(1)}, bf16[64,1024]{1,0:T(8,128)(2,1)S(1)}, u32[]{:S(2)}, u32[]{:S(2)}) %collective-permute-start.6) | collective-permute-done | bytes 131104 | tf_op jit(solution)/shard_map/ppermute | solution.py:224
  15.5 0.0 copy-done.3
  15.5 0.0 copy-done.10
  15.5 0.3 %inner.1 = (f32[64,1024]{1,0:T(8,128)S(1)}, bf16[64,1024]{1,0:T(8,128)(2,1)S(1)}, f32[64,128]{1,0:T(8,128)S(1)}, bf16[64,512]{1,0:T(8,128)(2,1)S(1)}) custom-call(bf16[64,1024]{1,0:T(8,128)(2,1)S(1)} %pair.1.pair_ref, bf16[64,1024]{1,0:T(8,128)(2,1)S(1)} %collective-permute-done.6.other_ref, bf16[64,1024]{1,0:T(8,128)(2,1)S(1)} %stream.1.stream_ref, ...), custom_call_target="tpu_custom_call" | custom-call | flops 40000000000 | tf_op jit(solution)/shard_map/inner/pallas_call | solution.py:313
  15.8 0.0 collective-permute-done.7.near_outer_ref
  15.8 0.7 %outer.1 = bf16[4,64,256]{2,1,0:T(8,128)(2,1)S(1)} custom-call(f32[64,1024]{1,0:T(8,128)S(1)} %get-tuple-element.20.mixed_ref, bf16[64,1024]{1,0:T(8,128)(2,1)S(1)} %get-tuple-element.21.input_ref, f32[64,128]{1,0:T(8,128)S(1)} %get-tuple-element.22.inverse_ref, bf16[64,512]{1,0:T(8,128)(2,1)S(1)} %get-tuple-element.23.own_hidden_ref, ...), custom_call_target="tpu_custom_call" | custom-call | tf_op jit(solution)/shard_map/outer/pallas_call | solution.py:326
  16.6 13.1 %all_to_all.5 = bf16[32,8,256]{2,1,0:T(8,128)(2,1)S(1)} all-to-all(bf16[32,8,256]{2,1,0:T(8,128)(2,1)S(1)} %bitcast.9), channel_id=1, replica_groups=mesh['rep'=8,'hi'=2,'lo'=2] {'hi','lo','rep'}, dimensions={0} | all-to-all | bytes 262144 | tf_op jit(solution)/shard_map/all_to_all | solution.py:337
  29.7 0.6 %copy.16 = bf16[8,2,8,256]{3,2,1,0:T(8,128)(2,1)} copy(bf16[8,2,8,256]{3,2,0,1:T(8,128)(2,1)S(1)} %bitcast.16) | data formatting | bytes 131072 | tf_op jit(solution)/shard_map/convert_element_type | solution.py:342
  (8 shorter events, 0.0 us)
Async XLA Ops:
  0.0 5.6 %collective-permute-start.2 = (bf16[128,256]{1,0:T(8,128)(2,1)}, bf16[128,256]{1,0:T(8,128)(2,1)S(1)}, u32[]{:S(2)}, u32[]{:S(2)}) collective-permute-start(bf16[128,256]{1,0:T(8,128)(2,1)} %own_ref.3), channel_id=1, source_target_pairs={{0,2},{1,3},{2,0},{3,1},{4,6},{5,7},{6,4},{7,5},{8,10},{9,11},{10,... | collective-permute-start | bytes 196616 | tf_op jit(solution)/shard_map/ppermute | solution.py:224
  3.0 2.6 %collective-permute-start.1 = (bf16[128,256]{1,0:T(8,128)(2,1)}, bf16[128,256]{1,0:T(8,128)(2,1)S(1)}, u32[]{:S(2)}, u32[]{:S(2)}) collective-permute-start(bf16[128,256]{1,0:T(8,128)(2,1)} %own_ref.3), channel_id=1, source_target_pairs={{0,1},{1,0},{2,3},{3,2},{4,5},{5,4},{6,7},{7,6},{8,9},{9,8},{10,11... | collective-permute-start | bytes 196616 | tf_op jit(solution)/shard_map/ppermute | solution.py:224
  3.0 4.0 %collective-permute-start = (bf16[128,256]{1,0:T(8,128)(2,1)}, bf16[128,256]{1,0:T(8,128)(2,1)S(1)}, u32[]{:S(2)}, u32[]{:S(2)}) collective-permute-start(bf16[128,256]{1,0:T(8,128)(2,1)} %own_ref.3), channel_id=1, source_target_pairs={{0,3},{1,2},{2,1},{3,0},{4,7},{5,6},{6,5},{7,4},{8,11},{9,10},{10,... | collective-permute-start | bytes 196616 | tf_op jit(solution)/shard_map/ppermute | solution.py:224
  3.1 6.4 %collective-permute-start.4 = (bf16[256,1024]{1,0:T(8,128)(2,1)}, bf16[256,1024]{1,0:T(8,128)(2,1)S(1)}, u32[]{:S(2)}, u32[]{:S(2)}) collective-permute-start(bf16[256,1024]{1,0:T(8,128)(2,1)} %w_out_ref.1), channel_id=1, source_target_pairs={{0,1},{1,0},{2,3},{3,2},{4,5},{5,4},{6,7},{7,6},{8,9},{9,8},{10,11... | collective-permute-start | bytes 1572872 | tf_op jit(solution)/shard_map/ppermute | solution.py:224
  3.5 6.0 %collective-permute-start.5 = (bf16[1024,512]{1,0:T(8,128)(2,1)}, bf16[1024,512]{1,0:T(8,128)(2,1)S(1)}, u32[]{:S(2)}, u32[]{:S(2)}) collective-permute-start(bf16[1024,512]{1,0:T(8,128)(2,1)} %w_inner_ref.1), channel_id=1, source_target_pairs={{0,1},{1,0},{2,3},{3,2},{4,5},{5,4},{6,7},{7,6},{8,9},{9,8},{10,11... | collective-permute-start | bytes 3145736 | tf_op jit(solution)/shard_map/ppermute | solution.py:224
  3.6 0.7 %copy-start.11 = (f32[32,4]{0,1:T(4,128)S(1)}, f32[32,4]{0,1:T(4,128)}, u32[]{:S(2)}) copy-start(f32[32,4]{0,1:T(4,128)} %param.24) | copy-start | bytes 1540
  3.6 0.7 %copy-start.12 = (s32[2,1]{0,1:T(1,128)S(1)}, s32[2,1]{0,1:T(1,128)}, u32[]{:S(2)}) copy-start(s32[2,1]{0,1:T(1,128)} %param.27) | copy-start | bytes 28
  3.6 0.7 %copy-start.13 = (s32[2,1]{0,1:T(1,128)S(1)}, s32[2,1]{0,1:T(1,128)}, u32[]{:S(2)}) copy-start(s32[2,1]{0,1:T(1,128)} %param.28) | copy-start | bytes 28
  3.6 0.7 %copy-start.14 = (s32[1,128]{1,0:T(1,128)S(1)}, s32[1,128]{1,0:T(1,128)}, u32[]{:S(2)}) copy-start(s32[1,128]{1,0:T(1,128)} %deal_ref.1) | copy-start | bytes 1540
  4.3 2.6 %copy-start.2 = (bf16[128,256]{1,0:T(8,128)(2,1)S(1)}, bf16[128,256]{1,0:T(8,128)(2,1)}, u32[]{:S(2)}) copy-start(bf16[128,256]{1,0:T(8,128)(2,1)} %own_ref.3) | copy-start | bytes 196612
  4.3 2.6 %copy-start.4 = (bf16[1024,256]{1,0:T(8,128)(2,1)S(1)}, bf16[1024,256]{1,0:T(8,128)(2,1)}, u32[]{:S(2)}) copy-start(bf16[1024,256]{1,0:T(8,128)(2,1)} %w_query_ref.1) | copy-start | bytes 1572868
  4.3 2.6 %copy-start.5 = (bf16[1024,256]{1,0:T(8,128)(2,1)S(1)}, bf16[1024,256]{1,0:T(8,128)(2,1)}, u32[]{:S(2)}) copy-start(bf16[1024,256]{1,0:T(8,128)(2,1)} %w_key_ref.1) | copy-start | bytes 1572868
  4.3 2.6 %copy-start.6 = (bf16[1024,256]{1,0:T(8,128)(2,1)S(1)}, bf16[1024,256]{1,0:T(8,128)(2,1)}, u32[]{:S(2)}) copy-start(bf16[1024,256]{1,0:T(8,128)(2,1)} %w_value_ref.1) | copy-start | bytes 1572868
  4.3 2.6 %copy-start.7 = (bf16[2,64,256]{2,1,0:T(8,128)(2,1)S(1)}, bf16[2,64,256]{2,1,0:T(8,128)(2,1)}, u32[]{:S(2)}) copy-start(bf16[2,64,256]{2,1,0:T(8,128)(2,1)} %cache_keys_ref.1) | copy-start | bytes 196612
  4.3 2.6 %copy-start.8 = (bf16[2,64,256]{2,1,0:T(8,128)(2,1)S(1)}, bf16[2,64,256]{2,1,0:T(8,128)(2,1)}, u32[]{:S(2)}) copy-start(bf16[2,64,256]{2,1,0:T(8,128)(2,1)} %cache_values_ref.1) | copy-start | bytes 196612
  5.4 1.5 %copy-start.9 = (f32[1024]{0:T(1024)S(1)}, f32[1024]{0:T(1024)}, u32[]{:S(2)}) copy-start(f32[1024]{0:T(1024)} %param.16) | copy-start | bytes 12292
  7.0 1.6 %copy-start.1 = (bf16[256,1024]{1,0:T(8,128)(2,1)S(1)}, bf16[256,1024]{1,0:T(8,128)(2,1)}, u32[]{:S(2)}) copy-start(bf16[256,1024]{1,0:T(8,128)(2,1)} %w_out_ref.1) | copy-start | bytes 1572868
  8.1 1.3 %collective-permute-start.3 = (bf16[64,256]{1,0:T(8,128)(2,1)S(1)}, bf16[64,256]{1,0:T(8,128)(2,1)S(1)}, u32[]{:S(2)}, u32[]{:S(2)}) collective-permute-start(bf16[64,256]{1,0:T(8,128)(2,1)S(1)} %get-tuple-element.18), channel_id=1, source_target_pairs={{0,1},{1,0},{2,3},{3,2},{4,5},{5,4},{6,7},{7,6},{8,9},{9,8},{10,11... | collective-permute-start | bytes 98312 | tf_op jit(solution)/shard_map/ppermute | solution.py:224
  8.9 2.1 %copy-start = (bf16[512,1024]{1,0:T(8,128)(2,1)S(1)}, bf16[512,1024]{1,0:T(8,128)(2,1)}, u32[]{:S(2)}) copy-start(bf16[512,1024]{1,0:T(8,128)(2,1)} %own_outer_ref.1) | copy-start | bytes 3145732
  8.9 6.6 %copy-start.3 = (bf16[1024,512]{1,0:T(8,128)(2,1)S(1)}, bf16[1024,512]{1,0:T(8,128)(2,1)}, u32[]{:S(2)}) copy-start(bf16[1024,512]{1,0:T(8,128)(2,1)} %w_inner_ref.1) | copy-start | bytes 3145732
  9.7 5.8 %copy-start.10 = (f32[1024]{0:T(1024)S(1)}, f32[1024]{0:T(1024)}, u32[]{:S(2)}) copy-start(f32[1024]{0:T(1024)} %param.17) | copy-start | bytes 12292
  9.7 5.8 %collective-permute-start.6 = (bf16[64,1024]{1,0:T(8,128)(2,1)S(1)}, bf16[64,1024]{1,0:T(8,128)(2,1)S(1)}, u32[]{:S(2)}, u32[]{:S(2)}) collective-permute-start(bf16[64,1024]{1,0:T(8,128)(2,1)S(1)} %pair.1.pair_ref), channel_id=1, source_target_pairs={{0,2},{1,3},{2,0},{3,1},{4,6},{5,7},{6,4},{7,5},{8,10},{9,11},{10,... | collective-permute-start | bytes 393224 | tf_op jit(solution)/shard_map/ppermute | solution.py:224
  11.1 4.8 %collective-permute-start.7 = (bf16[512,1024]{1,0:T(8,128)(2,1)S(1)}, bf16[512,1024]{1,0:T(8,128)(2,1)S(1)}, u32[]{:S(2)}, u32[]{:S(2)}) collective-permute-start(bf16[512,1024]{1,0:T(8,128)(2,1)S(1)} %copy-done), channel_id=1, source_target_pairs={{0,1},{1,0},{2,3},{3,2},{4,5},{5,4},{6,7},{7,6},{8,9},{9,8},{10,11... | collective-permute-start | bytes 3145736 | tf_op jit(solution)/shard_map/ppermute | solution.py:224

commit v10 on v9

--- a/solution.py
+++ b/solution.py
@@ -26,6 +26,10 @@
 def place():
     upper, lower = lax.axis_index("hi"), lax.axis_index("lo")
     return upper * 2 + lower, lower
+
+
+def straight(replicas, share):
+    return replicas * 3 // 4 if halved(share) and replicas % 4 == 0 else replicas
 
 
 def halved(share):
@@ -64,6 +68,8 @@
     row = lax.broadcasted_iota(jnp.int32, (rows, rows), 0)
     part = jnp.where(row < half, side, 1 - side)
     row = jnp.where(row < half, row, row - half)
+    crossed = row >= jnp.where(lax.axis_index("hi") == 0, half, straight(replicas, share) * half // replicas)
+    part = jnp.where(crossed, 1 - part, part)
     if halved(share):
         row = lax.div(row, share // 2) * share + part * (share // 2) + lax.rem(row, share // 2)
     else:
@@ -164,9 +170,13 @@
     keep_ref[...] = dot(dealt, w_out_ref[...])
 
 
-def pair_kernel(keep_ref, near_ref, near_out_ref, near_inner_ref, pair_ref):
+def pair_kernel(keep_ref, near_ref, near_out_ref, near_inner_ref, *pair_refs):
     del near_inner_ref
-    pair_ref[...] = (keep_ref[...] + dot(near_ref[...], near_out_ref[...])).astype(BF16)
+    pair = (keep_ref[...] + dot(near_ref[...], near_out_ref[...])).astype(BF16)
+    start = 0
+    for ref in pair_refs:
+        ref[...] = pair[start : start + ref.shape[0]]
+        start += ref.shape[0]
 
 
 def stream_kernel(own_ref, far_ref, near_ref, across_ref, picked_ref, stream_ref):
@@ -177,18 +187,12 @@
         stream_ref[:, columns_of(index ^ xor, width)] = dot(picked, ref[...]).astype(BF16)
 
 
-def inner_kernel(
-    pair_ref,
-    other_ref,
-    stream_ref,
-    gain_ref,
-    w_inner_ref,
-    mixed_ref,
-    input_ref,
-    inverse_ref,
-    hidden_ref,
-):
-    mixed = pair_ref[...].astype(F32) + other_ref[...].astype(F32) + stream_ref[...].astype(F32)
+def inner_kernel(stream_ref, gain_ref, w_inner_ref, *refs):
+    *sum_refs, mixed_ref, input_ref, inverse_ref, hidden_ref = refs
+    pieces = len(sum_refs) // 2
+    pair = jnp.concatenate([ref[...].astype(F32) for ref in sum_refs[:pieces]], axis=0)
+    other = jnp.concatenate([ref[...].astype(F32) for ref in sum_refs[pieces:]], axis=0)
+    mixed = pair + other + stream_ref[...].astype(F32)
     mixed_ref[...] = mixed
     square = jnp.sum(mixed * mixed, axis=1, keepdims=True)
     inverse = lax.rsqrt(square / mixed.shape[1] + EPSILON)
@@ -218,6 +222,16 @@
         value = value + dot(hidden, near_outer_ref[:, columns])
         value = value + jnp.where(upper == t // 2, mixed_ref[:, columns], 0.0)
         out_ref[t] = value.astype(BF16)
+
+
+def merge_kernel(parts_ref, out_ref):
+    replicas, share, _ = out_ref.shape
+    crossed = (lax.axis_index("rep") >= straight(replicas, share)).astype(jnp.int32)
+    halves = [
+        parts_ref[0, lower] + parts_ref[1, lower ^ crossed]
+        for lower in range(2)
+    ]
+    out_ref[...] = jnp.concatenate(halves, axis=1).astype(BF16)
 
 
 def swap(value, xor):
@@ -300,15 +314,19 @@
         out_specs=VMEM,
         name="stream",
     )(*blocks, picked)
+    share = rows // replicas
+    cut = straight(replicas, share) * half // replicas
+    sizes = (cut, half - cut) if cut < half else (half,)
     near_inner = swap(w_inner, 1)
     pair = local(
         pair_kernel,
-        out_shape=shape((half, model_width), BF16),
+        out_shape=tuple(shape((size, model_width), BF16) for size in sizes),
         in_specs=[VMEM] * 4,
-        out_specs=VMEM,
+        out_specs=(VMEM,) * len(sizes),
         name="pair",
     )(keep, swap(send, 1), swap(w_out, 1), near_inner)
-    late_outer, pair = lax.optimization_barrier((w_outer, pair))
+    late_outer, *pair = lax.optimization_barrier((w_outer, *pair))
+    others = [swap(piece, xor) for piece, xor in zip(pair, (2, 3))]
     ff_width = w_inner.shape[1]
     mixed, ffn_input, inverse, hidden = local(
         inner_kernel,
@@ -318,11 +336,11 @@
             shape((half, LANES), F32),
             shape((half, ff_width), BF16),
         ),
-        in_specs=[VMEM] * 5,
+        in_specs=[VMEM] * (3 + 2 * len(sizes)),
         out_specs=(VMEM,) * 4,
         cost_estimate=pl.CostEstimate(flops=INNER_FLOPS, bytes_accessed=0, transcendentals=0),
         name="inner",
-    )(pair, swap(pair, 2), stream, ffn_gain.reshape(1, model_width), w_inner)
+    )(stream, ffn_gain.reshape(1, model_width), w_inner, *pair, *others)
     out = local(
         outer_kernel,
         out_shape=shape((groups * 2, half, width), BF16),
@@ -330,7 +348,6 @@
         out_specs=VMEM,
         name="outer",
     )(mixed, ffn_input, inverse, hidden, near_inner, w_outer, swap(late_outer, 1))
-    share = rows // replicas
     if not halved(share):
         padded = jnp.zeros((groups * 2, rows, width), BF16)
         out = lax.dynamic_update_slice_in_dim(padded, out, side * half, 1)
@@ -339,7 +356,14 @@
     )
     parts = parts.reshape(groups, 2, replicas, -1, width).astype(F32)
     if halved(share):
-        return jnp.sum(parts, axis=0).swapaxes(0, 1).reshape(rows, width).astype(BF16)
+        merged = local(
+            merge_kernel,
+            out_shape=shape((replicas, share, width), BF16),
+            in_specs=[VMEM],
+            out_specs=VMEM,
+            name="merge",
+        )(parts)
+        return merged.reshape(rows, width)
     return jnp.sum(parts, axis=(0, 1)).reshape(rows, width).astype(BF16)
 
 

time: 30.5 us -> 30.2 us (level)
  waiting for transfers between devices: 6.34 us -> 5.01 us
  starting transfers between devices: 5.37 us -> 6.34 us
  Pallas kernels: 3.95 us -> 4.6 us
  local copies, waits for them, and re-layouts: 1.39 us -> 0.75 us
    ppermute x8 -> x9, waiting for transfers between devices: 6.34 us -> 5.01 us  [swap(): return lax.ppermute(value, ('hi', 'lo'), [(i, i ^ xor) for i in range(4)])]
    ppermute x8 -> x9, starting transfers between devices: 5.37 us -> 6.34 us  [swap(): return lax.ppermute(value, ('hi', 'lo'), [(i, i ^ xor) for i in range(4)])]
    pallas_call x1 -> x2, Pallas kernels: 0.21 us -> 0.86 us  [the longest x1 0.65 us: on_device(): local(merge_kernel, out_shape=shape((replicas, share, width), BF16), in_s...]
    convert_element_type x1 -> x0, local copies, waits for them, and re-layouts: 0.63 us -> none  [on_device(): jnp.sum(parts, axis=0).swapaxes(0, 1).reshape(rows, width).astype(BF16)]
  transfers between devices with their start and end apart: 8 -> 9, of which waited for: 4 -> 5; matrix products, arithmetic and copies ran while one was open for 0% -> 0% of each run, Pallas kernels for 10% -> 10%
where the time goes in v10:
time: 30.2 us; the launch traced here: 30 us
  blocking collectives  13.1 us (43%)
  starting transfers between devices  6.34 us (21%)
  waiting for transfers between devices  5.01 us (17%)
  Pallas kernels  4.6 us (15%)
  local copies, waits for them, and re-layouts  0.75 us (2%)
    all_to_all x1, blocking collectives, on_device(): lax.all_to_all(out.reshape(groups * 2 * replicas, -1, width), ('hi', 'lo'...  13.1 us
    ppermute x9, starting transfers between devices, swap(): return lax.ppermute(value, ('hi', 'lo'), [(i, i ^ xor) for i in range(4)])  6.34 us
    ppermute x9, waiting for transfers between devices, swap(): return lax.ppermute(value, ('hi', 'lo'), [(i, i ^ xor) for i in range(4)])  5.01 us
    pallas_call x1, Pallas kernels, on_device(): local(attend_kernel, out_shape=(shape((half, local_width), BF16), shape((...  1.14 us
    pallas_call x1, Pallas kernels, on_device(): local(functools.partial(prepare_kernel, replicas, cached), out_shape=(sha...  1.09 us
    unnamed x30, local copies, waits for them, and re-layouts  0.75 us
    pallas_call x1, Pallas kernels, on_device(): local(outer_kernel, out_shape=shape((groups * 2, half, width), BF16), in_...  0.74 us
    pallas_call x1, Pallas kernels, on_device(): local(merge_kernel, out_shape=shape((replicas, share, width), BF16), in_s...  0.65 us
  transfers between devices with their start and end apart: 9, of which 5 were waited for; matrix products, arithmetic and copies ran while one was open for 0% of the time, Pallas kernels for 10%

profile of v10, /device:TPU:0, one launch (start us, length us, event | category | flops | bytes accessed | tf_op | source)
XLA Modules:
  0.0 30.0 jit_solution(14541116979825303366)
XLA Ops:
  0.0 3.0 %collective-permute-start.2 = (bf16[128,256]{1,0:T(8,128)(2,1)}, bf16[128,256]{1,0:T(8,128)(2,1)S(1)}, u32[]{:S(2)}, u32[]{:S(2)}) collective-permute-start(bf16[128,256]{1,0:T(8,128)(2,1)} %own_ref.3), channel_id=1, source_target_pairs={{0,2},{1,3},{2,0},{3,1},{4,6},{5,7},{6,4},{7,5},{8,10},{9,11},{10,... | collective-permute-start | bytes 196616 | tf_op jit(solution)/shard_map/ppermute | solution.py:238
  3.0 0.0 collective-permute-start.1
  3.0 0.1 collective-permute-start
  3.1 0.4 %collective-permute-start.4 = (bf16[256,1024]{1,0:T(8,128)(2,1)}, bf16[256,1024]{1,0:T(8,128)(2,1)S(1)}, u32[]{:S(2)}, u32[]{:S(2)}) collective-permute-start(bf16[256,1024]{1,0:T(8,128)(2,1)} %w_out_ref.1), channel_id=1, source_target_pairs={{0,1},{1,0},{2,3},{3,2},{4,5},{5,4},{6,7},{7,6},{8,9},{9,8},{10,11... | collective-permute-start | bytes 1572872 | tf_op jit(solution)/shard_map/ppermute | solution.py:238
  3.5 0.1 collective-permute-start.5
  3.6 0.7 %copy-done.11 = f32[32,4]{0,1:T(4,128)S(1)} copy-done((f32[32,4]{0,1:T(4,128)S(1)}, f32[32,4]{0,1:T(4,128)}, u32[]{:S(2)}) %copy-start.11) | copy-done | bytes 536
  4.3 0.0 copy-done.12
  4.3 0.0 copy-done.13
  4.3 0.0 copy-done.14
  4.3 0.0 copy-start.6
  4.3 0.0 copy-start.7
  4.3 0.0 copy-start.8
  4.3 1.1 %prepare.1 = (f32[2,256,128]{2,1,0:T(8,128)S(1)}, bf16[128,128]{1,0:T(8,128)(2,1)S(1)}) custom-call(f32[4,32]{1,0:T(4,128)S(1)} %bitcast.12, s32[1,2]{1,0:T(1,128)S(1)} %bitcast.13, s32[1,2]{1,0:T(1,128)S(1)} %bitcast.14, s32[1,128]{1,0:T(1,128)S(1)} %copy-done.14), custom_call_target="tpu_custom_call" | custom-call | flops 7000000000 | tf_op jit(solution)/shard_map/prepare/pallas_call | solution.py:271
  5.4 0.0 copy-start.9
  5.4 0.1 collective-permute-done.2.across_ref
  5.6 0.0 collective-permute-done.1.near_ref
  5.6 1.3 %collective-permute-done.far_ref = bf16[128,256]{1,0:T(8,128)(2,1)S(1)} collective-permute-done((bf16[128,256]{1,0:T(8,128)(2,1)}, bf16[128,256]{1,0:T(8,128)(2,1)S(1)}, u32[]{:S(2)}, u32[]{:S(2)}) %collective-permute-start) | collective-permute-done | bytes 65568 | tf_op jit(solution)/shard_map/ppermute | solution.py:238
  6.9 0.0 copy-done.2
  6.9 0.0 copy-done.4
  6.9 0.0 copy-done.5
  6.9 0.0 copy-done.6
  6.9 0.0 copy-done.7
  7.0 0.0 copy-done.8
  7.0 0.0 copy-done.9
  7.0 0.0 copy-start.1
  7.0 1.1 %attend.1 = (bf16[64,256]{1,0:T(8,128)(2,1)S(1)}, bf16[128,256]{1,0:T(8,128)(2,1)S(1)}) custom-call(bf16[128,256]{1,0:T(8,128)(2,1)S(1)} %copy-done.2, bf16[128,256]{1,0:T(8,128)(2,1)S(1)} %collective-permute-done.far_ref, bf16[128,256]{1,0:T(8,128)(2,1)S(1)} %collective-permute-done.1.near_ref, bf16[128,256]{1,0:T(8,128)(2,1)S(1)} %collective-permute-done.2.across_ref, ...), custom_call_target="tpu_custom_call" | custom-call | flops 40000000000 | tf_op jit(solution)/shard_map/attend/pallas_call | solution.py:284
  8.1 0.5 %collective-permute-start.3 = (bf16[64,256]{1,0:T(8,128)(2,1)S(1)}, bf16[64,256]{1,0:T(8,128)(2,1)S(1)}, u32[]{:S(2)}, u32[]{:S(2)}) collective-permute-start(bf16[64,256]{1,0:T(8,128)(2,1)S(1)} %get-tuple-element.21), channel_id=1, source_target_pairs={{0,1},{1,0},{2,3},{3,2},{4,5},{5,4},{6,7},{7,6},{8,9},{9,8},{10,11... | collective-permute-start | bytes 98312 | tf_op jit(solution)/shard_map/ppermute | solution.py:238
  8.6 0.0 copy-done.1
  8.6 0.3 project.1.keep_ref
  8.9 0.0 copy-start
  8.9 0.0 copy-start.3
  8.9 0.5 %collective-permute-done.3.near_ref = bf16[64,256]{1,0:T(8,128)(2,1)S(1)} collective-permute-done((bf16[64,256]{1,0:T(8,128)(2,1)S(1)}, bf16[64,256]{1,0:T(8,128)(2,1)S(1)}, u32[]{:S(2)}, u32[]{:S(2)}) %collective-permute-start.3) | collective-permute-done | bytes 32800 | tf_op jit(solution)/shard_map/ppermute | solution.py:238
  9.5 0.0 collective-permute-done.4.near_out_ref
  9.5 0.0 collective-permute-done.5.near_inner_ref
  9.5 0.2 pair.1
  9.7 0.0 copy-start.10
  9.7 1.2 %collective-permute-start.6 = (bf16[48,1024]{1,0:T(8,128)(2,1)S(1)}, bf16[48,1024]{1,0:T(8,128)(2,1)S(1)}, u32[]{:S(2)}, u32[]{:S(2)}) collective-permute-start(bf16[48,1024]{1,0:T(8,128)(2,1)S(1)} %get-tuple-element.24.refs_0_), channel_id=1, source_target_pairs={{0,2},{1,3},{2,0},{3,1},{4,6},{5,7},{6,4},{7,5},{8,10},{9,11},{10,... | collective-permute-start | bytes 294920 | tf_op jit(solution)/shard_map/ppermute | solution.py:238
  10.9 0.6 %collective-permute-start.7 = (bf16[16,1024]{1,0:T(8,128)(2,1)S(1)}, bf16[16,1024]{1,0:T(8,128)(2,1)S(1)}, u32[]{:S(2)}, u32[]{:S(2)}) collective-permute-start(bf16[16,1024]{1,0:T(8,128)(2,1)S(1)} %get-tuple-element.25.refs_1_), channel_id=1, source_target_pairs={{0,3},{1,2},{2,1},{3,0},{4,7},{5,6},{6,5},{7,4},{8,11},{9,10},{10,... | collective-permute-start | bytes 98312 | tf_op jit(solution)/shard_map/ppermute | solution.py:238
  11.5 0.2 stream.1.stream_ref
  11.6 0.0 copy-done
  11.7 0.5 %collective-permute-start.8 = (bf16[512,1024]{1,0:T(8,128)(2,1)S(1)}, bf16[512,1024]{1,0:T(8,128)(2,1)S(1)}, u32[]{:S(2)}, u32[]{:S(2)}) collective-permute-start(bf16[512,1024]{1,0:T(8,128)(2,1)S(1)} %copy-done), channel_id=1, source_target_pairs={{0,1},{1,0},{2,3},{3,2},{4,5},{5,4},{6,7},{7,6},{8,9},{9,8},{10,11... | collective-permute-start | bytes 3145736 | tf_op jit(solution)/shard_map/ppermute | solution.py:238
  12.2 2.8 %collective-permute-done.7.refs_3_ = bf16[16,1024]{1,0:T(8,128)(2,1)S(1)} collective-permute-done((bf16[16,1024]{1,0:T(8,128)(2,1)S(1)}, bf16[16,1024]{1,0:T(8,128)(2,1)S(1)}, u32[]{:S(2)}, u32[]{:S(2)}) %collective-permute-start.7) | collective-permute-done | bytes 32800 | tf_op jit(solution)/shard_map/ppermute | solution.py:238
  14.9 0.2 collective-permute-done.6.refs_2_
  15.2 0.3 %inner.1 = (f32[64,1024]{1,0:T(8,128)S(1)}, bf16[64,1024]{1,0:T(8,128)(2,1)S(1)}, f32[64,128]{1,0:T(8,128)S(1)}, bf16[64,512]{1,0:T(8,128)(2,1)S(1)}) custom-call(bf16[64,1024]{1,0:T(8,128)(2,1)S(1)} %stream.1.stream_ref, f32[1,1024]{1,0:T(1,128)S(1)} %bitcast.11, bf16[1024,512]{1,0:T(8,128)(2,1)S(1)} %copy-done.3, ...), custom_call_target="tpu_custom_call" | custom-call | flops 40000000000 | tf_op jit(solution)/shard_map/inner/pallas_call | solution.py:331
  15.5 0.0 collective-permute-done.8.near_outer_ref
  15.5 0.7 %outer.1 = bf16[4,64,256]{2,1,0:T(8,128)(2,1)S(1)} custom-call(f32[64,1024]{1,0:T(8,128)S(1)} %get-tuple-element.26.mixed_ref, bf16[64,1024]{1,0:T(8,128)(2,1)S(1)} %get-tuple-element.27.input_ref, f32[64,128]{1,0:T(8,128)S(1)} %get-tuple-element.28.inverse_ref, bf16[64,512]{1,0:T(8,128)(2,1)S(1)} %get-tuple-element.29.own_hidden_ref, ...), custom_call_target="tpu_custom_call" | custom-call | tf_op jit(solution)/shard_map/outer/pallas_call | solution.py:344
  16.2 13.1 %all_to_all.5 = bf16[32,8,256]{2,1,0:T(8,128)(2,1)S(1)} all-to-all(bf16[32,8,256]{2,1,0:T(8,128)(2,1)S(1)} %bitcast.9), channel_id=1, replica_groups=mesh['rep'=8,'hi'=2,'lo'=2] {'hi','lo','rep'}, dimensions={0} | all-to-all | bytes 262144 | tf_op jit(solution)/shard_map/all_to_all | solution.py:354
  29.3 0.7 %merge.1 = bf16[8,16,256]{2,1,0:T(8,128)(2,1)} custom-call(f32[2,2,8,8,256]{4,3,2,1,0:T(8,128)S(1)} %convert.1.parts_ref), custom_call_target="tpu_custom_call" | custom-call | tf_op jit(solution)/shard_map/merge/pallas_call | solution.py:359
  (10 shorter events, 0.0 us)
Async XLA Ops:
  0.0 5.6 %collective-permute-start.2 = (bf16[128,256]{1,0:T(8,128)(2,1)}, bf16[128,256]{1,0:T(8,128)(2,1)S(1)}, u32[]{:S(2)}, u32[]{:S(2)}) collective-permute-start(bf16[128,256]{1,0:T(8,128)(2,1)} %own_ref.3), channel_id=1, source_target_pairs={{0,2},{1,3},{2,0},{3,1},{4,6},{5,7},{6,4},{7,5},{8,10},{9,11},{10,... | collective-permute-start | bytes 196616 | tf_op jit(solution)/shard_map/ppermute | solution.py:238
  3.0 2.6 %collective-permute-start.1 = (bf16[128,256]{1,0:T(8,128)(2,1)}, bf16[128,256]{1,0:T(8,128)(2,1)S(1)}, u32[]{:S(2)}, u32[]{:S(2)}) collective-permute-start(bf16[128,256]{1,0:T(8,128)(2,1)} %own_ref.3), channel_id=1, source_target_pairs={{0,1},{1,0},{2,3},{3,2},{4,5},{5,4},{6,7},{7,6},{8,9},{9,8},{10,11... | collective-permute-start | bytes 196616 | tf_op jit(solution)/shard_map/ppermute | solution.py:238
  3.0 4.0 %collective-permute-start = (bf16[128,256]{1,0:T(8,128)(2,1)}, bf16[128,256]{1,0:T(8,128)(2,1)S(1)}, u32[]{:S(2)}, u32[]{:S(2)}) collective-permute-start(bf16[128,256]{1,0:T(8,128)(2,1)} %own_ref.3), channel_id=1, source_target_pairs={{0,3},{1,2},{2,1},{3,0},{4,7},{5,6},{6,5},{7,4},{8,11},{9,10},{10,... | collective-permute-start | bytes 196616 | tf_op jit(solution)/shard_map/ppermute | solution.py:238
  3.1 6.4 %collective-permute-start.4 = (bf16[256,1024]{1,0:T(8,128)(2,1)}, bf16[256,1024]{1,0:T(8,128)(2,1)S(1)}, u32[]{:S(2)}, u32[]{:S(2)}) collective-permute-start(bf16[256,1024]{1,0:T(8,128)(2,1)} %w_out_ref.1), channel_id=1, source_target_pairs={{0,1},{1,0},{2,3},{3,2},{4,5},{5,4},{6,7},{7,6},{8,9},{9,8},{10,11... | collective-permute-start | bytes 1572872 | tf_op jit(solution)/shard_map/ppermute | solution.py:238
  3.5 6.0 %collective-permute-start.5 = (bf16[1024,512]{1,0:T(8,128)(2,1)}, bf16[1024,512]{1,0:T(8,128)(2,1)S(1)}, u32[]{:S(2)}, u32[]{:S(2)}) collective-permute-start(bf16[1024,512]{1,0:T(8,128)(2,1)} %w_inner_ref.1), channel_id=1, source_target_pairs={{0,1},{1,0},{2,3},{3,2},{4,5},{5,4},{6,7},{7,6},{8,9},{9,8},{10,11... | collective-permute-start | bytes 3145736 | tf_op jit(solution)/shard_map/ppermute | solution.py:238
  3.6 0.7 %copy-start.11 = (f32[32,4]{0,1:T(4,128)S(1)}, f32[32,4]{0,1:T(4,128)}, u32[]{:S(2)}) copy-start(f32[32,4]{0,1:T(4,128)} %param.24) | copy-start | bytes 1540
  3.6 0.7 %copy-start.12 = (s32[2,1]{0,1:T(1,128)S(1)}, s32[2,1]{0,1:T(1,128)}, u32[]{:S(2)}) copy-start(s32[2,1]{0,1:T(1,128)} %param.27) | copy-start | bytes 28
  3.6 0.7 %copy-start.13 = (s32[2,1]{0,1:T(1,128)S(1)}, s32[2,1]{0,1:T(1,128)}, u32[]{:S(2)}) copy-start(s32[2,1]{0,1:T(1,128)} %param.28) | copy-start | bytes 28
  3.6 0.7 %copy-start.14 = (s32[1,128]{1,0:T(1,128)S(1)}, s32[1,128]{1,0:T(1,128)}, u32[]{:S(2)}) copy-start(s32[1,128]{1,0:T(1,128)} %deal_ref.1) | copy-start | bytes 1540
  4.3 2.6 %copy-start.2 = (bf16[128,256]{1,0:T(8,128)(2,1)S(1)}, bf16[128,256]{1,0:T(8,128)(2,1)}, u32[]{:S(2)}) copy-start(bf16[128,256]{1,0:T(8,128)(2,1)} %own_ref.3) | copy-start | bytes 196612
  4.3 2.6 %copy-start.4 = (bf16[1024,256]{1,0:T(8,128)(2,1)S(1)}, bf16[1024,256]{1,0:T(8,128)(2,1)}, u32[]{:S(2)}) copy-start(bf16[1024,256]{1,0:T(8,128)(2,1)} %w_query_ref.1) | copy-start | bytes 1572868
  4.3 2.6 %copy-start.5 = (bf16[1024,256]{1,0:T(8,128)(2,1)S(1)}, bf16[1024,256]{1,0:T(8,128)(2,1)}, u32[]{:S(2)}) copy-start(bf16[1024,256]{1,0:T(8,128)(2,1)} %w_key_ref.1) | copy-start | bytes 1572868
  4.3 2.6 %copy-start.6 = (bf16[1024,256]{1,0:T(8,128)(2,1)S(1)}, bf16[1024,256]{1,0:T(8,128)(2,1)}, u32[]{:S(2)}) copy-start(bf16[1024,256]{1,0:T(8,128)(2,1)} %w_value_ref.1) | copy-start | bytes 1572868
  4.3 2.6 %copy-start.7 = (bf16[2,64,256]{2,1,0:T(8,128)(2,1)S(1)}, bf16[2,64,256]{2,1,0:T(8,128)(2,1)}, u32[]{:S(2)}) copy-start(bf16[2,64,256]{2,1,0:T(8,128)(2,1)} %cache_keys_ref.1) | copy-start | bytes 196612
  4.3 2.6 %copy-start.8 = (bf16[2,64,256]{2,1,0:T(8,128)(2,1)S(1)}, bf16[2,64,256]{2,1,0:T(8,128)(2,1)}, u32[]{:S(2)}) copy-start(bf16[2,64,256]{2,1,0:T(8,128)(2,1)} %cache_values_ref.1) | copy-start | bytes 196612
  5.4 1.5 %copy-start.9 = (f32[1024]{0:T(1024)S(1)}, f32[1024]{0:T(1024)}, u32[]{:S(2)}) copy-start(f32[1024]{0:T(1024)} %param.16) | copy-start | bytes 12292
  7.0 1.6 %copy-start.1 = (bf16[256,1024]{1,0:T(8,128)(2,1)S(1)}, bf16[256,1024]{1,0:T(8,128)(2,1)}, u32[]{:S(2)}) copy-start(bf16[256,1024]{1,0:T(8,128)(2,1)} %w_out_ref.1) | copy-start | bytes 1572868
  8.1 1.3 %collective-permute-start.3 = (bf16[64,256]{1,0:T(8,128)(2,1)S(1)}, bf16[64,256]{1,0:T(8,128)(2,1)S(1)}, u32[]{:S(2)}, u32[]{:S(2)}) collective-permute-start(bf16[64,256]{1,0:T(8,128)(2,1)S(1)} %get-tuple-element.21), channel_id=1, source_target_pairs={{0,1},{1,0},{2,3},{3,2},{4,5},{5,4},{6,7},{7,6},{8,9},{9,8},{10,11... | collective-permute-start | bytes 98312 | tf_op jit(solution)/shard_map/ppermute | solution.py:238
  8.9 2.7 %copy-start = (bf16[512,1024]{1,0:T(8,128)(2,1)S(1)}, bf16[512,1024]{1,0:T(8,128)(2,1)}, u32[]{:S(2)}) copy-start(bf16[512,1024]{1,0:T(8,128)(2,1)} %own_outer_ref.1) | copy-start | bytes 3145732
  8.9 6.2 %copy-start.3 = (bf16[1024,512]{1,0:T(8,128)(2,1)S(1)}, bf16[1024,512]{1,0:T(8,128)(2,1)}, u32[]{:S(2)}) copy-start(bf16[1024,512]{1,0:T(8,128)(2,1)} %w_inner_ref.1) | copy-start | bytes 3145732
  9.7 5.5 %copy-start.10 = (f32[1024]{0:T(1024)S(1)}, f32[1024]{0:T(1024)}, u32[]{:S(2)}) copy-start(f32[1024]{0:T(1024)} %param.17) | copy-start | bytes 12292
  9.7 5.5 %collective-permute-start.6 = (bf16[48,1024]{1,0:T(8,128)(2,1)S(1)}, bf16[48,1024]{1,0:T(8,128)(2,1)S(1)}, u32[]{:S(2)}, u32[]{:S(2)}) collective-permute-start(bf16[48,1024]{1,0:T(8,128)(2,1)S(1)} %get-tuple-element.24.refs_0_), channel_id=1, source_target_pairs={{0,2},{1,3},{2,0},{3,1},{4,6},{5,7},{6,4},{7,5},{8,10},{9,11},{10,... | collective-permute-start | bytes 294920 | tf_op jit(solution)/shard_map/ppermute | solution.py:238
  10.9 4.1 %collective-permute-start.7 = (bf16[16,1024]{1,0:T(8,128)(2,1)S(1)}, bf16[16,1024]{1,0:T(8,128)(2,1)S(1)}, u32[]{:S(2)}, u32[]{:S(2)}) collective-permute-start(bf16[16,1024]{1,0:T(8,128)(2,1)S(1)} %get-tuple-element.25.refs_1_), channel_id=1, source_target_pairs={{0,3},{1,2},{2,1},{3,0},{4,7},{5,6},{6,5},{7,4},{8,11},{9,10},{10,... | collective-permute-start | bytes 98312 | tf_op jit(solution)/shard_map/ppermute | solution.py:238
  11.7 3.8 %collective-permute-start.8 = (bf16[512,1024]{1,0:T(8,128)(2,1)S(1)}, bf16[512,1024]{1,0:T(8,128)(2,1)S(1)}, u32[]{:S(2)}, u32[]{:S(2)}) collective-permute-start(bf16[512,1024]{1,0:T(8,128)(2,1)S(1)} %copy-done), channel_id=1, source_target_pairs={{0,1},{1,0},{2,3},{3,2},{4,5},{5,4},{6,7},{7,6},{8,9},{9,8},{10,11... | collective-permute-start | bytes 3145736 | tf_op jit(solution)/shard_map/ppermute | solution.py:238

commit v11 on v10

--- a/solution.py
+++ b/solution.py
@@ -170,8 +170,8 @@
     keep_ref[...] = dot(dealt, w_out_ref[...])
 
 
-def pair_kernel(keep_ref, near_ref, near_out_ref, near_inner_ref, *pair_refs):
-    del near_inner_ref
+def pair_kernel(keep_ref, near_ref, near_out_ref, near_inner_ref, near_outer_ref, *pair_refs):
+    del near_inner_ref, near_outer_ref
     pair = (keep_ref[...] + dot(near_ref[...], near_out_ref[...])).astype(BF16)
     start = 0
     for ref in pair_refs:
@@ -187,40 +187,27 @@
         stream_ref[:, columns_of(index ^ xor, width)] = dot(picked, ref[...]).astype(BF16)
 
 
-def inner_kernel(stream_ref, gain_ref, w_inner_ref, *refs):
-    *sum_refs, mixed_ref, input_ref, inverse_ref, hidden_ref = refs
+def ffn_kernel(
+    stream_ref, gain_ref, own_inner_ref, near_inner_ref, own_outer_ref, near_outer_ref, *refs
+):
+    *sum_refs, out_ref = refs
     pieces = len(sum_refs) // 2
     pair = jnp.concatenate([ref[...].astype(F32) for ref in sum_refs[:pieces]], axis=0)
     other = jnp.concatenate([ref[...].astype(F32) for ref in sum_refs[pieces:]], axis=0)
     mixed = pair + other + stream_ref[...].astype(F32)
-    mixed_ref[...] = mixed
     square = jnp.sum(mixed * mixed, axis=1, keepdims=True)
     inverse = lax.rsqrt(square / mixed.shape[1] + EPSILON)
-    inverse_ref[...] = jnp.broadcast_to(inverse, inverse_ref.shape)
     scaled = (mixed * gain_ref[...]).astype(BF16)
-    input_ref[...] = scaled
-    hidden_ref[...] = jnp.maximum(dot(scaled, w_inner_ref[...]) * inverse, 0.0).astype(BF16)
-
-
-def outer_kernel(
-    mixed_ref,
-    input_ref,
-    inverse_ref,
-    own_hidden_ref,
-    near_inner_ref,
-    own_outer_ref,
-    near_outer_ref,
-    out_ref,
-):
+    own, near = (
+        jnp.maximum(dot(scaled, ref[...]) * inverse, 0.0).astype(BF16)
+        for ref in (own_inner_ref, near_inner_ref)
+    )
     upper = lax.axis_index("hi")
     width = out_ref.shape[2]
-    hidden = dot(input_ref[...], near_inner_ref[...]) * inverse_ref[:, :1]
-    hidden = jnp.maximum(hidden, 0.0).astype(BF16)
     for t in range(out_ref.shape[0]):
         columns = slice(t * width, (t + 1) * width)
-        value = dot(own_hidden_ref[...], own_outer_ref[:, columns])
-        value = value + dot(hidden, near_outer_ref[:, columns])
-        value = value + jnp.where(upper == t // 2, mixed_ref[:, columns], 0.0)
+        value = dot(own, own_outer_ref[:, columns]) + dot(near, near_outer_ref[:, columns])
+        value = value + jnp.where(upper == t // 2, mixed[:, columns], 0.0)
         out_ref[t] = value.astype(BF16)
 
 
@@ -317,37 +304,31 @@
     share = rows // replicas
     cut = straight(replicas, share) * half // replicas
     sizes = (cut, half - cut) if cut < half else (half,)
-    near_inner = swap(w_inner, 1)
+    near_inner, near_outer = swap(w_inner, 1), swap(w_outer, 1)
     pair = local(
         pair_kernel,
         out_shape=tuple(shape((size, model_width), BF16) for size in sizes),
-        in_specs=[VMEM] * 4,
+        in_specs=[VMEM] * 5,
         out_specs=(VMEM,) * len(sizes),
         name="pair",
-    )(keep, swap(send, 1), swap(w_out, 1), near_inner)
-    late_outer, *pair = lax.optimization_barrier((w_outer, *pair))
+    )(keep, swap(send, 1), swap(w_out, 1), near_inner, near_outer)
     others = [swap(piece, xor) for piece, xor in zip(pair, (2, 3))]
-    ff_width = w_inner.shape[1]
-    mixed, ffn_input, inverse, hidden = local(
-        inner_kernel,
-        out_shape=(
-            shape((half, model_width), F32),
-            shape((half, model_width), BF16),
-            shape((half, LANES), F32),
-            shape((half, ff_width), BF16),
-        ),
-        in_specs=[VMEM] * (3 + 2 * len(sizes)),
-        out_specs=(VMEM,) * 4,
-        cost_estimate=pl.CostEstimate(flops=INNER_FLOPS, bytes_accessed=0, transcendentals=0),
-        name="inner",
-    )(stream, ffn_gain.reshape(1, model_width), w_inner, *pair, *others)
     out = local(
-        outer_kernel,
+        ffn_kernel,
         out_shape=shape((groups * 2, half, width), BF16),
-        in_specs=[VMEM] * 7,
+        in_specs=[VMEM] * (6 + 2 * len(sizes)),
         out_specs=VMEM,
-        name="outer",
-    )(mixed, ffn_input, inverse, hidden, near_inner, w_outer, swap(late_outer, 1))
+        name="ffn",
+    )(
+        stream,
+        ffn_gain.reshape(1, model_width),
+        w_inner,
+        near_inner,
+        w_outer,
+        near_outer,
+        *pair,
+        *others,
+    )
     if not halved(share):
         padded = jnp.zeros((groups * 2, rows, width), BF16)
         out = lax.dynamic_update_slice_in_dim(padded, out, side * half, 1)

time: 30.2 us -> 30.1 us (level)
    pallas_call x2 -> x1, Pallas kernels: 1.04 us -> 0.92 us  [on_device(): local(ffn_kernel, out_shape=shape((groups * 2, half, width), BF16), in_sp...]
  transfers between devices with their start and end apart: 9 -> 9, of which waited for: 5 -> 5; matrix products, arithmetic and copies ran while one was open for 0% -> 0% of each run, Pallas kernels for 10% -> 9%
where the time goes in v11:
time: 30.1 us; the launch traced here: 29.9 us
  blocking collectives  13.1 us (44%)
  starting transfers between devices  6.18 us (21%)
  waiting for transfers between devices  5.18 us (17%)
  Pallas kernels  4.48 us (15%)
  local copies, waits for them, and re-layouts  0.75 us (2%)
    all_to_all x1, blocking collectives, on_device(): lax.all_to_all(out.reshape(groups * 2 * replicas, -1, width), ('hi', 'lo'...  13.1 us
    ppermute x9, starting transfers between devices, swap(): return lax.ppermute(value, ('hi', 'lo'), [(i, i ^ xor) for i in range(4)])  6.18 us
    ppermute x9, waiting for transfers between devices, swap(): return lax.ppermute(value, ('hi', 'lo'), [(i, i ^ xor) for i in range(4)])  5.18 us
    pallas_call x1, Pallas kernels, on_device(): local(attend_kernel, out_shape=(shape((half, local_width), BF16), shape((...  1.14 us
    pallas_call x1, Pallas kernels, on_device(): local(functools.partial(prepare_kernel, replicas, cached), out_shape=(sha...  1.09 us
    pallas_call x1, Pallas kernels, on_device(): local(ffn_kernel, out_shape=shape((groups * 2, half, width), BF16), in_sp...  0.92 us
    unnamed x30, local copies, waits for them, and re-layouts  0.75 us
    pallas_call x1, Pallas kernels, on_device(): local(merge_kernel, out_shape=shape((replicas, share, width), BF16), in_s...  0.65 us
  transfers between devices with their start and end apart: 9, of which 5 were waited for; matrix products, arithmetic and copies ran while one was open for 0% of the time, Pallas kernels for 9%

profile of v11, /device:TPU:0, one launch (start us, length us, event | category | flops | bytes accessed | tf_op | source)
XLA Modules:
  0.0 29.9 jit_solution(13751165708370830190)
XLA Ops:
  0.0 3.0 %collective-permute-start.2 = (bf16[128,256]{1,0:T(8,128)(2,1)}, bf16[128,256]{1,0:T(8,128)(2,1)S(1)}, u32[]{:S(2)}, u32[]{:S(2)}) collective-permute-start(bf16[128,256]{1,0:T(8,128)(2,1)} %own_ref.3), channel_id=1, source_target_pairs={{0,2},{1,3},{2,0},{3,1},{4,6},{5,7},{6,4},{7,5},{8,10},{9,11},{10,... | collective-permute-start | bytes 196616 | tf_op jit(solution)/shard_map/ppermute | solution.py:225
  3.0 0.0 collective-permute-start.1
  3.0 0.1 collective-permute-start
  3.1 0.4 %collective-permute-start.6 = (bf16[256,1024]{1,0:T(8,128)(2,1)}, bf16[256,1024]{1,0:T(8,128)(2,1)S(1)}, u32[]{:S(2)}, u32[]{:S(2)}) collective-permute-start(bf16[256,1024]{1,0:T(8,128)(2,1)} %w_out_ref.1), channel_id=1, source_target_pairs={{0,1},{1,0},{2,3},{3,2},{4,5},{5,4},{6,7},{7,6},{8,9},{9,8},{10,11... | collective-permute-start | bytes 1572872 | tf_op jit(solution)/shard_map/ppermute | solution.py:225
  3.5 0.1 collective-permute-start.3
  3.6 0.7 %copy-done.11 = f32[32,4]{0,1:T(4,128)S(1)} copy-done((f32[32,4]{0,1:T(4,128)S(1)}, f32[32,4]{0,1:T(4,128)}, u32[]{:S(2)}) %copy-start.11) | copy-done | bytes 536
  4.3 0.0 copy-done.12
  4.3 0.0 copy-done.13
  4.3 0.0 copy-done.14
  4.3 0.0 copy-start.6
  4.3 0.0 copy-start.7
  4.3 0.0 copy-start.8
  4.3 0.0 copy-start.9
  4.4 1.1 %prepare.1 = (f32[2,256,128]{2,1,0:T(8,128)S(1)}, bf16[128,128]{1,0:T(8,128)(2,1)S(1)}) custom-call(f32[4,32]{1,0:T(4,128)S(1)} %bitcast.12, s32[1,2]{1,0:T(1,128)S(1)} %bitcast.13, s32[1,2]{1,0:T(1,128)S(1)} %bitcast.14, s32[1,128]{1,0:T(1,128)S(1)} %copy-done.14), custom_call_target="tpu_custom_call" | custom-call | flops 7000000000 | tf_op jit(solution)/shard_map/prepare/pallas_call | solution.py:258
  5.4 0.0 copy-start.10
  5.5 0.1 collective-permute-done.2.across_ref
  5.6 0.0 copy-done.1
  5.6 0.3 %collective-permute-start.4 = (bf16[512,1024]{1,0:T(8,128)(2,1)S(1)}, bf16[512,1024]{1,0:T(8,128)(2,1)S(1)}, u32[]{:S(2)}, u32[]{:S(2)}) collective-permute-start(bf16[512,1024]{1,0:T(8,128)(2,1)S(1)} %copy-done.1), channel_id=1, source_target_pairs={{0,1},{1,0},{2,3},{3,2},{4,5},{5,4},{6,7},{7,6},{8,9},{9,8},{10,11... | collective-permute-start | bytes 3145736 | tf_op jit(solution)/shard_map/ppermute | solution.py:225
  5.9 0.0 collective-permute-done.1.near_ref
  5.9 1.0 %collective-permute-done.far_ref = bf16[128,256]{1,0:T(8,128)(2,1)S(1)} collective-permute-done((bf16[128,256]{1,0:T(8,128)(2,1)}, bf16[128,256]{1,0:T(8,128)(2,1)S(1)}, u32[]{:S(2)}, u32[]{:S(2)}) %collective-permute-start) | collective-permute-done | bytes 65568 | tf_op jit(solution)/shard_map/ppermute | solution.py:225
  6.9 0.0 copy-done.3
  6.9 0.0 copy-done.5
  6.9 0.0 copy-done.6
  6.9 0.0 copy-done.7
  6.9 0.0 copy-done.8
  7.0 0.0 copy-done.9
  7.0 0.0 copy-done.10
  7.0 0.0 copy-start.2
  7.0 1.1 %attend.1 = (bf16[64,256]{1,0:T(8,128)(2,1)S(1)}, bf16[128,256]{1,0:T(8,128)(2,1)S(1)}) custom-call(bf16[128,256]{1,0:T(8,128)(2,1)S(1)} %copy-done.3, bf16[128,256]{1,0:T(8,128)(2,1)S(1)} %collective-permute-done.far_ref, bf16[128,256]{1,0:T(8,128)(2,1)S(1)} %collective-permute-done.1.near_ref, bf16[128,256]{1,0:T(8,128)(2,1)S(1)} %collective-permute-done.2.across_ref, ...), custom_call_target="tpu_custom_call" | custom-call | flops 40000000000 | tf_op jit(solution)/shard_map/attend/pallas_call | solution.py:271
  8.1 0.5 %collective-permute-start.5 = (bf16[64,256]{1,0:T(8,128)(2,1)S(1)}, bf16[64,256]{1,0:T(8,128)(2,1)S(1)}, u32[]{:S(2)}, u32[]{:S(2)}) collective-permute-start(bf16[64,256]{1,0:T(8,128)(2,1)S(1)} %get-tuple-element.14), channel_id=1, source_target_pairs={{0,1},{1,0},{2,3},{3,2},{4,5},{5,4},{6,7},{7,6},{8,9},{9,8},{10,11... | collective-permute-start | bytes 98312 | tf_op jit(solution)/shard_map/ppermute | solution.py:225
  8.6 0.0 copy-done.2
  8.6 0.3 %project.1.keep_ref = f32[64,1024]{1,0:T(8,128)S(1)} custom-call(bf16[128,256]{1,0:T(8,128)(2,1)S(1)} %get-tuple-element.13.context_ref, bf16[128,128]{1,0:T(8,128)(2,1)S(1)} %get-tuple-element.11.picked_ref, bf16[256,1024]{1,0:T(8,128)(2,1)S(1)} %copy-done.2), custom_call_target="tpu_custom_call" | custom-call | tf_op jit(solution)/shard_map/project/pallas_call | solution.py:290
  8.9 0.0 copy-start
  8.9 0.5 %collective-permute-done.5.near_ref = bf16[64,256]{1,0:T(8,128)(2,1)S(1)} collective-permute-done((bf16[64,256]{1,0:T(8,128)(2,1)S(1)}, bf16[64,256]{1,0:T(8,128)(2,1)S(1)}, u32[]{:S(2)}, u32[]{:S(2)}) %collective-permute-start.5) | collective-permute-done | bytes 32800 | tf_op jit(solution)/shard_map/ppermute | solution.py:225
  9.5 0.0 collective-permute-done.6.near_out_ref
  9.5 0.0 collective-permute-done.3.near_inner_ref
  9.5 0.0 collective-permute-done.4.near_outer_ref
  9.5 0.2 pair.1
  9.7 1.3 %collective-permute-start.7 = (bf16[48,1024]{1,0:T(8,128)(2,1)S(1)}, bf16[48,1024]{1,0:T(8,128)(2,1)S(1)}, u32[]{:S(2)}, u32[]{:S(2)}) collective-permute-start(bf16[48,1024]{1,0:T(8,128)(2,1)S(1)} %get-tuple-element.15.refs_0_), channel_id=1, source_target_pairs={{0,2},{1,3},{2,0},{3,1},{4,6},{5,7},{6,4},{7,5},{8,10},{9,11},{10,... | collective-permute-start | bytes 294920 | tf_op jit(solution)/shard_map/ppermute | solution.py:225
  11.0 0.5 %collective-permute-start.8 = (bf16[16,1024]{1,0:T(8,128)(2,1)S(1)}, bf16[16,1024]{1,0:T(8,128)(2,1)S(1)}, u32[]{:S(2)}, u32[]{:S(2)}) collective-permute-start(bf16[16,1024]{1,0:T(8,128)(2,1)S(1)} %get-tuple-element.16.refs_1_), channel_id=1, source_target_pairs={{0,3},{1,2},{2,1},{3,0},{4,7},{5,6},{6,5},{7,4},{8,11},{9,10},{10,... | collective-permute-start | bytes 98312 | tf_op jit(solution)/shard_map/ppermute | solution.py:225
  11.5 0.2 stream.1.stream_ref
  11.6 3.3 %collective-permute-done.8.refs_3_ = bf16[16,1024]{1,0:T(8,128)(2,1)S(1)} collective-permute-done((bf16[16,1024]{1,0:T(8,128)(2,1)S(1)}, bf16[16,1024]{1,0:T(8,128)(2,1)S(1)}, u32[]{:S(2)}, u32[]{:S(2)}) %collective-permute-start.8) | collective-permute-done | bytes 32800 | tf_op jit(solution)/shard_map/ppermute | solution.py:225
  14.9 0.2 collective-permute-done.7.refs_2_
  15.2 0.0 copy-done
  15.2 0.0 copy-done.4
  15.2 0.9 %ffn.1 = bf16[4,64,256]{2,1,0:T(8,128)(2,1)S(1)} custom-call(bf16[64,1024]{1,0:T(8,128)(2,1)S(1)} %stream.1.stream_ref, f32[1,1024]{1,0:T(1,128)S(1)} %bitcast.10, bf16[1024,512]{1,0:T(8,128)(2,1)S(1)} %copy-done, bf16[1024,512]{1,0:T(8,128)(2,1)S(1)} %collective-permute-done.3.near_inner_ref, bf16[512,1024]{1,0:T(8,128)(2,1)S(1)} %copy-done.1, ...), custom_call_target="tpu_custom_call" | custom-call | tf_op jit(solution)/shard_map/ffn/pallas_call | solution.py:316
  16.1 13.1 %all_to_all.5 = bf16[32,8,256]{2,1,0:T(8,128)(2,1)S(1)} all-to-all(bf16[32,8,256]{2,1,0:T(8,128)(2,1)S(1)} %bitcast.9), channel_id=1, replica_groups=mesh['rep'=8,'hi'=2,'lo'=2] {'hi','lo','rep'}, dimensions={0} | all-to-all | bytes 262144 | tf_op jit(solution)/shard_map/all_to_all | solution.py:335
  29.2 0.7 %merge.1 = bf16[8,16,256]{2,1,0:T(8,128)(2,1)} custom-call(f32[2,2,8,8,256]{4,3,2,1,0:T(8,128)S(1)} %convert.1.parts_ref), custom_call_target="tpu_custom_call" | custom-call | tf_op jit(solution)/shard_map/merge/pallas_call | solution.py:340
  (9 shorter events, 0.0 us)
Async XLA Ops:
  0.0 5.6 %collective-permute-start.2 = (bf16[128,256]{1,0:T(8,128)(2,1)}, bf16[128,256]{1,0:T(8,128)(2,1)S(1)}, u32[]{:S(2)}, u32[]{:S(2)}) collective-permute-start(bf16[128,256]{1,0:T(8,128)(2,1)} %own_ref.3), channel_id=1, source_target_pairs={{0,2},{1,3},{2,0},{3,1},{4,6},{5,7},{6,4},{7,5},{8,10},{9,11},{10,... | collective-permute-start | bytes 196616 | tf_op jit(solution)/shard_map/ppermute | solution.py:225
  3.0 3.0 %collective-permute-start.1 = (bf16[128,256]{1,0:T(8,128)(2,1)}, bf16[128,256]{1,0:T(8,128)(2,1)S(1)}, u32[]{:S(2)}, u32[]{:S(2)}) collective-permute-start(bf16[128,256]{1,0:T(8,128)(2,1)} %own_ref.3), channel_id=1, source_target_pairs={{0,1},{1,0},{2,3},{3,2},{4,5},{5,4},{6,7},{7,6},{8,9},{9,8},{10,11... | collective-permute-start | bytes 196616 | tf_op jit(solution)/shard_map/ppermute | solution.py:225
  3.0 4.0 %collective-permute-start = (bf16[128,256]{1,0:T(8,128)(2,1)}, bf16[128,256]{1,0:T(8,128)(2,1)S(1)}, u32[]{:S(2)}, u32[]{:S(2)}) collective-permute-start(bf16[128,256]{1,0:T(8,128)(2,1)} %own_ref.3), channel_id=1, source_target_pairs={{0,3},{1,2},{2,1},{3,0},{4,7},{5,6},{6,5},{7,4},{8,11},{9,10},{10,... | collective-permute-start | bytes 196616 | tf_op jit(solution)/shard_map/ppermute | solution.py:225
  3.1 6.4 %collective-permute-start.6 = (bf16[256,1024]{1,0:T(8,128)(2,1)}, bf16[256,1024]{1,0:T(8,128)(2,1)S(1)}, u32[]{:S(2)}, u32[]{:S(2)}) collective-permute-start(bf16[256,1024]{1,0:T(8,128)(2,1)} %w_out_ref.1), channel_id=1, source_target_pairs={{0,1},{1,0},{2,3},{3,2},{4,5},{5,4},{6,7},{7,6},{8,9},{9,8},{10,11... | collective-permute-start | bytes 1572872 | tf_op jit(solution)/shard_map/ppermute | solution.py:225
  3.5 6.0 %collective-permute-start.3 = (bf16[1024,512]{1,0:T(8,128)(2,1)}, bf16[1024,512]{1,0:T(8,128)(2,1)S(1)}, u32[]{:S(2)}, u32[]{:S(2)}) collective-permute-start(bf16[1024,512]{1,0:T(8,128)(2,1)} %own_inner_ref.1), channel_id=1, source_target_pairs={{0,1},{1,0},{2,3},{3,2},{4,5},{5,4},{6,7},{7,6},{8,9},{9,8},{10,11... | collective-permute-start | bytes 3145736 | tf_op jit(solution)/shard_map/ppermute | solution.py:225
  3.6 0.7 %copy-start.11 = (f32[32,4]{0,1:T(4,128)S(1)}, f32[32,4]{0,1:T(4,128)}, u32[]{:S(2)}) copy-start(f32[32,4]{0,1:T(4,128)} %param.24) | copy-start | bytes 1540
  3.6 0.7 %copy-start.12 = (s32[2,1]{0,1:T(1,128)S(1)}, s32[2,1]{0,1:T(1,128)}, u32[]{:S(2)}) copy-start(s32[2,1]{0,1:T(1,128)} %param.27) | copy-start | bytes 28
  3.6 0.7 %copy-start.13 = (s32[2,1]{0,1:T(1,128)S(1)}, s32[2,1]{0,1:T(1,128)}, u32[]{:S(2)}) copy-start(s32[2,1]{0,1:T(1,128)} %param.28) | copy-start | bytes 28
  3.6 0.7 %copy-start.14 = (s32[1,128]{1,0:T(1,128)S(1)}, s32[1,128]{1,0:T(1,128)}, u32[]{:S(2)}) copy-start(s32[1,128]{1,0:T(1,128)} %deal_ref.1) | copy-start | bytes 1540
  4.3 1.3 %copy-start.1 = (bf16[512,1024]{1,0:T(8,128)(2,1)S(1)}, bf16[512,1024]{1,0:T(8,128)(2,1)}, u32[]{:S(2)}) copy-start(bf16[512,1024]{1,0:T(8,128)(2,1)} %own_outer_ref.1) | copy-start | bytes 3145732
  4.3 2.6 %copy-start.3 = (bf16[128,256]{1,0:T(8,128)(2,1)S(1)}, bf16[128,256]{1,0:T(8,128)(2,1)}, u32[]{:S(2)}) copy-start(bf16[128,256]{1,0:T(8,128)(2,1)} %own_ref.3) | copy-start | bytes 196612
  4.3 2.6 %copy-start.5 = (bf16[1024,256]{1,0:T(8,128)(2,1)S(1)}, bf16[1024,256]{1,0:T(8,128)(2,1)}, u32[]{:S(2)}) copy-start(bf16[1024,256]{1,0:T(8,128)(2,1)} %w_query_ref.1) | copy-start | bytes 1572868
  4.3 2.6 %copy-start.6 = (bf16[1024,256]{1,0:T(8,128)(2,1)S(1)}, bf16[1024,256]{1,0:T(8,128)(2,1)}, u32[]{:S(2)}) copy-start(bf16[1024,256]{1,0:T(8,128)(2,1)} %w_key_ref.1) | copy-start | bytes 1572868
  4.3 2.6 %copy-start.7 = (bf16[1024,256]{1,0:T(8,128)(2,1)S(1)}, bf16[1024,256]{1,0:T(8,128)(2,1)}, u32[]{:S(2)}) copy-start(bf16[1024,256]{1,0:T(8,128)(2,1)} %w_value_ref.1) | copy-start | bytes 1572868
  4.3 2.6 %copy-start.8 = (bf16[2,64,256]{2,1,0:T(8,128)(2,1)S(1)}, bf16[2,64,256]{2,1,0:T(8,128)(2,1)}, u32[]{:S(2)}) copy-start(bf16[2,64,256]{2,1,0:T(8,128)(2,1)} %cache_keys_ref.1) | copy-start | bytes 196612
  4.3 2.6 %copy-start.9 = (bf16[2,64,256]{2,1,0:T(8,128)(2,1)S(1)}, bf16[2,64,256]{2,1,0:T(8,128)(2,1)}, u32[]{:S(2)}) copy-start(bf16[2,64,256]{2,1,0:T(8,128)(2,1)} %cache_values_ref.1) | copy-start | bytes 196612
  5.4 1.5 %copy-start.10 = (f32[1024]{0:T(1024)S(1)}, f32[1024]{0:T(1024)}, u32[]{:S(2)}) copy-start(f32[1024]{0:T(1024)} %param.16) | copy-start | bytes 12292
  5.6 3.9 %collective-permute-start.4 = (bf16[512,1024]{1,0:T(8,128)(2,1)S(1)}, bf16[512,1024]{1,0:T(8,128)(2,1)S(1)}, u32[]{:S(2)}, u32[]{:S(2)}) collective-permute-start(bf16[512,1024]{1,0:T(8,128)(2,1)S(1)} %copy-done.1), channel_id=1, source_target_pairs={{0,1},{1,0},{2,3},{3,2},{4,5},{5,4},{6,7},{7,6},{8,9},{9,8},{10,11... | collective-permute-start | bytes 3145736 | tf_op jit(solution)/shard_map/ppermute | solution.py:225
  7.0 1.6 %copy-start.2 = (bf16[256,1024]{1,0:T(8,128)(2,1)S(1)}, bf16[256,1024]{1,0:T(8,128)(2,1)}, u32[]{:S(2)}) copy-start(bf16[256,1024]{1,0:T(8,128)(2,1)} %w_out_ref.1) | copy-start | bytes 1572868
  8.1 1.3 %collective-permute-start.5 = (bf16[64,256]{1,0:T(8,128)(2,1)S(1)}, bf16[64,256]{1,0:T(8,128)(2,1)S(1)}, u32[]{:S(2)}, u32[]{:S(2)}) collective-permute-start(bf16[64,256]{1,0:T(8,128)(2,1)S(1)} %get-tuple-element.14), channel_id=1, source_target_pairs={{0,1},{1,0},{2,3},{3,2},{4,5},{5,4},{6,7},{7,6},{8,9},{9,8},{10,11... | collective-permute-start | bytes 98312 | tf_op jit(solution)/shard_map/ppermute | solution.py:225
  8.9 6.2 %copy-start = (bf16[1024,512]{1,0:T(8,128)(2,1)S(1)}, bf16[1024,512]{1,0:T(8,128)(2,1)}, u32[]{:S(2)}) copy-start(bf16[1024,512]{1,0:T(8,128)(2,1)} %own_inner_ref.1) | copy-start | bytes 3145732
  9.7 5.5 %collective-permute-start.7 = (bf16[48,1024]{1,0:T(8,128)(2,1)S(1)}, bf16[48,1024]{1,0:T(8,128)(2,1)S(1)}, u32[]{:S(2)}, u32[]{:S(2)}) collective-permute-start(bf16[48,1024]{1,0:T(8,128)(2,1)S(1)} %get-tuple-element.15.refs_0_), channel_id=1, source_target_pairs={{0,2},{1,3},{2,0},{3,1},{4,6},{5,7},{6,4},{7,5},{8,10},{9,11},{10,... | collective-permute-start | bytes 294920 | tf_op jit(solution)/shard_map/ppermute | solution.py:225
  11.0 4.0 %collective-permute-start.8 = (bf16[16,1024]{1,0:T(8,128)(2,1)S(1)}, bf16[16,1024]{1,0:T(8,128)(2,1)S(1)}, u32[]{:S(2)}, u32[]{:S(2)}) collective-permute-start(bf16[16,1024]{1,0:T(8,128)(2,1)S(1)} %get-tuple-element.16.refs_1_), channel_id=1, source_target_pairs={{0,3},{1,2},{2,1},{3,0},{4,7},{5,6},{6,5},{7,4},{8,11},{9,10},{10,... | collective-permute-start | bytes 98312 | tf_op jit(solution)/shard_map/ppermute | solution.py:225
  11.5 3.7 %copy-start.4 = (f32[1024]{0:T(1024)S(1)}, f32[1024]{0:T(1024)}, u32[]{:S(2)}) copy-start(f32[1024]{0:T(1024)} %param.17) | copy-start | bytes 12292

commit v12 on v11

--- a/solution.py
+++ b/solution.py
@@ -29,7 +29,7 @@
 
 
 def straight(replicas, share):
-    return replicas * 3 // 4 if halved(share) and replicas % 4 == 0 else replicas
+    return replicas // 2 if halved(share) and replicas % 4 == 0 else replicas
 
 
 def halved(share):

time: 30.1 us -> 29.9 us (level)
    all_to_all x1, blocking collectives: 13.1 us -> 12.8 us  [on_device(): lax.all_to_all(out.reshape(groups * 2 * replicas, -1, width), ('hi', 'lo'...]
where the time goes in v12:
time: 29.9 us; the launch traced here: 29.7 us
  blocking collectives  12.8 us (43%)
  starting transfers between devices  6.18 us (21%)
  waiting for transfers between devices  5.33 us (18%)
  Pallas kernels  4.48 us (15%)
  local copies, waits for them, and re-layouts  0.75 us (3%)
    all_to_all x1, blocking collectives, on_device(): lax.all_to_all(out.reshape(groups * 2 * replicas, -1, width), ('hi', 'lo'...  12.8 us
    ppermute x9, starting transfers between devices, swap(): return lax.ppermute(value, ('hi', 'lo'), [(i, i ^ xor) for i in range(4)])  6.18 us
    ppermute x9, waiting for transfers between devices, swap(): return lax.ppermute(value, ('hi', 'lo'), [(i, i ^ xor) for i in range(4)])  5.33 us
    pallas_call x1, Pallas kernels, on_device(): local(attend_kernel, out_shape=(shape((half, local_width), BF16), shape((...  1.14 us
    pallas_call x1, Pallas kernels, on_device(): local(functools.partial(prepare_kernel, replicas, cached), out_shape=(sha...  1.09 us
    pallas_call x1, Pallas kernels, on_device(): local(ffn_kernel, out_shape=shape((groups * 2, half, width), BF16), in_sp...  0.92 us
    unnamed x30, local copies, waits for them, and re-layouts  0.75 us
    pallas_call x1, Pallas kernels, on_device(): local(merge_kernel, out_shape=shape((replicas, share, width), BF16), in_s...  0.65 us
  transfers between devices with their start and end apart: 9, of which 5 were waited for; matrix products, arithmetic and copies ran while one was open for 0% of the time, Pallas kernels for 9%

profile of v12, /device:TPU:0, one launch (start us, length us, event | category | flops | bytes accessed | tf_op | source)
XLA Modules:
  0.0 29.7 jit_solution(18085215998672850673)
XLA Ops:
  0.0 3.0 %collective-permute-start.2 = (bf16[128,256]{1,0:T(8,128)(2,1)}, bf16[128,256]{1,0:T(8,128)(2,1)S(1)}, u32[]{:S(2)}, u32[]{:S(2)}) collective-permute-start(bf16[128,256]{1,0:T(8,128)(2,1)} %own_ref.3), channel_id=1, source_target_pairs={{0,2},{1,3},{2,0},{3,1},{4,6},{5,7},{6,4},{7,5},{8,10},{9,11},{10,... | collective-permute-start | bytes 196616 | tf_op jit(solution)/shard_map/ppermute | solution.py:225
  3.0 0.0 collective-permute-start.1
  3.0 0.1 collective-permute-start
  3.1 0.4 %collective-permute-start.6 = (bf16[256,1024]{1,0:T(8,128)(2,1)}, bf16[256,1024]{1,0:T(8,128)(2,1)S(1)}, u32[]{:S(2)}, u32[]{:S(2)}) collective-permute-start(bf16[256,1024]{1,0:T(8,128)(2,1)} %w_out_ref.1), channel_id=1, source_target_pairs={{0,1},{1,0},{2,3},{3,2},{4,5},{5,4},{6,7},{7,6},{8,9},{9,8},{10,11... | collective-permute-start | bytes 1572872 | tf_op jit(solution)/shard_map/ppermute | solution.py:225
  3.5 0.1 collective-permute-start.3
  3.6 0.7 %copy-done.11 = f32[32,4]{0,1:T(4,128)S(1)} copy-done((f32[32,4]{0,1:T(4,128)S(1)}, f32[32,4]{0,1:T(4,128)}, u32[]{:S(2)}) %copy-start.11) | copy-done | bytes 536
  4.3 0.0 copy-done.12
  4.3 0.0 copy-done.13
  4.3 0.0 copy-done.14
  4.3 0.0 copy-start.6
  4.3 0.0 copy-start.7
  4.3 0.0 copy-start.8
  4.3 0.0 copy-start.9
  4.4 1.1 %prepare.1 = (f32[2,256,128]{2,1,0:T(8,128)S(1)}, bf16[128,128]{1,0:T(8,128)(2,1)S(1)}) custom-call(f32[4,32]{1,0:T(4,128)S(1)} %bitcast.12, s32[1,2]{1,0:T(1,128)S(1)} %bitcast.13, s32[1,2]{1,0:T(1,128)S(1)} %bitcast.14, s32[1,128]{1,0:T(1,128)S(1)} %copy-done.14), custom_call_target="tpu_custom_call" | custom-call | flops 7000000000 | tf_op jit(solution)/shard_map/prepare/pallas_call | solution.py:258
  5.4 0.0 copy-start.10
  5.5 0.1 collective-permute-done.2.across_ref
  5.6 0.0 copy-done.1
  5.6 0.3 %collective-permute-start.4 = (bf16[512,1024]{1,0:T(8,128)(2,1)S(1)}, bf16[512,1024]{1,0:T(8,128)(2,1)S(1)}, u32[]{:S(2)}, u32[]{:S(2)}) collective-permute-start(bf16[512,1024]{1,0:T(8,128)(2,1)S(1)} %copy-done.1), channel_id=1, source_target_pairs={{0,1},{1,0},{2,3},{3,2},{4,5},{5,4},{6,7},{7,6},{8,9},{9,8},{10,11... | collective-permute-start | bytes 3145736 | tf_op jit(solution)/shard_map/ppermute | solution.py:225
  5.9 0.0 collective-permute-done.1.near_ref
  5.9 1.0 %collective-permute-done.far_ref = bf16[128,256]{1,0:T(8,128)(2,1)S(1)} collective-permute-done((bf16[128,256]{1,0:T(8,128)(2,1)}, bf16[128,256]{1,0:T(8,128)(2,1)S(1)}, u32[]{:S(2)}, u32[]{:S(2)}) %collective-permute-start) | collective-permute-done | bytes 65568 | tf_op jit(solution)/shard_map/ppermute | solution.py:225
  6.9 0.0 copy-done.3
  6.9 0.0 copy-done.5
  6.9 0.0 copy-done.6
  6.9 0.0 copy-done.7
  6.9 0.0 copy-done.8
  7.0 0.0 copy-done.9
  7.0 0.0 copy-done.10
  7.0 0.0 copy-start.2
  7.0 1.1 %attend.1 = (bf16[64,256]{1,0:T(8,128)(2,1)S(1)}, bf16[128,256]{1,0:T(8,128)(2,1)S(1)}) custom-call(bf16[128,256]{1,0:T(8,128)(2,1)S(1)} %copy-done.3, bf16[128,256]{1,0:T(8,128)(2,1)S(1)} %collective-permute-done.far_ref, bf16[128,256]{1,0:T(8,128)(2,1)S(1)} %collective-permute-done.1.near_ref, bf16[128,256]{1,0:T(8,128)(2,1)S(1)} %collective-permute-done.2.across_ref, ...), custom_call_target="tpu_custom_call" | custom-call | flops 40000000000 | tf_op jit(solution)/shard_map/attend/pallas_call | solution.py:271
  8.1 0.5 %collective-permute-start.5 = (bf16[64,256]{1,0:T(8,128)(2,1)S(1)}, bf16[64,256]{1,0:T(8,128)(2,1)S(1)}, u32[]{:S(2)}, u32[]{:S(2)}) collective-permute-start(bf16[64,256]{1,0:T(8,128)(2,1)S(1)} %get-tuple-element.14), channel_id=1, source_target_pairs={{0,1},{1,0},{2,3},{3,2},{4,5},{5,4},{6,7},{7,6},{8,9},{9,8},{10,11... | collective-permute-start | bytes 98312 | tf_op jit(solution)/shard_map/ppermute | solution.py:225
  8.6 0.0 copy-done.2
  8.6 0.3 %project.1.keep_ref = f32[64,1024]{1,0:T(8,128)S(1)} custom-call(bf16[128,256]{1,0:T(8,128)(2,1)S(1)} %get-tuple-element.13.context_ref, bf16[128,128]{1,0:T(8,128)(2,1)S(1)} %get-tuple-element.11.picked_ref, bf16[256,1024]{1,0:T(8,128)(2,1)S(1)} %copy-done.2), custom_call_target="tpu_custom_call" | custom-call | tf_op jit(solution)/shard_map/project/pallas_call | solution.py:290
  8.9 0.0 copy-start
  8.9 0.5 %collective-permute-done.5.near_ref = bf16[64,256]{1,0:T(8,128)(2,1)S(1)} collective-permute-done((bf16[64,256]{1,0:T(8,128)(2,1)S(1)}, bf16[64,256]{1,0:T(8,128)(2,1)S(1)}, u32[]{:S(2)}, u32[]{:S(2)}) %collective-permute-start.5) | collective-permute-done | bytes 32800 | tf_op jit(solution)/shard_map/ppermute | solution.py:225
  9.5 0.0 collective-permute-done.6.near_out_ref
  9.5 0.0 collective-permute-done.3.near_inner_ref
  9.5 0.0 collective-permute-done.4.near_outer_ref
  9.5 0.2 pair.1
  9.7 1.3 %collective-permute-start.7 = (bf16[32,1024]{1,0:T(8,128)(2,1)S(1)}, bf16[32,1024]{1,0:T(8,128)(2,1)S(1)}, u32[]{:S(2)}, u32[]{:S(2)}) collective-permute-start(bf16[32,1024]{1,0:T(8,128)(2,1)S(1)} %get-tuple-element.15.refs_0_), channel_id=1, source_target_pairs={{0,2},{1,3},{2,0},{3,1},{4,6},{5,7},{6,4},{7,5},{8,10},{9,11},{10,... | collective-permute-start | bytes 196616 | tf_op jit(solution)/shard_map/ppermute | solution.py:225
  11.0 0.5 %collective-permute-start.8 = (bf16[32,1024]{1,0:T(8,128)(2,1)S(1)}, bf16[32,1024]{1,0:T(8,128)(2,1)S(1)}, u32[]{:S(2)}, u32[]{:S(2)}) collective-permute-start(bf16[32,1024]{1,0:T(8,128)(2,1)S(1)} %get-tuple-element.16.refs_1_), channel_id=1, source_target_pairs={{0,3},{1,2},{2,1},{3,0},{4,7},{5,6},{6,5},{7,4},{8,11},{9,10},{10,... | collective-permute-start | bytes 196616 | tf_op jit(solution)/shard_map/ppermute | solution.py:225
  11.5 0.2 stream.1.stream_ref
  11.6 2.7 %collective-permute-done.7.refs_2_ = bf16[32,1024]{1,0:T(8,128)(2,1)S(1)} collective-permute-done((bf16[32,1024]{1,0:T(8,128)(2,1)S(1)}, bf16[32,1024]{1,0:T(8,128)(2,1)S(1)}, u32[]{:S(2)}, u32[]{:S(2)}) %collective-permute-start.7) | collective-permute-done | bytes 65568 | tf_op jit(solution)/shard_map/ppermute | solution.py:225
  14.3 1.0 %collective-permute-done.8.refs_3_ = bf16[32,1024]{1,0:T(8,128)(2,1)S(1)} collective-permute-done((bf16[32,1024]{1,0:T(8,128)(2,1)S(1)}, bf16[32,1024]{1,0:T(8,128)(2,1)S(1)}, u32[]{:S(2)}, u32[]{:S(2)}) %collective-permute-start.8) | collective-permute-done | bytes 65568 | tf_op jit(solution)/shard_map/ppermute | solution.py:225
  15.3 0.0 copy-done
  15.3 0.0 copy-done.4
  15.3 0.9 %ffn.1 = bf16[4,64,256]{2,1,0:T(8,128)(2,1)S(1)} custom-call(bf16[64,1024]{1,0:T(8,128)(2,1)S(1)} %stream.1.stream_ref, f32[1,1024]{1,0:T(1,128)S(1)} %bitcast.10, bf16[1024,512]{1,0:T(8,128)(2,1)S(1)} %copy-done, bf16[1024,512]{1,0:T(8,128)(2,1)S(1)} %collective-permute-done.3.near_inner_ref, bf16[512,1024]{1,0:T(8,128)(2,1)S(1)} %copy-done.1, ...), custom_call_target="tpu_custom_call" | custom-call | tf_op jit(solution)/shard_map/ffn/pallas_call | solution.py:316
  16.2 12.8 %all_to_all.5 = bf16[32,8,256]{2,1,0:T(8,128)(2,1)S(1)} all-to-all(bf16[32,8,256]{2,1,0:T(8,128)(2,1)S(1)} %bitcast.9), channel_id=1, replica_groups=mesh['rep'=8,'hi'=2,'lo'=2] {'hi','lo','rep'}, dimensions={0} | all-to-all | bytes 262144 | tf_op jit(solution)/shard_map/all_to_all | solution.py:335
  29.1 0.7 %merge.1 = bf16[8,16,256]{2,1,0:T(8,128)(2,1)} custom-call(f32[2,2,8,8,256]{4,3,2,1,0:T(8,128)S(1)} %convert.1.parts_ref), custom_call_target="tpu_custom_call" | custom-call | tf_op jit(solution)/shard_map/merge/pallas_call | solution.py:340
  (9 shorter events, 0.0 us)
Async XLA Ops:
  0.0 5.6 %collective-permute-start.2 = (bf16[128,256]{1,0:T(8,128)(2,1)}, bf16[128,256]{1,0:T(8,128)(2,1)S(1)}, u32[]{:S(2)}, u32[]{:S(2)}) collective-permute-start(bf16[128,256]{1,0:T(8,128)(2,1)} %own_ref.3), channel_id=1, source_target_pairs={{0,2},{1,3},{2,0},{3,1},{4,6},{5,7},{6,4},{7,5},{8,10},{9,11},{10,... | collective-permute-start | bytes 196616 | tf_op jit(solution)/shard_map/ppermute | solution.py:225
  3.0 3.0 %collective-permute-start.1 = (bf16[128,256]{1,0:T(8,128)(2,1)}, bf16[128,256]{1,0:T(8,128)(2,1)S(1)}, u32[]{:S(2)}, u32[]{:S(2)}) collective-permute-start(bf16[128,256]{1,0:T(8,128)(2,1)} %own_ref.3), channel_id=1, source_target_pairs={{0,1},{1,0},{2,3},{3,2},{4,5},{5,4},{6,7},{7,6},{8,9},{9,8},{10,11... | collective-permute-start | bytes 196616 | tf_op jit(solution)/shard_map/ppermute | solution.py:225
  3.0 4.0 %collective-permute-start = (bf16[128,256]{1,0:T(8,128)(2,1)}, bf16[128,256]{1,0:T(8,128)(2,1)S(1)}, u32[]{:S(2)}, u32[]{:S(2)}) collective-permute-start(bf16[128,256]{1,0:T(8,128)(2,1)} %own_ref.3), channel_id=1, source_target_pairs={{0,3},{1,2},{2,1},{3,0},{4,7},{5,6},{6,5},{7,4},{8,11},{9,10},{10,... | collective-permute-start | bytes 196616 | tf_op jit(solution)/shard_map/ppermute | solution.py:225
  3.1 6.4 %collective-permute-start.6 = (bf16[256,1024]{1,0:T(8,128)(2,1)}, bf16[256,1024]{1,0:T(8,128)(2,1)S(1)}, u32[]{:S(2)}, u32[]{:S(2)}) collective-permute-start(bf16[256,1024]{1,0:T(8,128)(2,1)} %w_out_ref.1), channel_id=1, source_target_pairs={{0,1},{1,0},{2,3},{3,2},{4,5},{5,4},{6,7},{7,6},{8,9},{9,8},{10,11... | collective-permute-start | bytes 1572872 | tf_op jit(solution)/shard_map/ppermute | solution.py:225
  3.5 6.0 %collective-permute-start.3 = (bf16[1024,512]{1,0:T(8,128)(2,1)}, bf16[1024,512]{1,0:T(8,128)(2,1)S(1)}, u32[]{:S(2)}, u32[]{:S(2)}) collective-permute-start(bf16[1024,512]{1,0:T(8,128)(2,1)} %own_inner_ref.1), channel_id=1, source_target_pairs={{0,1},{1,0},{2,3},{3,2},{4,5},{5,4},{6,7},{7,6},{8,9},{9,8},{10,11... | collective-permute-start | bytes 3145736 | tf_op jit(solution)/shard_map/ppermute | solution.py:225
  3.6 0.7 %copy-start.11 = (f32[32,4]{0,1:T(4,128)S(1)}, f32[32,4]{0,1:T(4,128)}, u32[]{:S(2)}) copy-start(f32[32,4]{0,1:T(4,128)} %param.24) | copy-start | bytes 1540
  3.6 0.7 %copy-start.12 = (s32[2,1]{0,1:T(1,128)S(1)}, s32[2,1]{0,1:T(1,128)}, u32[]{:S(2)}) copy-start(s32[2,1]{0,1:T(1,128)} %param.27) | copy-start | bytes 28
  3.6 0.7 %copy-start.13 = (s32[2,1]{0,1:T(1,128)S(1)}, s32[2,1]{0,1:T(1,128)}, u32[]{:S(2)}) copy-start(s32[2,1]{0,1:T(1,128)} %param.28) | copy-start | bytes 28
  3.6 0.7 %copy-start.14 = (s32[1,128]{1,0:T(1,128)S(1)}, s32[1,128]{1,0:T(1,128)}, u32[]{:S(2)}) copy-start(s32[1,128]{1,0:T(1,128)} %deal_ref.1) | copy-start | bytes 1540
  4.3 1.3 %copy-start.1 = (bf16[512,1024]{1,0:T(8,128)(2,1)S(1)}, bf16[512,1024]{1,0:T(8,128)(2,1)}, u32[]{:S(2)}) copy-start(bf16[512,1024]{1,0:T(8,128)(2,1)} %own_outer_ref.1) | copy-start | bytes 3145732
  4.3 2.6 %copy-start.3 = (bf16[128,256]{1,0:T(8,128)(2,1)S(1)}, bf16[128,256]{1,0:T(8,128)(2,1)}, u32[]{:S(2)}) copy-start(bf16[128,256]{1,0:T(8,128)(2,1)} %own_ref.3) | copy-start | bytes 196612
  4.3 2.6 %copy-start.5 = (bf16[1024,256]{1,0:T(8,128)(2,1)S(1)}, bf16[1024,256]{1,0:T(8,128)(2,1)}, u32[]{:S(2)}) copy-start(bf16[1024,256]{1,0:T(8,128)(2,1)} %w_query_ref.1) | copy-start | bytes 1572868
  4.3 2.6 %copy-start.6 = (bf16[1024,256]{1,0:T(8,128)(2,1)S(1)}, bf16[1024,256]{1,0:T(8,128)(2,1)}, u32[]{:S(2)}) copy-start(bf16[1024,256]{1,0:T(8,128)(2,1)} %w_key_ref.1) | copy-start | bytes 1572868
  4.3 2.6 %copy-start.7 = (bf16[1024,256]{1,0:T(8,128)(2,1)S(1)}, bf16[1024,256]{1,0:T(8,128)(2,1)}, u32[]{:S(2)}) copy-start(bf16[1024,256]{1,0:T(8,128)(2,1)} %w_value_ref.1) | copy-start | bytes 1572868
  4.3 2.6 %copy-start.8 = (bf16[2,64,256]{2,1,0:T(8,128)(2,1)S(1)}, bf16[2,64,256]{2,1,0:T(8,128)(2,1)}, u32[]{:S(2)}) copy-start(bf16[2,64,256]{2,1,0:T(8,128)(2,1)} %cache_keys_ref.1) | copy-start | bytes 196612
  4.3 2.6 %copy-start.9 = (bf16[2,64,256]{2,1,0:T(8,128)(2,1)S(1)}, bf16[2,64,256]{2,1,0:T(8,128)(2,1)}, u32[]{:S(2)}) copy-start(bf16[2,64,256]{2,1,0:T(8,128)(2,1)} %cache_values_ref.1) | copy-start | bytes 196612
  5.4 1.5 %copy-start.10 = (f32[1024]{0:T(1024)S(1)}, f32[1024]{0:T(1024)}, u32[]{:S(2)}) copy-start(f32[1024]{0:T(1024)} %param.16) | copy-start | bytes 12292
  5.6 3.9 %collective-permute-start.4 = (bf16[512,1024]{1,0:T(8,128)(2,1)S(1)}, bf16[512,1024]{1,0:T(8,128)(2,1)S(1)}, u32[]{:S(2)}, u32[]{:S(2)}) collective-permute-start(bf16[512,1024]{1,0:T(8,128)(2,1)S(1)} %copy-done.1), channel_id=1, source_target_pairs={{0,1},{1,0},{2,3},{3,2},{4,5},{5,4},{6,7},{7,6},{8,9},{9,8},{10,11... | collective-permute-start | bytes 3145736 | tf_op jit(solution)/shard_map/ppermute | solution.py:225
  7.0 1.6 %copy-start.2 = (bf16[256,1024]{1,0:T(8,128)(2,1)S(1)}, bf16[256,1024]{1,0:T(8,128)(2,1)}, u32[]{:S(2)}) copy-start(bf16[256,1024]{1,0:T(8,128)(2,1)} %w_out_ref.1) | copy-start | bytes 1572868
  8.1 1.3 %collective-permute-start.5 = (bf16[64,256]{1,0:T(8,128)(2,1)S(1)}, bf16[64,256]{1,0:T(8,128)(2,1)S(1)}, u32[]{:S(2)}, u32[]{:S(2)}) collective-permute-start(bf16[64,256]{1,0:T(8,128)(2,1)S(1)} %get-tuple-element.14), channel_id=1, source_target_pairs={{0,1},{1,0},{2,3},{3,2},{4,5},{5,4},{6,7},{7,6},{8,9},{9,8},{10,11... | collective-permute-start | bytes 98312 | tf_op jit(solution)/shard_map/ppermute | solution.py:225
  8.9 6.4 %copy-start = (bf16[1024,512]{1,0:T(8,128)(2,1)S(1)}, bf16[1024,512]{1,0:T(8,128)(2,1)}, u32[]{:S(2)}) copy-start(bf16[1024,512]{1,0:T(8,128)(2,1)} %own_inner_ref.1) | copy-start | bytes 3145732
  9.7 4.6 %collective-permute-start.7 = (bf16[32,1024]{1,0:T(8,128)(2,1)S(1)}, bf16[32,1024]{1,0:T(8,128)(2,1)S(1)}, u32[]{:S(2)}, u32[]{:S(2)}) collective-permute-start(bf16[32,1024]{1,0:T(8,128)(2,1)S(1)} %get-tuple-element.15.refs_0_), channel_id=1, source_target_pairs={{0,2},{1,3},{2,0},{3,1},{4,6},{5,7},{6,4},{7,5},{8,10},{9,11},{10,... | collective-permute-start | bytes 196616 | tf_op jit(solution)/shard_map/ppermute | solution.py:225
  11.0 4.3 %collective-permute-start.8 = (bf16[32,1024]{1,0:T(8,128)(2,1)S(1)}, bf16[32,1024]{1,0:T(8,128)(2,1)S(1)}, u32[]{:S(2)}, u32[]{:S(2)}) collective-permute-start(bf16[32,1024]{1,0:T(8,128)(2,1)S(1)} %get-tuple-element.16.refs_1_), channel_id=1, source_target_pairs={{0,3},{1,2},{2,1},{3,0},{4,7},{5,6},{6,5},{7,4},{8,11},{9,10},{10,... | collective-permute-start | bytes 196616 | tf_op jit(solution)/shard_map/ppermute | solution.py:225
  11.5 3.9 %copy-start.4 = (f32[1024]{0:T(1024)S(1)}, f32[1024]{0:T(1024)}, u32[]{:S(2)}) copy-start(f32[1024]{0:T(1024)} %param.17) | copy-start | bytes 12292

commit v13 on v12

--- a/solution.py
+++ b/solution.py
@@ -170,13 +170,10 @@
     keep_ref[...] = dot(dealt, w_out_ref[...])
 
 
-def pair_kernel(keep_ref, near_ref, near_out_ref, near_inner_ref, near_outer_ref, *pair_refs):
+def pair_kernel(start, keep_ref, near_ref, near_out_ref, near_inner_ref, near_outer_ref, pair_ref):
     del near_inner_ref, near_outer_ref
-    pair = (keep_ref[...] + dot(near_ref[...], near_out_ref[...])).astype(BF16)
-    start = 0
-    for ref in pair_refs:
-        ref[...] = pair[start : start + ref.shape[0]]
-        start += ref.shape[0]
+    rows = slice(start, start + pair_ref.shape[0])
+    pair_ref[...] = (keep_ref[rows] + dot(near_ref[rows], near_out_ref[...])).astype(BF16)
 
 
 def stream_kernel(own_ref, far_ref, near_ref, across_ref, picked_ref, stream_ref):
@@ -305,13 +302,17 @@
     cut = straight(replicas, share) * half // replicas
     sizes = (cut, half - cut) if cut < half else (half,)
     near_inner, near_outer = swap(w_inner, 1), swap(w_outer, 1)
-    pair = local(
-        pair_kernel,
-        out_shape=tuple(shape((size, model_width), BF16) for size in sizes),
-        in_specs=[VMEM] * 5,
-        out_specs=(VMEM,) * len(sizes),
-        name="pair",
-    )(keep, swap(send, 1), swap(w_out, 1), near_inner, near_outer)
+    operands = (keep, swap(send, 1), swap(w_out, 1), near_inner, near_outer)
+    pair = [
+        local(
+            functools.partial(pair_kernel, start),
+            out_shape=shape((size, model_width), BF16),
+            in_specs=[VMEM] * 5,
+            out_specs=VMEM,
+            name="pair",
+        )(*operands)
+        for start, size in zip((0, cut), sizes)
+    ]
     others = [swap(piece, xor) for piece, xor in zip(pair, (2, 3))]
     out = local(
         ffn_kernel,

time: 29.9 us -> 30 us (level)
  transfers between devices with their start and end apart: 9 -> 9, of which waited for: 5 -> 5; matrix products, arithmetic and copies ran while one was open for 0% -> 0% of each run, Pallas kernels for 9% -> 10%
where the time goes in v13:
time: 30 us; the launch traced here: 29.8 us
  blocking collectives  12.7 us (42%)
  starting transfers between devices  6.23 us (21%)
  waiting for transfers between devices  5.26 us (18%)
  Pallas kernels  4.65 us (16%)
  local copies, waits for them, and re-layouts  0.75 us (2%)
    all_to_all x1, blocking collectives, on_device(): lax.all_to_all(out.reshape(groups * 2 * replicas, -1, width), ('hi', 'lo'...  12.7 us
    ppermute x9, starting transfers between devices, swap(): return lax.ppermute(value, ('hi', 'lo'), [(i, i ^ xor) for i in range(4)])  6.23 us
    ppermute x9, waiting for transfers between devices, swap(): return lax.ppermute(value, ('hi', 'lo'), [(i, i ^ xor) for i in range(4)])  5.26 us
    pallas_call x1, Pallas kernels, on_device(): local(attend_kernel, out_shape=(shape((half, local_width), BF16), shape((...  1.14 us
    pallas_call x1, Pallas kernels, on_device(): local(functools.partial(prepare_kernel, replicas, cached), out_shape=(sha...  1.09 us
    pallas_call x1, Pallas kernels, on_device(): local(ffn_kernel, out_shape=shape((groups * 2, half, width), BF16), in_sp...  0.93 us
    unnamed x30, local copies, waits for them, and re-layouts  0.75 us
    pallas_call x1, Pallas kernels, on_device(): local(merge_kernel, out_shape=shape((replicas, share, width), BF16), in_s...  0.65 us
  transfers between devices with their start and end apart: 9, of which 5 were waited for; matrix products, arithmetic and copies ran while one was open for 0% of the time, Pallas kernels for 10%

profile of v13, /device:TPU:0, one launch (start us, length us, event | category | flops | bytes accessed | tf_op | source)
XLA Modules:
  0.0 29.8 jit_solution(1568235308676189751)
XLA Ops:
  0.0 3.0 %collective-permute-start.2 = (bf16[128,256]{1,0:T(8,128)(2,1)}, bf16[128,256]{1,0:T(8,128)(2,1)S(1)}, u32[]{:S(2)}, u32[]{:S(2)}) collective-permute-start(bf16[128,256]{1,0:T(8,128)(2,1)} %own_ref.3), channel_id=1, source_target_pairs={{0,2},{1,3},{2,0},{3,1},{4,6},{5,7},{6,4},{7,5},{8,10},{9,11},{10,... | collective-permute-start | bytes 196616 | tf_op jit(solution)/shard_map/ppermute | solution.py:222
  3.0 0.0 collective-permute-start.1
  3.0 0.1 collective-permute-start
  3.1 0.4 %collective-permute-start.6 = (bf16[256,1024]{1,0:T(8,128)(2,1)}, bf16[256,1024]{1,0:T(8,128)(2,1)S(1)}, u32[]{:S(2)}, u32[]{:S(2)}) collective-permute-start(bf16[256,1024]{1,0:T(8,128)(2,1)} %w_out_ref.1), channel_id=1, source_target_pairs={{0,1},{1,0},{2,3},{3,2},{4,5},{5,4},{6,7},{7,6},{8,9},{9,8},{10,11... | collective-permute-start | bytes 1572872 | tf_op jit(solution)/shard_map/ppermute | solution.py:222
  3.5 0.1 collective-permute-start.3
  3.6 0.7 %copy-done.11 = f32[32,4]{0,1:T(4,128)S(1)} copy-done((f32[32,4]{0,1:T(4,128)S(1)}, f32[32,4]{0,1:T(4,128)}, u32[]{:S(2)}) %copy-start.11) | copy-done | bytes 536
  4.3 0.0 copy-done.12
  4.3 0.0 copy-done.13
  4.3 0.0 copy-done.14
  4.3 0.0 copy-start.6
  4.3 0.0 copy-start.7
  4.3 0.0 copy-start.8
  4.3 0.0 copy-start.9
  4.4 1.1 %prepare.1 = (f32[2,256,128]{2,1,0:T(8,128)S(1)}, bf16[128,128]{1,0:T(8,128)(2,1)S(1)}) custom-call(f32[4,32]{1,0:T(4,128)S(1)} %bitcast.12, s32[1,2]{1,0:T(1,128)S(1)} %bitcast.13, s32[1,2]{1,0:T(1,128)S(1)} %bitcast.14, s32[1,128]{1,0:T(1,128)S(1)} %copy-done.14), custom_call_target="tpu_custom_call" | custom-call | flops 7000000000 | tf_op jit(solution)/shard_map/prepare/pallas_call | solution.py:255
  5.4 0.0 copy-start.10
  5.5 0.1 collective-permute-done.2.across_ref
  5.6 0.0 copy-done.1
  5.6 0.3 %collective-permute-start.4 = (bf16[512,1024]{1,0:T(8,128)(2,1)S(1)}, bf16[512,1024]{1,0:T(8,128)(2,1)S(1)}, u32[]{:S(2)}, u32[]{:S(2)}) collective-permute-start(bf16[512,1024]{1,0:T(8,128)(2,1)S(1)} %copy-done.1), channel_id=1, source_target_pairs={{0,1},{1,0},{2,3},{3,2},{4,5},{5,4},{6,7},{7,6},{8,9},{9,8},{10,11... | collective-permute-start | bytes 3145736 | tf_op jit(solution)/shard_map/ppermute | solution.py:222
  5.9 0.0 collective-permute-done.1.near_ref
  5.9 1.0 %collective-permute-done.far_ref = bf16[128,256]{1,0:T(8,128)(2,1)S(1)} collective-permute-done((bf16[128,256]{1,0:T(8,128)(2,1)}, bf16[128,256]{1,0:T(8,128)(2,1)S(1)}, u32[]{:S(2)}, u32[]{:S(2)}) %collective-permute-start) | collective-permute-done | bytes 65568 | tf_op jit(solution)/shard_map/ppermute | solution.py:222
  6.9 0.0 copy-done.3
  6.9 0.0 copy-done.5
  6.9 0.0 copy-done.6
  6.9 0.0 copy-done.7
  6.9 0.0 copy-done.8
  7.0 0.0 copy-done.9
  7.0 0.0 copy-done.10
  7.0 0.0 copy-start.2
  7.0 1.1 %attend.1 = (bf16[64,256]{1,0:T(8,128)(2,1)S(1)}, bf16[128,256]{1,0:T(8,128)(2,1)S(1)}) custom-call(bf16[128,256]{1,0:T(8,128)(2,1)S(1)} %copy-done.3, bf16[128,256]{1,0:T(8,128)(2,1)S(1)} %collective-permute-done.far_ref, bf16[128,256]{1,0:T(8,128)(2,1)S(1)} %collective-permute-done.1.near_ref, bf16[128,256]{1,0:T(8,128)(2,1)S(1)} %collective-permute-done.2.across_ref, ...), custom_call_target="tpu_custom_call" | custom-call | flops 40000000000 | tf_op jit(solution)/shard_map/attend/pallas_call | solution.py:268
  8.1 0.5 %collective-permute-start.5 = (bf16[64,256]{1,0:T(8,128)(2,1)S(1)}, bf16[64,256]{1,0:T(8,128)(2,1)S(1)}, u32[]{:S(2)}, u32[]{:S(2)}) collective-permute-start(bf16[64,256]{1,0:T(8,128)(2,1)S(1)} %get-tuple-element.12), channel_id=1, source_target_pairs={{0,1},{1,0},{2,3},{3,2},{4,5},{5,4},{6,7},{7,6},{8,9},{9,8},{10,11... | collective-permute-start | bytes 98312 | tf_op jit(solution)/shard_map/ppermute | solution.py:222
  8.6 0.0 copy-done.2
  8.6 0.3 %project.1.keep_ref = f32[64,1024]{1,0:T(8,128)S(1)} custom-call(bf16[128,256]{1,0:T(8,128)(2,1)S(1)} %get-tuple-element.11.context_ref, bf16[128,128]{1,0:T(8,128)(2,1)S(1)} %get-tuple-element.9.picked_ref, bf16[256,1024]{1,0:T(8,128)(2,1)S(1)} %copy-done.2), custom_call_target="tpu_custom_call" | custom-call | tf_op jit(solution)/shard_map/project/pallas_call | solution.py:287
  8.9 0.6 %collective-permute-done.5.near_ref = bf16[64,256]{1,0:T(8,128)(2,1)S(1)} collective-permute-done((bf16[64,256]{1,0:T(8,128)(2,1)S(1)}, bf16[64,256]{1,0:T(8,128)(2,1)S(1)}, u32[]{:S(2)}, u32[]{:S(2)}) %collective-permute-start.5) | collective-permute-done | bytes 32800 | tf_op jit(solution)/shard_map/ppermute | solution.py:222
  9.5 0.0 collective-permute-done.6.near_out_ref
  9.5 0.0 collective-permute-done.3.near_inner_ref
  9.5 0.0 collective-permute-done.4.near_outer_ref
  9.5 0.2 pair.2.refs_0_
  9.7 1.3 %collective-permute-start.7 = (bf16[32,1024]{1,0:T(8,128)(2,1)S(1)}, bf16[32,1024]{1,0:T(8,128)(2,1)S(1)}, u32[]{:S(2)}, u32[]{:S(2)}) collective-permute-start(bf16[32,1024]{1,0:T(8,128)(2,1)S(1)} %pair.2.refs_0_), channel_id=1, source_target_pairs={{0,2},{1,3},{2,0},{3,1},{4,6},{5,7},{6,4},{7,5},{8,10},{9,11},{10,... | collective-permute-start | bytes 196616 | tf_op jit(solution)/shard_map/ppermute | solution.py:222
  11.0 0.2 pair.3.refs_1_
  11.1 0.5 %collective-permute-start.8 = (bf16[32,1024]{1,0:T(8,128)(2,1)S(1)}, bf16[32,1024]{1,0:T(8,128)(2,1)S(1)}, u32[]{:S(2)}, u32[]{:S(2)}) collective-permute-start(bf16[32,1024]{1,0:T(8,128)(2,1)S(1)} %pair.3.refs_1_), channel_id=1, source_target_pairs={{0,3},{1,2},{2,1},{3,0},{4,7},{5,6},{6,5},{7,4},{8,11},{9,10},{10,... | collective-permute-start | bytes 196616 | tf_op jit(solution)/shard_map/ppermute | solution.py:222
  11.7 0.2 stream.1.stream_ref
  11.9 2.2 %collective-permute-done.7.refs_2_ = bf16[32,1024]{1,0:T(8,128)(2,1)S(1)} collective-permute-done((bf16[32,1024]{1,0:T(8,128)(2,1)S(1)}, bf16[32,1024]{1,0:T(8,128)(2,1)S(1)}, u32[]{:S(2)}, u32[]{:S(2)}) %collective-permute-start.7) | collective-permute-done | bytes 65568 | tf_op jit(solution)/shard_map/ppermute | solution.py:222
  14.1 1.4 %collective-permute-done.8.refs_3_ = bf16[32,1024]{1,0:T(8,128)(2,1)S(1)} collective-permute-done((bf16[32,1024]{1,0:T(8,128)(2,1)S(1)}, bf16[32,1024]{1,0:T(8,128)(2,1)S(1)}, u32[]{:S(2)}, u32[]{:S(2)}) %collective-permute-start.8) | collective-permute-done | bytes 65568 | tf_op jit(solution)/shard_map/ppermute | solution.py:222
  15.4 0.0 copy-done
  15.4 0.0 copy-done.4
  15.4 0.9 %ffn.1 = bf16[4,64,256]{2,1,0:T(8,128)(2,1)S(1)} custom-call(bf16[64,1024]{1,0:T(8,128)(2,1)S(1)} %stream.1.stream_ref, f32[1,1024]{1,0:T(1,128)S(1)} %bitcast.10, bf16[1024,512]{1,0:T(8,128)(2,1)S(1)} %copy-done, bf16[1024,512]{1,0:T(8,128)(2,1)S(1)} %collective-permute-done.3.near_inner_ref, bf16[512,1024]{1,0:T(8,128)(2,1)S(1)} %copy-done.1, ...), custom_call_target="tpu_custom_call" | custom-call | tf_op jit(solution)/shard_map/ffn/pallas_call | solution.py:317
  16.4 12.7 %all_to_all.5 = bf16[32,8,256]{2,1,0:T(8,128)(2,1)S(1)} all-to-all(bf16[32,8,256]{2,1,0:T(8,128)(2,1)S(1)} %bitcast.9), channel_id=1, replica_groups=mesh['rep'=8,'hi'=2,'lo'=2] {'hi','lo','rep'}, dimensions={0} | all-to-all | bytes 262144 | tf_op jit(solution)/shard_map/all_to_all | solution.py:336
  29.1 0.7 %merge.1 = bf16[8,16,256]{2,1,0:T(8,128)(2,1)} custom-call(f32[2,2,8,8,256]{4,3,2,1,0:T(8,128)S(1)} %convert.1.parts_ref), custom_call_target="tpu_custom_call" | custom-call | tf_op jit(solution)/shard_map/merge/pallas_call | solution.py:341
  (10 shorter events, 0.0 us)
Async XLA Ops:
  0.0 5.6 %collective-permute-start.2 = (bf16[128,256]{1,0:T(8,128)(2,1)}, bf16[128,256]{1,0:T(8,128)(2,1)S(1)}, u32[]{:S(2)}, u32[]{:S(2)}) collective-permute-start(bf16[128,256]{1,0:T(8,128)(2,1)} %own_ref.3), channel_id=1, source_target_pairs={{0,2},{1,3},{2,0},{3,1},{4,6},{5,7},{6,4},{7,5},{8,10},{9,11},{10,... | collective-permute-start | bytes 196616 | tf_op jit(solution)/shard_map/ppermute | solution.py:222
  3.0 3.0 %collective-permute-start.1 = (bf16[128,256]{1,0:T(8,128)(2,1)}, bf16[128,256]{1,0:T(8,128)(2,1)S(1)}, u32[]{:S(2)}, u32[]{:S(2)}) collective-permute-start(bf16[128,256]{1,0:T(8,128)(2,1)} %own_ref.3), channel_id=1, source_target_pairs={{0,1},{1,0},{2,3},{3,2},{4,5},{5,4},{6,7},{7,6},{8,9},{9,8},{10,11... | collective-permute-start | bytes 196616 | tf_op jit(solution)/shard_map/ppermute | solution.py:222
  3.0 4.0 %collective-permute-start = (bf16[128,256]{1,0:T(8,128)(2,1)}, bf16[128,256]{1,0:T(8,128)(2,1)S(1)}, u32[]{:S(2)}, u32[]{:S(2)}) collective-permute-start(bf16[128,256]{1,0:T(8,128)(2,1)} %own_ref.3), channel_id=1, source_target_pairs={{0,3},{1,2},{2,1},{3,0},{4,7},{5,6},{6,5},{7,4},{8,11},{9,10},{10,... | collective-permute-start | bytes 196616 | tf_op jit(solution)/shard_map/ppermute | solution.py:222
  3.1 6.4 %collective-permute-start.6 = (bf16[256,1024]{1,0:T(8,128)(2,1)}, bf16[256,1024]{1,0:T(8,128)(2,1)S(1)}, u32[]{:S(2)}, u32[]{:S(2)}) collective-permute-start(bf16[256,1024]{1,0:T(8,128)(2,1)} %w_out_ref.1), channel_id=1, source_target_pairs={{0,1},{1,0},{2,3},{3,2},{4,5},{5,4},{6,7},{7,6},{8,9},{9,8},{10,11... | collective-permute-start | bytes 1572872 | tf_op jit(solution)/shard_map/ppermute | solution.py:222
  3.5 6.0 %collective-permute-start.3 = (bf16[1024,512]{1,0:T(8,128)(2,1)}, bf16[1024,512]{1,0:T(8,128)(2,1)S(1)}, u32[]{:S(2)}, u32[]{:S(2)}) collective-permute-start(bf16[1024,512]{1,0:T(8,128)(2,1)} %own_inner_ref.1), channel_id=1, source_target_pairs={{0,1},{1,0},{2,3},{3,2},{4,5},{5,4},{6,7},{7,6},{8,9},{9,8},{10,11... | collective-permute-start | bytes 3145736 | tf_op jit(solution)/shard_map/ppermute | solution.py:222
  3.6 0.7 %copy-start.11 = (f32[32,4]{0,1:T(4,128)S(1)}, f32[32,4]{0,1:T(4,128)}, u32[]{:S(2)}) copy-start(f32[32,4]{0,1:T(4,128)} %param.24) | copy-start | bytes 1540
  3.6 0.7 %copy-start.12 = (s32[2,1]{0,1:T(1,128)S(1)}, s32[2,1]{0,1:T(1,128)}, u32[]{:S(2)}) copy-start(s32[2,1]{0,1:T(1,128)} %param.27) | copy-start | bytes 28
  3.6 0.7 %copy-start.13 = (s32[2,1]{0,1:T(1,128)S(1)}, s32[2,1]{0,1:T(1,128)}, u32[]{:S(2)}) copy-start(s32[2,1]{0,1:T(1,128)} %param.28) | copy-start | bytes 28
  3.6 0.7 %copy-start.14 = (s32[1,128]{1,0:T(1,128)S(1)}, s32[1,128]{1,0:T(1,128)}, u32[]{:S(2)}) copy-start(s32[1,128]{1,0:T(1,128)} %deal_ref.1) | copy-start | bytes 1540
  4.3 1.3 %copy-start.1 = (bf16[512,1024]{1,0:T(8,128)(2,1)S(1)}, bf16[512,1024]{1,0:T(8,128)(2,1)}, u32[]{:S(2)}) copy-start(bf16[512,1024]{1,0:T(8,128)(2,1)} %own_outer_ref.1) | copy-start | bytes 3145732
  4.3 2.6 %copy-start.3 = (bf16[128,256]{1,0:T(8,128)(2,1)S(1)}, bf16[128,256]{1,0:T(8,128)(2,1)}, u32[]{:S(2)}) copy-start(bf16[128,256]{1,0:T(8,128)(2,1)} %own_ref.3) | copy-start | bytes 196612
  4.3 2.6 %copy-start.5 = (bf16[1024,256]{1,0:T(8,128)(2,1)S(1)}, bf16[1024,256]{1,0:T(8,128)(2,1)}, u32[]{:S(2)}) copy-start(bf16[1024,256]{1,0:T(8,128)(2,1)} %w_query_ref.1) | copy-start | bytes 1572868
  4.3 2.6 %copy-start.6 = (bf16[1024,256]{1,0:T(8,128)(2,1)S(1)}, bf16[1024,256]{1,0:T(8,128)(2,1)}, u32[]{:S(2)}) copy-start(bf16[1024,256]{1,0:T(8,128)(2,1)} %w_key_ref.1) | copy-start | bytes 1572868
  4.3 2.6 %copy-start.7 = (bf16[1024,256]{1,0:T(8,128)(2,1)S(1)}, bf16[1024,256]{1,0:T(8,128)(2,1)}, u32[]{:S(2)}) copy-start(bf16[1024,256]{1,0:T(8,128)(2,1)} %w_value_ref.1) | copy-start | bytes 1572868
  4.3 2.6 %copy-start.8 = (bf16[2,64,256]{2,1,0:T(8,128)(2,1)S(1)}, bf16[2,64,256]{2,1,0:T(8,128)(2,1)}, u32[]{:S(2)}) copy-start(bf16[2,64,256]{2,1,0:T(8,128)(2,1)} %cache_keys_ref.1) | copy-start | bytes 196612
  4.3 2.6 %copy-start.9 = (bf16[2,64,256]{2,1,0:T(8,128)(2,1)S(1)}, bf16[2,64,256]{2,1,0:T(8,128)(2,1)}, u32[]{:S(2)}) copy-start(bf16[2,64,256]{2,1,0:T(8,128)(2,1)} %cache_values_ref.1) | copy-start | bytes 196612
  5.4 1.5 %copy-start.10 = (f32[1024]{0:T(1024)S(1)}, f32[1024]{0:T(1024)}, u32[]{:S(2)}) copy-start(f32[1024]{0:T(1024)} %param.16) | copy-start | bytes 12292
  5.6 3.9 %collective-permute-start.4 = (bf16[512,1024]{1,0:T(8,128)(2,1)S(1)}, bf16[512,1024]{1,0:T(8,128)(2,1)S(1)}, u32[]{:S(2)}, u32[]{:S(2)}) collective-permute-start(bf16[512,1024]{1,0:T(8,128)(2,1)S(1)} %copy-done.1), channel_id=1, source_target_pairs={{0,1},{1,0},{2,3},{3,2},{4,5},{5,4},{6,7},{7,6},{8,9},{9,8},{10,11... | collective-permute-start | bytes 3145736 | tf_op jit(solution)/shard_map/ppermute | solution.py:222
  7.0 1.6 %copy-start.2 = (bf16[256,1024]{1,0:T(8,128)(2,1)S(1)}, bf16[256,1024]{1,0:T(8,128)(2,1)}, u32[]{:S(2)}) copy-start(bf16[256,1024]{1,0:T(8,128)(2,1)} %w_out_ref.1) | copy-start | bytes 1572868
  8.1 1.3 %collective-permute-start.5 = (bf16[64,256]{1,0:T(8,128)(2,1)S(1)}, bf16[64,256]{1,0:T(8,128)(2,1)S(1)}, u32[]{:S(2)}, u32[]{:S(2)}) collective-permute-start(bf16[64,256]{1,0:T(8,128)(2,1)S(1)} %get-tuple-element.12), channel_id=1, source_target_pairs={{0,1},{1,0},{2,3},{3,2},{4,5},{5,4},{6,7},{7,6},{8,9},{9,8},{10,11... | collective-permute-start | bytes 98312 | tf_op jit(solution)/shard_map/ppermute | solution.py:222
  9.7 5.8 %copy-start = (bf16[1024,512]{1,0:T(8,128)(2,1)S(1)}, bf16[1024,512]{1,0:T(8,128)(2,1)}, u32[]{:S(2)}) copy-start(bf16[1024,512]{1,0:T(8,128)(2,1)} %own_inner_ref.1) | copy-start | bytes 3145732
  9.7 4.4 %collective-permute-start.7 = (bf16[32,1024]{1,0:T(8,128)(2,1)S(1)}, bf16[32,1024]{1,0:T(8,128)(2,1)S(1)}, u32[]{:S(2)}, u32[]{:S(2)}) collective-permute-start(bf16[32,1024]{1,0:T(8,128)(2,1)S(1)} %pair.2.refs_0_), channel_id=1, source_target_pairs={{0,2},{1,3},{2,0},{3,1},{4,6},{5,7},{6,4},{7,5},{8,10},{9,11},{10,... | collective-permute-start | bytes 196616 | tf_op jit(solution)/shard_map/ppermute | solution.py:222
  11.1 4.3 %collective-permute-start.8 = (bf16[32,1024]{1,0:T(8,128)(2,1)S(1)}, bf16[32,1024]{1,0:T(8,128)(2,1)S(1)}, u32[]{:S(2)}, u32[]{:S(2)}) collective-permute-start(bf16[32,1024]{1,0:T(8,128)(2,1)S(1)} %pair.3.refs_1_), channel_id=1, source_target_pairs={{0,3},{1,2},{2,1},{3,0},{4,7},{5,6},{6,5},{7,4},{8,11},{9,10},{10,... | collective-permute-start | bytes 196616 | tf_op jit(solution)/shard_map/ppermute | solution.py:222
  11.7 3.8 %copy-start.4 = (f32[1024]{0:T(1024)S(1)}, f32[1024]{0:T(1024)}, u32[]{:S(2)}) copy-start(f32[1024]{0:T(1024)} %param.17) | copy-start | bytes 12292
